TPU v7x, 32 devices: a whole 2x2x4 slice. The times are simulated.
32 devices in a mesh: dp: 2 (over x), dom: 16 (over z, y, core).
Axes of the slice: x: 2, y: 2, z: 4, core: 2. Of those that a mesh axis runs over, the one named last changes fastest.
Arguments:
- features: bfloat16 [2, 16384, 256], P('dp', 'dom'), may hold values from -6 to 6
- send_order: int32 [16, 1024], P('dom'), may hold values from 0 to 1023, each once within a row
- adj_count: int32 [128], P('dom'), may hold values from 2 to 4, as said below
- adj_target: int32 [128, 4], P('dom'), may hold values from 6 to 17, as said below
- adj_vals: bfloat16 [128, 4, 128, 128], P('dom'), may hold values from -0.3125 to 0.3125
- w_edge: bfloat16 [256, 256], replicated, may hold values from -0.375 to 0.375
- w_node: bfloat16 [512, 256], replicated, may hold values from -0.25 to 0.25
- cotangent: bfloat16 [2, 16384, 256], P('dp', 'dom'), may hold values from -6 to 6
Outputs:
- node_out: bfloat16 [2, 16384, 256], P('dp', 'dom')
- grad_features: bfloat16 [2, 16384, 256], P('dp', 'dom')
- grad_edge: float32 [256, 256], replicated
- grad_node: float32 [512, 256], replicated
Inputs may be any that keep to these rules, and one draw needn't show every extreme that they name: Each row of send_order is a permutation of 0 to 1023. `adj_count`: every partition has its own most count, reached by one of its blocks; some partition's most is 4. `adj_target`: targets lie in the own partition's blocks or in the last 2 blocks of the previous partition or the first 2 blocks of the next one; slot 0 of each partition's first column block targets the previous partition, and slot 1 of its last column block targets the next one.
All inputs are finite; a program needn't handle non-finite values.
Results may differ from a plain program's by a relative error of at most 0.009.
Values may be sent and summed in bfloat16 or wider, within the bound.
No kernel may reach another device: no remote copies, remote signals or barrier semaphores. Data moves between devices by JAX's collectives and lax.ppermute only.
A program may use at most 64 MiB of HBM per device.

v0:
```python
import functools
import math

import jax
import jax.numpy as jnp
from jax import lax
from jax.experimental import pallas as pl
from jax.experimental.pallas import tpu as pltpu
from jax.sharding import PartitionSpec as P

ROWS = 128
RIM = 2
ANY = pl.BlockSpec(memory_space=pl.ANY)
VMEM = pl.BlockSpec(memory_space=pltpu.VMEM)
SMEM = pl.BlockSpec(memory_space=pltpu.SMEM)
BF16 = jnp.bfloat16
F32 = jnp.float32
MIB = 1024 * 1024
CORE, ALONG_Y, ALONG_Z = 1, 2, 4


def swapped(x, axis, mask):
    peers = lax.axis_size(axis)
    return lax.ppermute(x, axis, [(i, i ^ mask) for i in range(peers)])


def swapped_across(x, axis):
    peers = lax.axis_size(axis)
    return lax.ppermute(x, axis, [(i, (i + 1 if i % 2 else i - 1) % peers) for i in range(peers)])


def dot(a, b, contract=((1,), (0,))):
    return lax.dot_general(a, b, (contract, ((), ())), preferred_element_type=F32)


def shape(*dims, dtype=BF16):
    return jax.ShapeDtypeStruct(dims, dtype)


def call(body, outs, args, specs=None, scratch=(), flops=0, nbytes=0, limit=24 * MIB):
    return pl.pallas_call(
        body,
        out_shape=outs,
        in_specs=specs or [VMEM] * len(args),
        out_specs=[VMEM] * len(outs),
        scratch_shapes=list(scratch),
        cost_estimate=pl.CostEstimate(flops=flops, bytes_accessed=nbytes, transcendentals=0),
        compiler_params=pltpu.CompilerParams(vmem_limit_bytes=limit),
    )(*args)


def pick_body(order_hbm, feat_hbm, out_ref, order_ref, feat_ref, hot_ref, order_sem, feat_sem):
    rows = feat_ref.shape[0]
    early = hot_ref.shape[0] // ROWS
    load_order = pltpu.make_async_copy(order_hbm, order_ref, order_sem)
    load_feat = pltpu.make_async_copy(feat_hbm, feat_ref, feat_sem)
    load_order.start()
    load_feat.start()
    lane = lax.broadcasted_iota(jnp.int32, (ROWS, rows), 1).astype(F32)
    load_order.wait()

    def hot_rows(k):
        row = order_ref[:, k * ROWS : (k + 1) * ROWS].astype(F32)
        col = jnp.transpose(jnp.broadcast_to(row, (ROWS, ROWS)))
        wide = jnp.concatenate([col] * (rows // ROWS), axis=1)
        return jnp.where(wide == lane, 1.0, 0.0).astype(BF16)

    for k in range(early):
        hot_ref[k * ROWS : (k + 1) * ROWS, :] = hot_rows(k)
    load_feat.wait()
    feat = feat_ref[...]
    for k in range(rows // ROWS):
        mine = slice(k * ROWS, (k + 1) * ROWS)
        hot = hot_ref[mine, :] if k < early else hot_rows(k)
        out_ref[mine, :] = dot(hot, feat).astype(BF16)


def build_body(cnt_ref, tgt_ref, vals_ref, own_ref, rim_ref, at_ref, a_ref):
    blocks, slots = vals_ref.shape[:2]
    spare = blocks + 2 * RIM
    a_ref[...] = jnp.zeros_like(a_ref)
    at_ref[...] = jnp.zeros_like(at_ref)
    for c in range(blocks):
        mine = slice(c * ROWS, (c + 1) * ROWS)
        for s in range(slots):
            w = tgt_ref[c, s]
            at = jnp.where(w < blocks, w + RIM, jnp.where(w < 2 * blocks, w - blocks, w - blocks + RIM))
            at = jnp.where(s < cnt_ref[c], at, spare)
            value = vals_ref[c, s].astype(F32)
            a_ref[at, :, mine] = (a_ref[at, :, mine].astype(F32) + value).astype(BF16)
            lanes = pl.ds(pl.multiple_of(at * ROWS, ROWS), ROWS)
            at_ref[mine, lanes] = (at_ref[mine, lanes].astype(F32) + jnp.transpose(value)).astype(BF16)
    own_ref[...] = a_ref[:blocks]
    rim_ref[...] = a_ref[blocks:spare]


def chosen(first, second):
    odd = lax.rem(lax.axis_index("dom"), 2) == 1
    return jnp.where(odd, first, second), jnp.where(odd, second, first)


def message_body(nodes_ref, a_hbm, w_edge_ref, near_ref, far_ref, msg_ref, a_ref, a_sem):
    rows = nodes_ref.shape[0]
    rim = RIM * ROWS
    load = pltpu.make_async_copy(a_hbm, a_ref, a_sem)
    load.start()
    for k in range(rows // rim):
        mine = slice(k * rim, (k + 1) * rim)
        pre = dot(nodes_ref[mine, :], w_edge_ref[...])
        msg_ref[mine, :] = (pre * jax.nn.sigmoid(pre)).astype(BF16)
    load.wait()
    sums = dot(a_ref[...].reshape(2 * rim, rows), msg_ref[...])
    near, far = chosen(sums[:rim], sums[rim:])
    near_ref[...] = near.astype(BF16)
    far_ref[...] = far.astype(BF16)


def node_step(nodes, agg, gout, w_node):
    width = nodes.shape[1]
    pre = dot(nodes, w_node[:width]) + dot(agg, w_node[width:])
    sig = jax.nn.sigmoid(pre)
    out = (nodes.astype(F32) + pre * sig).astype(BF16)
    gout = gout.astype(F32)
    d_node = (gout * (sig * (1.0 + pre * (1.0 - sig)))).astype(BF16)
    back = dot(d_node, w_node, ((1,), (1,)))
    return out, d_node, gout + back[:, :width], back[:, width:].astype(BF16)


def own_body(
    nodes_ref, msg_ref, a_hbm, cot_ref, w_node_ref,
    own_ref, out_ref, agg_ref, d_node_ref, d_nodes1_ref, d_agg_ref, a_ref, a_sems,
):
    rows, width = nodes_ref.shape
    rim = RIM * ROWS
    msg = msg_ref[...]
    loads = []
    for k in range(rows // rim):
        part = pl.ds(k * RIM, RIM)
        loads.append(pltpu.make_async_copy(a_hbm.at[part], a_ref.at[part], a_sems.at[k]))
        loads[k].start()
    for k in range(rows // rim):
        mine = slice(k * rim, (k + 1) * rim)
        loads[k].wait()
        window = dot(a_ref[k * RIM : (k + 1) * RIM].reshape(rim, rows), msg).astype(BF16)
        if k == 0:
            own_ref[:rim, :] = window
        elif k == rows // rim - 1:
            own_ref[rim:, :] = window
        else:
            here = slice((k - 1) * rim, k * rim)
            agg_ref[here, :] = window
            out, d_node, d_nodes1, d_agg = node_step(nodes_ref[mine, :], window, cot_ref[mine, :], w_node_ref[...])
            out_ref[here, :] = out
            d_node_ref[here, :] = d_node
            d_nodes1_ref[here, :] = d_nodes1
            d_agg_ref[here, :] = d_agg


def rim_body(
    nodes_ref, own_ref, near_in_ref, far_in_ref, cot_ref, w_node_ref,
    near_ref, far_ref, out_ref, agg_ref, d_node_ref, d_nodes1_ref, d_agg_ref,
):
    rows = nodes_ref.shape[0]
    rim = RIM * ROWS
    arrived = chosen(near_in_ref[...].astype(F32), far_in_ref[...].astype(F32))
    rims = []
    for k in range(2):
        mine = slice(k * (rows - rim), k * (rows - rim) + rim)
        here = slice(k * rim, (k + 1) * rim)
        agg = (own_ref[here, :].astype(F32) + arrived[k]).astype(BF16)
        agg_ref[here, :] = agg
        out, d_node, d_nodes1, d_agg = node_step(nodes_ref[mine, :], agg, cot_ref[mine, :], w_node_ref[...])
        out_ref[here, :] = out
        d_node_ref[here, :] = d_node
        d_nodes1_ref[here, :] = d_nodes1
        d_agg_ref[here, :] = d_agg
        rims.append(d_agg)
    near_ref[...], far_ref[...] = chosen(rims[0], rims[1])


def in_order(mid_ref, rim_ref):
    rim = RIM * ROWS
    return jnp.concatenate([rim_ref[:rim, :], mid_ref[...], rim_ref[rim:, :]], axis=0)


def grad_node_body(scale, nodes_ref, agg_mid_ref, agg_rim_ref, d_node_mid_ref, d_node_rim_ref, *out_refs):
    width = nodes_ref.shape[1]
    d_node = in_order(d_node_mid_ref, d_node_rim_ref)
    agg = in_order(agg_mid_ref, agg_rim_ref)
    first = lax.axis_index("dp") == 0
    for k, left in enumerate((nodes_ref[...], agg)):
        mine = slice(k * width, (k + 1) * width)
        grad = dot(left, d_node, ((0,), (0,))) * scale
        if len(out_refs) == 1:
            out_refs[0][mine, :] = grad
            continue
        half = width // 2
        out_refs[0][mine, :] = jnp.where(first, grad[:, :half], grad[:, half:])
        out_refs[1][mine, :] = jnp.where(first, grad[:, half:], grad[:, :half]).astype(BF16)


def behind_body(
    nodes_ref, at_ref, w_edge_ref, out_mid_ref, out_rim_ref, d_agg_mid_ref, d_agg_rim_ref,
    out_ref, d_msg_ref, slope_ref,
):
    rows = nodes_ref.shape[0]
    rim = RIM * ROWS
    out_ref[...] = in_order(out_mid_ref, out_rim_ref)
    d_agg = in_order(d_agg_mid_ref, d_agg_rim_ref)
    for k in range(rows // rim):
        mine = slice(k * rim, (k + 1) * rim)
        d_msg_ref[mine, :] = dot(at_ref[mine, :rows], d_agg)
        pre = dot(nodes_ref[mine, :], w_edge_ref[...])
        sig = jax.nn.sigmoid(pre)
        slope_ref[mine, :] = sig * (1.0 + pre * (1.0 - sig))


def edge_body(
    scale, nodes_ref, at_ref, near_ref, far_ref, d_msg_ref, slope_ref, mid_ref, rim_ref, w_edge_ref,
    back_ref, g_edge_ref, d_edge_ref,
):
    rows, width = nodes_ref.shape
    rim = RIM * ROWS
    prev, after = chosen(near_ref[...], far_ref[...])
    rims = jnp.concatenate([prev, after], axis=0)
    w_edge = w_edge_ref[...]
    for k in range(rows // rim):
        mine = slice(k * rim, (k + 1) * rim)
        d_msg = d_msg_ref[mine, :] + dot(at_ref[mine, rows : rows + 2 * rim], rims)
        d_edge = (d_msg.astype(BF16).astype(F32) * slope_ref[mine, :]).astype(BF16)
        d_edge_ref[mine, :] = d_edge
        if k == 0:
            d_nodes1 = rim_ref[:rim, :]
        elif k == rows // rim - 1:
            d_nodes1 = rim_ref[rim:, :]
        else:
            d_nodes1 = mid_ref[(k - 1) * rim : k * rim, :]
        back_ref[mine, :] = (d_nodes1 + dot(d_edge, w_edge, ((1,), (1,)))).astype(BF16)
    g_edge_ref[...] = dot(nodes_ref[...], d_edge_ref[...], ((0,), (0,))) * scale


def bit_of(mask):
    return lax.rem(lax.div(lax.axis_index("dom"), mask), 2)


def cut_rows(total_ref, mask, keep_ref, send_ref):
    size = keep_ref.shape[0]
    bit = bit_of(mask)
    keep_ref[...] = total_ref[pl.ds(pl.multiple_of(bit * size, 16), size), :]
    send_ref[...] = total_ref[pl.ds(pl.multiple_of((1 - bit) * size, 16), size), :].astype(BF16)


def first_cut_body(mask, edge_ref, node_ref, node_in_ref, keep_ref, send_ref, total_ref):
    half = node_ref.shape[1]
    few, more = edge_ref.shape[0] // 4, node_ref.shape[0] // 4
    for q in range(4):
        row = q * (2 * few + more)
        mine = slice(q * more, (q + 1) * more)
        total_ref[row : row + more, :] = node_ref[mine, :] + node_in_ref[mine, :].astype(F32)
        row += more
        mine = slice(q * few, (q + 1) * few)
        total_ref[row : row + few, :] = edge_ref[mine, :half]
        total_ref[row + few : row + 2 * few, :] = edge_ref[mine, half:]
    cut_rows(total_ref, mask, keep_ref, send_ref)


def next_cut_body(mask, mine_ref, in_ref, keep_ref, send_ref, total_ref):
    total_ref[...] = mine_ref[...] + in_ref[...].astype(F32)
    cut_rows(total_ref, mask, keep_ref, send_ref)


def sum_body(mine_ref, in_ref, out_ref):
    out_ref[...] = (mine_ref[...].astype(F32) + in_ref[...].astype(F32)).astype(BF16)


def join_lanes_body(mine_ref, in_ref, out_ref):
    size, half = mine_ref.shape
    more = size // 2
    few = more // 2
    first = lax.axis_index("dp") == 0
    mine, other = mine_ref[:more, :], in_ref[:more, :]
    out_ref[few:, :half] = jnp.where(first, mine, other)
    out_ref[few:, half:] = jnp.where(first, other, mine)
    total = (mine_ref[more:, :].astype(F32) + in_ref[more:, :].astype(F32)).astype(BF16)
    out_ref[:few, :half] = total[:few]
    out_ref[:few, half:] = total[few:]


def join_rows_body(mask, mine_ref, in_ref, out_ref):
    size = mine_ref.shape[0]
    low = bit_of(mask) == 0
    mine, other = mine_ref[...], in_ref[...]
    out_ref[:size, :] = jnp.where(low, mine, other)
    out_ref[size:, :] = jnp.where(low, other, mine)


def finish_body(mask, mine_ref, in_ref, edge_ref, node_ref):
    few, more = edge_ref.shape[0] // 4, node_ref.shape[0] // 4
    low = bit_of(mask) == 0
    mine, other = mine_ref[...].astype(F32), in_ref[...].astype(F32)
    for side, value in enumerate((jnp.where(low, mine, other), jnp.where(low, other, mine))):
        for part in range(2):
            q = 2 * side + part
            row = part * (few + more)
            edge_ref[q * few : (q + 1) * few, :] = value[row : row + few]
            node_ref[q * more : (q + 1) * more, :] = value[row + few : row + few + more]


def cut_before(edge_part, node_part):
    half = node_part[0].shape[1]
    size = node_part[0].shape[0] + 2 * edge_part.shape[0]

    def cut(body, mask, args, size):
        return call(
            functools.partial(body, mask),
            [shape(size // 2, half, dtype=F32), shape(size // 2, half)],
            args,
            scratch=[pltpu.VMEM((size, half), F32)],
        )

    keep, send = cut(first_cut_body, CORE, (edge_part, *node_part), size)
    return cut(next_cut_body, ALONG_Y, (keep, swapped(send, "dom", CORE)), size // 2)


def reduced(keep, send, back, width):
    quarter, half = keep.shape
    few = width // 4
    (mine,) = call(sum_body, [shape(quarter, half)], (keep, swapped(send, "dom", ALONG_Y)))
    for mask in (ALONG_Z, 2 * ALONG_Z):
        (mine,) = call(sum_body, [shape(quarter, half)], (mine, swapped(mine, "dom", mask)))
    (mine,) = call(join_lanes_body, [shape(3 * few, width)], (mine, swapped(mine, "dp", 1)))
    mine, back = lax.optimization_barrier((mine, back))
    (mine,) = call(
        functools.partial(join_rows_body, ALONG_Y), [shape(6 * few, width)], (mine, swapped(mine, "dom", ALONG_Y))
    )
    grad_edge, grad_node = call(
        functools.partial(finish_body, CORE),
        [shape(width, width, dtype=F32), shape(2 * width, width, dtype=F32)],
        (mine, swapped(mine, "dom", CORE)),
    )
    return grad_edge, grad_node, back


def place_body(order_ref, back_ref, out_ref):
    rows = back_ref.shape[0]
    back = back_ref[...]
    order = jnp.broadcast_to(order_ref[...], (ROWS, rows))
    for k in range(rows // ROWS):
        mine = slice(k * ROWS, (k + 1) * ROWS)
        row = lax.broadcasted_iota(jnp.int32, (ROWS, rows), 0) + k * ROWS
        hot = jnp.where(order == row, 1.0, 0.0).astype(BF16)
        out_ref[mine, :] = dot(hot, back).astype(BF16)


def shards(features, send_order, adj_count, adj_target, adj_vals, w_edge, w_node, cotangent):
    ndp = lax.axis_size("dp")
    ndom = lax.axis_size("dom")
    rows, width = features.shape[1:]
    per_peer = rows // ndom
    blocks, slots = adj_vals.shape[:2]
    rim = RIM * ROWS
    scale = 1.0 / math.sqrt(float(ndp * rows * ndom))
    tall = shape(rows, width)
    tall_f = shape(rows, width, dtype=F32)
    edge = shape(rim, width)
    rims = shape(2 * rim, width)
    mid = shape(rows - 2 * rim, width)
    unit = rows * width * 2
    square = 2 * rows * width * width

    (picked,) = call(
        pick_body,
        [tall],
        (send_order, features[0]),
        [ANY, ANY],
        [
            pltpu.VMEM((1, rows), jnp.int32),
            pltpu.VMEM((rows, width), BF16),
            pltpu.VMEM((2 * ROWS, rows), BF16),
            pltpu.SemaphoreType.DMA,
            pltpu.SemaphoreType.DMA,
        ],
        flops=2 * rows * rows * width,
        nbytes=2 * unit,
        limit=56 * MIB,
    )
    nodes = lax.all_to_all(
        picked.reshape(ndom, per_peer, width), "dom", split_axis=0, concat_axis=0, tiled=True
    ).reshape(rows, width)
    spots = blocks + 2 * RIM + 1
    adj, adj_rim, adj_t = call(
        build_body,
        [shape(blocks, ROWS, rows), shape(2 * RIM, ROWS, rows), shape(rows, spots * ROWS)],
        (adj_count, adj_target, adj_vals),
        [SMEM, SMEM, VMEM],
        [pltpu.VMEM((spots, ROWS, rows), BF16)],
        nbytes=16 * unit,
    )
    near, far, msg = call(
        message_body,
        [edge, edge, tall],
        (nodes, adj_rim, w_edge),
        [VMEM, ANY, VMEM],
        [pltpu.VMEM((2 * RIM, ROWS, rows), BF16), pltpu.SemaphoreType.DMA],
        flops=square + 4 * rim * rows * width,
        nbytes=4 * unit,
    )
    far = swapped_across(far, "dom")
    near = swapped(near, "dom", 1)
    cot = cotangent[0]
    own, out_mid, agg_mid, d_node_mid, d_nodes1_mid, d_agg_mid = call(
        own_body,
        [rims, mid, mid, mid, shape(*mid.shape, dtype=F32), mid],
        (nodes, msg, adj, cot, w_node),
        [VMEM, VMEM, ANY, VMEM, VMEM],
        [pltpu.VMEM((blocks, ROWS, rows), BF16), pltpu.SemaphoreType.DMA((rows // rim,))],
        flops=2 * rows * rows * width + 2 * square,
        nbytes=8 * unit,
    )
    near, far, out_rim, agg_rim, d_node_rim, d_nodes1_rim, d_agg_rim = call(
        rim_body,
        [edge, edge, rims, rims, rims, shape(*rims.shape, dtype=F32), rims],
        (nodes, own, near, far, cot, w_node),
        flops=2 * square,
        nbytes=4 * unit,
    )
    far = swapped_across(far, "dom")
    near = swapped(near, "dom", 1)
    tiled = ndp == 2 and ndom == 16

    node_part = call(
        functools.partial(grad_node_body, scale),
        [shape(2 * width, width // 2, dtype=F32), shape(2 * width, width // 2)]
        if tiled
        else [shape(2 * width, width, dtype=F32)],
        (nodes, agg_mid, agg_rim, d_node_mid, d_node_rim),
        flops=2 * square,
        nbytes=3 * unit,
    )
    if tiled:
        node_part = (node_part[0], swapped(node_part[1], "dp", 1))
    node_out, d_msg, slope = call(
        behind_body,
        [tall, tall_f, tall_f],
        (nodes, adj_t, w_edge, out_mid, out_rim, d_agg_mid, d_agg_rim),
        flops=2 * rows * rows * width + square,
        nbytes=8 * unit,
    )
    back, edge_part = call(
        functools.partial(edge_body, scale),
        [tall, shape(width, width, dtype=F32)],
        (nodes, adj_t, near, far, d_msg, slope, d_nodes1_mid, d_nodes1_rim, w_edge),
        scratch=[pltpu.VMEM((rows, width), BF16)],
        flops=2 * square + 4 * rim * rows * width,
        nbytes=8 * unit,
    )
    if tiled:
        keep, send = cut_before(edge_part, node_part)
        back, send = lax.optimization_barrier((back, send))
    back = lax.all_to_all(
        back.reshape(ndom, per_peer, width), "dom", split_axis=0, concat_axis=0, tiled=True
    ).reshape(rows, width)
    if tiled:
        grad_edge, grad_node, back = reduced(keep, send, back, width)
    else:
        grad_edge, grad_node = (lax.psum(part, ("dp", "dom")) for part in (edge_part, node_part[0]))
    (grad_brick,) = call(place_body, [tall], (send_order, back), flops=2 * rows * rows * width, nbytes=2 * unit)
    return (node_out[None], grad_brick[None], grad_edge, grad_node)


def solution(mesh):
    in_specs = (
        P("dp", "dom", None),
        P("dom", None),
        P("dom"),
        P("dom", None),
        P("dom", None, None, None),
        P(),
        P(),
        P("dp", "dom", None),
    )
    out_specs = (P("dp", "dom", None), P("dp", "dom", None), P(), P())
    return jax.shard_map(shards, mesh=mesh, in_specs=in_specs, out_specs=out_specs, check_vma=False)
```

profile of v0, /device:TPU:0, one launch (start us, length us, event | category | flops | bytes accessed | tf_op | source)
XLA Modules:
  0.0 79.8 jit_solution(12367065185864032286)
XLA Ops:
  0.6 0.0 copy-start.3
  0.6 0.0 copy-start.7
  0.7 0.0 copy-start.2
  0.7 2.7 %shard_map.111 = bf16[1024,256]{1,0:T(8,128)(2,1)} custom-call(s32[1,1024]{1,0:T(1,128)} %order_ref.1, bf16[1024,256]{1,0:T(8,128)(2,1)} %bitcast.18), custom_call_target="tpu_custom_call" | custom-call | flops 536870912 | bytes 1048576 | tf_op jit(solution)/shard_map/pallas_call | solution.py:41
  3.4 7.4 %all-to-all-start = ((bf16[16,64,256]{2,1,0:T(8,128)(2,1)}), bf16[16,64,256]{2,1,0:T(8,128)(2,1)S(1)}, u32[]{:S(2)}, u32[]{:S(2)}) async-start(bf16[16,64,256]{2,1,0:T(8,128)(2,1)} %bitcast.17), calls=%async_computation | async-start | bytes 1048576 | tf_op jit(solution)/shard_map/all_to_all | solution.py:387
  10.8 0.8 copy.12.tgt_ref
  11.5 0.0 copy-start.4
  11.5 1.2 %copy-done.4 = bf16[8,4,128,128]{3,2,1,0:T(8,128)(2,1)S(1)} copy-done((bf16[8,4,128,128]{3,2,1,0:T(8,128)(2,1)S(1)}, bf16[8,4,128,128]{3,2,1,0:T(8,128)(2,1)}, u32[]{:S(2)}) %copy-start.4) | copy-done | bytes 1048600
  12.8 0.0 copy-start.8
  12.8 0.7 copy-done.8
  13.4 2.2 %shard_map.112 = (bf16[8,128,1024]{2,1,0:T(8,128)(2,1)S(1)}, bf16[4,128,1024]{2,1,0:T(8,128)(2,1)S(1)}, bf16[1024,1664]{1,0:T(8,128)(2,1)S(1)}) custom-call(s32[8]{0:T(128)S(1)} %copy-done.8, s32[8,4]{1,0:T(8,128)S(1)} %copy.12.tgt_ref, bf16[8,4,128,128]{3,2,1,0:T(8,128)(2,1)S(1)} %copy-done.4), custom_call_target="tpu_custom_call" | custom-call | bytes 8388608 | tf_op jit(solution)/shard_map/pallas_call | solution.py:41
  15.7 0.0 copy-start
  15.7 1.7 %copy-done = bf16[1024,1664]{1,0:T(8,128)(2,1)} copy-done((bf16[1024,1664]{1,0:T(8,128)(2,1)}, bf16[1024,1664]{1,0:T(8,128)(2,1)S(1)}, u32[]{:S(2)}) %copy-start) | copy-done | bytes 3407896
  17.4 0.0 copy-start.5
  17.4 1.0 %copy-done.5 = bf16[4,128,1024]{2,1,0:T(8,128)(2,1)} copy-done((bf16[4,128,1024]{2,1,0:T(8,128)(2,1)}, bf16[4,128,1024]{2,1,0:T(8,128)(2,1)S(1)}, u32[]{:S(2)}) %copy-start.5) | copy-done | bytes 1048600
  18.3 6.9 %all-to-all-done = bf16[16,64,256]{2,1,0:T(8,128)(2,1)S(1)} async-done(((bf16[16,64,256]{2,1,0:T(8,128)(2,1)}), bf16[16,64,256]{2,1,0:T(8,128)(2,1)S(1)}, u32[]{:S(2)}, u32[]{:S(2)}) %all-to-all-start) | async-done | bytes 524320 | tf_op jit(solution)/shard_map/all_to_all | solution.py:387
  25.2 0.0 copy-done.3
  25.2 0.0 copy-start.6
  25.2 1.2 %copy-done.6 = bf16[4,128,1024]{2,1,0:T(8,128)(2,1)S(1)} copy-done((bf16[4,128,1024]{2,1,0:T(8,128)(2,1)S(1)}, bf16[4,128,1024]{2,1,0:T(8,128)(2,1)}, u32[]{:S(2)}) %copy-start.6) | copy-done | bytes 1048600
  26.5 0.8 %shard_map.113 = (bf16[256,256]{1,0:T(8,128)(2,1)S(1)}, bf16[256,256]{1,0:T(8,128)(2,1)S(1)}, bf16[1024,256]{1,0:T(8,128)(2,1)S(1)}) custom-call(bf16[1024,256]{1,0:T(8,128)(2,1)S(1)} %bitcast.8, bf16[4,128,1024]{2,1,0:T(8,128)(2,1)S(1)} %copy-done.6, bf16[256,256]{1,0:T(8,128)(2,1)S(1)} %copy-done.3), custom_call_target="tpu_custom_call" | custom-call | flops 402653184 | bytes 2097152 | tf_op jit(solution)/shard_map/pallas_call | solution.py:41
  27.3 0.1 collective-permute-start
  27.4 2.8 %collective-permute-start.1 = (bf16[256,256]{1,0:T(8,128)(2,1)S(1)}, bf16[256,256]{1,0:T(8,128)(2,1)S(1)}, u32[]{:S(2)}, u32[]{:S(2)}) collective-permute-start(bf16[256,256]{1,0:T(8,128)(2,1)S(1)} %get-tuple-element.47), channel_id=1, source_target_pairs={{0,15},{1,2},{2,1},{3,4},{4,3},{5,6},{6,5},{7,8},{8,7},{9,10},{10,... | collective-permute-start | bytes 393224 | tf_op jit(solution)/shard_map/ppermute | solution.py:29
  30.2 0.0 copy-done.7
  30.2 0.0 copy-done.2
  30.2 0.0 copy-start.1
  30.2 2.6 %shard_map.114 = (bf16[512,256]{1,0:T(8,128)(2,1)S(1)}, bf16[512,256]{1,0:T(8,128)(2,1)S(1)}, bf16[512,256]{1,0:T(8,128)(2,1)S(1)}, bf16[512,256]{1,0:T(8,128)(2...) custom-call(bf16[1024,256]{1,0:T(8,128)(2,1)S(1)} %bitcast.9, ...), custom_call_target="tpu_custom_call" | custom-call | flops 805306368 | bytes 4194304 | tf_op jit(solution)/shard_map/pallas_call | solution.py:41
  32.8 0.0 collective-permute-done.near_in_ref
  32.9 1.7 %collective-permute-done.1.far_in_ref = bf16[256,256]{1,0:T(8,128)(2,1)S(1)} collective-permute-done((bf16[256,256]{1,0:T(8,128)(2,1)S(1)}, bf16[256,256]{1,0:T(8,128)(2,1)S(1)}, u32[]{:S(2)}, u32[]{:S(2)}) %collective-permute-start.1) | collective-permute-done | bytes 131104 | tf_op jit(solution)/shard_map/ppermute | solution.py:29
  34.5 0.7 shard_map.115
  35.2 0.1 collective-permute-start.2
  35.3 2.8 %collective-permute-start.3 = (bf16[256,256]{1,0:T(8,128)(2,1)S(1)}, bf16[256,256]{1,0:T(8,128)(2,1)S(1)}, u32[]{:S(2)}, u32[]{:S(2)}) collective-permute-start(bf16[256,256]{1,0:T(8,128)(2,1)S(1)} %get-tuple-element.53), channel_id=1, source_target_pairs={{0,15},{1,2},{2,1},{3,4},{4,3},{5,6},{6,5},{7,8},{8,7},{9,10},{10,... | collective-permute-start | bytes 393224 | tf_op jit(solution)/shard_map/ppermute | solution.py:29
  38.1 0.5 shard_map.118
  38.6 1.6 %collective-permute-start.4 = (bf16[512,128]{1,0:T(8,128)(2,1)S(1)}, bf16[512,128]{1,0:T(8,128)(2,1)S(1)}, u32[]{:S(2)}, u32[]{:S(2)}) collective-permute-start(bf16[512,128]{1,0:T(8,128)(2,1)S(1)} %get-tuple-element.64), channel_id=1, source_target_pairs={{0,16},{16,0},{1,17},{17,1},{2,18},{18,2},{3,19},{19,3},{4,20},{20... | collective-permute-start | bytes 393224 | tf_op jit(solution)/shard_map/ppermute | solution.py:24
  40.2 0.0 copy-done.1
  40.2 1.6 %shard_map.116 = (bf16[1024,256]{1,0:T(8,128)(2,1)}, f32[1024,256]{1,0:T(8,128)S(1)}, f32[1024,256]{1,0:T(8,128)S(1)}) custom-call(bf16[1024,256]{1,0:T(8,128)(2,1)S(1)} %bitcast.12, bf16[1024,1664]{1,0:T(8,128)(2,1)S(1)} %copy-done.1, bf16[256,256]{1,0:T(8,128)(2,1)S(1)} %copy-done.3, bf16[512,256]{1,0:T(8,128)(2,1)S(1)} %get-tuple-element.44.out_mid_ref, ...), custom_call_target="tpu_custom_call" | custom-call | flops 671088640 | bytes 4194304 | tf_op jit(solution)/shard_map/pallas_call | solution.py:41
  41.8 0.0 collective-permute-done.2.near_ref
  41.8 0.7 collective-permute-done.3.far_ref
  42.5 0.0 copy-start.9
  42.5 1.8 %shard_map.117 = (bf16[1024,256]{1,0:T(8,128)(2,1)}, f32[256,256]{1,0:T(8,128)S(1)}) custom-call(bf16[1024,256]{1,0:T(8,128)(2,1)S(1)} %bitcast.13, bf16[1024,1664]{1,0:T(8,128)(2,1)S(1)} %copy-done.1, bf16[256,256]{1,0:T(8,128)(2,1)S(1)} %collective-permute-done.2.near_ref, bf16[256,256]{1,0:T(8,128)(2,1)S(1)} %collective-permute-done.3.far_ref, ...), custom_call_target="tpu_custom_call" | custom-call | flops 536870912 | bytes 4194304 | tf_op jit(solution)/shard_map/pallas_call | solution.py:41
  44.2 0.0 collective-permute-done.4.node_in_ref
  44.2 0.1 shard_map.119
  44.3 0.1 collective-permute-start.5
  44.4 1.3 %collective-permute-done.5.in_ref = bf16[512,128]{1,0:T(8,128)(2,1)S(1)} collective-permute-done((bf16[512,128]{1,0:T(8,128)(2,1)S(1)}, bf16[512,128]{1,0:T(8,128)(2,1)S(1)}, u32[]{:S(2)}, u32[]{:S(2)}) %collective-permute-start.5) | collective-permute-done | bytes 131104 | tf_op jit(solution)/shard_map/ppermute | solution.py:24
  45.8 4.2 %all-to-all-start.1 = ((bf16[16,64,256]{2,1,0:T(8,128)(2,1)}), bf16[16,64,256]{2,1,0:T(8,128)(2,1)S(1)}, u32[]{:S(2)}, u32[]{:S(2)}) async-start(bf16[16,64,256]{2,1,0:T(8,128)(2,1)} %bitcast.5), calls=%async_computation.1 | async-start | bytes 1048576 | tf_op jit(solution)/shard_map/all_to_all | solution.py:460
  50.0 1.9 %collective-permute-start.6 = (bf16[256,128]{1,0:T(8,128)(2,1)S(1)}, bf16[256,128]{1,0:T(8,128)(2,1)S(1)}, u32[]{:S(2)}, u32[]{:S(2)}) collective-permute-start(bf16[256,128]{1,0:T(8,128)(2,1)S(1)} %get-tuple-element.70), channel_id=1, source_target_pairs={{0,2},{1,3},{2,0},{3,1},{4,6},{5,7},{6,4},{7,5},{8,10},{9,11},{10,... | collective-permute-start | bytes 196616 | tf_op jit(solution)/shard_map/ppermute | solution.py:24
  51.9 5.7 %collective-permute-done.6.in_ref = bf16[256,128]{1,0:T(8,128)(2,1)S(1)} collective-permute-done((bf16[256,128]{1,0:T(8,128)(2,1)S(1)}, bf16[256,128]{1,0:T(8,128)(2,1)S(1)}, u32[]{:S(2)}, u32[]{:S(2)}) %collective-permute-start.6) | collective-permute-done | bytes 65568 | tf_op jit(solution)/shard_map/ppermute | solution.py:24
  57.6 1.0 %collective-permute-start.7 = (bf16[256,128]{1,0:T(8,128)(2,1)S(1)}, bf16[256,128]{1,0:T(8,128)(2,1)S(1)}, u32[]{:S(2)}, u32[]{:S(2)}) collective-permute-start(bf16[256,128]{1,0:T(8,128)(2,1)S(1)} %shard_map.121.mine_ref), channel_id=1, source_target_pairs={{0,4},{1,5},{2,6},{3,7},{4,0},{5,1},{6,2},{7,3},{8,12},{9,13},{10,... | collective-permute-start | bytes 196616 | tf_op jit(solution)/shard_map/ppermute | solution.py:24
  58.6 3.6 %collective-permute-done.7.in_ref = bf16[256,128]{1,0:T(8,128)(2,1)S(1)} collective-permute-done((bf16[256,128]{1,0:T(8,128)(2,1)S(1)}, bf16[256,128]{1,0:T(8,128)(2,1)S(1)}, u32[]{:S(2)}, u32[]{:S(2)}) %collective-permute-start.7) | collective-permute-done | bytes 65568 | tf_op jit(solution)/shard_map/ppermute | solution.py:24
  62.2 3.3 %collective-permute-start.8 = (bf16[256,128]{1,0:T(8,128)(2,1)S(1)}, bf16[256,128]{1,0:T(8,128)(2,1)S(1)}, u32[]{:S(2)}, u32[]{:S(2)}) collective-permute-start(bf16[256,128]{1,0:T(8,128)(2,1)S(1)} %shard_map.122.mine_ref), channel_id=1, source_target_pairs={{0,8},{1,9},{2,10},{3,11},{4,12},{5,13},{6,14},{7,15},{8,0},{9,1},... | collective-permute-start | bytes 196616 | tf_op jit(solution)/shard_map/ppermute | solution.py:24
  65.5 2.5 %collective-permute-done.8.in_ref = bf16[256,128]{1,0:T(8,128)(2,1)S(1)} collective-permute-done((bf16[256,128]{1,0:T(8,128)(2,1)S(1)}, bf16[256,128]{1,0:T(8,128)(2,1)S(1)}, u32[]{:S(2)}, u32[]{:S(2)}) %collective-permute-start.8) | collective-permute-done | bytes 65568 | tf_op jit(solution)/shard_map/ppermute | solution.py:24
  68.1 1.6 %collective-permute-start.9 = (bf16[256,128]{1,0:T(8,128)(2,1)S(1)}, bf16[256,128]{1,0:T(8,128)(2,1)S(1)}, u32[]{:S(2)}, u32[]{:S(2)}) collective-permute-start(bf16[256,128]{1,0:T(8,128)(2,1)S(1)} %shard_map.123.mine_ref), channel_id=1, source_target_pairs={{0,16},{16,0},{1,17},{17,1},{2,18},{18,2},{3,19},{19,3},{4,20},{20... | collective-permute-start | bytes 196616 | tf_op jit(solution)/shard_map/ppermute | solution.py:24
  69.7 2.8 %collective-permute-done.9.in_ref = bf16[256,128]{1,0:T(8,128)(2,1)S(1)} collective-permute-done((bf16[256,128]{1,0:T(8,128)(2,1)S(1)}, bf16[256,128]{1,0:T(8,128)(2,1)S(1)}, u32[]{:S(2)}, u32[]{:S(2)}) %collective-permute-start.9) | collective-permute-done | bytes 65568 | tf_op jit(solution)/shard_map/ppermute | solution.py:24
  72.5 0.0 all-to-all-done.1
  72.5 1.5 %collective-permute-start.10 = (bf16[192,256]{1,0:T(8,128)(2,1)S(1)}, bf16[192,256]{1,0:T(8,128)(2,1)S(1)}, u32[]{:S(2)}, u32[]{:S(2)}) collective-permute-start(bf16[192,256]{1,0:T(8,128)(2,1)S(1)} %shard_map.124.mine_ref), channel_id=1, source_target_pairs={{0,2},{1,3},{2,0},{3,1},{4,6},{5,7},{6,4},{7,5},{8,10},{9,11},{10,... | collective-permute-start | bytes 294920 | tf_op jit(solution)/shard_map/ppermute | solution.py:24
  74.0 3.1 %collective-permute-done.10.in_ref = bf16[192,256]{1,0:T(8,128)(2,1)S(1)} collective-permute-done((bf16[192,256]{1,0:T(8,128)(2,1)S(1)}, bf16[192,256]{1,0:T(8,128)(2,1)S(1)}, u32[]{:S(2)}, u32[]{:S(2)}) %collective-permute-start.10) | collective-permute-done | bytes 98336 | tf_op jit(solution)/shard_map/ppermute | solution.py:24
  77.2 0.1 collective-permute-start.11
  77.3 0.0 copy-done.9
  77.3 1.5 %shard_map.125 = bf16[1024,256]{1,0:T(8,128)(2,1)} custom-call(s32[1,1024]{1,0:T(1,128)S(1)} %copy-done.9, bf16[1024,256]{1,0:T(8,128)(2,1)S(1)} %bitcast.16), custom_call_target="tpu_custom_call" | custom-call | flops 536870912 | bytes 1048576 | tf_op jit(solution)/shard_map/pallas_call | solution.py:41
  78.8 0.0 collective-permute-done.11.in_ref
  78.8 1.0 %shard_map.127 = (f32[256,256]{1,0:T(8,128)}, f32[512,256]{1,0:T(8,128)}) custom-call(bf16[384,256]{1,0:T(8,128)(2,1)S(1)} %shard_map.126.mine_ref, bf16[384,256]{1,0:T(8,128)(2,1)S(1)} %collective-permute-done.11.in_ref), custom_call_target="tpu_custom_call" | custom-call | tf_op jit(solution)/shard_map/pallas_call | solution.py:41
  (6 shorter events, 0.1 us)
Async XLA Ops:
  0.6 24.6 %copy-start.3 = (bf16[256,256]{1,0:T(8,128)(2,1)S(1)}, bf16[256,256]{1,0:T(8,128)(2,1)}, u32[]{:S(2)}) copy-start(bf16[256,256]{1,0:T(8,128)(2,1)} %w_edge_ref.5) | copy-start | bytes 393220
  0.6 29.6 %copy-start.7 = (bf16[512,256]{1,0:T(8,128)(2,1)S(1)}, bf16[512,256]{1,0:T(8,128)(2,1)}, u32[]{:S(2)}) copy-start(bf16[512,256]{1,0:T(8,128)(2,1)} %w_node_ref.3) | copy-start | bytes 786436
  0.7 29.6 %copy-start.2 = (bf16[1,1024,256]{2,1,0:T(8,128)(2,1)S(1)}, bf16[1,1024,256]{2,1,0:T(8,128)(2,1)}, u32[]{:S(2)}) copy-start(bf16[1,1024,256]{2,1,0:T(8,128)(2,1)} %param.15) | copy-start | bytes 1572868
  3.4 21.9 %all-to-all-start = ((bf16[16,64,256]{2,1,0:T(8,128)(2,1)}), bf16[16,64,256]{2,1,0:T(8,128)(2,1)S(1)}, u32[]{:S(2)}, u32[]{:S(2)}) async-start(bf16[16,64,256]{2,1,0:T(8,128)(2,1)} %bitcast.17), calls=%async_computation | async-start | bytes 1048576 | tf_op jit(solution)/shard_map/all_to_all | solution.py:387
  11.5 1.2 %copy-start.4 = (bf16[8,4,128,128]{3,2,1,0:T(8,128)(2,1)S(1)}, bf16[8,4,128,128]{3,2,1,0:T(8,128)(2,1)}, u32[]{:S(2)}) copy-start(bf16[8,4,128,128]{3,2,1,0:T(8,128)(2,1)} %vals_ref.1) | copy-start | bytes 3145732
  12.8 0.7 copy-start.8
  15.7 1.7 %copy-start = (bf16[1024,1664]{1,0:T(8,128)(2,1)}, bf16[1024,1664]{1,0:T(8,128)(2,1)S(1)}, u32[]{:S(2)}) copy-start(bf16[1024,1664]{1,0:T(8,128)(2,1)S(1)} %get-tuple-element.40.at_ref) | copy-start | bytes 10223620
  17.4 1.0 %copy-start.5 = (bf16[4,128,1024]{2,1,0:T(8,128)(2,1)}, bf16[4,128,1024]{2,1,0:T(8,128)(2,1)S(1)}, u32[]{:S(2)}) copy-start(bf16[4,128,1024]{2,1,0:T(8,128)(2,1)S(1)} %get-tuple-element.41.a_hbm) | copy-start | bytes 3145732
  25.2 1.2 %copy-start.6 = (bf16[4,128,1024]{2,1,0:T(8,128)(2,1)S(1)}, bf16[4,128,1024]{2,1,0:T(8,128)(2,1)}, u32[]{:S(2)}) copy-start(bf16[4,128,1024]{2,1,0:T(8,128)(2,1)} %copy-done.5) | copy-start | bytes 3145732
  27.3 5.5 %collective-permute-start = (bf16[256,256]{1,0:T(8,128)(2,1)S(1)}, bf16[256,256]{1,0:T(8,128)(2,1)S(1)}, u32[]{:S(2)}, u32[]{:S(2)}) collective-permute-start(bf16[256,256]{1,0:T(8,128)(2,1)S(1)} %get-tuple-element.46), channel_id=1, source_target_pairs={{0,1},{1,0},{2,3},{3,2},{4,5},{5,4},{6,7},{7,6},{8,9},{9,8},{10,11... | collective-permute-start | bytes 393224 | tf_op jit(solution)/shard_map/ppermute | solution.py:24
  27.4 7.2 %collective-permute-start.1 = (bf16[256,256]{1,0:T(8,128)(2,1)S(1)}, bf16[256,256]{1,0:T(8,128)(2,1)S(1)}, u32[]{:S(2)}, u32[]{:S(2)}) collective-permute-start(bf16[256,256]{1,0:T(8,128)(2,1)S(1)} %get-tuple-element.47), channel_id=1, source_target_pairs={{0,15},{1,2},{2,1},{3,4},{4,3},{5,6},{6,5},{7,8},{8,7},{9,10},{10,... | collective-permute-start | bytes 393224 | tf_op jit(solution)/shard_map/ppermute | solution.py:29
  30.2 10.0 %copy-start.1 = (bf16[1024,1664]{1,0:T(8,128)(2,1)S(1)}, bf16[1024,1664]{1,0:T(8,128)(2,1)}, u32[]{:S(2)}) copy-start(bf16[1024,1664]{1,0:T(8,128)(2,1)} %copy-done) | copy-start | bytes 10223620
  35.2 6.6 %collective-permute-start.2 = (bf16[256,256]{1,0:T(8,128)(2,1)S(1)}, bf16[256,256]{1,0:T(8,128)(2,1)S(1)}, u32[]{:S(2)}, u32[]{:S(2)}) collective-permute-start(bf16[256,256]{1,0:T(8,128)(2,1)S(1)} %get-tuple-element.52), channel_id=1, source_target_pairs={{0,1},{1,0},{2,3},{3,2},{4,5},{5,4},{6,7},{7,6},{8,9},{9,8},{10,11... | collective-permute-start | bytes 393224 | tf_op jit(solution)/shard_map/ppermute | solution.py:24
  35.3 7.2 %collective-permute-start.3 = (bf16[256,256]{1,0:T(8,128)(2,1)S(1)}, bf16[256,256]{1,0:T(8,128)(2,1)S(1)}, u32[]{:S(2)}, u32[]{:S(2)}) collective-permute-start(bf16[256,256]{1,0:T(8,128)(2,1)S(1)} %get-tuple-element.53), channel_id=1, source_target_pairs={{0,15},{1,2},{2,1},{3,4},{4,3},{5,6},{6,5},{7,8},{8,7},{9,10},{10,... | collective-permute-start | bytes 393224 | tf_op jit(solution)/shard_map/ppermute | solution.py:29
  38.6 5.6 %collective-permute-start.4 = (bf16[512,128]{1,0:T(8,128)(2,1)S(1)}, bf16[512,128]{1,0:T(8,128)(2,1)S(1)}, u32[]{:S(2)}, u32[]{:S(2)}) collective-permute-start(bf16[512,128]{1,0:T(8,128)(2,1)S(1)} %get-tuple-element.64), channel_id=1, source_target_pairs={{0,16},{16,0},{1,17},{17,1},{2,18},{18,2},{3,19},{19,3},{4,20},{20... | collective-permute-start | bytes 393224 | tf_op jit(solution)/shard_map/ppermute | solution.py:24
  42.5 34.8 %copy-start.9 = (s32[1,1024]{1,0:T(1,128)S(1)}, s32[1,1024]{1,0:T(1,128)}, u32[]{:S(2)}) copy-start(s32[1,1024]{1,0:T(1,128)} %order_ref.1) | copy-start | bytes 12292
  44.3 1.4 %collective-permute-start.5 = (bf16[512,128]{1,0:T(8,128)(2,1)S(1)}, bf16[512,128]{1,0:T(8,128)(2,1)S(1)}, u32[]{:S(2)}, u32[]{:S(2)}) collective-permute-start(bf16[512,128]{1,0:T(8,128)(2,1)S(1)} %get-tuple-element.66), channel_id=1, source_target_pairs={{0,1},{1,0},{2,3},{3,2},{4,5},{5,4},{6,7},{7,6},{8,9},{9,8},{10,11... | collective-permute-start | bytes 393224 | tf_op jit(solution)/shard_map/ppermute | solution.py:24
  45.8 26.7 %all-to-all-start.1 = ((bf16[16,64,256]{2,1,0:T(8,128)(2,1)}), bf16[16,64,256]{2,1,0:T(8,128)(2,1)S(1)}, u32[]{:S(2)}, u32[]{:S(2)}) async-start(bf16[16,64,256]{2,1,0:T(8,128)(2,1)} %bitcast.5), calls=%async_computation.1 | async-start | bytes 1048576 | tf_op jit(solution)/shard_map/all_to_all | solution.py:460
  50.0 7.6 %collective-permute-start.6 = (bf16[256,128]{1,0:T(8,128)(2,1)S(1)}, bf16[256,128]{1,0:T(8,128)(2,1)S(1)}, u32[]{:S(2)}, u32[]{:S(2)}) collective-permute-start(bf16[256,128]{1,0:T(8,128)(2,1)S(1)} %get-tuple-element.70), channel_id=1, source_target_pairs={{0,2},{1,3},{2,0},{3,1},{4,6},{5,7},{6,4},{7,5},{8,10},{9,11},{10,... | collective-permute-start | bytes 196616 | tf_op jit(solution)/shard_map/ppermute | solution.py:24
  57.6 4.6 %collective-permute-start.7 = (bf16[256,128]{1,0:T(8,128)(2,1)S(1)}, bf16[256,128]{1,0:T(8,128)(2,1)S(1)}, u32[]{:S(2)}, u32[]{:S(2)}) collective-permute-start(bf16[256,128]{1,0:T(8,128)(2,1)S(1)} %shard_map.121.mine_ref), channel_id=1, source_target_pairs={{0,4},{1,5},{2,6},{3,7},{4,0},{5,1},{6,2},{7,3},{8,12},{9,13},{10,... | collective-permute-start | bytes 196616 | tf_op jit(solution)/shard_map/ppermute | solution.py:24
  62.2 5.8 %collective-permute-start.8 = (bf16[256,128]{1,0:T(8,128)(2,1)S(1)}, bf16[256,128]{1,0:T(8,128)(2,1)S(1)}, u32[]{:S(2)}, u32[]{:S(2)}) collective-permute-start(bf16[256,128]{1,0:T(8,128)(2,1)S(1)} %shard_map.122.mine_ref), channel_id=1, source_target_pairs={{0,8},{1,9},{2,10},{3,11},{4,12},{5,13},{6,14},{7,15},{8,0},{9,1},... | collective-permute-start | bytes 196616 | tf_op jit(solution)/shard_map/ppermute | solution.py:24
  68.1 4.3 %collective-permute-start.9 = (bf16[256,128]{1,0:T(8,128)(2,1)S(1)}, bf16[256,128]{1,0:T(8,128)(2,1)S(1)}, u32[]{:S(2)}, u32[]{:S(2)}) collective-permute-start(bf16[256,128]{1,0:T(8,128)(2,1)S(1)} %shard_map.123.mine_ref), channel_id=1, source_target_pairs={{0,16},{16,0},{1,17},{17,1},{2,18},{18,2},{3,19},{19,3},{4,20},{20... | collective-permute-start | bytes 196616 | tf_op jit(solution)/shard_map/ppermute | solution.py:24
  72.5 4.7 %collective-permute-start.10 = (bf16[192,256]{1,0:T(8,128)(2,1)S(1)}, bf16[192,256]{1,0:T(8,128)(2,1)S(1)}, u32[]{:S(2)}, u32[]{:S(2)}) collective-permute-start(bf16[192,256]{1,0:T(8,128)(2,1)S(1)} %shard_map.124.mine_ref), channel_id=1, source_target_pairs={{0,2},{1,3},{2,0},{3,1},{4,6},{5,7},{6,4},{7,5},{8,10},{9,11},{10,... | collective-permute-start | bytes 294920 | tf_op jit(solution)/shard_map/ppermute | solution.py:24
  77.2 1.6 %collective-permute-start.11 = (bf16[384,256]{1,0:T(8,128)(2,1)S(1)}, bf16[384,256]{1,0:T(8,128)(2,1)S(1)}, u32[]{:S(2)}, u32[]{:S(2)}) collective-permute-start(bf16[384,256]{1,0:T(8,128)(2,1)S(1)} %shard_map.126.mine_ref), channel_id=1, source_target_pairs={{0,1},{1,0},{2,3},{3,2},{4,5},{5,4},{6,7},{7,6},{8,9},{9,8},{10,11... | collective-permute-start | bytes 589832 | tf_op jit(solution)/shard_map/ppermute | solution.py:24
where the time goes:
time: 80.3 us; the launch traced here: 79.8 us
  starting transfers between devices  28.4 us (35%)
  waiting for transfers between devices  28.3 us (35%)
  Pallas kernels  15.6 us (19%)
  local copies, waits for them, and re-layouts  6.55 us (8%)
  between operations  0.82 us (1%)
    ppermute x10, waiting for transfers between devices, swapped(): return lax.ppermute(x, axis, [(i, i ^ mask) for i in range(peers)])  19.1 us
    pallas_call x17, Pallas kernels, call(): pl.pallas_call(body, out_shape=outs, in_specs=specs or [VMEM] * len(args)...  15.6 us
    ppermute x10, starting transfers between devices, swapped(): return lax.ppermute(x, axis, [(i, i ^ mask) for i in range(peers)])  11.2 us
    all_to_all x1, starting transfers between devices, shards(): lax.all_to_all(picked.reshape(ndom, per_peer, width), 'dom', split_axis=0...  7.39 us
    all_to_all x1, waiting for transfers between devices, shards(): lax.all_to_all(picked.reshape(ndom, per_peer, width), 'dom', split_axis=0...  6.91 us
    unnamed x21, local copies, waits for them, and re-layouts  6.55 us
    ppermute x2, starting transfers between devices, swapped_across(): lax.ppermute(x, axis, [(i, (i + 1 if i % 2 else i - 1) % peers) for i in...  5.63 us
    all_to_all x1, starting transfers between devices, shards(): lax.all_to_all(back.reshape(ndom, per_peer, width), 'dom', split_axis=0,...  4.19 us
  transfers between devices with their start and end apart: 14, of which 9 were waited for; matrix products, arithmetic and copies ran while one was open for 1% of the time, Pallas kernels for 13%

commit v1 on v0

--- a/solution.py
+++ b/solution.py
@@ -273,25 +273,23 @@
     out_ref[...] = (mine_ref[...].astype(F32) + in_ref[...].astype(F32)).astype(BF16)
 
 
-def join_lanes_body(mine_ref, in_ref, out_ref):
+def join_body(mask, mine_ref, dp_ref, y_ref, both_ref, out_ref):
     size, half = mine_ref.shape
     more = size // 2
     few = more // 2
     first = lax.axis_index("dp") == 0
-    mine, other = mine_ref[:more, :], in_ref[:more, :]
-    out_ref[few:, :half] = jnp.where(first, mine, other)
-    out_ref[few:, half:] = jnp.where(first, other, mine)
-    total = (mine_ref[more:, :].astype(F32) + in_ref[more:, :].astype(F32)).astype(BF16)
-    out_ref[:few, :half] = total[:few]
-    out_ref[:few, half:] = total[few:]
-
-
-def join_rows_body(mask, mine_ref, in_ref, out_ref):
-    size = mine_ref.shape[0]
     low = bit_of(mask) == 0
-    mine, other = mine_ref[...], in_ref[...]
-    out_ref[:size, :] = jnp.where(low, mine, other)
-    out_ref[size:, :] = jnp.where(low, other, mine)
+    mine = [ref[...] for ref in (mine_ref, dp_ref)]
+    other = [ref[...] for ref in (y_ref, both_ref)]
+    for side in range(2):
+        a, b = (jnp.where(low, x, y) if side == 0 else jnp.where(low, y, x) for x, y in zip(mine, other))
+        row = side * (few + more)
+        total = (a[more:].astype(F32) + b[more:].astype(F32)).astype(BF16)
+        out_ref[row : row + few, :half] = total[:few]
+        out_ref[row : row + few, half:] = total[few:]
+        row += few
+        out_ref[row : row + more, :half] = jnp.where(first, a[:more], b[:more])
+        out_ref[row : row + more, half:] = jnp.where(first, b[:more], a[:more])
 
 
 def finish_body(mask, mine_ref, in_ref, edge_ref, node_ref):
@@ -306,7 +304,13 @@
             node_ref[q * more : (q + 1) * more, :] = value[row + few : row + few + more]
 
 
-def cut_before(edge_part, node_part):
+def swapped_both(x, mask):
+    peers = lax.axis_size("dom")
+    total = 2 * peers
+    return lax.ppermute(x, ("dp", "dom"), [(i, (i + peers) % total ^ mask) for i in range(total)])
+
+
+def cut_and_summed(edge_part, node_part):
     half = node_part[0].shape[1]
     size = node_part[0].shape[0] + 2 * edge_part.shape[0]
 
@@ -319,20 +323,20 @@
         )
 
     keep, send = cut(first_cut_body, CORE, (edge_part, *node_part), size)
-    return cut(next_cut_body, ALONG_Y, (keep, swapped(send, "dom", CORE)), size // 2)
-
-
-def reduced(keep, send, back, width):
-    quarter, half = keep.shape
-    few = width // 4
-    (mine,) = call(sum_body, [shape(quarter, half)], (keep, swapped(send, "dom", ALONG_Y)))
-    for mask in (ALONG_Z, 2 * ALONG_Z):
-        (mine,) = call(sum_body, [shape(quarter, half)], (mine, swapped(mine, "dom", mask)))
-    (mine,) = call(join_lanes_body, [shape(3 * few, width)], (mine, swapped(mine, "dp", 1)))
+    keep, send = cut(next_cut_body, ALONG_Y, (keep, swapped(send, "dom", CORE)), size // 2)
+    out = [shape(*send.shape)]
+    (mine,) = call(sum_body, out, (keep, swapped(send, "dom", ALONG_Y)))
+    return call(sum_body, out, (mine, swapped(mine, "dom", ALONG_Z)))[0]
+
+
+def joined(mine, back, width):
+    (mine,) = call(sum_body, [shape(*mine.shape)], (mine, swapped(mine, "dom", 2 * ALONG_Z)))
+    (mine,) = call(
+        functools.partial(join_body, ALONG_Y),
+        [shape(6 * (width // 4), width)],
+        (mine, swapped(mine, "dp", 1), swapped(mine, "dom", ALONG_Y), swapped_both(mine, ALONG_Y)),
+    )
     mine, back = lax.optimization_barrier((mine, back))
-    (mine,) = call(
-        functools.partial(join_rows_body, ALONG_Y), [shape(6 * few, width)], (mine, swapped(mine, "dom", ALONG_Y))
-    )
     grad_edge, grad_node = call(
         functools.partial(finish_body, CORE),
         [shape(width, width, dtype=F32), shape(2 * width, width, dtype=F32)],
@@ -455,13 +459,13 @@
         nbytes=8 * unit,
     )
     if tiled:
-        keep, send = cut_before(edge_part, node_part)
-        back, send = lax.optimization_barrier((back, send))
+        mine = cut_and_summed(edge_part, node_part)
+        back, mine = lax.optimization_barrier((back, mine))
     back = lax.all_to_all(
         back.reshape(ndom, per_peer, width), "dom", split_axis=0, concat_axis=0, tiled=True
     ).reshape(rows, width)
     if tiled:
-        grad_edge, grad_node, back = reduced(keep, send, back, width)
+        grad_edge, grad_node, back = joined(mine, back, width)
     else:
         grad_edge, grad_node = (lax.psum(part, ("dp", "dom")) for part in (edge_part, node_part[0]))
     (grad_brick,) = call(place_body, [tall], (send_order, back), flops=2 * rows * rows * width, nbytes=2 * unit)

time: 80.3 us -> 87.3 us (1.087)
  waiting for transfers between devices: 28.3 us -> 38.1 us
  starting transfers between devices: 28.4 us -> 25.7 us
    ppermute x10, waiting for transfers between devices: 19.1 us -> 27.1 us  [swapped(): return lax.ppermute(x, axis, [(i, i ^ mask) for i in range(peers)])]
    ppermute x10, starting transfers between devices: 11.2 us -> 5.92 us  [swapped(): return lax.ppermute(x, axis, [(i, i ^ mask) for i in range(peers)])]
    ppermute x0 -> x1, starting transfers between devices: none -> 2.46 us  [swapped_both(): lax.ppermute(x, ('dp', 'dom'), [(i, (i + peers) % total ^ mask) for i in...]
    ppermute x0 -> x1, waiting for transfers between devices: none -> 1.78 us  [swapped_both(): lax.ppermute(x, ('dp', 'dom'), [(i, (i + peers) % total ^ mask) for i in...]
    pallas_call x17 -> x16, Pallas kernels: 15.6 us -> 15.6 us  [call(): pl.pallas_call(body, out_shape=outs, in_specs=specs or [VMEM] * len(args)...]
  transfers between devices with their start and end apart: 14 -> 15, of which waited for: 9 -> 10; matrix products, arithmetic and copies ran while one was open for 1% -> 1% of each run, Pallas kernels for 13% -> 12%
where the time goes in v1:
time: 87.3 us; the launch traced here: 86.8 us
  waiting for transfers between devices  38.1 us (44%)
  starting transfers between devices  25.7 us (29%)
  Pallas kernels  15.6 us (18%)
  local copies, waits for them, and re-layouts  6.54 us (7%)
    ppermute x10, waiting for transfers between devices, swapped(): return lax.ppermute(x, axis, [(i, i ^ mask) for i in range(peers)])  27.1 us
    pallas_call x16, Pallas kernels, call(): pl.pallas_call(body, out_shape=outs, in_specs=specs or [VMEM] * len(args)...  15.6 us
    all_to_all x1, starting transfers between devices, shards(): lax.all_to_all(picked.reshape(ndom, per_peer, width), 'dom', split_axis=0...  7.39 us
    all_to_all x1, waiting for transfers between devices, shards(): lax.all_to_all(picked.reshape(ndom, per_peer, width), 'dom', split_axis=0...  6.92 us
    unnamed x21, local copies, waits for them, and re-layouts  6.54 us
    ppermute x10, starting transfers between devices, swapped(): return lax.ppermute(x, axis, [(i, i ^ mask) for i in range(peers)])  5.92 us
    ppermute x2, starting transfers between devices, swapped_across(): lax.ppermute(x, axis, [(i, (i + 1 if i % 2 else i - 1) % peers) for i in...  5.63 us
    all_to_all x1, starting transfers between devices, shards(): lax.all_to_all(back.reshape(ndom, per_peer, width), 'dom', split_axis=0,...  4.27 us
  transfers between devices with their start and end apart: 15, of which 10 were waited for; matrix products, arithmetic and copies ran while one was open for 1% of the time, Pallas kernels for 12%

profile of v1, /device:TPU:0, one launch (start us, length us, event | category | flops | bytes accessed | tf_op | source)
XLA Modules:
  0.0 86.8 jit_solution(9884545232862311238)
XLA Ops:
  0.6 0.0 copy-start.3
  0.6 0.0 copy-start.7
  0.7 0.0 copy-start.2
  0.7 2.7 %shard_map.111 = bf16[1024,256]{1,0:T(8,128)(2,1)} custom-call(s32[1,1024]{1,0:T(1,128)} %order_ref.1, bf16[1024,256]{1,0:T(8,128)(2,1)} %bitcast.18), custom_call_target="tpu_custom_call" | custom-call | flops 536870912 | bytes 1048576 | tf_op jit(solution)/shard_map/pallas_call | solution.py:41
  3.4 7.4 %all-to-all-start = ((bf16[16,64,256]{2,1,0:T(8,128)(2,1)}), bf16[16,64,256]{2,1,0:T(8,128)(2,1)S(1)}, u32[]{:S(2)}, u32[]{:S(2)}) async-start(bf16[16,64,256]{2,1,0:T(8,128)(2,1)} %bitcast.17), calls=%async_computation | async-start | bytes 1048576 | tf_op jit(solution)/shard_map/all_to_all | solution.py:391
  10.8 0.8 copy.12.tgt_ref
  11.5 0.0 copy-start.4
  11.5 1.2 %copy-done.4 = bf16[8,4,128,128]{3,2,1,0:T(8,128)(2,1)S(1)} copy-done((bf16[8,4,128,128]{3,2,1,0:T(8,128)(2,1)S(1)}, bf16[8,4,128,128]{3,2,1,0:T(8,128)(2,1)}, u32[]{:S(2)}) %copy-start.4) | copy-done | bytes 1048600
  12.8 0.0 copy-start.8
  12.8 0.7 copy-done.8
  13.4 2.2 %shard_map.112 = (bf16[8,128,1024]{2,1,0:T(8,128)(2,1)S(1)}, bf16[4,128,1024]{2,1,0:T(8,128)(2,1)S(1)}, bf16[1024,1664]{1,0:T(8,128)(2,1)S(1)}) custom-call(s32[8]{0:T(128)S(1)} %copy-done.8, s32[8,4]{1,0:T(8,128)S(1)} %copy.12.tgt_ref, bf16[8,4,128,128]{3,2,1,0:T(8,128)(2,1)S(1)} %copy-done.4), custom_call_target="tpu_custom_call" | custom-call | bytes 8388608 | tf_op jit(solution)/shard_map/pallas_call | solution.py:41
  15.7 0.0 copy-start
  15.7 1.7 %copy-done = bf16[1024,1664]{1,0:T(8,128)(2,1)} copy-done((bf16[1024,1664]{1,0:T(8,128)(2,1)}, bf16[1024,1664]{1,0:T(8,128)(2,1)S(1)}, u32[]{:S(2)}) %copy-start) | copy-done | bytes 3407896
  17.4 0.0 copy-start.5
  17.4 1.0 %copy-done.5 = bf16[4,128,1024]{2,1,0:T(8,128)(2,1)} copy-done((bf16[4,128,1024]{2,1,0:T(8,128)(2,1)}, bf16[4,128,1024]{2,1,0:T(8,128)(2,1)S(1)}, u32[]{:S(2)}) %copy-start.5) | copy-done | bytes 1048600
  18.3 6.9 %all-to-all-done = bf16[16,64,256]{2,1,0:T(8,128)(2,1)S(1)} async-done(((bf16[16,64,256]{2,1,0:T(8,128)(2,1)}), bf16[16,64,256]{2,1,0:T(8,128)(2,1)S(1)}, u32[]{:S(2)}, u32[]{:S(2)}) %all-to-all-start) | async-done | bytes 524320 | tf_op jit(solution)/shard_map/all_to_all | solution.py:391
  25.2 0.0 copy-done.3
  25.2 0.0 copy-start.6
  25.2 1.2 %copy-done.6 = bf16[4,128,1024]{2,1,0:T(8,128)(2,1)S(1)} copy-done((bf16[4,128,1024]{2,1,0:T(8,128)(2,1)S(1)}, bf16[4,128,1024]{2,1,0:T(8,128)(2,1)}, u32[]{:S(2)}) %copy-start.6) | copy-done | bytes 1048600
  26.5 0.8 shard_map.113
  27.3 0.1 collective-permute-start
  27.4 2.8 %collective-permute-start.1 = (bf16[256,256]{1,0:T(8,128)(2,1)S(1)}, bf16[256,256]{1,0:T(8,128)(2,1)S(1)}, u32[]{:S(2)}, u32[]{:S(2)}) collective-permute-start(bf16[256,256]{1,0:T(8,128)(2,1)S(1)} %get-tuple-element.47), channel_id=1, source_target_pairs={{0,15},{1,2},{2,1},{3,4},{4,3},{5,6},{6,5},{7,8},{8,7},{9,10},{10,... | collective-permute-start | bytes 393224 | tf_op jit(solution)/shard_map/ppermute | solution.py:29
  30.2 0.0 copy-done.7
  30.2 0.0 copy-done.2
  30.2 0.0 copy-start.1
  30.2 2.6 %shard_map.114 = (bf16[512,256]{1,0:T(8,128)(2,1)S(1)}, bf16[512,256]{1,0:T(8,128)(2,1)S(1)}, bf16[512,256]{1,0:T(8,128)(2,1)S(1)}, bf16[512,256]{1,0:T(8,128)(2...) custom-call(bf16[1024,256]{1,0:T(8,128)(2,1)S(1)} %bitcast.9, ...), custom_call_target="tpu_custom_call" | custom-call | flops 805306368 | bytes 4194304 | tf_op jit(solution)/shard_map/pallas_call | solution.py:41
  32.8 0.0 collective-permute-done.near_in_ref
  32.9 1.7 %collective-permute-done.1.far_in_ref = bf16[256,256]{1,0:T(8,128)(2,1)S(1)} collective-permute-done((bf16[256,256]{1,0:T(8,128)(2,1)S(1)}, bf16[256,256]{1,0:T(8,128)(2,1)S(1)}, u32[]{:S(2)}, u32[]{:S(2)}) %collective-permute-start.1) | collective-permute-done | bytes 131104 | tf_op jit(solution)/shard_map/ppermute | solution.py:29
  34.5 0.7 shard_map.115
  35.2 0.1 collective-permute-start.2
  35.3 2.8 %collective-permute-start.3 = (bf16[256,256]{1,0:T(8,128)(2,1)S(1)}, bf16[256,256]{1,0:T(8,128)(2,1)S(1)}, u32[]{:S(2)}, u32[]{:S(2)}) collective-permute-start(bf16[256,256]{1,0:T(8,128)(2,1)S(1)} %get-tuple-element.53), channel_id=1, source_target_pairs={{0,15},{1,2},{2,1},{3,4},{4,3},{5,6},{6,5},{7,8},{8,7},{9,10},{10,... | collective-permute-start | bytes 393224 | tf_op jit(solution)/shard_map/ppermute | solution.py:29
  38.1 0.5 shard_map.118
  38.6 1.6 %collective-permute-start.4 = (bf16[512,128]{1,0:T(8,128)(2,1)S(1)}, bf16[512,128]{1,0:T(8,128)(2,1)S(1)}, u32[]{:S(2)}, u32[]{:S(2)}) collective-permute-start(bf16[512,128]{1,0:T(8,128)(2,1)S(1)} %get-tuple-element.65), channel_id=1, source_target_pairs={{0,16},{16,0},{1,17},{17,1},{2,18},{18,2},{3,19},{19,3},{4,20},{20... | collective-permute-start | bytes 393224 | tf_op jit(solution)/shard_map/ppermute | solution.py:24
  40.2 0.0 copy-done.1
  40.2 1.6 %shard_map.116 = (bf16[1024,256]{1,0:T(8,128)(2,1)}, f32[1024,256]{1,0:T(8,128)S(1)}, f32[1024,256]{1,0:T(8,128)S(1)}) custom-call(bf16[1024,256]{1,0:T(8,128)(2,1)S(1)} %bitcast.12, bf16[1024,1664]{1,0:T(8,128)(2,1)S(1)} %copy-done.1, bf16[256,256]{1,0:T(8,128)(2,1)S(1)} %copy-done.3, bf16[512,256]{1,0:T(8,128)(2,1)S(1)} %get-tuple-element.44.out_mid_ref, ...), custom_call_target="tpu_custom_call" | custom-call | flops 671088640 | bytes 4194304 | tf_op jit(solution)/shard_map/pallas_call | solution.py:41
  41.8 0.0 collective-permute-done.2.near_ref
  41.8 0.7 collective-permute-done.3.far_ref
  42.5 0.0 copy-start.9
  42.5 1.8 %shard_map.117 = (bf16[1024,256]{1,0:T(8,128)(2,1)}, f32[256,256]{1,0:T(8,128)S(1)}) custom-call(bf16[1024,256]{1,0:T(8,128)(2,1)S(1)} %bitcast.13, bf16[1024,1664]{1,0:T(8,128)(2,1)S(1)} %copy-done.1, bf16[256,256]{1,0:T(8,128)(2,1)S(1)} %collective-permute-done.2.near_ref, bf16[256,256]{1,0:T(8,128)(2,1)S(1)} %collective-permute-done.3.far_ref, ...), custom_call_target="tpu_custom_call" | custom-call | flops 536870912 | bytes 4194304 | tf_op jit(solution)/shard_map/pallas_call | solution.py:41
  44.2 0.0 collective-permute-done.4.node_in_ref
  44.2 0.1 shard_map.119
  44.3 0.1 collective-permute-start.5
  44.4 1.3 %collective-permute-done.5.in_ref = bf16[512,128]{1,0:T(8,128)(2,1)S(1)} collective-permute-done((bf16[512,128]{1,0:T(8,128)(2,1)S(1)}, bf16[512,128]{1,0:T(8,128)(2,1)S(1)}, u32[]{:S(2)}, u32[]{:S(2)}) %collective-permute-start.5) | collective-permute-done | bytes 131104 | tf_op jit(solution)/shard_map/ppermute | solution.py:24
  45.8 0.1 collective-permute-start.6
  45.8 4.3 %collective-permute-done.6.in_ref = bf16[256,128]{1,0:T(8,128)(2,1)S(1)} collective-permute-done((bf16[256,128]{1,0:T(8,128)(2,1)S(1)}, bf16[256,128]{1,0:T(8,128)(2,1)S(1)}, u32[]{:S(2)}, u32[]{:S(2)}) %collective-permute-start.6) | collective-permute-done | bytes 65568 | tf_op jit(solution)/shard_map/ppermute | solution.py:24
  50.1 0.1 collective-permute-start.7
  50.2 4.3 %collective-permute-done.7.in_ref = bf16[256,128]{1,0:T(8,128)(2,1)S(1)} collective-permute-done((bf16[256,128]{1,0:T(8,128)(2,1)S(1)}, bf16[256,128]{1,0:T(8,128)(2,1)S(1)}, u32[]{:S(2)}, u32[]{:S(2)}) %collective-permute-start.7) | collective-permute-done | bytes 65568 | tf_op jit(solution)/shard_map/ppermute | solution.py:24
  54.5 4.3 %all-to-all-start.1 = ((bf16[16,64,256]{2,1,0:T(8,128)(2,1)}), bf16[16,64,256]{2,1,0:T(8,128)(2,1)S(1)}, u32[]{:S(2)}, u32[]{:S(2)}) async-start(bf16[16,64,256]{2,1,0:T(8,128)(2,1)} %bitcast.5), calls=%async_computation.1 | async-start | bytes 1048576 | tf_op jit(solution)/shard_map/all_to_all | solution.py:464
  58.7 2.8 %collective-permute-start.8 = (bf16[256,128]{1,0:T(8,128)(2,1)S(1)}, bf16[256,128]{1,0:T(8,128)(2,1)S(1)}, u32[]{:S(2)}, u32[]{:S(2)}) collective-permute-start(bf16[256,128]{1,0:T(8,128)(2,1)S(1)} %shard_map.122.mine_ref), channel_id=1, source_target_pairs={{0,8},{1,9},{2,10},{3,11},{4,12},{5,13},{6,14},{7,15},{8,0},{9,1},... | collective-permute-start | bytes 196616 | tf_op jit(solution)/shard_map/ppermute | solution.py:24
  61.6 15.3 %collective-permute-done.8.in_ref = bf16[256,128]{1,0:T(8,128)(2,1)S(1)} collective-permute-done((bf16[256,128]{1,0:T(8,128)(2,1)S(1)}, bf16[256,128]{1,0:T(8,128)(2,1)S(1)}, u32[]{:S(2)}, u32[]{:S(2)}) %collective-permute-start.8) | collective-permute-done | bytes 65568 | tf_op jit(solution)/shard_map/ppermute | solution.py:24
  76.9 2.5 %collective-permute-start.11 = (bf16[256,128]{1,0:T(8,128)(2,1)S(1)}, bf16[256,128]{1,0:T(8,128)(2,1)S(1)}, u32[]{:S(2)}, u32[]{:S(2)}) collective-permute-start(bf16[256,128]{1,0:T(8,128)(2,1)S(1)} %shard_map.123.mine_ref), channel_id=1, source_target_pairs={{0,18},{1,19},{2,16},{3,17},{4,22},{5,23},{6,20},{7,21},{8,26},{9,... | collective-permute-start | bytes 196616 | tf_op jit(solution)/shard_map/ppermute | solution.py:310
  79.3 0.6 collective-permute-start.10
  79.9 0.5 collective-permute-start.9
  80.4 1.8 %collective-permute-done.11.both_ref = bf16[256,128]{1,0:T(8,128)(2,1)S(1)} collective-permute-done((bf16[256,128]{1,0:T(8,128)(2,1)S(1)}, bf16[256,128]{1,0:T(8,128)(2,1)S(1)}, u32[]{:S(2)}, u32[]{:S(2)}) %collective-permute-start.11) | collective-permute-done | bytes 65568 | tf_op jit(solution)/shard_map/ppermute | solution.py:310
  82.2 1.4 %collective-permute-done.10.y_ref = bf16[256,128]{1,0:T(8,128)(2,1)S(1)} collective-permute-done((bf16[256,128]{1,0:T(8,128)(2,1)S(1)}, bf16[256,128]{1,0:T(8,128)(2,1)S(1)}, u32[]{:S(2)}, u32[]{:S(2)}) %collective-permute-start.10) | collective-permute-done | bytes 65568 | tf_op jit(solution)/shard_map/ppermute | solution.py:24
  83.6 0.6 collective-permute-done.9.dp_ref
  84.1 0.1 shard_map.124.mine_ref
  84.2 0.0 all-to-all-done.1
  84.2 0.1 collective-permute-start.12
  84.3 0.0 copy-done.9
  84.3 1.5 %shard_map.125 = bf16[1024,256]{1,0:T(8,128)(2,1)} custom-call(s32[1,1024]{1,0:T(1,128)S(1)} %copy-done.9, bf16[1024,256]{1,0:T(8,128)(2,1)S(1)} %bitcast.16), custom_call_target="tpu_custom_call" | custom-call | flops 536870912 | bytes 1048576 | tf_op jit(solution)/shard_map/pallas_call | solution.py:41
  85.8 0.0 collective-permute-done.12.in_ref
  85.8 1.0 %shard_map.126 = (f32[256,256]{1,0:T(8,128)}, f32[512,256]{1,0:T(8,128)}) custom-call(bf16[384,256]{1,0:T(8,128)(2,1)S(1)} %shard_map.124.mine_ref, bf16[384,256]{1,0:T(8,128)(2,1)S(1)} %collective-permute-done.12.in_ref), custom_call_target="tpu_custom_call" | custom-call | tf_op jit(solution)/shard_map/pallas_call | solution.py:41
  (4 shorter events, 0.1 us)
Async XLA Ops:
  0.6 24.6 %copy-start.3 = (bf16[256,256]{1,0:T(8,128)(2,1)S(1)}, bf16[256,256]{1,0:T(8,128)(2,1)}, u32[]{:S(2)}) copy-start(bf16[256,256]{1,0:T(8,128)(2,1)} %w_edge_ref.5) | copy-start | bytes 393220
  0.6 29.6 %copy-start.7 = (bf16[512,256]{1,0:T(8,128)(2,1)S(1)}, bf16[512,256]{1,0:T(8,128)(2,1)}, u32[]{:S(2)}) copy-start(bf16[512,256]{1,0:T(8,128)(2,1)} %w_node_ref.3) | copy-start | bytes 786436
  0.7 29.6 %copy-start.2 = (bf16[1,1024,256]{2,1,0:T(8,128)(2,1)S(1)}, bf16[1,1024,256]{2,1,0:T(8,128)(2,1)}, u32[]{:S(2)}) copy-start(bf16[1,1024,256]{2,1,0:T(8,128)(2,1)} %param.15) | copy-start | bytes 1572868
  3.4 21.9 %all-to-all-start = ((bf16[16,64,256]{2,1,0:T(8,128)(2,1)}), bf16[16,64,256]{2,1,0:T(8,128)(2,1)S(1)}, u32[]{:S(2)}, u32[]{:S(2)}) async-start(bf16[16,64,256]{2,1,0:T(8,128)(2,1)} %bitcast.17), calls=%async_computation | async-start | bytes 1048576 | tf_op jit(solution)/shard_map/all_to_all | solution.py:391
  11.5 1.2 %copy-start.4 = (bf16[8,4,128,128]{3,2,1,0:T(8,128)(2,1)S(1)}, bf16[8,4,128,128]{3,2,1,0:T(8,128)(2,1)}, u32[]{:S(2)}) copy-start(bf16[8,4,128,128]{3,2,1,0:T(8,128)(2,1)} %vals_ref.1) | copy-start | bytes 3145732
  12.8 0.7 copy-start.8
  15.7 1.7 %copy-start = (bf16[1024,1664]{1,0:T(8,128)(2,1)}, bf16[1024,1664]{1,0:T(8,128)(2,1)S(1)}, u32[]{:S(2)}) copy-start(bf16[1024,1664]{1,0:T(8,128)(2,1)S(1)} %get-tuple-element.40.at_ref) | copy-start | bytes 10223620
  17.4 1.0 %copy-start.5 = (bf16[4,128,1024]{2,1,0:T(8,128)(2,1)}, bf16[4,128,1024]{2,1,0:T(8,128)(2,1)S(1)}, u32[]{:S(2)}) copy-start(bf16[4,128,1024]{2,1,0:T(8,128)(2,1)S(1)} %get-tuple-element.41.a_hbm) | copy-start | bytes 3145732
  25.2 1.2 %copy-start.6 = (bf16[4,128,1024]{2,1,0:T(8,128)(2,1)S(1)}, bf16[4,128,1024]{2,1,0:T(8,128)(2,1)}, u32[]{:S(2)}) copy-start(bf16[4,128,1024]{2,1,0:T(8,128)(2,1)} %copy-done.5) | copy-start | bytes 3145732
  27.3 5.5 %collective-permute-start = (bf16[256,256]{1,0:T(8,128)(2,1)S(1)}, bf16[256,256]{1,0:T(8,128)(2,1)S(1)}, u32[]{:S(2)}, u32[]{:S(2)}) collective-permute-start(bf16[256,256]{1,0:T(8,128)(2,1)S(1)} %get-tuple-element.46), channel_id=1, source_target_pairs={{0,1},{1,0},{2,3},{3,2},{4,5},{5,4},{6,7},{7,6},{8,9},{9,8},{10,11... | collective-permute-start | bytes 393224 | tf_op jit(solution)/shard_map/ppermute | solution.py:24
  27.4 7.2 %collective-permute-start.1 = (bf16[256,256]{1,0:T(8,128)(2,1)S(1)}, bf16[256,256]{1,0:T(8,128)(2,1)S(1)}, u32[]{:S(2)}, u32[]{:S(2)}) collective-permute-start(bf16[256,256]{1,0:T(8,128)(2,1)S(1)} %get-tuple-element.47), channel_id=1, source_target_pairs={{0,15},{1,2},{2,1},{3,4},{4,3},{5,6},{6,5},{7,8},{8,7},{9,10},{10,... | collective-permute-start | bytes 393224 | tf_op jit(solution)/shard_map/ppermute | solution.py:29
  30.2 10.0 %copy-start.1 = (bf16[1024,1664]{1,0:T(8,128)(2,1)S(1)}, bf16[1024,1664]{1,0:T(8,128)(2,1)}, u32[]{:S(2)}) copy-start(bf16[1024,1664]{1,0:T(8,128)(2,1)} %copy-done) | copy-start | bytes 10223620
  35.2 6.6 %collective-permute-start.2 = (bf16[256,256]{1,0:T(8,128)(2,1)S(1)}, bf16[256,256]{1,0:T(8,128)(2,1)S(1)}, u32[]{:S(2)}, u32[]{:S(2)}) collective-permute-start(bf16[256,256]{1,0:T(8,128)(2,1)S(1)} %get-tuple-element.52), channel_id=1, source_target_pairs={{0,1},{1,0},{2,3},{3,2},{4,5},{5,4},{6,7},{7,6},{8,9},{9,8},{10,11... | collective-permute-start | bytes 393224 | tf_op jit(solution)/shard_map/ppermute | solution.py:24
  35.3 7.2 %collective-permute-start.3 = (bf16[256,256]{1,0:T(8,128)(2,1)S(1)}, bf16[256,256]{1,0:T(8,128)(2,1)S(1)}, u32[]{:S(2)}, u32[]{:S(2)}) collective-permute-start(bf16[256,256]{1,0:T(8,128)(2,1)S(1)} %get-tuple-element.53), channel_id=1, source_target_pairs={{0,15},{1,2},{2,1},{3,4},{4,3},{5,6},{6,5},{7,8},{8,7},{9,10},{10,... | collective-permute-start | bytes 393224 | tf_op jit(solution)/shard_map/ppermute | solution.py:29
  38.6 5.6 %collective-permute-start.4 = (bf16[512,128]{1,0:T(8,128)(2,1)S(1)}, bf16[512,128]{1,0:T(8,128)(2,1)S(1)}, u32[]{:S(2)}, u32[]{:S(2)}) collective-permute-start(bf16[512,128]{1,0:T(8,128)(2,1)S(1)} %get-tuple-element.65), channel_id=1, source_target_pairs={{0,16},{16,0},{1,17},{17,1},{2,18},{18,2},{3,19},{19,3},{4,20},{20... | collective-permute-start | bytes 393224 | tf_op jit(solution)/shard_map/ppermute | solution.py:24
  42.5 41.9 %copy-start.9 = (s32[1,1024]{1,0:T(1,128)S(1)}, s32[1,1024]{1,0:T(1,128)}, u32[]{:S(2)}) copy-start(s32[1,1024]{1,0:T(1,128)} %order_ref.1) | copy-start | bytes 12292
  44.3 1.4 %collective-permute-start.5 = (bf16[512,128]{1,0:T(8,128)(2,1)S(1)}, bf16[512,128]{1,0:T(8,128)(2,1)S(1)}, u32[]{:S(2)}, u32[]{:S(2)}) collective-permute-start(bf16[512,128]{1,0:T(8,128)(2,1)S(1)} %get-tuple-element.67), channel_id=1, source_target_pairs={{0,1},{1,0},{2,3},{3,2},{4,5},{5,4},{6,7},{7,6},{8,9},{9,8},{10,11... | collective-permute-start | bytes 393224 | tf_op jit(solution)/shard_map/ppermute | solution.py:24
  45.8 4.3 %collective-permute-start.6 = (bf16[256,128]{1,0:T(8,128)(2,1)S(1)}, bf16[256,128]{1,0:T(8,128)(2,1)S(1)}, u32[]{:S(2)}, u32[]{:S(2)}) collective-permute-start(bf16[256,128]{1,0:T(8,128)(2,1)S(1)} %get-tuple-element.69), channel_id=1, source_target_pairs={{0,2},{1,3},{2,0},{3,1},{4,6},{5,7},{6,4},{7,5},{8,10},{9,11},{10,... | collective-permute-start | bytes 196616 | tf_op jit(solution)/shard_map/ppermute | solution.py:24
  50.1 4.3 %collective-permute-start.7 = (bf16[256,128]{1,0:T(8,128)(2,1)S(1)}, bf16[256,128]{1,0:T(8,128)(2,1)S(1)}, u32[]{:S(2)}, u32[]{:S(2)}) collective-permute-start(bf16[256,128]{1,0:T(8,128)(2,1)S(1)} %shard_map.121.mine_ref), channel_id=1, source_target_pairs={{0,4},{1,5},{2,6},{3,7},{4,0},{5,1},{6,2},{7,3},{8,12},{9,13},{10,... | collective-permute-start | bytes 196616 | tf_op jit(solution)/shard_map/ppermute | solution.py:24
  54.5 29.8 %all-to-all-start.1 = ((bf16[16,64,256]{2,1,0:T(8,128)(2,1)}), bf16[16,64,256]{2,1,0:T(8,128)(2,1)S(1)}, u32[]{:S(2)}, u32[]{:S(2)}) async-start(bf16[16,64,256]{2,1,0:T(8,128)(2,1)} %bitcast.5), calls=%async_computation.1 | async-start | bytes 1048576 | tf_op jit(solution)/shard_map/all_to_all | solution.py:464
  58.7 18.1 %collective-permute-start.8 = (bf16[256,128]{1,0:T(8,128)(2,1)S(1)}, bf16[256,128]{1,0:T(8,128)(2,1)S(1)}, u32[]{:S(2)}, u32[]{:S(2)}) collective-permute-start(bf16[256,128]{1,0:T(8,128)(2,1)S(1)} %shard_map.122.mine_ref), channel_id=1, source_target_pairs={{0,8},{1,9},{2,10},{3,11},{4,12},{5,13},{6,14},{7,15},{8,0},{9,1},... | collective-permute-start | bytes 196616 | tf_op jit(solution)/shard_map/ppermute | solution.py:24
  76.9 5.3 %collective-permute-start.11 = (bf16[256,128]{1,0:T(8,128)(2,1)S(1)}, bf16[256,128]{1,0:T(8,128)(2,1)S(1)}, u32[]{:S(2)}, u32[]{:S(2)}) collective-permute-start(bf16[256,128]{1,0:T(8,128)(2,1)S(1)} %shard_map.123.mine_ref), channel_id=1, source_target_pairs={{0,18},{1,19},{2,16},{3,17},{4,22},{5,23},{6,20},{7,21},{8,26},{9,... | collective-permute-start | bytes 196616 | tf_op jit(solution)/shard_map/ppermute | solution.py:310
  79.3 4.3 %collective-permute-start.10 = (bf16[256,128]{1,0:T(8,128)(2,1)S(1)}, bf16[256,128]{1,0:T(8,128)(2,1)S(1)}, u32[]{:S(2)}, u32[]{:S(2)}) collective-permute-start(bf16[256,128]{1,0:T(8,128)(2,1)S(1)} %shard_map.123.mine_ref), channel_id=1, source_target_pairs={{0,2},{1,3},{2,0},{3,1},{4,6},{5,7},{6,4},{7,5},{8,10},{9,11},{10,... | collective-permute-start | bytes 196616 | tf_op jit(solution)/shard_map/ppermute | solution.py:24
  79.9 4.3 %collective-permute-start.9 = (bf16[256,128]{1,0:T(8,128)(2,1)S(1)}, bf16[256,128]{1,0:T(8,128)(2,1)S(1)}, u32[]{:S(2)}, u32[]{:S(2)}) collective-permute-start(bf16[256,128]{1,0:T(8,128)(2,1)S(1)} %shard_map.123.mine_ref), channel_id=1, source_target_pairs={{0,16},{16,0},{1,17},{17,1},{2,18},{18,2},{3,19},{19,3},{4,20},{20... | collective-permute-start | bytes 196616 | tf_op jit(solution)/shard_map/ppermute | solution.py:24
  84.2 1.6 %collective-permute-start.12 = (bf16[384,256]{1,0:T(8,128)(2,1)S(1)}, bf16[384,256]{1,0:T(8,128)(2,1)S(1)}, u32[]{:S(2)}, u32[]{:S(2)}) collective-permute-start(bf16[384,256]{1,0:T(8,128)(2,1)S(1)} %shard_map.124.mine_ref), channel_id=1, source_target_pairs={{0,1},{1,0},{2,3},{3,2},{4,5},{5,4},{6,7},{7,6},{8,9},{9,8},{10,11... | collective-permute-start | bytes 589832 | tf_op jit(solution)/shard_map/ppermute | solution.py:24

commit v2 on v1

--- a/solution.py
+++ b/solution.py
@@ -16,6 +16,7 @@
 BF16 = jnp.bfloat16
 F32 = jnp.float32
 MIB = 1024 * 1024
+STORE = 24 * MIB
 CORE, ALONG_Y, ALONG_Z = 1, 2, 4
 
 
@@ -37,12 +38,12 @@
     return jax.ShapeDtypeStruct(dims, dtype)
 
 
-def call(body, outs, args, specs=None, scratch=(), flops=0, nbytes=0, limit=24 * MIB):
+def call(body, outs, args, specs=None, scratch=(), flops=0, nbytes=0, limit=24 * MIB, out_specs=None):
     return pl.pallas_call(
         body,
         out_shape=outs,
         in_specs=specs or [VMEM] * len(args),
-        out_specs=[VMEM] * len(outs),
+        out_specs=out_specs or [VMEM] * len(outs),
         scratch_shapes=list(scratch),
         cost_estimate=pl.CostEstimate(flops=flops, bytes_accessed=nbytes, transcendentals=0),
         compiler_params=pltpu.CompilerParams(vmem_limit_bytes=limit),
@@ -75,7 +76,7 @@
         out_ref[mine, :] = dot(hot, feat).astype(BF16)
 
 
-def build_body(cnt_ref, tgt_ref, vals_ref, own_ref, rim_ref, at_ref, a_ref):
+def build_body(cnt_ref, tgt_ref, vals_ref, own_ref, at_ref, rim_hbm, a_ref, sem):
     blocks, slots = vals_ref.shape[:2]
     spare = blocks + 2 * RIM
     a_ref[...] = jnp.zeros_like(a_ref)
@@ -90,8 +91,10 @@
             a_ref[at, :, mine] = (a_ref[at, :, mine].astype(F32) + value).astype(BF16)
             lanes = pl.ds(pl.multiple_of(at * ROWS, ROWS), ROWS)
             at_ref[mine, lanes] = (at_ref[mine, lanes].astype(F32) + jnp.transpose(value)).astype(BF16)
+    put = pltpu.make_async_copy(a_ref.at[pl.ds(blocks, 2 * RIM)], rim_hbm.at[pl.ds(0, 2 * RIM)], sem)
+    put.start()
     own_ref[...] = a_ref[:blocks]
-    rim_ref[...] = a_ref[blocks:spare]
+    put.wait()
 
 
 def chosen(first, second):
@@ -99,16 +102,18 @@
     return jnp.where(odd, first, second), jnp.where(odd, second, first)
 
 
-def message_body(nodes_ref, a_hbm, w_edge_ref, near_ref, far_ref, msg_ref, a_ref, a_sem):
+def message_body(nodes_ref, a_hbm, w_edge_ref, near_ref, far_ref, msg_ref, a_ref, a_sems):
     rows = nodes_ref.shape[0]
     rim = RIM * ROWS
-    load = pltpu.make_async_copy(a_hbm, a_ref, a_sem)
-    load.start()
+    loads = [pltpu.make_async_copy(a_hbm.at[b], a_ref.at[b], a_sems.at[b]) for b in range(2 * RIM)]
+    for load in loads:
+        load.start()
     for k in range(rows // rim):
         mine = slice(k * rim, (k + 1) * rim)
         pre = dot(nodes_ref[mine, :], w_edge_ref[...])
         msg_ref[mine, :] = (pre * jax.nn.sigmoid(pre)).astype(BF16)
-    load.wait()
+    for load in loads:
+        load.wait()
     sums = dot(a_ref[...].reshape(2 * rim, rows), msg_ref[...])
     near, far = chosen(sums[:rim], sums[rim:])
     near_ref[...] = near.astype(BF16)
@@ -243,30 +248,33 @@
     return lax.rem(lax.div(lax.axis_index("dom"), mask), 2)
 
 
-def cut_rows(total_ref, mask, keep_ref, send_ref):
-    size = keep_ref.shape[0]
-    bit = bit_of(mask)
-    keep_ref[...] = total_ref[pl.ds(pl.multiple_of(bit * size, 16), size), :]
-    send_ref[...] = total_ref[pl.ds(pl.multiple_of((1 - bit) * size, 16), size), :].astype(BF16)
-
-
-def first_cut_body(mask, edge_ref, node_ref, node_in_ref, keep_ref, send_ref, total_ref):
-    half = node_ref.shape[1]
+def cut_body(edge_ref, node_ref, node_in_ref, keep_ref, *refs):
+    send_refs, total_ref = refs[:-1], refs[-1]
+    size, half = keep_ref.shape
     few, more = edge_ref.shape[0] // 4, node_ref.shape[0] // 4
     for q in range(4):
-        row = q * (2 * few + more)
+        row = q * size
         mine = slice(q * more, (q + 1) * more)
         total_ref[row : row + more, :] = node_ref[mine, :] + node_in_ref[mine, :].astype(F32)
         row += more
         mine = slice(q * few, (q + 1) * few)
         total_ref[row : row + few, :] = edge_ref[mine, :half]
         total_ref[row + few : row + 2 * few, :] = edge_ref[mine, half:]
-    cut_rows(total_ref, mask, keep_ref, send_ref)
-
-
-def next_cut_body(mask, mine_ref, in_ref, keep_ref, send_ref, total_ref):
-    total_ref[...] = mine_ref[...] + in_ref[...].astype(F32)
-    cut_rows(total_ref, mask, keep_ref, send_ref)
+    core, side = bit_of(CORE), bit_of(ALONG_Y)
+
+    def piece(core, side):
+        return total_ref[pl.ds(pl.multiple_of((2 * core + side) * size, 16), size), :]
+
+    keep_ref[...] = piece(core, side)
+    for ref, (c, y) in zip(send_refs, ((1 - core, side), (core, 1 - side), (1 - core, 1 - side))):
+        ref[...] = piece(c, y).astype(BF16)
+
+
+def sum_all_body(keep_ref, *refs):
+    total = keep_ref[...]
+    for ref in refs[:-1]:
+        total = total + ref[...].astype(F32)
+    refs[-1][...] = total.astype(BF16)
 
 
 def sum_body(mine_ref, in_ref, out_ref):
@@ -310,37 +318,37 @@
     return lax.ppermute(x, ("dp", "dom"), [(i, (i + peers) % total ^ mask) for i in range(total)])
 
 
-def cut_and_summed(edge_part, node_part):
+def cut_grads(edge_part, node_part):
     half = node_part[0].shape[1]
     size = node_part[0].shape[0] + 2 * edge_part.shape[0]
-
-    def cut(body, mask, args, size):
-        return call(
-            functools.partial(body, mask),
-            [shape(size // 2, half, dtype=F32), shape(size // 2, half)],
-            args,
-            scratch=[pltpu.VMEM((size, half), F32)],
-        )
-
-    keep, send = cut(first_cut_body, CORE, (edge_part, *node_part), size)
-    keep, send = cut(next_cut_body, ALONG_Y, (keep, swapped(send, "dom", CORE)), size // 2)
-    out = [shape(*send.shape)]
-    (mine,) = call(sum_body, out, (keep, swapped(send, "dom", ALONG_Y)))
-    return call(sum_body, out, (mine, swapped(mine, "dom", ALONG_Z)))[0]
-
-
-def joined(mine, back, width):
-    (mine,) = call(sum_body, [shape(*mine.shape)], (mine, swapped(mine, "dom", 2 * ALONG_Z)))
+    piece = shape(size // 4, half)
+    keep, *send = call(
+        cut_body,
+        [shape(size // 4, half, dtype=F32), piece, piece, piece],
+        (edge_part, *node_part),
+        scratch=[pltpu.VMEM((size, half), F32)],
+    )
+    masks = (CORE, ALONG_Y, CORE | ALONG_Y)
+    return keep, [swapped(part, "dom", mask) for part, mask in zip(send, masks)]
+
+
+def joined(keep, parts, back, width, stage):
+    out = [shape(*keep.shape)]
+    (mine,) = call(sum_all_body, out, (keep, *parts), nbytes=stage)
+    for mask in (ALONG_Z, 2 * ALONG_Z):
+        (mine,) = call(sum_body, out, (mine, swapped(mine, "dom", mask)), nbytes=stage)
     (mine,) = call(
         functools.partial(join_body, ALONG_Y),
         [shape(6 * (width // 4), width)],
         (mine, swapped(mine, "dp", 1), swapped(mine, "dom", ALONG_Y), swapped_both(mine, ALONG_Y)),
+        nbytes=stage,
     )
     mine, back = lax.optimization_barrier((mine, back))
     grad_edge, grad_node = call(
         functools.partial(finish_body, CORE),
         [shape(width, width, dtype=F32), shape(2 * width, width, dtype=F32)],
         (mine, swapped(mine, "dom", CORE)),
+        nbytes=stage,
     )
     return grad_edge, grad_node, back
 
@@ -392,22 +400,25 @@
         picked.reshape(ndom, per_peer, width), "dom", split_axis=0, concat_axis=0, tiled=True
     ).reshape(rows, width)
     spots = blocks + 2 * RIM + 1
-    adj, adj_rim, adj_t = call(
+    adj, adj_t, adj_rim = call(
         build_body,
-        [shape(blocks, ROWS, rows), shape(2 * RIM, ROWS, rows), shape(rows, spots * ROWS)],
+        [shape(blocks, ROWS, rows), shape(rows, spots * ROWS), shape(STORE // (2 * ROWS * rows), ROWS, rows)],
         (adj_count, adj_target, adj_vals),
         [SMEM, SMEM, VMEM],
-        [pltpu.VMEM((spots, ROWS, rows), BF16)],
+        [pltpu.VMEM((spots, ROWS, rows), BF16), pltpu.SemaphoreType.DMA],
         nbytes=16 * unit,
+        out_specs=[VMEM, VMEM, ANY],
+        limit=40 * MIB,
     )
     near, far, msg = call(
         message_body,
         [edge, edge, tall],
         (nodes, adj_rim, w_edge),
         [VMEM, ANY, VMEM],
-        [pltpu.VMEM((2 * RIM, ROWS, rows), BF16), pltpu.SemaphoreType.DMA],
+        [pltpu.VMEM((2 * RIM, ROWS, rows), BF16), pltpu.SemaphoreType.DMA((2 * RIM,))],
         flops=square + 4 * rim * rows * width,
         nbytes=4 * unit,
+        limit=40 * MIB,
     )
     far = swapped_across(far, "dom")
     near = swapped(near, "dom", 1)
@@ -459,13 +470,12 @@
         nbytes=8 * unit,
     )
     if tiled:
-        mine = cut_and_summed(edge_part, node_part)
-        back, mine = lax.optimization_barrier((back, mine))
+        keep, parts = cut_grads(edge_part, node_part)
     back = lax.all_to_all(
         back.reshape(ndom, per_peer, width), "dom", split_axis=0, concat_axis=0, tiled=True
     ).reshape(rows, width)
     if tiled:
-        grad_edge, grad_node, back = joined(mine, back, width)
+        grad_edge, grad_node, back = joined(keep, parts, back, width, 32 * unit)
     else:
         grad_edge, grad_node = (lax.psum(part, ("dp", "dom")) for part in (edge_part, node_part[0]))
     (grad_brick,) = call(place_body, [tall], (send_order, back), flops=2 * rows * rows * width, nbytes=2 * unit)

time: 87.3 us -> 83.4 us (0.955)
  waiting for transfers between devices: 38.1 us -> 30.6 us
  starting transfers between devices: 25.7 us -> 30 us
  local copies, waits for them, and re-layouts: 6.54 us -> 4.35 us
  Pallas kernels: 15.6 us -> 17.2 us
    ppermute x10 -> x11, waiting for transfers between devices: 27.1 us -> 17.2 us  [swapped(): return lax.ppermute(x, axis, [(i, i ^ mask) for i in range(peers)])]
    ppermute x10 -> x11, starting transfers between devices: 5.92 us -> 10.5 us  [swapped(): return lax.ppermute(x, axis, [(i, i ^ mask) for i in range(peers)])]
    unnamed x21 -> x17, local copies, waits for them, and re-layouts: 6.54 us -> 4.35 us
    ppermute x2, waiting for transfers between devices: 2.34 us -> 4.4 us  [swapped_across(): lax.ppermute(x, axis, [(i, (i + 1 if i % 2 else i - 1) % peers) for i in...]
    pallas_call x16 -> x15, Pallas kernels: 15.6 us -> 17.2 us  [call(): pl.pallas_call(body, out_shape=outs, in_specs=specs or [VMEM] * len(args)...]
  transfers between devices with their start and end apart: 15 -> 16, of which waited for: 10 -> 11; matrix products, arithmetic and copies ran while one was open for 1% -> 1% of each run, Pallas kernels for 12% -> 11%
where the time goes in v2:
time: 83.4 us; the launch traced here: 82.9 us
  waiting for transfers between devices  30.6 us (37%)
  starting transfers between devices  30 us (36%)
  Pallas kernels  17.2 us (21%)
  local copies, waits for them, and re-layouts  4.35 us (5%)
    ppermute x11, waiting for transfers between devices, swapped(): return lax.ppermute(x, axis, [(i, i ^ mask) for i in range(peers)])  17.2 us
    pallas_call x15, Pallas kernels, call(): pl.pallas_call(body, out_shape=outs, in_specs=specs or [VMEM] * len(args)...  17.2 us
    ppermute x11, starting transfers between devices, swapped(): return lax.ppermute(x, axis, [(i, i ^ mask) for i in range(peers)])  10.5 us
    all_to_all x1, starting transfers between devices, shards(): lax.all_to_all(picked.reshape(ndom, per_peer, width), 'dom', split_axis=0...  7.4 us
    all_to_all x1, waiting for transfers between devices, shards(): lax.all_to_all(picked.reshape(ndom, per_peer, width), 'dom', split_axis=0...  7.34 us
    ppermute x2, starting transfers between devices, swapped_across(): lax.ppermute(x, axis, [(i, (i + 1 if i % 2 else i - 1) % peers) for i in...  5.63 us
    ppermute x2, waiting for transfers between devices, swapped_across(): lax.ppermute(x, axis, [(i, (i + 1 if i % 2 else i - 1) % peers) for i in...  4.4 us
    unnamed x17, local copies, waits for them, and re-layouts  4.35 us
  transfers between devices with their start and end apart: 16, of which 11 were waited for; matrix products, arithmetic and copies ran while one was open for 1% of the time, Pallas kernels for 11%

profile of v2, /device:TPU:0, one launch (start us, length us, event | category | flops | bytes accessed | tf_op | source)
XLA Modules:
  0.0 82.9 jit_solution(5157006209357996924)
XLA Ops:
  0.6 0.0 copy-start.3
  0.6 2.7 %shard_map.111 = bf16[1024,256]{1,0:T(8,128)(2,1)} custom-call(s32[1,1024]{1,0:T(1,128)} %order_ref.1, bf16[1024,256]{1,0:T(8,128)(2,1)} %bitcast.18), custom_call_target="tpu_custom_call" | custom-call | flops 536870912 | bytes 1048576 | tf_op jit(solution)/shard_map/pallas_call | solution.py:42
  3.3 7.4 %all-to-all-start = ((bf16[16,64,256]{2,1,0:T(8,128)(2,1)}), bf16[16,64,256]{2,1,0:T(8,128)(2,1)S(1)}, u32[]{:S(2)}, u32[]{:S(2)}) async-start(bf16[16,64,256]{2,1,0:T(8,128)(2,1)} %bitcast.17), calls=%async_computation | async-start | bytes 1048576 | tf_op jit(solution)/shard_map/all_to_all | solution.py:399
  10.7 0.8 copy.12.tgt_ref
  11.5 0.0 copy-start.4
  11.5 1.2 %copy-done.4 = bf16[8,4,128,128]{3,2,1,0:T(8,128)(2,1)S(1)} copy-done((bf16[8,4,128,128]{3,2,1,0:T(8,128)(2,1)S(1)}, bf16[8,4,128,128]{3,2,1,0:T(8,128)(2,1)}, u32[]{:S(2)}) %copy-start.4) | copy-done | bytes 1048600
  12.7 0.0 copy-start.6
  12.7 0.7 copy-done.6
  13.4 2.8 %shard_map.112 = (bf16[8,128,1024]{2,1,0:T(8,128)(2,1)S(1)}, bf16[1024,1664]{1,0:T(8,128)(2,1)S(1)}, bf16[96,128,1024]{2,1,0:T(8,128)(2,1)}) custom-call(s32[8]{0:T(128)S(1)} %copy-done.6, s32[8,4]{1,0:T(8,128)S(1)} %copy.12.tgt_ref, bf16[8,4,128,128]{3,2,1,0:T(8,128)(2,1)S(1)} %copy-done.4), custom_call_target="tpu_custom_call" | custom-call | bytes 8388608 | tf_op jit(solution)/shard_map/pallas_call | solution.py:42
  16.1 0.0 copy-start
  16.2 1.7 %copy-done = bf16[1024,1664]{1,0:T(8,128)(2,1)} copy-done((bf16[1024,1664]{1,0:T(8,128)(2,1)}, bf16[1024,1664]{1,0:T(8,128)(2,1)S(1)}, u32[]{:S(2)}) %copy-start) | copy-done | bytes 3407896
  17.8 7.3 %all-to-all-done = bf16[16,64,256]{2,1,0:T(8,128)(2,1)S(1)} async-done(((bf16[16,64,256]{2,1,0:T(8,128)(2,1)}), bf16[16,64,256]{2,1,0:T(8,128)(2,1)S(1)}, u32[]{:S(2)}, u32[]{:S(2)}) %all-to-all-start) | async-done | bytes 524320 | tf_op jit(solution)/shard_map/all_to_all | solution.py:399
  25.2 0.0 copy-done.3
  25.2 0.0 copy-start.2
  25.2 0.0 copy-start.5
  25.2 1.9 %shard_map.113 = (bf16[256,256]{1,0:T(8,128)(2,1)S(1)}, bf16[256,256]{1,0:T(8,128)(2,1)S(1)}, bf16[1024,256]{1,0:T(8,128)(2,1)S(1)}) custom-call(bf16[1024,256]{1,0:T(8,128)(2,1)S(1)} %bitcast.8, bf16[96,128,1024]{2,1,0:T(8,128)(2,1)} %get-tuple-element.39.a_hbm, bf16[256,256]{1,0:T(8,128)(2,1)S(1)} %copy-done.3), custom_call_target="tpu_custom_call" | custom-call | flops 402653184 | bytes 2097152 | tf_op jit(solution)/shard_map/pallas_call | solution.py:42
  27.1 0.0 copy-start.1
  27.1 0.1 collective-permute-start
  27.2 2.8 %collective-permute-start.1 = (bf16[256,256]{1,0:T(8,128)(2,1)S(1)}, bf16[256,256]{1,0:T(8,128)(2,1)S(1)}, u32[]{:S(2)}, u32[]{:S(2)}) collective-permute-start(bf16[256,256]{1,0:T(8,128)(2,1)S(1)} %get-tuple-element.45), channel_id=1, source_target_pairs={{0,15},{1,2},{2,1},{3,4},{4,3},{5,6},{6,5},{7,8},{8,7},{9,10},{10,... | collective-permute-start | bytes 393224 | tf_op jit(solution)/shard_map/ppermute | solution.py:30
  30.0 0.0 copy-done.2
  30.0 0.0 copy-done.5
  30.0 2.6 %shard_map.114 = (bf16[512,256]{1,0:T(8,128)(2,1)S(1)}, bf16[512,256]{1,0:T(8,128)(2,1)S(1)}, bf16[512,256]{1,0:T(8,128)(2,1)S(1)}, bf16[512,256]{1,0:T(8,128)(2...) custom-call(bf16[1024,256]{1,0:T(8,128)(2,1)S(1)} %bitcast.9, ...), custom_call_target="tpu_custom_call" | custom-call | flops 805306368 | bytes 4194304 | tf_op jit(solution)/shard_map/pallas_call | solution.py:42
  32.6 0.0 collective-permute-done.near_in_ref
  32.6 1.7 %collective-permute-done.1.far_in_ref = bf16[256,256]{1,0:T(8,128)(2,1)S(1)} collective-permute-done((bf16[256,256]{1,0:T(8,128)(2,1)S(1)}, bf16[256,256]{1,0:T(8,128)(2,1)S(1)}, u32[]{:S(2)}, u32[]{:S(2)}) %collective-permute-start.1) | collective-permute-done | bytes 131104 | tf_op jit(solution)/shard_map/ppermute | solution.py:30
  34.3 0.7 shard_map.115
  35.0 0.1 collective-permute-start.2
  35.1 2.8 %collective-permute-start.3 = (bf16[256,256]{1,0:T(8,128)(2,1)S(1)}, bf16[256,256]{1,0:T(8,128)(2,1)S(1)}, u32[]{:S(2)}, u32[]{:S(2)}) collective-permute-start(bf16[256,256]{1,0:T(8,128)(2,1)S(1)} %get-tuple-element.51), channel_id=1, source_target_pairs={{0,15},{1,2},{2,1},{3,4},{4,3},{5,6},{6,5},{7,8},{8,7},{9,10},{10,... | collective-permute-start | bytes 393224 | tf_op jit(solution)/shard_map/ppermute | solution.py:30
  37.9 0.0 copy-done.1
  37.9 1.6 %shard_map.116 = (bf16[1024,256]{1,0:T(8,128)(2,1)}, f32[1024,256]{1,0:T(8,128)S(1)}, f32[1024,256]{1,0:T(8,128)S(1)}) custom-call(bf16[1024,256]{1,0:T(8,128)(2,1)S(1)} %bitcast.11, bf16[1024,1664]{1,0:T(8,128)(2,1)S(1)} %copy-done.1, bf16[256,256]{1,0:T(8,128)(2,1)S(1)} %copy-done.3, bf16[512,256]{1,0:T(8,128)(2,1)S(1)} %get-tuple-element.42.out_mid_ref, ...), custom_call_target="tpu_custom_call" | custom-call | flops 671088640 | bytes 4194304 | tf_op jit(solution)/shard_map/pallas_call | solution.py:42
  39.5 0.0 collective-permute-done.2.near_ref
  39.5 2.7 %collective-permute-done.3.far_ref = bf16[256,256]{1,0:T(8,128)(2,1)S(1)} collective-permute-done((bf16[256,256]{1,0:T(8,128)(2,1)S(1)}, bf16[256,256]{1,0:T(8,128)(2,1)S(1)}, u32[]{:S(2)}, u32[]{:S(2)}) %collective-permute-start.3) | collective-permute-done | bytes 131104 | tf_op jit(solution)/shard_map/ppermute | solution.py:30
  42.2 1.8 %shard_map.117 = (bf16[1024,256]{1,0:T(8,128)(2,1)}, f32[256,256]{1,0:T(8,128)S(1)}) custom-call(bf16[1024,256]{1,0:T(8,128)(2,1)S(1)} %bitcast.12, bf16[1024,1664]{1,0:T(8,128)(2,1)S(1)} %copy-done.1, bf16[256,256]{1,0:T(8,128)(2,1)S(1)} %collective-permute-done.2.near_ref, bf16[256,256]{1,0:T(8,128)(2,1)S(1)} %collective-permute-done.3.far_ref, ...), custom_call_target="tpu_custom_call" | custom-call | flops 536870912 | bytes 4194304 | tf_op jit(solution)/shard_map/pallas_call | solution.py:42
  44.0 0.0 copy-start.7
  44.0 4.3 %all-to-all-start.1 = ((bf16[16,64,256]{2,1,0:T(8,128)(2,1)}), bf16[16,64,256]{2,1,0:T(8,128)(2,1)S(1)}, u32[]{:S(2)}, u32[]{:S(2)}) async-start(bf16[16,64,256]{2,1,0:T(8,128)(2,1)} %bitcast.5), calls=%async_computation.1 | async-start | bytes 1048576 | tf_op jit(solution)/shard_map/all_to_all | solution.py:474
  48.3 0.5 shard_map.118
  48.8 1.6 %collective-permute-start.4 = (bf16[512,128]{1,0:T(8,128)(2,1)S(1)}, bf16[512,128]{1,0:T(8,128)(2,1)S(1)}, u32[]{:S(2)}, u32[]{:S(2)}) collective-permute-start(bf16[512,128]{1,0:T(8,128)(2,1)S(1)} %get-tuple-element.62), channel_id=1, source_target_pairs={{0,16},{16,0},{1,17},{17,1},{2,18},{18,2},{3,19},{19,3},{4,20},{20... | collective-permute-start | bytes 393224 | tf_op jit(solution)/shard_map/ppermute | solution.py:25
  50.3 4.3 %collective-permute-done.4.node_in_ref = bf16[512,128]{1,0:T(8,128)(2,1)S(1)} collective-permute-done((bf16[512,128]{1,0:T(8,128)(2,1)S(1)}, bf16[512,128]{1,0:T(8,128)(2,1)S(1)}, u32[]{:S(2)}, u32[]{:S(2)}) %collective-permute-start.4) | collective-permute-done | bytes 131104 | tf_op jit(solution)/shard_map/ppermute | solution.py:25
  54.6 0.1 shard_map.119
  54.7 0.1 collective-permute-start.5
  54.8 1.7 %collective-permute-start.6 = (bf16[256,128]{1,0:T(8,128)(2,1)S(1)}, bf16[256,128]{1,0:T(8,128)(2,1)S(1)}, u32[]{:S(2)}, u32[]{:S(2)}) collective-permute-start(bf16[256,128]{1,0:T(8,128)(2,1)S(1)} %get-tuple-element.65), channel_id=1, source_target_pairs={{0,2},{1,3},{2,0},{3,1},{4,6},{5,7},{6,4},{7,5},{8,10},{9,11},{10,... | collective-permute-start | bytes 196616 | tf_op jit(solution)/shard_map/ppermute | solution.py:25
  56.5 0.2 collective-permute-start.7
  56.7 0.0 collective-permute-done.5.refs_0_
  56.7 3.3 %collective-permute-done.6.refs_1_ = bf16[256,128]{1,0:T(8,128)(2,1)S(1)} collective-permute-done((bf16[256,128]{1,0:T(8,128)(2,1)S(1)}, bf16[256,128]{1,0:T(8,128)(2,1)S(1)}, u32[]{:S(2)}, u32[]{:S(2)}) %collective-permute-start.6) | collective-permute-done | bytes 65568 | tf_op jit(solution)/shard_map/ppermute | solution.py:25
  59.9 1.3 %collective-permute-done.7.refs_2_ = bf16[256,128]{1,0:T(8,128)(2,1)S(1)} collective-permute-done((bf16[256,128]{1,0:T(8,128)(2,1)S(1)}, bf16[256,128]{1,0:T(8,128)(2,1)S(1)}, u32[]{:S(2)}, u32[]{:S(2)}) %collective-permute-start.7) | collective-permute-done | bytes 65568 | tf_op jit(solution)/shard_map/ppermute | solution.py:25
  61.2 2.5 %collective-permute-start.8 = (bf16[256,128]{1,0:T(8,128)(2,1)S(1)}, bf16[256,128]{1,0:T(8,128)(2,1)S(1)}, u32[]{:S(2)}, u32[]{:S(2)}) collective-permute-start(bf16[256,128]{1,0:T(8,128)(2,1)S(1)} %shard_map.120.mine_ref), channel_id=1, source_target_pairs={{0,4},{1,5},{2,6},{3,7},{4,0},{5,1},{6,2},{7,3},{8,12},{9,13},{10,... | collective-permute-start | bytes 196616 | tf_op jit(solution)/shard_map/ppermute | solution.py:25
  63.7 2.6 %collective-permute-done.8.in_ref = bf16[256,128]{1,0:T(8,128)(2,1)S(1)} collective-permute-done((bf16[256,128]{1,0:T(8,128)(2,1)S(1)}, bf16[256,128]{1,0:T(8,128)(2,1)S(1)}, u32[]{:S(2)}, u32[]{:S(2)}) %collective-permute-start.8) | collective-permute-done | bytes 65568 | tf_op jit(solution)/shard_map/ppermute | solution.py:25
  66.3 3.0 %collective-permute-start.9 = (bf16[256,128]{1,0:T(8,128)(2,1)S(1)}, bf16[256,128]{1,0:T(8,128)(2,1)S(1)}, u32[]{:S(2)}, u32[]{:S(2)}) collective-permute-start(bf16[256,128]{1,0:T(8,128)(2,1)S(1)} %shard_map.121.mine_ref), channel_id=1, source_target_pairs={{0,8},{1,9},{2,10},{3,11},{4,12},{5,13},{6,14},{7,15},{8,0},{9,1},... | collective-permute-start | bytes 196616 | tf_op jit(solution)/shard_map/ppermute | solution.py:25
  69.3 3.7 %collective-permute-done.9.in_ref = bf16[256,128]{1,0:T(8,128)(2,1)S(1)} collective-permute-done((bf16[256,128]{1,0:T(8,128)(2,1)S(1)}, bf16[256,128]{1,0:T(8,128)(2,1)S(1)}, u32[]{:S(2)}, u32[]{:S(2)}) %collective-permute-start.9) | collective-permute-done | bytes 65568 | tf_op jit(solution)/shard_map/ppermute | solution.py:25
  73.0 2.2 %collective-permute-start.12 = (bf16[256,128]{1,0:T(8,128)(2,1)S(1)}, bf16[256,128]{1,0:T(8,128)(2,1)S(1)}, u32[]{:S(2)}, u32[]{:S(2)}) collective-permute-start(bf16[256,128]{1,0:T(8,128)(2,1)S(1)} %shard_map.122.mine_ref), channel_id=1, source_target_pairs={{0,18},{1,19},{2,16},{3,17},{4,22},{5,23},{6,20},{7,21},{8,26},{9,... | collective-permute-start | bytes 196616 | tf_op jit(solution)/shard_map/ppermute | solution.py:318
  75.1 0.9 %collective-permute-start.11 = (bf16[256,128]{1,0:T(8,128)(2,1)S(1)}, bf16[256,128]{1,0:T(8,128)(2,1)S(1)}, u32[]{:S(2)}, u32[]{:S(2)}) collective-permute-start(bf16[256,128]{1,0:T(8,128)(2,1)S(1)} %shard_map.122.mine_ref), channel_id=1, source_target_pairs={{0,2},{1,3},{2,0},{3,1},{4,6},{5,7},{6,4},{7,5},{8,10},{9,11},{10,... | collective-permute-start | bytes 196616 | tf_op jit(solution)/shard_map/ppermute | solution.py:25
  76.0 0.5 collective-permute-start.10
  76.5 1.7 %collective-permute-done.12.both_ref = bf16[256,128]{1,0:T(8,128)(2,1)S(1)} collective-permute-done((bf16[256,128]{1,0:T(8,128)(2,1)S(1)}, bf16[256,128]{1,0:T(8,128)(2,1)S(1)}, u32[]{:S(2)}, u32[]{:S(2)}) %collective-permute-start.12) | collective-permute-done | bytes 65568 | tf_op jit(solution)/shard_map/ppermute | solution.py:318
  78.2 1.2 %collective-permute-done.11.y_ref = bf16[256,128]{1,0:T(8,128)(2,1)S(1)} collective-permute-done((bf16[256,128]{1,0:T(8,128)(2,1)S(1)}, bf16[256,128]{1,0:T(8,128)(2,1)S(1)}, u32[]{:S(2)}, u32[]{:S(2)}) %collective-permute-start.11) | collective-permute-done | bytes 65568 | tf_op jit(solution)/shard_map/ppermute | solution.py:25
  79.4 0.9 %collective-permute-done.10.dp_ref = bf16[256,128]{1,0:T(8,128)(2,1)S(1)} collective-permute-done((bf16[256,128]{1,0:T(8,128)(2,1)S(1)}, bf16[256,128]{1,0:T(8,128)(2,1)S(1)}, u32[]{:S(2)}, u32[]{:S(2)}) %collective-permute-start.10) | collective-permute-done | bytes 65568 | tf_op jit(solution)/shard_map/ppermute | solution.py:25
  80.2 0.1 shard_map.123.mine_ref
  80.3 0.0 all-to-all-done.1
  80.3 0.1 collective-permute-start.13
  80.4 0.0 copy-done.7
  80.4 1.5 %shard_map.124 = bf16[1024,256]{1,0:T(8,128)(2,1)} custom-call(s32[1,1024]{1,0:T(1,128)S(1)} %copy-done.7, bf16[1024,256]{1,0:T(8,128)(2,1)S(1)} %bitcast.16), custom_call_target="tpu_custom_call" | custom-call | flops 536870912 | bytes 1048576 | tf_op jit(solution)/shard_map/pallas_call | solution.py:42
  81.9 0.0 collective-permute-done.13.in_ref
  82.0 1.0 %shard_map.125 = (f32[256,256]{1,0:T(8,128)}, f32[512,256]{1,0:T(8,128)}) custom-call(bf16[384,256]{1,0:T(8,128)(2,1)S(1)} %shard_map.123.mine_ref, bf16[384,256]{1,0:T(8,128)(2,1)S(1)} %collective-permute-done.13.in_ref), custom_call_target="tpu_custom_call" | custom-call | bytes 16777216 | tf_op jit(solution)/shard_map/pallas_call | solution.py:42
  (3 shorter events, 0.1 us)
Async XLA Ops:
  0.6 24.6 %copy-start.3 = (bf16[256,256]{1,0:T(8,128)(2,1)S(1)}, bf16[256,256]{1,0:T(8,128)(2,1)}, u32[]{:S(2)}) copy-start(bf16[256,256]{1,0:T(8,128)(2,1)} %w_edge_ref.5) | copy-start | bytes 393220
  3.3 21.9 %all-to-all-start = ((bf16[16,64,256]{2,1,0:T(8,128)(2,1)}), bf16[16,64,256]{2,1,0:T(8,128)(2,1)S(1)}, u32[]{:S(2)}, u32[]{:S(2)}) async-start(bf16[16,64,256]{2,1,0:T(8,128)(2,1)} %bitcast.17), calls=%async_computation | async-start | bytes 1048576 | tf_op jit(solution)/shard_map/all_to_all | solution.py:399
  11.5 1.2 %copy-start.4 = (bf16[8,4,128,128]{3,2,1,0:T(8,128)(2,1)S(1)}, bf16[8,4,128,128]{3,2,1,0:T(8,128)(2,1)}, u32[]{:S(2)}) copy-start(bf16[8,4,128,128]{3,2,1,0:T(8,128)(2,1)} %vals_ref.1) | copy-start | bytes 3145732
  12.7 0.7 copy-start.6
  16.1 1.7 %copy-start = (bf16[1024,1664]{1,0:T(8,128)(2,1)}, bf16[1024,1664]{1,0:T(8,128)(2,1)S(1)}, u32[]{:S(2)}) copy-start(bf16[1024,1664]{1,0:T(8,128)(2,1)S(1)} %get-tuple-element.38.at_ref) | copy-start | bytes 10223620
  25.2 4.8 %copy-start.2 = (bf16[1,1024,256]{2,1,0:T(8,128)(2,1)S(1)}, bf16[1,1024,256]{2,1,0:T(8,128)(2,1)}, u32[]{:S(2)}) copy-start(bf16[1,1024,256]{2,1,0:T(8,128)(2,1)} %param.15) | copy-start | bytes 1572868
  25.2 4.8 %copy-start.5 = (bf16[512,256]{1,0:T(8,128)(2,1)S(1)}, bf16[512,256]{1,0:T(8,128)(2,1)}, u32[]{:S(2)}) copy-start(bf16[512,256]{1,0:T(8,128)(2,1)} %w_node_ref.3) | copy-start | bytes 786436
  27.1 10.8 %copy-start.1 = (bf16[1024,1664]{1,0:T(8,128)(2,1)S(1)}, bf16[1024,1664]{1,0:T(8,128)(2,1)}, u32[]{:S(2)}) copy-start(bf16[1024,1664]{1,0:T(8,128)(2,1)} %copy-done) | copy-start | bytes 10223620
  27.1 5.5 %collective-permute-start = (bf16[256,256]{1,0:T(8,128)(2,1)S(1)}, bf16[256,256]{1,0:T(8,128)(2,1)S(1)}, u32[]{:S(2)}, u32[]{:S(2)}) collective-permute-start(bf16[256,256]{1,0:T(8,128)(2,1)S(1)} %get-tuple-element.44), channel_id=1, source_target_pairs={{0,1},{1,0},{2,3},{3,2},{4,5},{5,4},{6,7},{7,6},{8,9},{9,8},{10,11... | collective-permute-start | bytes 393224 | tf_op jit(solution)/shard_map/ppermute | solution.py:25
  27.2 7.2 %collective-permute-start.1 = (bf16[256,256]{1,0:T(8,128)(2,1)S(1)}, bf16[256,256]{1,0:T(8,128)(2,1)S(1)}, u32[]{:S(2)}, u32[]{:S(2)}) collective-permute-start(bf16[256,256]{1,0:T(8,128)(2,1)S(1)} %get-tuple-element.45), channel_id=1, source_target_pairs={{0,15},{1,2},{2,1},{3,4},{4,3},{5,6},{6,5},{7,8},{8,7},{9,10},{10,... | collective-permute-start | bytes 393224 | tf_op jit(solution)/shard_map/ppermute | solution.py:30
  35.0 4.5 %collective-permute-start.2 = (bf16[256,256]{1,0:T(8,128)(2,1)S(1)}, bf16[256,256]{1,0:T(8,128)(2,1)S(1)}, u32[]{:S(2)}, u32[]{:S(2)}) collective-permute-start(bf16[256,256]{1,0:T(8,128)(2,1)S(1)} %get-tuple-element.50), channel_id=1, source_target_pairs={{0,1},{1,0},{2,3},{3,2},{4,5},{5,4},{6,7},{7,6},{8,9},{9,8},{10,11... | collective-permute-start | bytes 393224 | tf_op jit(solution)/shard_map/ppermute | solution.py:25
  35.1 7.2 %collective-permute-start.3 = (bf16[256,256]{1,0:T(8,128)(2,1)S(1)}, bf16[256,256]{1,0:T(8,128)(2,1)S(1)}, u32[]{:S(2)}, u32[]{:S(2)}) collective-permute-start(bf16[256,256]{1,0:T(8,128)(2,1)S(1)} %get-tuple-element.51), channel_id=1, source_target_pairs={{0,15},{1,2},{2,1},{3,4},{4,3},{5,6},{6,5},{7,8},{8,7},{9,10},{10,... | collective-permute-start | bytes 393224 | tf_op jit(solution)/shard_map/ppermute | solution.py:30
  44.0 36.4 %copy-start.7 = (s32[1,1024]{1,0:T(1,128)S(1)}, s32[1,1024]{1,0:T(1,128)}, u32[]{:S(2)}) copy-start(s32[1,1024]{1,0:T(1,128)} %order_ref.1) | copy-start | bytes 12292
  44.0 36.3 %all-to-all-start.1 = ((bf16[16,64,256]{2,1,0:T(8,128)(2,1)}), bf16[16,64,256]{2,1,0:T(8,128)(2,1)S(1)}, u32[]{:S(2)}, u32[]{:S(2)}) async-start(bf16[16,64,256]{2,1,0:T(8,128)(2,1)} %bitcast.5), calls=%async_computation.1 | async-start | bytes 1048576 | tf_op jit(solution)/shard_map/all_to_all | solution.py:474
  48.8 5.9 %collective-permute-start.4 = (bf16[512,128]{1,0:T(8,128)(2,1)S(1)}, bf16[512,128]{1,0:T(8,128)(2,1)S(1)}, u32[]{:S(2)}, u32[]{:S(2)}) collective-permute-start(bf16[512,128]{1,0:T(8,128)(2,1)S(1)} %get-tuple-element.62), channel_id=1, source_target_pairs={{0,16},{16,0},{1,17},{17,1},{2,18},{18,2},{3,19},{19,3},{4,20},{20... | collective-permute-start | bytes 393224 | tf_op jit(solution)/shard_map/ppermute | solution.py:25
  54.7 1.9 %collective-permute-start.5 = (bf16[256,128]{1,0:T(8,128)(2,1)S(1)}, bf16[256,128]{1,0:T(8,128)(2,1)S(1)}, u32[]{:S(2)}, u32[]{:S(2)}) collective-permute-start(bf16[256,128]{1,0:T(8,128)(2,1)S(1)} %get-tuple-element.64), channel_id=1, source_target_pairs={{0,1},{1,0},{2,3},{3,2},{4,5},{5,4},{6,7},{7,6},{8,9},{9,8},{10,11... | collective-permute-start | bytes 196616 | tf_op jit(solution)/shard_map/ppermute | solution.py:25
  54.8 5.1 %collective-permute-start.6 = (bf16[256,128]{1,0:T(8,128)(2,1)S(1)}, bf16[256,128]{1,0:T(8,128)(2,1)S(1)}, u32[]{:S(2)}, u32[]{:S(2)}) collective-permute-start(bf16[256,128]{1,0:T(8,128)(2,1)S(1)} %get-tuple-element.65), channel_id=1, source_target_pairs={{0,2},{1,3},{2,0},{3,1},{4,6},{5,7},{6,4},{7,5},{8,10},{9,11},{10,... | collective-permute-start | bytes 196616 | tf_op jit(solution)/shard_map/ppermute | solution.py:25
  56.5 4.7 %collective-permute-start.7 = (bf16[256,128]{1,0:T(8,128)(2,1)S(1)}, bf16[256,128]{1,0:T(8,128)(2,1)S(1)}, u32[]{:S(2)}, u32[]{:S(2)}) collective-permute-start(bf16[256,128]{1,0:T(8,128)(2,1)S(1)} %get-tuple-element.66), channel_id=1, source_target_pairs={{0,3},{1,2},{2,1},{3,0},{4,7},{5,6},{6,5},{7,4},{8,11},{9,10},{10,... | collective-permute-start | bytes 196616 | tf_op jit(solution)/shard_map/ppermute | solution.py:25
  61.2 5.1 %collective-permute-start.8 = (bf16[256,128]{1,0:T(8,128)(2,1)S(1)}, bf16[256,128]{1,0:T(8,128)(2,1)S(1)}, u32[]{:S(2)}, u32[]{:S(2)}) collective-permute-start(bf16[256,128]{1,0:T(8,128)(2,1)S(1)} %shard_map.120.mine_ref), channel_id=1, source_target_pairs={{0,4},{1,5},{2,6},{3,7},{4,0},{5,1},{6,2},{7,3},{8,12},{9,13},{10,... | collective-permute-start | bytes 196616 | tf_op jit(solution)/shard_map/ppermute | solution.py:25
  66.3 6.6 %collective-permute-start.9 = (bf16[256,128]{1,0:T(8,128)(2,1)S(1)}, bf16[256,128]{1,0:T(8,128)(2,1)S(1)}, u32[]{:S(2)}, u32[]{:S(2)}) collective-permute-start(bf16[256,128]{1,0:T(8,128)(2,1)S(1)} %shard_map.121.mine_ref), channel_id=1, source_target_pairs={{0,8},{1,9},{2,10},{3,11},{4,12},{5,13},{6,14},{7,15},{8,0},{9,1},... | collective-permute-start | bytes 196616 | tf_op jit(solution)/shard_map/ppermute | solution.py:25
  73.0 5.2 %collective-permute-start.12 = (bf16[256,128]{1,0:T(8,128)(2,1)S(1)}, bf16[256,128]{1,0:T(8,128)(2,1)S(1)}, u32[]{:S(2)}, u32[]{:S(2)}) collective-permute-start(bf16[256,128]{1,0:T(8,128)(2,1)S(1)} %shard_map.122.mine_ref), channel_id=1, source_target_pairs={{0,18},{1,19},{2,16},{3,17},{4,22},{5,23},{6,20},{7,21},{8,26},{9,... | collective-permute-start | bytes 196616 | tf_op jit(solution)/shard_map/ppermute | solution.py:318
  75.1 4.3 %collective-permute-start.11 = (bf16[256,128]{1,0:T(8,128)(2,1)S(1)}, bf16[256,128]{1,0:T(8,128)(2,1)S(1)}, u32[]{:S(2)}, u32[]{:S(2)}) collective-permute-start(bf16[256,128]{1,0:T(8,128)(2,1)S(1)} %shard_map.122.mine_ref), channel_id=1, source_target_pairs={{0,2},{1,3},{2,0},{3,1},{4,6},{5,7},{6,4},{7,5},{8,10},{9,11},{10,... | collective-permute-start | bytes 196616 | tf_op jit(solution)/shard_map/ppermute | solution.py:25
  76.0 4.3 %collective-permute-start.10 = (bf16[256,128]{1,0:T(8,128)(2,1)S(1)}, bf16[256,128]{1,0:T(8,128)(2,1)S(1)}, u32[]{:S(2)}, u32[]{:S(2)}) collective-permute-start(bf16[256,128]{1,0:T(8,128)(2,1)S(1)} %shard_map.122.mine_ref), channel_id=1, source_target_pairs={{0,16},{16,0},{1,17},{17,1},{2,18},{18,2},{3,19},{19,3},{4,20},{20... | collective-permute-start | bytes 196616 | tf_op jit(solution)/shard_map/ppermute | solution.py:25
  80.3 1.6 %collective-permute-start.13 = (bf16[384,256]{1,0:T(8,128)(2,1)S(1)}, bf16[384,256]{1,0:T(8,128)(2,1)S(1)}, u32[]{:S(2)}, u32[]{:S(2)}) collective-permute-start(bf16[384,256]{1,0:T(8,128)(2,1)S(1)} %shard_map.123.mine_ref), channel_id=1, source_target_pairs={{0,1},{1,0},{2,3},{3,2},{4,5},{5,4},{6,7},{7,6},{8,9},{9,8},{10,11... | collective-permute-start | bytes 589832 | tf_op jit(solution)/shard_map/ppermute | solution.py:25

commit v3 on v2

--- a/solution.py
+++ b/solution.py
@@ -76,7 +76,7 @@
         out_ref[mine, :] = dot(hot, feat).astype(BF16)
 
 
-def build_body(cnt_ref, tgt_ref, vals_ref, own_ref, at_ref, rim_hbm, a_ref, sem):
+def build_body(cnt_ref, tgt_ref, vals_ref, rim_ref, at_ref, own_hbm, a_ref, sem):
     blocks, slots = vals_ref.shape[:2]
     spare = blocks + 2 * RIM
     a_ref[...] = jnp.zeros_like(a_ref)
@@ -91,9 +91,9 @@
             a_ref[at, :, mine] = (a_ref[at, :, mine].astype(F32) + value).astype(BF16)
             lanes = pl.ds(pl.multiple_of(at * ROWS, ROWS), ROWS)
             at_ref[mine, lanes] = (at_ref[mine, lanes].astype(F32) + jnp.transpose(value)).astype(BF16)
-    put = pltpu.make_async_copy(a_ref.at[pl.ds(blocks, 2 * RIM)], rim_hbm.at[pl.ds(0, 2 * RIM)], sem)
+    put = pltpu.make_async_copy(a_ref.at[pl.ds(0, blocks)], own_hbm.at[pl.ds(0, blocks)], sem)
     put.start()
-    own_ref[...] = a_ref[:blocks]
+    rim_ref[...] = a_ref[blocks:spare]
     put.wait()
 
 
@@ -102,18 +102,13 @@
     return jnp.where(odd, first, second), jnp.where(odd, second, first)
 
 
-def message_body(nodes_ref, a_hbm, w_edge_ref, near_ref, far_ref, msg_ref, a_ref, a_sems):
+def message_body(nodes_ref, a_ref, w_edge_ref, near_ref, far_ref, msg_ref):
     rows = nodes_ref.shape[0]
     rim = RIM * ROWS
-    loads = [pltpu.make_async_copy(a_hbm.at[b], a_ref.at[b], a_sems.at[b]) for b in range(2 * RIM)]
-    for load in loads:
-        load.start()
     for k in range(rows // rim):
         mine = slice(k * rim, (k + 1) * rim)
         pre = dot(nodes_ref[mine, :], w_edge_ref[...])
         msg_ref[mine, :] = (pre * jax.nn.sigmoid(pre)).astype(BF16)
-    for load in loads:
-        load.wait()
     sums = dot(a_ref[...].reshape(2 * rim, rows), msg_ref[...])
     near, far = chosen(sums[:rim], sums[rim:])
     near_ref[...] = near.astype(BF16)
@@ -300,16 +295,41 @@
         out_ref[row : row + more, half:] = jnp.where(first, b[:more], a[:more])
 
 
-def finish_body(mask, mine_ref, in_ref, edge_ref, node_ref):
-    few, more = edge_ref.shape[0] // 4, node_ref.shape[0] // 4
-    low = bit_of(mask) == 0
-    mine, other = mine_ref[...].astype(F32), in_ref[...].astype(F32)
-    for side, value in enumerate((jnp.where(low, mine, other), jnp.where(low, other, mine))):
-        for part in range(2):
-            q = 2 * side + part
-            row = part * (few + more)
-            edge_ref[q * few : (q + 1) * few, :] = value[row : row + few]
-            node_ref[q * more : (q + 1) * more, :] = value[row + few : row + few + more]
+def finish_body(own, *refs):
+    part_ref = refs[0]
+    edge_hbm, node_hbm, edge_ref, node_ref, sems = refs[-5:]
+    few, more = edge_ref.shape[0] // 2, node_ref.shape[0] // 2
+    for k in range(2):
+        row = k * (few + more)
+        edge_ref[k * few : (k + 1) * few, :] = part_ref[row : row + few, :].astype(F32)
+        node_ref[k * more : (k + 1) * more, :] = part_ref[row + few : row + few + more, :].astype(F32)
+    side = bit_of(CORE) if own else 1 - bit_of(CORE)
+    puts = []
+    for k, (ref, hbm) in enumerate(((edge_ref, edge_hbm), (node_ref, node_hbm))):
+        size = ref.shape[0]
+        to = hbm.at[pl.ds(pl.multiple_of(side * size, 8), size), :]
+        puts.append(pltpu.make_async_copy(ref, to, sems.at[k]))
+        puts[k].start()
+    for put in puts:
+        put.wait()
+
+
+def finished(own, part, grads, width):
+    outs = [shape(width, width, dtype=F32), shape(2 * width, width, dtype=F32)]
+    return pl.pallas_call(
+        functools.partial(finish_body, own),
+        out_shape=outs,
+        in_specs=[VMEM] + [ANY] * len(grads),
+        out_specs=[ANY, ANY],
+        scratch_shapes=[
+            pltpu.VMEM((width // 2, width), F32),
+            pltpu.VMEM((width, width), F32),
+            pltpu.SemaphoreType.DMA((2,)),
+        ],
+        input_output_aliases={1: 0, 2: 1} if grads else {},
+        cost_estimate=pl.CostEstimate(flops=0, bytes_accessed=3 * width * width * 4, transcendentals=0),
+        compiler_params=pltpu.CompilerParams(vmem_limit_bytes=24 * MIB),
+    )(part, *grads)
 
 
 def swapped_both(x, mask):
@@ -332,7 +352,7 @@
     return keep, [swapped(part, "dom", mask) for part, mask in zip(send, masks)]
 
 
-def joined(keep, parts, back, width, stage):
+def joined(keep, parts, width, stage):
     out = [shape(*keep.shape)]
     (mine,) = call(sum_all_body, out, (keep, *parts), nbytes=stage)
     for mask in (ALONG_Z, 2 * ALONG_Z):
@@ -343,14 +363,14 @@
         (mine, swapped(mine, "dp", 1), swapped(mine, "dom", ALONG_Y), swapped_both(mine, ALONG_Y)),
         nbytes=stage,
     )
-    mine, back = lax.optimization_barrier((mine, back))
-    grad_edge, grad_node = call(
-        functools.partial(finish_body, CORE),
-        [shape(width, width, dtype=F32), shape(2 * width, width, dtype=F32)],
-        (mine, swapped(mine, "dom", CORE)),
-        nbytes=stage,
-    )
-    return grad_edge, grad_node, back
+    return mine
+
+
+def ended(mine, grad_brick, width):
+    mine, grad_brick = lax.optimization_barrier((mine, grad_brick))
+    other = swapped(mine, "dom", CORE)
+    grads = finished(True, mine, (), width)
+    return *finished(False, other, grads, width), grad_brick
 
 
 def place_body(order_ref, back_ref, out_ref):
@@ -400,9 +420,9 @@
         picked.reshape(ndom, per_peer, width), "dom", split_axis=0, concat_axis=0, tiled=True
     ).reshape(rows, width)
     spots = blocks + 2 * RIM + 1
-    adj, adj_t, adj_rim = call(
+    adj_rim, adj_t, adj = call(
         build_body,
-        [shape(blocks, ROWS, rows), shape(rows, spots * ROWS), shape(STORE // (2 * ROWS * rows), ROWS, rows)],
+        [shape(2 * RIM, ROWS, rows), shape(rows, spots * ROWS), shape(STORE // (2 * ROWS * rows), ROWS, rows)],
         (adj_count, adj_target, adj_vals),
         [SMEM, SMEM, VMEM],
         [pltpu.VMEM((spots, ROWS, rows), BF16), pltpu.SemaphoreType.DMA],
@@ -414,11 +434,8 @@
         message_body,
         [edge, edge, tall],
         (nodes, adj_rim, w_edge),
-        [VMEM, ANY, VMEM],
-        [pltpu.VMEM((2 * RIM, ROWS, rows), BF16), pltpu.SemaphoreType.DMA((2 * RIM,))],
         flops=square + 4 * rim * rows * width,
         nbytes=4 * unit,
-        limit=40 * MIB,
     )
     far = swapped_across(far, "dom")
     near = swapped(near, "dom", 1)
@@ -431,6 +448,7 @@
         [pltpu.VMEM((blocks, ROWS, rows), BF16), pltpu.SemaphoreType.DMA((rows // rim,))],
         flops=2 * rows * rows * width + 2 * square,
         nbytes=8 * unit,
+        limit=40 * MIB,
     )
     near, far, out_rim, agg_rim, d_node_rim, d_nodes1_rim, d_agg_rim = call(
         rim_body,
@@ -470,15 +488,18 @@
         nbytes=8 * unit,
     )
     if tiled:
-        keep, parts = cut_grads(edge_part, node_part)
+        back, node_in = lax.optimization_barrier((back, node_part[1]))
+        keep, parts = cut_grads(edge_part, (node_part[0], node_in))
     back = lax.all_to_all(
         back.reshape(ndom, per_peer, width), "dom", split_axis=0, concat_axis=0, tiled=True
     ).reshape(rows, width)
     if tiled:
-        grad_edge, grad_node, back = joined(keep, parts, back, width, 32 * unit)
+        mine = joined(keep, parts, width, 32 * unit)
     else:
         grad_edge, grad_node = (lax.psum(part, ("dp", "dom")) for part in (edge_part, node_part[0]))
     (grad_brick,) = call(place_body, [tall], (send_order, back), flops=2 * rows * rows * width, nbytes=2 * unit)
+    if tiled:
+        grad_edge, grad_node, grad_brick = ended(mine, grad_brick, width)
     return (node_out[None], grad_brick[None], grad_edge, grad_node)
 
 

time: 83.4 us -> 81.6 us (0.978)
  starting transfers between devices: 30 us -> 26.1 us
  local copies, waits for them, and re-layouts: 4.35 us -> 7.38 us
  waiting for transfers between devices: 30.6 us -> 29 us
    unnamed x17 -> x19, local copies, waits for them, and re-layouts: 4.35 us -> 7.38 us
    ppermute x2, waiting for transfers between devices: 4.4 us -> 1.73 us  [swapped_across(): lax.ppermute(x, axis, [(i, (i + 1 if i % 2 else i - 1) % peers) for i in...]
    ppermute x11, starting transfers between devices: 10.5 us -> 8.4 us  [swapped(): return lax.ppermute(x, axis, [(i, i ^ mask) for i in range(peers)])]
    pallas_call x0 -> x2, Pallas kernels: none -> 1.55 us  [finished(): pl.pallas_call(functools.partial(finish_body, own), out_shape=outs, in_sp...]
    ppermute x11, waiting for transfers between devices: 17.2 us -> 18.5 us  [swapped(): return lax.ppermute(x, axis, [(i, i ^ mask) for i in range(peers)])]
    ppermute x2, starting transfers between devices: 5.63 us -> 4.57 us  [swapped_across(): lax.ppermute(x, axis, [(i, (i + 1 if i % 2 else i - 1) % peers) for i in...]
    pallas_call x15 -> x14, Pallas kernels: 17.2 us -> 16.2 us  [call(): pl.pallas_call(body, out_shape=outs, in_specs=specs or [VMEM] * len(args)...]
  transfers between devices with their start and end apart: 16 -> 16, of which waited for: 11 -> 10; matrix products, arithmetic and copies ran while one was open for 1% -> 1% of each run, Pallas kernels for 11% -> 14%
where the time goes in v3:
time: 81.6 us; the launch traced here: 81.1 us
  waiting for transfers between devices  29 us (36%)
  starting transfers between devices  26.1 us (32%)
  Pallas kernels  17.8 us (22%)
  local copies, waits for them, and re-layouts  7.38 us (9%)
    ppermute x11, waiting for transfers between devices, swapped(): return lax.ppermute(x, axis, [(i, i ^ mask) for i in range(peers)])  18.5 us
    pallas_call x14, Pallas kernels, call(): pl.pallas_call(body, out_shape=outs, in_specs=specs or [VMEM] * len(args)...  16.2 us
    ppermute x11, starting transfers between devices, swapped(): return lax.ppermute(x, axis, [(i, i ^ mask) for i in range(peers)])  8.4 us
    all_to_all x1, starting transfers between devices, shards(): lax.all_to_all(picked.reshape(ndom, per_peer, width), 'dom', split_axis=0...  7.4 us
    unnamed x19, local copies, waits for them, and re-layouts  7.38 us
    all_to_all x1, waiting for transfers between devices, shards(): lax.all_to_all(picked.reshape(ndom, per_peer, width), 'dom', split_axis=0...  6.99 us
    ppermute x2, starting transfers between devices, swapped_across(): lax.ppermute(x, axis, [(i, (i + 1 if i % 2 else i - 1) % peers) for i in...  4.57 us
    all_to_all x1, starting transfers between devices, shards(): lax.all_to_all(back.reshape(ndom, per_peer, width), 'dom', split_axis=0,...  3.57 us
  transfers between devices with their start and end apart: 16, of which 10 were waited for; matrix products, arithmetic and copies ran while one was open for 1% of the time, Pallas kernels for 14%

profile of v3, /device:TPU:0, one launch (start us, length us, event | category | flops | bytes accessed | tf_op | source)
XLA Modules:
  0.0 81.1 jit_solution(11321847302713363336)
XLA Ops:
  0.6 0.0 copy-start.4
  0.6 2.7 %shard_map.111 = bf16[1024,256]{1,0:T(8,128)(2,1)} custom-call(s32[1,1024]{1,0:T(1,128)} %order_ref.1, bf16[1024,256]{1,0:T(8,128)(2,1)} %bitcast.18), custom_call_target="tpu_custom_call" | custom-call | flops 536870912 | bytes 1048576 | tf_op jit(solution)/shard_map/pallas_call | solution.py:42
  3.3 0.0 copy-start.8
  3.3 7.4 %all-to-all-start = ((bf16[16,64,256]{2,1,0:T(8,128)(2,1)}), bf16[16,64,256]{2,1,0:T(8,128)(2,1)S(1)}, u32[]{:S(2)}, u32[]{:S(2)}) async-start(bf16[16,64,256]{2,1,0:T(8,128)(2,1)} %bitcast.17), calls=%async_computation | async-start | bytes 1048576 | tf_op jit(solution)/shard_map/all_to_all | solution.py:419
  10.7 0.8 copy.14.tgt_ref
  11.5 0.0 copy-start.6
  11.5 1.2 %copy-done.6 = bf16[8,4,128,128]{3,2,1,0:T(8,128)(2,1)S(1)} copy-done((bf16[8,4,128,128]{3,2,1,0:T(8,128)(2,1)S(1)}, bf16[8,4,128,128]{3,2,1,0:T(8,128)(2,1)}, u32[]{:S(2)}) %copy-start.6) | copy-done | bytes 1048600
  12.7 0.0 copy-start.7
  12.7 0.7 copy-done.7
  13.4 3.1 %shard_map.112 = (bf16[4,128,1024]{2,1,0:T(8,128)(2,1)S(1)}, bf16[1024,1664]{1,0:T(8,128)(2,1)S(1)}, bf16[96,128,1024]{2,1,0:T(8,128)(2,1)}) custom-call(s32[8]{0:T(128)S(1)} %copy-done.7, s32[8,4]{1,0:T(8,128)S(1)} %copy.14.tgt_ref, bf16[8,4,128,128]{3,2,1,0:T(8,128)(2,1)S(1)} %copy-done.6), custom_call_target="tpu_custom_call" | custom-call | bytes 8388608 | tf_op jit(solution)/shard_map/pallas_call | solution.py:42
  16.5 0.0 copy-start
  16.5 1.7 %copy-done = bf16[1024,1664]{1,0:T(8,128)(2,1)} copy-done((bf16[1024,1664]{1,0:T(8,128)(2,1)}, bf16[1024,1664]{1,0:T(8,128)(2,1)S(1)}, u32[]{:S(2)}) %copy-start) | copy-done | bytes 3407896
  18.2 7.0 %all-to-all-done = bf16[16,64,256]{2,1,0:T(8,128)(2,1)S(1)} async-done(((bf16[16,64,256]{2,1,0:T(8,128)(2,1)}), bf16[16,64,256]{2,1,0:T(8,128)(2,1)S(1)}, u32[]{:S(2)}, u32[]{:S(2)}) %all-to-all-start) | async-done | bytes 524320 | tf_op jit(solution)/shard_map/all_to_all | solution.py:419
  25.2 0.0 copy-start.1
  25.2 0.0 copy-start.3
  25.2 1.1 %copy-done.3 = bf16[256,256]{1,0:T(8,128)(2,1)S(1)} copy-done((bf16[256,256]{1,0:T(8,128)(2,1)S(1)}, bf16[256,256]{1,0:T(8,128)(2,1)}, u32[]{:S(2)}) %copy-start.3) | copy-done | bytes 131096
  26.3 0.7 shard_map.113
  27.0 0.1 collective-permute-start
  27.0 2.8 %collective-permute-start.1 = (bf16[256,256]{1,0:T(8,128)(2,1)S(1)}, bf16[256,256]{1,0:T(8,128)(2,1)S(1)}, u32[]{:S(2)}, u32[]{:S(2)}) collective-permute-start(bf16[256,256]{1,0:T(8,128)(2,1)S(1)} %get-tuple-element.49), channel_id=1, source_target_pairs={{0,15},{1,2},{2,1},{3,4},{4,3},{5,6},{6,5},{7,8},{8,7},{9,10},{10,... | collective-permute-start | bytes 393224 | tf_op jit(solution)/shard_map/ppermute | solution.py:30
  29.9 0.0 copy-start.2
  29.9 1.0 %copy-done.2 = bf16[1,1024,256]{2,1,0:T(8,128)(2,1)S(1)} copy-done((bf16[1,1024,256]{2,1,0:T(8,128)(2,1)S(1)}, bf16[1,1024,256]{2,1,0:T(8,128)(2,1)}, u32[]{:S(2)}) %copy-start.2) | copy-done | bytes 524312
  30.9 0.0 copy-start.5
  30.9 0.9 %copy-done.5 = bf16[512,256]{1,0:T(8,128)(2,1)S(1)} copy-done((bf16[512,256]{1,0:T(8,128)(2,1)S(1)}, bf16[512,256]{1,0:T(8,128)(2,1)}, u32[]{:S(2)}) %copy-start.5) | copy-done | bytes 262168
  31.9 3.5 %shard_map.114 = (bf16[512,256]{1,0:T(8,128)(2,1)S(1)}, bf16[512,256]{1,0:T(8,128)(2,1)S(1)}, bf16[512,256]{1,0:T(8,128)(2,1)S(1)}, bf16[512,256]{1,0:T(8,128)(2...) custom-call(bf16[1024,256]{1,0:T(8,128)(2,1)S(1)} %bitcast.9, ...), custom_call_target="tpu_custom_call" | custom-call | flops 805306368 | bytes 4194304 | tf_op jit(solution)/shard_map/pallas_call | solution.py:42
  35.4 0.0 collective-permute-done.near_in_ref
  35.4 0.0 collective-permute-done.1.far_in_ref
  35.4 0.7 shard_map.115
  36.1 0.1 collective-permute-start.2
  36.1 1.8 %collective-permute-start.3 = (bf16[256,256]{1,0:T(8,128)(2,1)S(1)}, bf16[256,256]{1,0:T(8,128)(2,1)S(1)}, u32[]{:S(2)}, u32[]{:S(2)}) collective-permute-start(bf16[256,256]{1,0:T(8,128)(2,1)S(1)} %get-tuple-element.55), channel_id=1, source_target_pairs={{0,15},{1,2},{2,1},{3,4},{4,3},{5,6},{6,5},{7,8},{8,7},{9,10},{10,... | collective-permute-start | bytes 393224 | tf_op jit(solution)/shard_map/ppermute | solution.py:30
  37.9 0.5 shard_map.118
  38.4 1.6 %collective-permute-start.4 = (bf16[512,128]{1,0:T(8,128)(2,1)S(1)}, bf16[512,128]{1,0:T(8,128)(2,1)S(1)}, u32[]{:S(2)}, u32[]{:S(2)}) collective-permute-start(bf16[512,128]{1,0:T(8,128)(2,1)S(1)} %get-tuple-element.67), channel_id=1, source_target_pairs={{0,16},{16,0},{1,17},{17,1},{2,18},{18,2},{3,19},{19,3},{4,20},{20... | collective-permute-start | bytes 393224 | tf_op jit(solution)/shard_map/ppermute | solution.py:25
  39.9 0.0 copy-done.4
  39.9 0.0 copy-done.1
  39.9 1.6 %shard_map.116 = (bf16[1024,256]{1,0:T(8,128)(2,1)}, f32[1024,256]{1,0:T(8,128)S(1)}, f32[1024,256]{1,0:T(8,128)S(1)}) custom-call(bf16[1024,256]{1,0:T(8,128)(2,1)S(1)} %bitcast.12, bf16[1024,1664]{1,0:T(8,128)(2,1)S(1)} %copy-done.1, bf16[256,256]{1,0:T(8,128)(2,1)S(1)} %copy-done.4, bf16[512,256]{1,0:T(8,128)(2,1)S(1)} %get-tuple-element.46.out_mid_ref, ...), custom_call_target="tpu_custom_call" | custom-call | flops 671088640 | bytes 4194304 | tf_op jit(solution)/shard_map/pallas_call | solution.py:42
  41.6 0.0 collective-permute-done.2.near_ref
  41.6 1.7 %collective-permute-done.3.far_ref = bf16[256,256]{1,0:T(8,128)(2,1)S(1)} collective-permute-done((bf16[256,256]{1,0:T(8,128)(2,1)S(1)}, bf16[256,256]{1,0:T(8,128)(2,1)S(1)}, u32[]{:S(2)}, u32[]{:S(2)}) %collective-permute-start.3) | collective-permute-done | bytes 131104 | tf_op jit(solution)/shard_map/ppermute | solution.py:30
  43.3 1.8 %shard_map.117 = (bf16[1024,256]{1,0:T(8,128)(2,1)}, f32[256,256]{1,0:T(8,128)S(1)}) custom-call(bf16[1024,256]{1,0:T(8,128)(2,1)S(1)} %bitcast.13, bf16[1024,1664]{1,0:T(8,128)(2,1)S(1)} %copy-done.1, bf16[256,256]{1,0:T(8,128)(2,1)S(1)} %collective-permute-done.2.near_ref, bf16[256,256]{1,0:T(8,128)(2,1)S(1)} %collective-permute-done.3.far_ref, ...), custom_call_target="tpu_custom_call" | custom-call | flops 536870912 | bytes 4194304 | tf_op jit(solution)/shard_map/pallas_call | solution.py:42
  45.0 0.0 collective-permute-done.4.node_in_ref
  45.0 3.6 %all-to-all-start.1 = ((bf16[16,64,256]{2,1,0:T(8,128)(2,1)}), bf16[16,64,256]{2,1,0:T(8,128)(2,1)S(1)}, u32[]{:S(2)}, u32[]{:S(2)}) async-start(bf16[16,64,256]{2,1,0:T(8,128)(2,1)} %bitcast.5), calls=%async_computation.1 | async-start | bytes 1048576 | tf_op jit(solution)/shard_map/all_to_all | solution.py:493
  48.6 0.1 shard_map.119
  48.7 0.3 collective-permute-start.5
  49.1 1.7 %collective-permute-start.6 = (bf16[256,128]{1,0:T(8,128)(2,1)S(1)}, bf16[256,128]{1,0:T(8,128)(2,1)S(1)}, u32[]{:S(2)}, u32[]{:S(2)}) collective-permute-start(bf16[256,128]{1,0:T(8,128)(2,1)S(1)} %get-tuple-element.71), channel_id=1, source_target_pairs={{0,2},{1,3},{2,0},{3,1},{4,6},{5,7},{6,4},{7,5},{8,10},{9,11},{10,... | collective-permute-start | bytes 196616 | tf_op jit(solution)/shard_map/ppermute | solution.py:25
  50.8 0.0 collective-permute-start.7
  50.8 0.0 collective-permute-done.5.refs_0_
  50.8 6.3 %collective-permute-done.6.refs_1_ = bf16[256,128]{1,0:T(8,128)(2,1)S(1)} collective-permute-done((bf16[256,128]{1,0:T(8,128)(2,1)S(1)}, bf16[256,128]{1,0:T(8,128)(2,1)S(1)}, u32[]{:S(2)}, u32[]{:S(2)}) %collective-permute-start.6) | collective-permute-done | bytes 65568 | tf_op jit(solution)/shard_map/ppermute | solution.py:25
  57.0 0.5 collective-permute-done.7.refs_2_
  57.5 1.4 %collective-permute-start.8 = (bf16[256,128]{1,0:T(8,128)(2,1)S(1)}, bf16[256,128]{1,0:T(8,128)(2,1)S(1)}, u32[]{:S(2)}, u32[]{:S(2)}) collective-permute-start(bf16[256,128]{1,0:T(8,128)(2,1)S(1)} %shard_map.120.mine_ref), channel_id=1, source_target_pairs={{0,4},{1,5},{2,6},{3,7},{4,0},{5,1},{6,2},{7,3},{8,12},{9,13},{10,... | collective-permute-start | bytes 196616 | tf_op jit(solution)/shard_map/ppermute | solution.py:25
  58.9 4.7 %collective-permute-done.8.in_ref = bf16[256,128]{1,0:T(8,128)(2,1)S(1)} collective-permute-done((bf16[256,128]{1,0:T(8,128)(2,1)S(1)}, bf16[256,128]{1,0:T(8,128)(2,1)S(1)}, u32[]{:S(2)}, u32[]{:S(2)}) %collective-permute-start.8) | collective-permute-done | bytes 65568 | tf_op jit(solution)/shard_map/ppermute | solution.py:25
  63.7 1.9 %collective-permute-start.9 = (bf16[256,128]{1,0:T(8,128)(2,1)S(1)}, bf16[256,128]{1,0:T(8,128)(2,1)S(1)}, u32[]{:S(2)}, u32[]{:S(2)}) collective-permute-start(bf16[256,128]{1,0:T(8,128)(2,1)S(1)} %shard_map.121.mine_ref), channel_id=1, source_target_pairs={{0,8},{1,9},{2,10},{3,11},{4,12},{5,13},{6,14},{7,15},{8,0},{9,1},... | collective-permute-start | bytes 196616 | tf_op jit(solution)/shard_map/ppermute | solution.py:25
  65.5 4.4 %collective-permute-done.9.in_ref = bf16[256,128]{1,0:T(8,128)(2,1)S(1)} collective-permute-done((bf16[256,128]{1,0:T(8,128)(2,1)S(1)}, bf16[256,128]{1,0:T(8,128)(2,1)S(1)}, u32[]{:S(2)}, u32[]{:S(2)}) %collective-permute-start.9) | collective-permute-done | bytes 65568 | tf_op jit(solution)/shard_map/ppermute | solution.py:25
  70.0 2.2 %collective-permute-start.12 = (bf16[256,128]{1,0:T(8,128)(2,1)S(1)}, bf16[256,128]{1,0:T(8,128)(2,1)S(1)}, u32[]{:S(2)}, u32[]{:S(2)}) collective-permute-start(bf16[256,128]{1,0:T(8,128)(2,1)S(1)} %shard_map.122.mine_ref), channel_id=1, source_target_pairs={{0,18},{1,19},{2,16},{3,17},{4,22},{5,23},{6,20},{7,21},{8,26},{9,... | collective-permute-start | bytes 196616 | tf_op jit(solution)/shard_map/ppermute | solution.py:338
  72.2 0.8 %collective-permute-start.11 = (bf16[256,128]{1,0:T(8,128)(2,1)S(1)}, bf16[256,128]{1,0:T(8,128)(2,1)S(1)}, u32[]{:S(2)}, u32[]{:S(2)}) collective-permute-start(bf16[256,128]{1,0:T(8,128)(2,1)S(1)} %shard_map.122.mine_ref), channel_id=1, source_target_pairs={{0,2},{1,3},{2,0},{3,1},{4,6},{5,7},{6,4},{7,5},{8,10},{9,11},{10,... | collective-permute-start | bytes 196616 | tf_op jit(solution)/shard_map/ppermute | solution.py:25
  73.0 0.5 collective-permute-start.10
  73.5 1.8 %collective-permute-done.12.both_ref = bf16[256,128]{1,0:T(8,128)(2,1)S(1)} collective-permute-done((bf16[256,128]{1,0:T(8,128)(2,1)S(1)}, bf16[256,128]{1,0:T(8,128)(2,1)S(1)}, u32[]{:S(2)}, u32[]{:S(2)}) %collective-permute-start.12) | collective-permute-done | bytes 65568 | tf_op jit(solution)/shard_map/ppermute | solution.py:338
  75.3 1.3 %collective-permute-done.11.y_ref = bf16[256,128]{1,0:T(8,128)(2,1)S(1)} collective-permute-done((bf16[256,128]{1,0:T(8,128)(2,1)S(1)}, bf16[256,128]{1,0:T(8,128)(2,1)S(1)}, u32[]{:S(2)}, u32[]{:S(2)}) %collective-permute-start.11) | collective-permute-done | bytes 65568 | tf_op jit(solution)/shard_map/ppermute | solution.py:25
  76.6 0.7 collective-permute-done.10.dp_ref
  77.3 0.1 shard_map.123.refs_0_
  77.4 0.0 all-to-all-done.1
  77.4 0.0 copy-done.8
  77.4 1.5 %shard_map.124 = bf16[1024,256]{1,0:T(8,128)(2,1)} custom-call(s32[1,1024]{1,0:T(1,128)S(1)} %copy-done.8, bf16[1024,256]{1,0:T(8,128)(2,1)S(1)} %bitcast.16), custom_call_target="tpu_custom_call" | custom-call | flops 536870912 | bytes 1048576 | tf_op jit(solution)/shard_map/pallas_call | solution.py:42
  78.9 0.0 collective-permute-start.13
  78.9 0.8 shard_map.125
  79.7 0.7 collective-permute-done.13.refs_0_
  80.3 0.8 shard_map.126
  (3 shorter events, 0.1 us)
Async XLA Ops:
  0.6 39.3 %copy-start.4 = (bf16[256,256]{1,0:T(8,128)(2,1)S(1)}, bf16[256,256]{1,0:T(8,128)(2,1)}, u32[]{:S(2)}) copy-start(bf16[256,256]{1,0:T(8,128)(2,1)} %w_edge_ref.5) | copy-start | bytes 393220
  3.3 74.1 %copy-start.8 = (s32[1,1024]{1,0:T(1,128)S(1)}, s32[1,1024]{1,0:T(1,128)}, u32[]{:S(2)}) copy-start(s32[1,1024]{1,0:T(1,128)} %order_ref.1) | copy-start | bytes 12292
  3.3 21.9 %all-to-all-start = ((bf16[16,64,256]{2,1,0:T(8,128)(2,1)}), bf16[16,64,256]{2,1,0:T(8,128)(2,1)S(1)}, u32[]{:S(2)}, u32[]{:S(2)}) async-start(bf16[16,64,256]{2,1,0:T(8,128)(2,1)} %bitcast.17), calls=%async_computation | async-start | bytes 1048576 | tf_op jit(solution)/shard_map/all_to_all | solution.py:419
  11.5 1.2 %copy-start.6 = (bf16[8,4,128,128]{3,2,1,0:T(8,128)(2,1)S(1)}, bf16[8,4,128,128]{3,2,1,0:T(8,128)(2,1)}, u32[]{:S(2)}) copy-start(bf16[8,4,128,128]{3,2,1,0:T(8,128)(2,1)} %vals_ref.1) | copy-start | bytes 3145732
  12.7 0.7 copy-start.7
  16.5 1.7 %copy-start = (bf16[1024,1664]{1,0:T(8,128)(2,1)}, bf16[1024,1664]{1,0:T(8,128)(2,1)S(1)}, u32[]{:S(2)}) copy-start(bf16[1024,1664]{1,0:T(8,128)(2,1)S(1)} %get-tuple-element.42.at_ref) | copy-start | bytes 10223620
  25.2 14.7 %copy-start.1 = (bf16[1024,1664]{1,0:T(8,128)(2,1)S(1)}, bf16[1024,1664]{1,0:T(8,128)(2,1)}, u32[]{:S(2)}) copy-start(bf16[1024,1664]{1,0:T(8,128)(2,1)} %copy-done) | copy-start | bytes 10223620
  25.2 1.1 %copy-start.3 = (bf16[256,256]{1,0:T(8,128)(2,1)S(1)}, bf16[256,256]{1,0:T(8,128)(2,1)}, u32[]{:S(2)}) copy-start(bf16[256,256]{1,0:T(8,128)(2,1)} %w_edge_ref.5) | copy-start | bytes 393220
  27.0 8.4 %collective-permute-start = (bf16[256,256]{1,0:T(8,128)(2,1)S(1)}, bf16[256,256]{1,0:T(8,128)(2,1)S(1)}, u32[]{:S(2)}, u32[]{:S(2)}) collective-permute-start(bf16[256,256]{1,0:T(8,128)(2,1)S(1)} %get-tuple-element.48), channel_id=1, source_target_pairs={{0,1},{1,0},{2,3},{3,2},{4,5},{5,4},{6,7},{7,6},{8,9},{9,8},{10,11... | collective-permute-start | bytes 393224 | tf_op jit(solution)/shard_map/ppermute | solution.py:25
  27.0 8.3 %collective-permute-start.1 = (bf16[256,256]{1,0:T(8,128)(2,1)S(1)}, bf16[256,256]{1,0:T(8,128)(2,1)S(1)}, u32[]{:S(2)}, u32[]{:S(2)}) collective-permute-start(bf16[256,256]{1,0:T(8,128)(2,1)S(1)} %get-tuple-element.49), channel_id=1, source_target_pairs={{0,15},{1,2},{2,1},{3,4},{4,3},{5,6},{6,5},{7,8},{8,7},{9,10},{10,... | collective-permute-start | bytes 393224 | tf_op jit(solution)/shard_map/ppermute | solution.py:30
  29.9 1.0 %copy-start.2 = (bf16[1,1024,256]{2,1,0:T(8,128)(2,1)S(1)}, bf16[1,1024,256]{2,1,0:T(8,128)(2,1)}, u32[]{:S(2)}) copy-start(bf16[1,1024,256]{2,1,0:T(8,128)(2,1)} %param.15) | copy-start | bytes 1572868
  30.9 0.9 %copy-start.5 = (bf16[512,256]{1,0:T(8,128)(2,1)S(1)}, bf16[512,256]{1,0:T(8,128)(2,1)}, u32[]{:S(2)}) copy-start(bf16[512,256]{1,0:T(8,128)(2,1)} %w_node_ref.3) | copy-start | bytes 786436
  36.1 5.5 %collective-permute-start.2 = (bf16[256,256]{1,0:T(8,128)(2,1)S(1)}, bf16[256,256]{1,0:T(8,128)(2,1)S(1)}, u32[]{:S(2)}, u32[]{:S(2)}) collective-permute-start(bf16[256,256]{1,0:T(8,128)(2,1)S(1)} %get-tuple-element.54), channel_id=1, source_target_pairs={{0,1},{1,0},{2,3},{3,2},{4,5},{5,4},{6,7},{7,6},{8,9},{9,8},{10,11... | collective-permute-start | bytes 393224 | tf_op jit(solution)/shard_map/ppermute | solution.py:25
  36.1 7.2 %collective-permute-start.3 = (bf16[256,256]{1,0:T(8,128)(2,1)S(1)}, bf16[256,256]{1,0:T(8,128)(2,1)S(1)}, u32[]{:S(2)}, u32[]{:S(2)}) collective-permute-start(bf16[256,256]{1,0:T(8,128)(2,1)S(1)} %get-tuple-element.55), channel_id=1, source_target_pairs={{0,15},{1,2},{2,1},{3,4},{4,3},{5,6},{6,5},{7,8},{8,7},{9,10},{10,... | collective-permute-start | bytes 393224 | tf_op jit(solution)/shard_map/ppermute | solution.py:30
  38.4 6.7 %collective-permute-start.4 = (bf16[512,128]{1,0:T(8,128)(2,1)S(1)}, bf16[512,128]{1,0:T(8,128)(2,1)S(1)}, u32[]{:S(2)}, u32[]{:S(2)}) collective-permute-start(bf16[512,128]{1,0:T(8,128)(2,1)S(1)} %get-tuple-element.67), channel_id=1, source_target_pairs={{0,16},{16,0},{1,17},{17,1},{2,18},{18,2},{3,19},{19,3},{4,20},{20... | collective-permute-start | bytes 393224 | tf_op jit(solution)/shard_map/ppermute | solution.py:25
  45.0 32.3 %all-to-all-start.1 = ((bf16[16,64,256]{2,1,0:T(8,128)(2,1)}), bf16[16,64,256]{2,1,0:T(8,128)(2,1)S(1)}, u32[]{:S(2)}, u32[]{:S(2)}) async-start(bf16[16,64,256]{2,1,0:T(8,128)(2,1)} %bitcast.5), calls=%async_computation.1 | async-start | bytes 1048576 | tf_op jit(solution)/shard_map/all_to_all | solution.py:493
  48.7 2.0 %collective-permute-start.5 = (bf16[256,128]{1,0:T(8,128)(2,1)S(1)}, bf16[256,128]{1,0:T(8,128)(2,1)S(1)}, u32[]{:S(2)}, u32[]{:S(2)}) collective-permute-start(bf16[256,128]{1,0:T(8,128)(2,1)S(1)} %get-tuple-element.70), channel_id=1, source_target_pairs={{0,1},{1,0},{2,3},{3,2},{4,5},{5,4},{6,7},{7,6},{8,9},{9,8},{10,11... | collective-permute-start | bytes 196616 | tf_op jit(solution)/shard_map/ppermute | solution.py:25
  49.1 8.0 %collective-permute-start.6 = (bf16[256,128]{1,0:T(8,128)(2,1)S(1)}, bf16[256,128]{1,0:T(8,128)(2,1)S(1)}, u32[]{:S(2)}, u32[]{:S(2)}) collective-permute-start(bf16[256,128]{1,0:T(8,128)(2,1)S(1)} %get-tuple-element.71), channel_id=1, source_target_pairs={{0,2},{1,3},{2,0},{3,1},{4,6},{5,7},{6,4},{7,5},{8,10},{9,11},{10,... | collective-permute-start | bytes 196616 | tf_op jit(solution)/shard_map/ppermute | solution.py:25
  50.8 6.7 %collective-permute-start.7 = (bf16[256,128]{1,0:T(8,128)(2,1)S(1)}, bf16[256,128]{1,0:T(8,128)(2,1)S(1)}, u32[]{:S(2)}, u32[]{:S(2)}) collective-permute-start(bf16[256,128]{1,0:T(8,128)(2,1)S(1)} %get-tuple-element.72), channel_id=1, source_target_pairs={{0,3},{1,2},{2,1},{3,0},{4,7},{5,6},{6,5},{7,4},{8,11},{9,10},{10,... | collective-permute-start | bytes 196616 | tf_op jit(solution)/shard_map/ppermute | solution.py:25
  57.5 6.1 %collective-permute-start.8 = (bf16[256,128]{1,0:T(8,128)(2,1)S(1)}, bf16[256,128]{1,0:T(8,128)(2,1)S(1)}, u32[]{:S(2)}, u32[]{:S(2)}) collective-permute-start(bf16[256,128]{1,0:T(8,128)(2,1)S(1)} %shard_map.120.mine_ref), channel_id=1, source_target_pairs={{0,4},{1,5},{2,6},{3,7},{4,0},{5,1},{6,2},{7,3},{8,12},{9,13},{10,... | collective-permute-start | bytes 196616 | tf_op jit(solution)/shard_map/ppermute | solution.py:25
  63.7 6.3 %collective-permute-start.9 = (bf16[256,128]{1,0:T(8,128)(2,1)S(1)}, bf16[256,128]{1,0:T(8,128)(2,1)S(1)}, u32[]{:S(2)}, u32[]{:S(2)}) collective-permute-start(bf16[256,128]{1,0:T(8,128)(2,1)S(1)} %shard_map.121.mine_ref), channel_id=1, source_target_pairs={{0,8},{1,9},{2,10},{3,11},{4,12},{5,13},{6,14},{7,15},{8,0},{9,1},... | collective-permute-start | bytes 196616 | tf_op jit(solution)/shard_map/ppermute | solution.py:25
  70.0 5.3 %collective-permute-start.12 = (bf16[256,128]{1,0:T(8,128)(2,1)S(1)}, bf16[256,128]{1,0:T(8,128)(2,1)S(1)}, u32[]{:S(2)}, u32[]{:S(2)}) collective-permute-start(bf16[256,128]{1,0:T(8,128)(2,1)S(1)} %shard_map.122.mine_ref), channel_id=1, source_target_pairs={{0,18},{1,19},{2,16},{3,17},{4,22},{5,23},{6,20},{7,21},{8,26},{9,... | collective-permute-start | bytes 196616 | tf_op jit(solution)/shard_map/ppermute | solution.py:338
  72.2 4.5 %collective-permute-start.11 = (bf16[256,128]{1,0:T(8,128)(2,1)S(1)}, bf16[256,128]{1,0:T(8,128)(2,1)S(1)}, u32[]{:S(2)}, u32[]{:S(2)}) collective-permute-start(bf16[256,128]{1,0:T(8,128)(2,1)S(1)} %shard_map.122.mine_ref), channel_id=1, source_target_pairs={{0,2},{1,3},{2,0},{3,1},{4,6},{5,7},{6,4},{7,5},{8,10},{9,11},{10,... | collective-permute-start | bytes 196616 | tf_op jit(solution)/shard_map/ppermute | solution.py:25
  73.0 4.3 %collective-permute-start.10 = (bf16[256,128]{1,0:T(8,128)(2,1)S(1)}, bf16[256,128]{1,0:T(8,128)(2,1)S(1)}, u32[]{:S(2)}, u32[]{:S(2)}) collective-permute-start(bf16[256,128]{1,0:T(8,128)(2,1)S(1)} %shard_map.122.mine_ref), channel_id=1, source_target_pairs={{0,16},{16,0},{1,17},{17,1},{2,18},{18,2},{3,19},{19,3},{4,20},{20... | collective-permute-start | bytes 196616 | tf_op jit(solution)/shard_map/ppermute | solution.py:25
  78.9 1.4 %collective-permute-start.13 = (bf16[384,256]{1,0:T(8,128)(2,1)S(1)}, bf16[384,256]{1,0:T(8,128)(2,1)S(1)}, u32[]{:S(2)}, u32[]{:S(2)}) collective-permute-start(bf16[384,256]{1,0:T(8,128)(2,1)S(1)} %shard_map.123.refs_0_), channel_id=1, source_target_pairs={{0,1},{1,0},{2,3},{3,2},{4,5},{5,4},{6,7},{7,6},{8,9},{9,8},{10,11... | collective-permute-start | bytes 589832 | tf_op jit(solution)/shard_map/ppermute | solution.py:25

commit v4 on v1

--- a/solution.py
+++ b/solution.py
@@ -37,19 +37,19 @@
     return jax.ShapeDtypeStruct(dims, dtype)
 
 
-def call(body, outs, args, specs=None, scratch=(), flops=0, nbytes=0, limit=24 * MIB):
+def call(body, outs, args, specs=None, scratch=(), flops=0, nbytes=0, limit=24 * MIB, out_specs=None):
     return pl.pallas_call(
         body,
         out_shape=outs,
         in_specs=specs or [VMEM] * len(args),
-        out_specs=[VMEM] * len(outs),
+        out_specs=out_specs or [VMEM] * len(outs),
         scratch_shapes=list(scratch),
         cost_estimate=pl.CostEstimate(flops=flops, bytes_accessed=nbytes, transcendentals=0),
         compiler_params=pltpu.CompilerParams(vmem_limit_bytes=limit),
     )(*args)
 
 
-def pick_body(order_hbm, feat_hbm, out_ref, order_ref, feat_ref, hot_ref, order_sem, feat_sem):
+def pick_body(order_hbm, feat_hbm, out_hbm, order_ref, feat_ref, hot_ref, out_ref, order_sem, feat_sem, out_sems):
     rows = feat_ref.shape[0]
     early = hot_ref.shape[0] // ROWS
     load_order = pltpu.make_async_copy(order_hbm, order_ref, order_sem)
@@ -69,10 +69,15 @@
         hot_ref[k * ROWS : (k + 1) * ROWS, :] = hot_rows(k)
     load_feat.wait()
     feat = feat_ref[...]
+    puts = []
     for k in range(rows // ROWS):
         mine = slice(k * ROWS, (k + 1) * ROWS)
         hot = hot_ref[mine, :] if k < early else hot_rows(k)
         out_ref[mine, :] = dot(hot, feat).astype(BF16)
+        puts.append(pltpu.make_async_copy(out_ref.at[pl.ds(k * ROWS, ROWS)], out_hbm.at[pl.ds(k * ROWS, ROWS)], out_sems.at[k]))
+        puts[k].start()
+    for put in puts:
+        put.wait()
 
 
 def build_body(cnt_ref, tgt_ref, vals_ref, own_ref, rim_ref, at_ref, a_ref):
@@ -99,16 +104,13 @@
     return jnp.where(odd, first, second), jnp.where(odd, second, first)
 
 
-def message_body(nodes_ref, a_hbm, w_edge_ref, near_ref, far_ref, msg_ref, a_ref, a_sem):
+def message_body(nodes_ref, a_ref, w_edge_ref, near_ref, far_ref, msg_ref):
     rows = nodes_ref.shape[0]
     rim = RIM * ROWS
-    load = pltpu.make_async_copy(a_hbm, a_ref, a_sem)
-    load.start()
     for k in range(rows // rim):
         mine = slice(k * rim, (k + 1) * rim)
         pre = dot(nodes_ref[mine, :], w_edge_ref[...])
         msg_ref[mine, :] = (pre * jax.nn.sigmoid(pre)).astype(BF16)
-    load.wait()
     sums = dot(a_ref[...].reshape(2 * rim, rows), msg_ref[...])
     near, far = chosen(sums[:rim], sums[rim:])
     near_ref[...] = near.astype(BF16)
@@ -217,13 +219,14 @@
 
 def edge_body(
     scale, nodes_ref, at_ref, near_ref, far_ref, d_msg_ref, slope_ref, mid_ref, rim_ref, w_edge_ref,
-    back_ref, g_edge_ref, d_edge_ref,
+    back_hbm, g_edge_ref, d_edge_ref, back_ref, sems,
 ):
     rows, width = nodes_ref.shape
     rim = RIM * ROWS
     prev, after = chosen(near_ref[...], far_ref[...])
     rims = jnp.concatenate([prev, after], axis=0)
     w_edge = w_edge_ref[...]
+    puts = []
     for k in range(rows // rim):
         mine = slice(k * rim, (k + 1) * rim)
         d_msg = d_msg_ref[mine, :] + dot(at_ref[mine, rows : rows + 2 * rim], rims)
@@ -236,7 +239,12 @@
         else:
             d_nodes1 = mid_ref[(k - 1) * rim : k * rim, :]
         back_ref[mine, :] = (d_nodes1 + dot(d_edge, w_edge, ((1,), (1,)))).astype(BF16)
+        part = pl.ds(k * rim, rim)
+        puts.append(pltpu.make_async_copy(back_ref.at[part], back_hbm.at[part], sems.at[k]))
+        puts[k].start()
     g_edge_ref[...] = dot(nodes_ref[...], d_edge_ref[...], ((0,), (0,))) * scale
+    for put in puts:
+        put.wait()
 
 
 def bit_of(mask):
@@ -292,16 +300,41 @@
         out_ref[row : row + more, half:] = jnp.where(first, b[:more], a[:more])
 
 
-def finish_body(mask, mine_ref, in_ref, edge_ref, node_ref):
-    few, more = edge_ref.shape[0] // 4, node_ref.shape[0] // 4
-    low = bit_of(mask) == 0
-    mine, other = mine_ref[...].astype(F32), in_ref[...].astype(F32)
-    for side, value in enumerate((jnp.where(low, mine, other), jnp.where(low, other, mine))):
-        for part in range(2):
-            q = 2 * side + part
-            row = part * (few + more)
-            edge_ref[q * few : (q + 1) * few, :] = value[row : row + few]
-            node_ref[q * more : (q + 1) * more, :] = value[row + few : row + few + more]
+def finish_body(own, *refs):
+    part_ref = refs[0]
+    edge_hbm, node_hbm, edge_ref, node_ref, sems = refs[-5:]
+    few, more = edge_ref.shape[0] // 2, node_ref.shape[0] // 2
+    for k in range(2):
+        row = k * (few + more)
+        edge_ref[k * few : (k + 1) * few, :] = part_ref[row : row + few, :].astype(F32)
+        node_ref[k * more : (k + 1) * more, :] = part_ref[row + few : row + few + more, :].astype(F32)
+    side = bit_of(CORE) if own else 1 - bit_of(CORE)
+    puts = []
+    for k, (ref, hbm) in enumerate(((edge_ref, edge_hbm), (node_ref, node_hbm))):
+        size = ref.shape[0]
+        to = hbm.at[pl.ds(pl.multiple_of(side * size, 8), size), :]
+        puts.append(pltpu.make_async_copy(ref, to, sems.at[k]))
+        puts[k].start()
+    for put in puts:
+        put.wait()
+
+
+def finished(own, part, grads, width):
+    outs = [shape(width, width, dtype=F32), shape(2 * width, width, dtype=F32)]
+    return pl.pallas_call(
+        functools.partial(finish_body, own),
+        out_shape=outs,
+        in_specs=[VMEM] + [ANY] * len(grads),
+        out_specs=[ANY, ANY],
+        scratch_shapes=[
+            pltpu.VMEM((width // 2, width), F32),
+            pltpu.VMEM((width, width), F32),
+            pltpu.SemaphoreType.DMA((2,)),
+        ],
+        input_output_aliases={1: 0, 2: 1} if grads else {},
+        cost_estimate=pl.CostEstimate(flops=0, bytes_accessed=3 * width * width * 4, transcendentals=0),
+        compiler_params=pltpu.CompilerParams(vmem_limit_bytes=24 * MIB),
+    )(part, *grads)
 
 
 def swapped_both(x, mask):
@@ -310,7 +343,7 @@
     return lax.ppermute(x, ("dp", "dom"), [(i, (i + peers) % total ^ mask) for i in range(total)])
 
 
-def cut_and_summed(edge_part, node_part):
+def cut_grads(edge_part, node_part):
     half = node_part[0].shape[1]
     size = node_part[0].shape[0] + 2 * edge_part.shape[0]
 
@@ -323,26 +356,31 @@
         )
 
     keep, send = cut(first_cut_body, CORE, (edge_part, *node_part), size)
-    keep, send = cut(next_cut_body, ALONG_Y, (keep, swapped(send, "dom", CORE)), size // 2)
+    return cut(next_cut_body, ALONG_Y, (keep, swapped(send, "dom", CORE)), size // 2)
+
+
+def joined(keep, send, back, send_order, width):
     out = [shape(*send.shape)]
     (mine,) = call(sum_body, out, (keep, swapped(send, "dom", ALONG_Y)))
-    return call(sum_body, out, (mine, swapped(mine, "dom", ALONG_Z)))[0]
-
-
-def joined(mine, back, width):
-    (mine,) = call(sum_body, [shape(*mine.shape)], (mine, swapped(mine, "dom", 2 * ALONG_Z)))
-    (mine,) = call(
-        functools.partial(join_body, ALONG_Y),
-        [shape(6 * (width // 4), width)],
-        (mine, swapped(mine, "dp", 1), swapped(mine, "dom", ALONG_Y), swapped_both(mine, ALONG_Y)),
-    )
-    mine, back = lax.optimization_barrier((mine, back))
-    grad_edge, grad_node = call(
-        functools.partial(finish_body, CORE),
-        [shape(width, width, dtype=F32), shape(2 * width, width, dtype=F32)],
-        (mine, swapped(mine, "dom", CORE)),
-    )
-    return grad_edge, grad_node, back
+    for mask in (ALONG_Z, 2 * ALONG_Z):
+        (mine,) = call(sum_body, out, (mine, swapped(mine, "dom", mask)))
+    others = swapped(mine, "dp", 1), swapped(mine, "dom", ALONG_Y), swapped_both(mine, ALONG_Y)
+    grad_brick = placed(send_order, back)
+    mine, grad_brick = lax.optimization_barrier((mine, grad_brick))
+    (mine,) = call(functools.partial(join_body, ALONG_Y), [shape(6 * (width // 4), width)], (mine, *others))
+    grads = finished(True, mine, (), width)
+    return *finished(False, swapped(mine, "dom", CORE), grads, width), grad_brick
+
+
+def placed(send_order, back):
+    rows, width = back.shape
+    return call(
+        place_body,
+        [shape(rows, width)],
+        (send_order, back),
+        flops=2 * rows * rows * width,
+        nbytes=4 * rows * width,
+    )[0]
 
 
 def place_body(order_ref, back_ref, out_ref):
@@ -381,11 +419,14 @@
             pltpu.VMEM((1, rows), jnp.int32),
             pltpu.VMEM((rows, width), BF16),
             pltpu.VMEM((2 * ROWS, rows), BF16),
+            pltpu.VMEM((rows, width), BF16),
             pltpu.SemaphoreType.DMA,
             pltpu.SemaphoreType.DMA,
+            pltpu.SemaphoreType.DMA((blocks,)),
         ],
         flops=2 * rows * rows * width,
         nbytes=2 * unit,
+        out_specs=[ANY],
         limit=56 * MIB,
     )
     nodes = lax.all_to_all(
@@ -404,8 +445,6 @@
         message_body,
         [edge, edge, tall],
         (nodes, adj_rim, w_edge),
-        [VMEM, ANY, VMEM],
-        [pltpu.VMEM((2 * RIM, ROWS, rows), BF16), pltpu.SemaphoreType.DMA],
         flops=square + 4 * rim * rows * width,
         nbytes=4 * unit,
     )
@@ -454,21 +493,26 @@
         functools.partial(edge_body, scale),
         [tall, shape(width, width, dtype=F32)],
         (nodes, adj_t, near, far, d_msg, slope, d_nodes1_mid, d_nodes1_rim, w_edge),
-        scratch=[pltpu.VMEM((rows, width), BF16)],
+        scratch=[
+            pltpu.VMEM((rows, width), BF16),
+            pltpu.VMEM((rows, width), BF16),
+            pltpu.SemaphoreType.DMA((rows // rim,)),
+        ],
+        out_specs=[ANY, VMEM],
         flops=2 * square + 4 * rim * rows * width,
         nbytes=8 * unit,
     )
     if tiled:
-        mine = cut_and_summed(edge_part, node_part)
-        back, mine = lax.optimization_barrier((back, mine))
+        keep, send = cut_grads(edge_part, node_part)
+        back, send = lax.optimization_barrier((back, send))
     back = lax.all_to_all(
         back.reshape(ndom, per_peer, width), "dom", split_axis=0, concat_axis=0, tiled=True
     ).reshape(rows, width)
     if tiled:
-        grad_edge, grad_node, back = joined(mine, back, width)
+        grad_edge, grad_node, grad_brick = joined(keep, send, back, send_order, width)
     else:
         grad_edge, grad_node = (lax.psum(part, ("dp", "dom")) for part in (edge_part, node_part[0]))
-    (grad_brick,) = call(place_body, [tall], (send_order, back), flops=2 * rows * rows * width, nbytes=2 * unit)
+        grad_brick = placed(send_order, back)
     return (node_out[None], grad_brick[None], grad_edge, grad_node)
 
 

time: 87.3 us -> 77.9 us (0.89)
  waiting for transfers between devices: 38.1 us -> 25.3 us
  starting transfers between devices: 25.7 us -> 28.9 us
    ppermute x10, waiting for transfers between devices: 27.1 us -> 15.7 us  [swapped(): return lax.ppermute(x, axis, [(i, i ^ mask) for i in range(peers)])]
    ppermute x10, starting transfers between devices: 5.92 us -> 9.2 us  [swapped(): return lax.ppermute(x, axis, [(i, i ^ mask) for i in range(peers)])]
    pallas_call x0 -> x2, Pallas kernels: none -> 1.55 us  [finished(): pl.pallas_call(functools.partial(finish_body, own), out_shape=outs, in_sp...]
    ppermute x1, waiting for transfers between devices: 1.78 us -> 0.26 us  [swapped_both(): lax.ppermute(x, ('dp', 'dom'), [(i, (i + peers) % total ^ mask) for i in...]
    pallas_call x16 -> x15, Pallas kernels: 15.6 us -> 14.4 us  [call(): pl.pallas_call(body, out_shape=outs, in_specs=specs or [VMEM] * len(args)...]
  transfers between devices with their start and end apart: 15 -> 15, of which waited for: 10 -> 11; matrix products, arithmetic and copies ran while one was open for 1% -> 1% of each run, Pallas kernels for 12% -> 14%
where the time goes in v4:
time: 77.9 us; the launch traced here: 77.5 us
  starting transfers between devices  28.9 us (37%)
  waiting for transfers between devices  25.3 us (32%)
  Pallas kernels  15.9 us (20%)
  local copies, waits for them, and re-layouts  6.56 us (8%)
  between operations  0.83 us (1%)
    ppermute x10, waiting for transfers between devices, swapped(): return lax.ppermute(x, axis, [(i, i ^ mask) for i in range(peers)])  15.7 us
    pallas_call x15, Pallas kernels, call(): pl.pallas_call(body, out_shape=outs, in_specs=specs or [VMEM] * len(args)...  14.4 us
    ppermute x10, starting transfers between devices, swapped(): return lax.ppermute(x, axis, [(i, i ^ mask) for i in range(peers)])  9.2 us
    all_to_all x1, starting transfers between devices, shards(): lax.all_to_all(picked.reshape(ndom, per_peer, width), 'dom', split_axis=0...  7.4 us
    all_to_all x1, waiting for transfers between devices, shards(): lax.all_to_all(picked.reshape(ndom, per_peer, width), 'dom', split_axis=0...  6.89 us
    unnamed x21, local copies, waits for them, and re-layouts  6.56 us
    ppermute x2, starting transfers between devices, swapped_across(): lax.ppermute(x, axis, [(i, (i + 1 if i % 2 else i - 1) % peers) for i in...  5.63 us
    all_to_all x1, starting transfers between devices, shards(): lax.all_to_all(back.reshape(ndom, per_peer, width), 'dom', split_axis=0,...  4.19 us
  transfers between devices with their start and end apart: 15, of which 11 were waited for; matrix products, arithmetic and copies ran while one was open for 1% of the time, Pallas kernels for 14%

profile of v4, /device:TPU:0, one launch (start us, length us, event | category | flops | bytes accessed | tf_op | source)
XLA Modules:
  0.0 77.5 jit_solution(2558409567552113069)
XLA Ops:
  0.6 0.0 copy-start.3
  0.6 0.0 copy-start.7
  0.7 0.0 copy-start.2
  0.7 2.6 %shard_map.111 = bf16[1024,256]{1,0:T(8,128)(2,1)} custom-call(s32[1,1024]{1,0:T(1,128)} %order_ref.1, bf16[1024,256]{1,0:T(8,128)(2,1)} %bitcast.18), custom_call_target="tpu_custom_call" | custom-call | flops 536870912 | bytes 1048576 | tf_op jit(solution)/shard_map/pallas_call | solution.py:41
  3.3 7.4 %all-to-all-start = ((bf16[16,64,256]{2,1,0:T(8,128)(2,1)}), bf16[16,64,256]{2,1,0:T(8,128)(2,1)S(1)}, u32[]{:S(2)}, u32[]{:S(2)}) async-start(bf16[16,64,256]{2,1,0:T(8,128)(2,1)} %bitcast.17), calls=%async_computation | async-start | bytes 1048576 | tf_op jit(solution)/shard_map/all_to_all | solution.py:432
  10.7 0.8 copy.14.tgt_ref
  11.5 0.0 copy-start.4
  11.5 1.2 %copy-done.4 = bf16[8,4,128,128]{3,2,1,0:T(8,128)(2,1)S(1)} copy-done((bf16[8,4,128,128]{3,2,1,0:T(8,128)(2,1)S(1)}, bf16[8,4,128,128]{3,2,1,0:T(8,128)(2,1)}, u32[]{:S(2)}) %copy-start.4) | copy-done | bytes 1048600
  12.7 0.0 copy-start.8
  12.7 0.7 copy-done.8
  13.4 2.2 %shard_map.112 = (bf16[8,128,1024]{2,1,0:T(8,128)(2,1)S(1)}, bf16[4,128,1024]{2,1,0:T(8,128)(2,1)S(1)}, bf16[1024,1664]{1,0:T(8,128)(2,1)S(1)}) custom-call(s32[8]{0:T(128)S(1)} %copy-done.8, s32[8,4]{1,0:T(8,128)S(1)} %copy.14.tgt_ref, bf16[8,4,128,128]{3,2,1,0:T(8,128)(2,1)S(1)} %copy-done.4), custom_call_target="tpu_custom_call" | custom-call | bytes 8388608 | tf_op jit(solution)/shard_map/pallas_call | solution.py:41
  15.6 0.0 copy-start
  15.6 1.7 %copy-done = bf16[1024,1664]{1,0:T(8,128)(2,1)} copy-done((bf16[1024,1664]{1,0:T(8,128)(2,1)}, bf16[1024,1664]{1,0:T(8,128)(2,1)S(1)}, u32[]{:S(2)}) %copy-start) | copy-done | bytes 3407896
  17.3 0.0 copy-start.5
  17.3 1.0 %copy-done.5 = bf16[4,128,1024]{2,1,0:T(8,128)(2,1)} copy-done((bf16[4,128,1024]{2,1,0:T(8,128)(2,1)}, bf16[4,128,1024]{2,1,0:T(8,128)(2,1)S(1)}, u32[]{:S(2)}) %copy-start.5) | copy-done | bytes 1048600
  18.3 6.9 %all-to-all-done = bf16[16,64,256]{2,1,0:T(8,128)(2,1)S(1)} async-done(((bf16[16,64,256]{2,1,0:T(8,128)(2,1)}), bf16[16,64,256]{2,1,0:T(8,128)(2,1)S(1)}, u32[]{:S(2)}, u32[]{:S(2)}) %all-to-all-start) | async-done | bytes 524320 | tf_op jit(solution)/shard_map/all_to_all | solution.py:432
  25.2 0.0 copy-done.3
  25.2 0.0 copy-start.6
  25.2 1.2 %copy-done.6 = bf16[4,128,1024]{2,1,0:T(8,128)(2,1)S(1)} copy-done((bf16[4,128,1024]{2,1,0:T(8,128)(2,1)S(1)}, bf16[4,128,1024]{2,1,0:T(8,128)(2,1)}, u32[]{:S(2)}) %copy-start.6) | copy-done | bytes 1048600
  26.4 0.7 shard_map.113
  27.1 0.1 collective-permute-start
  27.2 2.8 %collective-permute-start.1 = (bf16[256,256]{1,0:T(8,128)(2,1)S(1)}, bf16[256,256]{1,0:T(8,128)(2,1)S(1)}, u32[]{:S(2)}, u32[]{:S(2)}) collective-permute-start(bf16[256,256]{1,0:T(8,128)(2,1)S(1)} %get-tuple-element.49), channel_id=1, source_target_pairs={{0,15},{1,2},{2,1},{3,4},{4,3},{5,6},{6,5},{7,8},{8,7},{9,10},{10,... | collective-permute-start | bytes 393224 | tf_op jit(solution)/shard_map/ppermute | solution.py:29
  30.0 0.0 copy-done.7
  30.0 0.0 copy-done.2
  30.0 0.0 copy-start.1
  30.0 2.6 %shard_map.114 = (bf16[512,256]{1,0:T(8,128)(2,1)S(1)}, bf16[512,256]{1,0:T(8,128)(2,1)S(1)}, bf16[512,256]{1,0:T(8,128)(2,1)S(1)}, bf16[512,256]{1,0:T(8,128)(2...) custom-call(bf16[1024,256]{1,0:T(8,128)(2,1)S(1)} %bitcast.9, ...), custom_call_target="tpu_custom_call" | custom-call | flops 805306368 | bytes 4194304 | tf_op jit(solution)/shard_map/pallas_call | solution.py:41
  32.7 0.0 collective-permute-done.near_in_ref
  32.7 1.7 %collective-permute-done.1.far_in_ref = bf16[256,256]{1,0:T(8,128)(2,1)S(1)} collective-permute-done((bf16[256,256]{1,0:T(8,128)(2,1)S(1)}, bf16[256,256]{1,0:T(8,128)(2,1)S(1)}, u32[]{:S(2)}, u32[]{:S(2)}) %collective-permute-start.1) | collective-permute-done | bytes 131104 | tf_op jit(solution)/shard_map/ppermute | solution.py:29
  34.4 0.7 shard_map.115
  35.0 0.1 collective-permute-start.2
  35.1 2.8 %collective-permute-start.3 = (bf16[256,256]{1,0:T(8,128)(2,1)S(1)}, bf16[256,256]{1,0:T(8,128)(2,1)S(1)}, u32[]{:S(2)}, u32[]{:S(2)}) collective-permute-start(bf16[256,256]{1,0:T(8,128)(2,1)S(1)} %get-tuple-element.55), channel_id=1, source_target_pairs={{0,15},{1,2},{2,1},{3,4},{4,3},{5,6},{6,5},{7,8},{8,7},{9,10},{10,... | collective-permute-start | bytes 393224 | tf_op jit(solution)/shard_map/ppermute | solution.py:29
  37.9 0.5 shard_map.118
  38.4 1.6 %collective-permute-start.4 = (bf16[512,128]{1,0:T(8,128)(2,1)S(1)}, bf16[512,128]{1,0:T(8,128)(2,1)S(1)}, u32[]{:S(2)}, u32[]{:S(2)}) collective-permute-start(bf16[512,128]{1,0:T(8,128)(2,1)S(1)} %get-tuple-element.66), channel_id=1, source_target_pairs={{0,16},{16,0},{1,17},{17,1},{2,18},{18,2},{3,19},{19,3},{4,20},{20... | collective-permute-start | bytes 393224 | tf_op jit(solution)/shard_map/ppermute | solution.py:24
  40.0 0.0 copy-done.1
  40.0 1.6 %shard_map.116 = (bf16[1024,256]{1,0:T(8,128)(2,1)}, f32[1024,256]{1,0:T(8,128)S(1)}, f32[1024,256]{1,0:T(8,128)S(1)}) custom-call(bf16[1024,256]{1,0:T(8,128)(2,1)S(1)} %bitcast.12, bf16[1024,1664]{1,0:T(8,128)(2,1)S(1)} %copy-done.1, bf16[256,256]{1,0:T(8,128)(2,1)S(1)} %copy-done.3, bf16[512,256]{1,0:T(8,128)(2,1)S(1)} %get-tuple-element.46.out_mid_ref, ...), custom_call_target="tpu_custom_call" | custom-call | flops 671088640 | bytes 4194304 | tf_op jit(solution)/shard_map/pallas_call | solution.py:41
  41.6 0.0 collective-permute-done.2.near_ref
  41.6 0.7 collective-permute-done.3.far_ref
  42.3 0.0 copy-start.9
  42.3 1.7 %shard_map.117 = (bf16[1024,256]{1,0:T(8,128)(2,1)}, f32[256,256]{1,0:T(8,128)S(1)}) custom-call(bf16[1024,256]{1,0:T(8,128)(2,1)S(1)} %bitcast.13, bf16[1024,1664]{1,0:T(8,128)(2,1)S(1)} %copy-done.1, bf16[256,256]{1,0:T(8,128)(2,1)S(1)} %collective-permute-done.2.near_ref, bf16[256,256]{1,0:T(8,128)(2,1)S(1)} %collective-permute-done.3.far_ref, ...), custom_call_target="tpu_custom_call" | custom-call | flops 536870912 | bytes 4194304 | tf_op jit(solution)/shard_map/pallas_call | solution.py:41
  43.9 0.0 collective-permute-done.4.node_in_ref
  43.9 0.1 shard_map.119
  44.0 0.1 collective-permute-start.5
  44.1 1.3 %collective-permute-done.5.in_ref = bf16[512,128]{1,0:T(8,128)(2,1)S(1)} collective-permute-done((bf16[512,128]{1,0:T(8,128)(2,1)S(1)}, bf16[512,128]{1,0:T(8,128)(2,1)S(1)}, u32[]{:S(2)}, u32[]{:S(2)}) %collective-permute-start.5) | collective-permute-done | bytes 131104 | tf_op jit(solution)/shard_map/ppermute | solution.py:24
  45.5 4.2 %all-to-all-start.1 = ((bf16[16,64,256]{2,1,0:T(8,128)(2,1)}), bf16[16,64,256]{2,1,0:T(8,128)(2,1)S(1)}, u32[]{:S(2)}, u32[]{:S(2)}) async-start(bf16[16,64,256]{2,1,0:T(8,128)(2,1)} %bitcast.5), calls=%async_computation.1 | async-start | bytes 1048576 | tf_op jit(solution)/shard_map/all_to_all | solution.py:508
  49.7 1.9 %collective-permute-start.6 = (bf16[256,128]{1,0:T(8,128)(2,1)S(1)}, bf16[256,128]{1,0:T(8,128)(2,1)S(1)}, u32[]{:S(2)}, u32[]{:S(2)}) collective-permute-start(bf16[256,128]{1,0:T(8,128)(2,1)S(1)} %get-tuple-element.72), channel_id=1, source_target_pairs={{0,2},{1,3},{2,0},{3,1},{4,6},{5,7},{6,4},{7,5},{8,10},{9,11},{10,... | collective-permute-start | bytes 196616 | tf_op jit(solution)/shard_map/ppermute | solution.py:24
  51.6 5.7 %collective-permute-done.6.in_ref = bf16[256,128]{1,0:T(8,128)(2,1)S(1)} collective-permute-done((bf16[256,128]{1,0:T(8,128)(2,1)S(1)}, bf16[256,128]{1,0:T(8,128)(2,1)S(1)}, u32[]{:S(2)}, u32[]{:S(2)}) %collective-permute-start.6) | collective-permute-done | bytes 65568 | tf_op jit(solution)/shard_map/ppermute | solution.py:24
  57.3 1.0 %collective-permute-start.7 = (bf16[256,128]{1,0:T(8,128)(2,1)S(1)}, bf16[256,128]{1,0:T(8,128)(2,1)S(1)}, u32[]{:S(2)}, u32[]{:S(2)}) collective-permute-start(bf16[256,128]{1,0:T(8,128)(2,1)S(1)} %shard_map.121.mine_ref), channel_id=1, source_target_pairs={{0,4},{1,5},{2,6},{3,7},{4,0},{5,1},{6,2},{7,3},{8,12},{9,13},{10,... | collective-permute-start | bytes 196616 | tf_op jit(solution)/shard_map/ppermute | solution.py:24
  58.4 3.6 %collective-permute-done.7.in_ref = bf16[256,128]{1,0:T(8,128)(2,1)S(1)} collective-permute-done((bf16[256,128]{1,0:T(8,128)(2,1)S(1)}, bf16[256,128]{1,0:T(8,128)(2,1)S(1)}, u32[]{:S(2)}, u32[]{:S(2)}) %collective-permute-start.7) | collective-permute-done | bytes 65568 | tf_op jit(solution)/shard_map/ppermute | solution.py:24
  62.0 3.3 %collective-permute-start.8 = (bf16[256,128]{1,0:T(8,128)(2,1)S(1)}, bf16[256,128]{1,0:T(8,128)(2,1)S(1)}, u32[]{:S(2)}, u32[]{:S(2)}) collective-permute-start(bf16[256,128]{1,0:T(8,128)(2,1)S(1)} %shard_map.122.mine_ref), channel_id=1, source_target_pairs={{0,8},{1,9},{2,10},{3,11},{4,12},{5,13},{6,14},{7,15},{8,0},{9,1},... | collective-permute-start | bytes 196616 | tf_op jit(solution)/shard_map/ppermute | solution.py:24
  65.3 2.5 %collective-permute-done.8.in_ref = bf16[256,128]{1,0:T(8,128)(2,1)S(1)} collective-permute-done((bf16[256,128]{1,0:T(8,128)(2,1)S(1)}, bf16[256,128]{1,0:T(8,128)(2,1)S(1)}, u32[]{:S(2)}, u32[]{:S(2)}) %collective-permute-start.8) | collective-permute-done | bytes 65568 | tf_op jit(solution)/shard_map/ppermute | solution.py:24
  67.8 2.5 %collective-permute-start.11 = (bf16[256,128]{1,0:T(8,128)(2,1)S(1)}, bf16[256,128]{1,0:T(8,128)(2,1)S(1)}, u32[]{:S(2)}, u32[]{:S(2)}) collective-permute-start(bf16[256,128]{1,0:T(8,128)(2,1)S(1)} %shard_map.123.mine_ref), channel_id=1, source_target_pairs={{0,18},{1,19},{2,16},{3,17},{4,22},{5,23},{6,20},{7,21},{8,26},{9,... | collective-permute-start | bytes 196616 | tf_op jit(solution)/shard_map/ppermute | solution.py:343
  70.3 0.6 collective-permute-start.10
  70.9 0.5 collective-permute-start.9
  71.4 0.0 all-to-all-done.1
  71.4 0.0 copy-done.9
  71.4 1.5 %shard_map.124 = bf16[1024,256]{1,0:T(8,128)(2,1)} custom-call(s32[1,1024]{1,0:T(1,128)S(1)} %copy-done.9, bf16[1024,256]{1,0:T(8,128)(2,1)S(1)} %bitcast.16), custom_call_target="tpu_custom_call" | custom-call | flops 536870912 | bytes 1048576 | tf_op jit(solution)/shard_map/pallas_call | solution.py:41
  72.9 0.3 collective-permute-done.11.both_ref
  73.2 1.4 %collective-permute-done.10.y_ref = bf16[256,128]{1,0:T(8,128)(2,1)S(1)} collective-permute-done((bf16[256,128]{1,0:T(8,128)(2,1)S(1)}, bf16[256,128]{1,0:T(8,128)(2,1)S(1)}, u32[]{:S(2)}, u32[]{:S(2)}) %collective-permute-start.10) | collective-permute-done | bytes 65568 | tf_op jit(solution)/shard_map/ppermute | solution.py:24
  74.6 0.6 collective-permute-done.9.dp_ref
  75.1 0.1 shard_map.125.refs_0_
  75.2 0.1 collective-permute-start.12
  75.3 0.8 shard_map.126
  76.1 0.6 collective-permute-done.12.refs_0_
  76.7 0.8 shard_map.127
  (4 shorter events, 0.1 us)
Async XLA Ops:
  0.6 24.6 %copy-start.3 = (bf16[256,256]{1,0:T(8,128)(2,1)S(1)}, bf16[256,256]{1,0:T(8,128)(2,1)}, u32[]{:S(2)}) copy-start(bf16[256,256]{1,0:T(8,128)(2,1)} %w_edge_ref.5) | copy-start | bytes 393220
  0.6 29.4 %copy-start.7 = (bf16[512,256]{1,0:T(8,128)(2,1)S(1)}, bf16[512,256]{1,0:T(8,128)(2,1)}, u32[]{:S(2)}) copy-start(bf16[512,256]{1,0:T(8,128)(2,1)} %w_node_ref.3) | copy-start | bytes 786436
  0.7 29.4 %copy-start.2 = (bf16[1,1024,256]{2,1,0:T(8,128)(2,1)S(1)}, bf16[1,1024,256]{2,1,0:T(8,128)(2,1)}, u32[]{:S(2)}) copy-start(bf16[1,1024,256]{2,1,0:T(8,128)(2,1)} %param.15) | copy-start | bytes 1572868
  3.3 21.9 %all-to-all-start = ((bf16[16,64,256]{2,1,0:T(8,128)(2,1)}), bf16[16,64,256]{2,1,0:T(8,128)(2,1)S(1)}, u32[]{:S(2)}, u32[]{:S(2)}) async-start(bf16[16,64,256]{2,1,0:T(8,128)(2,1)} %bitcast.17), calls=%async_computation | async-start | bytes 1048576 | tf_op jit(solution)/shard_map/all_to_all | solution.py:432
  11.5 1.2 %copy-start.4 = (bf16[8,4,128,128]{3,2,1,0:T(8,128)(2,1)S(1)}, bf16[8,4,128,128]{3,2,1,0:T(8,128)(2,1)}, u32[]{:S(2)}) copy-start(bf16[8,4,128,128]{3,2,1,0:T(8,128)(2,1)} %vals_ref.1) | copy-start | bytes 3145732
  12.7 0.7 copy-start.8
  15.6 1.7 %copy-start = (bf16[1024,1664]{1,0:T(8,128)(2,1)}, bf16[1024,1664]{1,0:T(8,128)(2,1)S(1)}, u32[]{:S(2)}) copy-start(bf16[1024,1664]{1,0:T(8,128)(2,1)S(1)} %get-tuple-element.42.at_ref) | copy-start | bytes 10223620
  17.3 1.0 %copy-start.5 = (bf16[4,128,1024]{2,1,0:T(8,128)(2,1)}, bf16[4,128,1024]{2,1,0:T(8,128)(2,1)S(1)}, u32[]{:S(2)}) copy-start(bf16[4,128,1024]{2,1,0:T(8,128)(2,1)S(1)} %get-tuple-element.43.a_ref) | copy-start | bytes 3145732
  25.2 1.2 %copy-start.6 = (bf16[4,128,1024]{2,1,0:T(8,128)(2,1)S(1)}, bf16[4,128,1024]{2,1,0:T(8,128)(2,1)}, u32[]{:S(2)}) copy-start(bf16[4,128,1024]{2,1,0:T(8,128)(2,1)} %copy-done.5) | copy-start | bytes 3145732
  27.1 5.5 %collective-permute-start = (bf16[256,256]{1,0:T(8,128)(2,1)S(1)}, bf16[256,256]{1,0:T(8,128)(2,1)S(1)}, u32[]{:S(2)}, u32[]{:S(2)}) collective-permute-start(bf16[256,256]{1,0:T(8,128)(2,1)S(1)} %get-tuple-element.48), channel_id=1, source_target_pairs={{0,1},{1,0},{2,3},{3,2},{4,5},{5,4},{6,7},{7,6},{8,9},{9,8},{10,11... | collective-permute-start | bytes 393224 | tf_op jit(solution)/shard_map/ppermute | solution.py:24
  27.2 7.2 %collective-permute-start.1 = (bf16[256,256]{1,0:T(8,128)(2,1)S(1)}, bf16[256,256]{1,0:T(8,128)(2,1)S(1)}, u32[]{:S(2)}, u32[]{:S(2)}) collective-permute-start(bf16[256,256]{1,0:T(8,128)(2,1)S(1)} %get-tuple-element.49), channel_id=1, source_target_pairs={{0,15},{1,2},{2,1},{3,4},{4,3},{5,6},{6,5},{7,8},{8,7},{9,10},{10,... | collective-permute-start | bytes 393224 | tf_op jit(solution)/shard_map/ppermute | solution.py:29
  30.0 10.0 %copy-start.1 = (bf16[1024,1664]{1,0:T(8,128)(2,1)S(1)}, bf16[1024,1664]{1,0:T(8,128)(2,1)}, u32[]{:S(2)}) copy-start(bf16[1024,1664]{1,0:T(8,128)(2,1)} %copy-done) | copy-start | bytes 10223620
  35.0 6.6 %collective-permute-start.2 = (bf16[256,256]{1,0:T(8,128)(2,1)S(1)}, bf16[256,256]{1,0:T(8,128)(2,1)S(1)}, u32[]{:S(2)}, u32[]{:S(2)}) collective-permute-start(bf16[256,256]{1,0:T(8,128)(2,1)S(1)} %get-tuple-element.54), channel_id=1, source_target_pairs={{0,1},{1,0},{2,3},{3,2},{4,5},{5,4},{6,7},{7,6},{8,9},{9,8},{10,11... | collective-permute-start | bytes 393224 | tf_op jit(solution)/shard_map/ppermute | solution.py:24
  35.1 7.2 %collective-permute-start.3 = (bf16[256,256]{1,0:T(8,128)(2,1)S(1)}, bf16[256,256]{1,0:T(8,128)(2,1)S(1)}, u32[]{:S(2)}, u32[]{:S(2)}) collective-permute-start(bf16[256,256]{1,0:T(8,128)(2,1)S(1)} %get-tuple-element.55), channel_id=1, source_target_pairs={{0,15},{1,2},{2,1},{3,4},{4,3},{5,6},{6,5},{7,8},{8,7},{9,10},{10,... | collective-permute-start | bytes 393224 | tf_op jit(solution)/shard_map/ppermute | solution.py:29
  38.4 5.5 %collective-permute-start.4 = (bf16[512,128]{1,0:T(8,128)(2,1)S(1)}, bf16[512,128]{1,0:T(8,128)(2,1)S(1)}, u32[]{:S(2)}, u32[]{:S(2)}) collective-permute-start(bf16[512,128]{1,0:T(8,128)(2,1)S(1)} %get-tuple-element.66), channel_id=1, source_target_pairs={{0,16},{16,0},{1,17},{17,1},{2,18},{18,2},{3,19},{19,3},{4,20},{20... | collective-permute-start | bytes 393224 | tf_op jit(solution)/shard_map/ppermute | solution.py:24
  42.3 29.1 %copy-start.9 = (s32[1,1024]{1,0:T(1,128)S(1)}, s32[1,1024]{1,0:T(1,128)}, u32[]{:S(2)}) copy-start(s32[1,1024]{1,0:T(1,128)} %order_ref.1) | copy-start | bytes 12292
  44.0 1.4 %collective-permute-start.5 = (bf16[512,128]{1,0:T(8,128)(2,1)S(1)}, bf16[512,128]{1,0:T(8,128)(2,1)S(1)}, u32[]{:S(2)}, u32[]{:S(2)}) collective-permute-start(bf16[512,128]{1,0:T(8,128)(2,1)S(1)} %get-tuple-element.68), channel_id=1, source_target_pairs={{0,1},{1,0},{2,3},{3,2},{4,5},{5,4},{6,7},{7,6},{8,9},{9,8},{10,11... | collective-permute-start | bytes 393224 | tf_op jit(solution)/shard_map/ppermute | solution.py:24
  45.5 25.9 %all-to-all-start.1 = ((bf16[16,64,256]{2,1,0:T(8,128)(2,1)}), bf16[16,64,256]{2,1,0:T(8,128)(2,1)S(1)}, u32[]{:S(2)}, u32[]{:S(2)}) async-start(bf16[16,64,256]{2,1,0:T(8,128)(2,1)} %bitcast.5), calls=%async_computation.1 | async-start | bytes 1048576 | tf_op jit(solution)/shard_map/all_to_all | solution.py:508
  49.7 7.6 %collective-permute-start.6 = (bf16[256,128]{1,0:T(8,128)(2,1)S(1)}, bf16[256,128]{1,0:T(8,128)(2,1)S(1)}, u32[]{:S(2)}, u32[]{:S(2)}) collective-permute-start(bf16[256,128]{1,0:T(8,128)(2,1)S(1)} %get-tuple-element.72), channel_id=1, source_target_pairs={{0,2},{1,3},{2,0},{3,1},{4,6},{5,7},{6,4},{7,5},{8,10},{9,11},{10,... | collective-permute-start | bytes 196616 | tf_op jit(solution)/shard_map/ppermute | solution.py:24
  57.3 4.6 %collective-permute-start.7 = (bf16[256,128]{1,0:T(8,128)(2,1)S(1)}, bf16[256,128]{1,0:T(8,128)(2,1)S(1)}, u32[]{:S(2)}, u32[]{:S(2)}) collective-permute-start(bf16[256,128]{1,0:T(8,128)(2,1)S(1)} %shard_map.121.mine_ref), channel_id=1, source_target_pairs={{0,4},{1,5},{2,6},{3,7},{4,0},{5,1},{6,2},{7,3},{8,12},{9,13},{10,... | collective-permute-start | bytes 196616 | tf_op jit(solution)/shard_map/ppermute | solution.py:24
  62.0 5.8 %collective-permute-start.8 = (bf16[256,128]{1,0:T(8,128)(2,1)S(1)}, bf16[256,128]{1,0:T(8,128)(2,1)S(1)}, u32[]{:S(2)}, u32[]{:S(2)}) collective-permute-start(bf16[256,128]{1,0:T(8,128)(2,1)S(1)} %shard_map.122.mine_ref), channel_id=1, source_target_pairs={{0,8},{1,9},{2,10},{3,11},{4,12},{5,13},{6,14},{7,15},{8,0},{9,1},... | collective-permute-start | bytes 196616 | tf_op jit(solution)/shard_map/ppermute | solution.py:24
  67.8 5.3 %collective-permute-start.11 = (bf16[256,128]{1,0:T(8,128)(2,1)S(1)}, bf16[256,128]{1,0:T(8,128)(2,1)S(1)}, u32[]{:S(2)}, u32[]{:S(2)}) collective-permute-start(bf16[256,128]{1,0:T(8,128)(2,1)S(1)} %shard_map.123.mine_ref), channel_id=1, source_target_pairs={{0,18},{1,19},{2,16},{3,17},{4,22},{5,23},{6,20},{7,21},{8,26},{9,... | collective-permute-start | bytes 196616 | tf_op jit(solution)/shard_map/ppermute | solution.py:343
  70.3 4.3 %collective-permute-start.10 = (bf16[256,128]{1,0:T(8,128)(2,1)S(1)}, bf16[256,128]{1,0:T(8,128)(2,1)S(1)}, u32[]{:S(2)}, u32[]{:S(2)}) collective-permute-start(bf16[256,128]{1,0:T(8,128)(2,1)S(1)} %shard_map.123.mine_ref), channel_id=1, source_target_pairs={{0,2},{1,3},{2,0},{3,1},{4,6},{5,7},{6,4},{7,5},{8,10},{9,11},{10,... | collective-permute-start | bytes 196616 | tf_op jit(solution)/shard_map/ppermute | solution.py:24
  70.9 4.3 %collective-permute-start.9 = (bf16[256,128]{1,0:T(8,128)(2,1)S(1)}, bf16[256,128]{1,0:T(8,128)(2,1)S(1)}, u32[]{:S(2)}, u32[]{:S(2)}) collective-permute-start(bf16[256,128]{1,0:T(8,128)(2,1)S(1)} %shard_map.123.mine_ref), channel_id=1, source_target_pairs={{0,16},{16,0},{1,17},{17,1},{2,18},{18,2},{3,19},{19,3},{4,20},{20... | collective-permute-start | bytes 196616 | tf_op jit(solution)/shard_map/ppermute | solution.py:24
  75.2 1.5 %collective-permute-start.12 = (bf16[384,256]{1,0:T(8,128)(2,1)S(1)}, bf16[384,256]{1,0:T(8,128)(2,1)S(1)}, u32[]{:S(2)}, u32[]{:S(2)}) collective-permute-start(bf16[384,256]{1,0:T(8,128)(2,1)S(1)} %shard_map.125.refs_0_), channel_id=1, source_target_pairs={{0,1},{1,0},{2,3},{3,2},{4,5},{5,4},{6,7},{7,6},{8,9},{9,8},{10,11... | collective-permute-start | bytes 589832 | tf_op jit(solution)/shard_map/ppermute | solution.py:24

commit v5 on v4

--- a/solution.py
+++ b/solution.py
@@ -56,14 +56,18 @@
     load_feat = pltpu.make_async_copy(feat_hbm, feat_ref, feat_sem)
     load_order.start()
     load_feat.start()
-    lane = lax.broadcasted_iota(jnp.int32, (ROWS, rows), 1).astype(F32)
+    lane = lax.broadcasted_iota(jnp.int32, (ROWS, ROWS), 1).astype(F32)
+    zero = jnp.zeros((ROWS, ROWS), BF16)
     load_order.wait()
 
+    def column(row):
+        return jnp.transpose(jnp.broadcast_to(row.astype(F32), (ROWS, ROWS)))
+
     def hot_rows(k):
-        row = order_ref[:, k * ROWS : (k + 1) * ROWS].astype(F32)
-        col = jnp.transpose(jnp.broadcast_to(row, (ROWS, ROWS)))
-        wide = jnp.concatenate([col] * (rows // ROWS), axis=1)
-        return jnp.where(wide == lane, 1.0, 0.0).astype(BF16)
+        row = order_ref[:, k * ROWS : (k + 1) * ROWS]
+        high = column(row // ROWS).astype(BF16)
+        low = jnp.where(column(row % ROWS) == lane, 1.0, 0.0).astype(BF16)
+        return jnp.concatenate([jnp.where(high == b, low, zero) for b in range(rows // ROWS)], axis=1)
 
     for k in range(early):
         hot_ref[k * ROWS : (k + 1) * ROWS, :] = hot_rows(k)
@@ -386,11 +390,14 @@
 def place_body(order_ref, back_ref, out_ref):
     rows = back_ref.shape[0]
     back = back_ref[...]
-    order = jnp.broadcast_to(order_ref[...], (ROWS, rows))
+    order = order_ref[...]
+    high = jnp.broadcast_to((order // ROWS).astype(F32), (ROWS, rows)).astype(BF16)
+    row = lax.broadcasted_iota(jnp.int32, (ROWS, rows), 0)
+    low = jnp.where(jnp.broadcast_to(order % ROWS, (ROWS, rows)) == row, 1.0, 0.0).astype(BF16)
+    zero = jnp.zeros((ROWS, rows), BF16)
     for k in range(rows // ROWS):
         mine = slice(k * ROWS, (k + 1) * ROWS)
-        row = lax.broadcasted_iota(jnp.int32, (ROWS, rows), 0) + k * ROWS
-        hot = jnp.where(order == row, 1.0, 0.0).astype(BF16)
+        hot = jnp.where(high == k, low, zero)
         out_ref[mine, :] = dot(hot, back).astype(BF16)
 
 
@@ -503,8 +510,8 @@
         nbytes=8 * unit,
     )
     if tiled:
-        keep, send = cut_grads(edge_part, node_part)
-        back, send = lax.optimization_barrier((back, send))
+        back, node_in = lax.optimization_barrier((back, node_part[1]))
+        keep, send = cut_grads(edge_part, (node_part[0], node_in))
     back = lax.all_to_all(
         back.reshape(ndom, per_peer, width), "dom", split_axis=0, concat_axis=0, tiled=True
     ).reshape(rows, width)

time: 77.9 us -> 76.3 us (0.979)
  waiting for transfers between devices: 25.3 us -> 22.5 us
  starting transfers between devices: 28.9 us -> 30.1 us
    ppermute x10, waiting for transfers between devices: 15.7 us -> 13 us  [swapped(): return lax.ppermute(x, axis, [(i, i ^ mask) for i in range(peers)])]
    ppermute x10, starting transfers between devices: 9.2 us -> 10.5 us  [swapped(): return lax.ppermute(x, axis, [(i, i ^ mask) for i in range(peers)])]
  transfers between devices with their start and end apart: 15 -> 15, of which waited for: 11 -> 11; matrix products, arithmetic and copies ran while one was open for 1% -> 1% of each run, Pallas kernels for 14% -> 15%
where the time goes in v5:
time: 76.3 us; the launch traced here: 75.8 us
  starting transfers between devices  30.1 us (39%)
  waiting for transfers between devices  22.5 us (29%)
  Pallas kernels  15.9 us (21%)
  local copies, waits for them, and re-layouts  6.56 us (9%)
  between operations  0.82 us (1%)
    pallas_call x15, Pallas kernels, call(): pl.pallas_call(body, out_shape=outs, in_specs=specs or [VMEM] * len(args)...  14.4 us
    ppermute x10, waiting for transfers between devices, swapped(): return lax.ppermute(x, axis, [(i, i ^ mask) for i in range(peers)])  13 us
    ppermute x10, starting transfers between devices, swapped(): return lax.ppermute(x, axis, [(i, i ^ mask) for i in range(peers)])  10.5 us
    all_to_all x1, starting transfers between devices, shards(): lax.all_to_all(picked.reshape(ndom, per_peer, width), 'dom', split_axis=0...  7.4 us
    all_to_all x1, waiting for transfers between devices, shards(): lax.all_to_all(picked.reshape(ndom, per_peer, width), 'dom', split_axis=0...  6.89 us
    unnamed x21, local copies, waits for them, and re-layouts  6.56 us
    ppermute x2, starting transfers between devices, swapped_across(): lax.ppermute(x, axis, [(i, (i + 1 if i % 2 else i - 1) % peers) for i in...  5.63 us
    all_to_all x1, starting transfers between devices, shards(): lax.all_to_all(back.reshape(ndom, per_peer, width), 'dom', split_axis=0,...  4.14 us
  transfers between devices with their start and end apart: 15, of which 11 were waited for; matrix products, arithmetic and copies ran while one was open for 1% of the time, Pallas kernels for 15%

profile of v5, /device:TPU:0, one launch (start us, length us, event | category | flops | bytes accessed | tf_op | source)
XLA Modules:
  0.0 75.8 jit_solution(3115867640657733128)
XLA Ops:
  0.6 0.0 copy-start.3
  0.6 0.0 copy-start.7
  0.7 0.0 copy-start.2
  0.7 2.6 %shard_map.111 = bf16[1024,256]{1,0:T(8,128)(2,1)} custom-call(s32[1,1024]{1,0:T(1,128)} %order_ref.1, bf16[1024,256]{1,0:T(8,128)(2,1)} %bitcast.18), custom_call_target="tpu_custom_call" | custom-call | flops 536870912 | bytes 1048576 | tf_op jit(solution)/shard_map/pallas_call | solution.py:41
  3.3 7.4 %all-to-all-start = ((bf16[16,64,256]{2,1,0:T(8,128)(2,1)}), bf16[16,64,256]{2,1,0:T(8,128)(2,1)S(1)}, u32[]{:S(2)}, u32[]{:S(2)}) async-start(bf16[16,64,256]{2,1,0:T(8,128)(2,1)} %bitcast.17), calls=%async_computation | async-start | bytes 1048576 | tf_op jit(solution)/shard_map/all_to_all | solution.py:439
  10.7 0.8 copy.14.tgt_ref
  11.4 0.0 copy-start.4
  11.4 1.2 %copy-done.4 = bf16[8,4,128,128]{3,2,1,0:T(8,128)(2,1)S(1)} copy-done((bf16[8,4,128,128]{3,2,1,0:T(8,128)(2,1)S(1)}, bf16[8,4,128,128]{3,2,1,0:T(8,128)(2,1)}, u32[]{:S(2)}) %copy-start.4) | copy-done | bytes 1048600
  12.7 0.0 copy-start.8
  12.7 0.7 copy-done.8
  13.3 2.2 %shard_map.112 = (bf16[8,128,1024]{2,1,0:T(8,128)(2,1)S(1)}, bf16[4,128,1024]{2,1,0:T(8,128)(2,1)S(1)}, bf16[1024,1664]{1,0:T(8,128)(2,1)S(1)}) custom-call(s32[8]{0:T(128)S(1)} %copy-done.8, s32[8,4]{1,0:T(8,128)S(1)} %copy.14.tgt_ref, bf16[8,4,128,128]{3,2,1,0:T(8,128)(2,1)S(1)} %copy-done.4), custom_call_target="tpu_custom_call" | custom-call | bytes 8388608 | tf_op jit(solution)/shard_map/pallas_call | solution.py:41
  15.6 0.0 copy-start
  15.6 1.7 %copy-done = bf16[1024,1664]{1,0:T(8,128)(2,1)} copy-done((bf16[1024,1664]{1,0:T(8,128)(2,1)}, bf16[1024,1664]{1,0:T(8,128)(2,1)S(1)}, u32[]{:S(2)}) %copy-start) | copy-done | bytes 3407896
  17.3 0.0 copy-start.5
  17.3 1.0 %copy-done.5 = bf16[4,128,1024]{2,1,0:T(8,128)(2,1)} copy-done((bf16[4,128,1024]{2,1,0:T(8,128)(2,1)}, bf16[4,128,1024]{2,1,0:T(8,128)(2,1)S(1)}, u32[]{:S(2)}) %copy-start.5) | copy-done | bytes 1048600
  18.3 6.9 %all-to-all-done = bf16[16,64,256]{2,1,0:T(8,128)(2,1)S(1)} async-done(((bf16[16,64,256]{2,1,0:T(8,128)(2,1)}), bf16[16,64,256]{2,1,0:T(8,128)(2,1)S(1)}, u32[]{:S(2)}, u32[]{:S(2)}) %all-to-all-start) | async-done | bytes 524320 | tf_op jit(solution)/shard_map/all_to_all | solution.py:439
  25.1 0.0 copy-done.3
  25.1 0.0 copy-start.6
  25.1 1.2 %copy-done.6 = bf16[4,128,1024]{2,1,0:T(8,128)(2,1)S(1)} copy-done((bf16[4,128,1024]{2,1,0:T(8,128)(2,1)S(1)}, bf16[4,128,1024]{2,1,0:T(8,128)(2,1)}, u32[]{:S(2)}) %copy-start.6) | copy-done | bytes 1048600
  26.4 0.7 shard_map.113
  27.1 0.1 collective-permute-start
  27.2 2.8 %collective-permute-start.1 = (bf16[256,256]{1,0:T(8,128)(2,1)S(1)}, bf16[256,256]{1,0:T(8,128)(2,1)S(1)}, u32[]{:S(2)}, u32[]{:S(2)}) collective-permute-start(bf16[256,256]{1,0:T(8,128)(2,1)S(1)} %get-tuple-element.49), channel_id=1, source_target_pairs={{0,15},{1,2},{2,1},{3,4},{4,3},{5,6},{6,5},{7,8},{8,7},{9,10},{10,... | collective-permute-start | bytes 393224 | tf_op jit(solution)/shard_map/ppermute | solution.py:29
  30.0 0.0 copy-done.7
  30.0 0.0 copy-done.2
  30.0 0.0 copy-start.1
  30.0 2.6 %shard_map.114 = (bf16[512,256]{1,0:T(8,128)(2,1)S(1)}, bf16[512,256]{1,0:T(8,128)(2,1)S(1)}, bf16[512,256]{1,0:T(8,128)(2,1)S(1)}, bf16[512,256]{1,0:T(8,128)(2...) custom-call(bf16[1024,256]{1,0:T(8,128)(2,1)S(1)} %bitcast.9, ...), custom_call_target="tpu_custom_call" | custom-call | flops 805306368 | bytes 4194304 | tf_op jit(solution)/shard_map/pallas_call | solution.py:41
  32.6 0.0 collective-permute-done.near_in_ref
  32.6 1.7 %collective-permute-done.1.far_in_ref = bf16[256,256]{1,0:T(8,128)(2,1)S(1)} collective-permute-done((bf16[256,256]{1,0:T(8,128)(2,1)S(1)}, bf16[256,256]{1,0:T(8,128)(2,1)S(1)}, u32[]{:S(2)}, u32[]{:S(2)}) %collective-permute-start.1) | collective-permute-done | bytes 131104 | tf_op jit(solution)/shard_map/ppermute | solution.py:29
  34.3 0.7 shard_map.115
  35.0 0.1 collective-permute-start.2
  35.1 2.8 %collective-permute-start.3 = (bf16[256,256]{1,0:T(8,128)(2,1)S(1)}, bf16[256,256]{1,0:T(8,128)(2,1)S(1)}, u32[]{:S(2)}, u32[]{:S(2)}) collective-permute-start(bf16[256,256]{1,0:T(8,128)(2,1)S(1)} %get-tuple-element.55), channel_id=1, source_target_pairs={{0,15},{1,2},{2,1},{3,4},{4,3},{5,6},{6,5},{7,8},{8,7},{9,10},{10,... | collective-permute-start | bytes 393224 | tf_op jit(solution)/shard_map/ppermute | solution.py:29
  37.9 0.5 shard_map.118
  38.4 1.6 %collective-permute-start.4 = (bf16[512,128]{1,0:T(8,128)(2,1)S(1)}, bf16[512,128]{1,0:T(8,128)(2,1)S(1)}, u32[]{:S(2)}, u32[]{:S(2)}) collective-permute-start(bf16[512,128]{1,0:T(8,128)(2,1)S(1)} %get-tuple-element.67), channel_id=1, source_target_pairs={{0,16},{16,0},{1,17},{17,1},{2,18},{18,2},{3,19},{19,3},{4,20},{20... | collective-permute-start | bytes 393224 | tf_op jit(solution)/shard_map/ppermute | solution.py:24
  39.9 0.0 copy-done.1
  39.9 1.6 %shard_map.116 = (bf16[1024,256]{1,0:T(8,128)(2,1)}, f32[1024,256]{1,0:T(8,128)S(1)}, f32[1024,256]{1,0:T(8,128)S(1)}) custom-call(bf16[1024,256]{1,0:T(8,128)(2,1)S(1)} %bitcast.12, bf16[1024,1664]{1,0:T(8,128)(2,1)S(1)} %copy-done.1, bf16[256,256]{1,0:T(8,128)(2,1)S(1)} %copy-done.3, bf16[512,256]{1,0:T(8,128)(2,1)S(1)} %get-tuple-element.46.out_mid_ref, ...), custom_call_target="tpu_custom_call" | custom-call | flops 671088640 | bytes 4194304 | tf_op jit(solution)/shard_map/pallas_call | solution.py:41
  41.6 0.0 collective-permute-done.2.near_ref
  41.6 0.7 collective-permute-done.3.far_ref
  42.2 0.0 copy-start.9
  42.2 1.7 %shard_map.117 = (bf16[1024,256]{1,0:T(8,128)(2,1)}, f32[256,256]{1,0:T(8,128)S(1)}) custom-call(bf16[1024,256]{1,0:T(8,128)(2,1)S(1)} %bitcast.13, bf16[1024,1664]{1,0:T(8,128)(2,1)S(1)} %copy-done.1, bf16[256,256]{1,0:T(8,128)(2,1)S(1)} %collective-permute-done.2.near_ref, bf16[256,256]{1,0:T(8,128)(2,1)S(1)} %collective-permute-done.3.far_ref, ...), custom_call_target="tpu_custom_call" | custom-call | flops 536870912 | bytes 4194304 | tf_op jit(solution)/shard_map/pallas_call | solution.py:41
  43.9 0.0 collective-permute-done.4.node_in_ref
  43.9 4.1 %all-to-all-start.1 = ((bf16[16,64,256]{2,1,0:T(8,128)(2,1)}), bf16[16,64,256]{2,1,0:T(8,128)(2,1)S(1)}, u32[]{:S(2)}, u32[]{:S(2)}) async-start(bf16[16,64,256]{2,1,0:T(8,128)(2,1)} %bitcast.5), calls=%async_computation.1 | async-start | bytes 1048576 | tf_op jit(solution)/shard_map/all_to_all | solution.py:515
  48.0 0.1 shard_map.119
  48.1 0.5 collective-permute-start.5
  48.6 1.0 %collective-permute-done.5.in_ref = bf16[512,128]{1,0:T(8,128)(2,1)S(1)} collective-permute-done((bf16[512,128]{1,0:T(8,128)(2,1)S(1)}, bf16[512,128]{1,0:T(8,128)(2,1)S(1)}, u32[]{:S(2)}, u32[]{:S(2)}) %collective-permute-start.5) | collective-permute-done | bytes 131104 | tf_op jit(solution)/shard_map/ppermute | solution.py:24
  49.6 1.9 %collective-permute-start.6 = (bf16[256,128]{1,0:T(8,128)(2,1)S(1)}, bf16[256,128]{1,0:T(8,128)(2,1)S(1)}, u32[]{:S(2)}, u32[]{:S(2)}) collective-permute-start(bf16[256,128]{1,0:T(8,128)(2,1)S(1)} %get-tuple-element.72), channel_id=1, source_target_pairs={{0,2},{1,3},{2,0},{3,1},{4,6},{5,7},{6,4},{7,5},{8,10},{9,11},{10,... | collective-permute-start | bytes 196616 | tf_op jit(solution)/shard_map/ppermute | solution.py:24
  51.6 4.1 %collective-permute-done.6.in_ref = bf16[256,128]{1,0:T(8,128)(2,1)S(1)} collective-permute-done((bf16[256,128]{1,0:T(8,128)(2,1)S(1)}, bf16[256,128]{1,0:T(8,128)(2,1)S(1)}, u32[]{:S(2)}, u32[]{:S(2)}) %collective-permute-start.6) | collective-permute-done | bytes 65568 | tf_op jit(solution)/shard_map/ppermute | solution.py:24
  55.7 1.9 %collective-permute-start.7 = (bf16[256,128]{1,0:T(8,128)(2,1)S(1)}, bf16[256,128]{1,0:T(8,128)(2,1)S(1)}, u32[]{:S(2)}, u32[]{:S(2)}) collective-permute-start(bf16[256,128]{1,0:T(8,128)(2,1)S(1)} %shard_map.121.mine_ref), channel_id=1, source_target_pairs={{0,4},{1,5},{2,6},{3,7},{4,0},{5,1},{6,2},{7,3},{8,12},{9,13},{10,... | collective-permute-start | bytes 196616 | tf_op jit(solution)/shard_map/ppermute | solution.py:24
  57.6 2.7 %collective-permute-done.7.in_ref = bf16[256,128]{1,0:T(8,128)(2,1)S(1)} collective-permute-done((bf16[256,128]{1,0:T(8,128)(2,1)S(1)}, bf16[256,128]{1,0:T(8,128)(2,1)S(1)}, u32[]{:S(2)}, u32[]{:S(2)}) %collective-permute-start.7) | collective-permute-done | bytes 65568 | tf_op jit(solution)/shard_map/ppermute | solution.py:24
  60.3 3.3 %collective-permute-start.8 = (bf16[256,128]{1,0:T(8,128)(2,1)S(1)}, bf16[256,128]{1,0:T(8,128)(2,1)S(1)}, u32[]{:S(2)}, u32[]{:S(2)}) collective-permute-start(bf16[256,128]{1,0:T(8,128)(2,1)S(1)} %shard_map.122.mine_ref), channel_id=1, source_target_pairs={{0,8},{1,9},{2,10},{3,11},{4,12},{5,13},{6,14},{7,15},{8,0},{9,1},... | collective-permute-start | bytes 196616 | tf_op jit(solution)/shard_map/ppermute | solution.py:24
  63.6 2.5 %collective-permute-done.8.in_ref = bf16[256,128]{1,0:T(8,128)(2,1)S(1)} collective-permute-done((bf16[256,128]{1,0:T(8,128)(2,1)S(1)}, bf16[256,128]{1,0:T(8,128)(2,1)S(1)}, u32[]{:S(2)}, u32[]{:S(2)}) %collective-permute-start.8) | collective-permute-done | bytes 65568 | tf_op jit(solution)/shard_map/ppermute | solution.py:24
  66.2 2.5 %collective-permute-start.11 = (bf16[256,128]{1,0:T(8,128)(2,1)S(1)}, bf16[256,128]{1,0:T(8,128)(2,1)S(1)}, u32[]{:S(2)}, u32[]{:S(2)}) collective-permute-start(bf16[256,128]{1,0:T(8,128)(2,1)S(1)} %shard_map.123.mine_ref), channel_id=1, source_target_pairs={{0,18},{1,19},{2,16},{3,17},{4,22},{5,23},{6,20},{7,21},{8,26},{9,... | collective-permute-start | bytes 196616 | tf_op jit(solution)/shard_map/ppermute | solution.py:347
  68.7 0.6 collective-permute-start.10
  69.2 0.5 collective-permute-start.9
  69.7 0.0 all-to-all-done.1
  69.7 0.0 copy-done.9
  69.8 1.5 %shard_map.124 = bf16[1024,256]{1,0:T(8,128)(2,1)} custom-call(s32[1,1024]{1,0:T(1,128)S(1)} %copy-done.9, bf16[1024,256]{1,0:T(8,128)(2,1)S(1)} %bitcast.16), custom_call_target="tpu_custom_call" | custom-call | flops 536870912 | bytes 1048576 | tf_op jit(solution)/shard_map/pallas_call | solution.py:41
  71.3 0.2 collective-permute-done.11.both_ref
  71.5 1.4 %collective-permute-done.10.y_ref = bf16[256,128]{1,0:T(8,128)(2,1)S(1)} collective-permute-done((bf16[256,128]{1,0:T(8,128)(2,1)S(1)}, bf16[256,128]{1,0:T(8,128)(2,1)S(1)}, u32[]{:S(2)}, u32[]{:S(2)}) %collective-permute-start.10) | collective-permute-done | bytes 65568 | tf_op jit(solution)/shard_map/ppermute | solution.py:24
  72.9 0.6 collective-permute-done.9.dp_ref
  73.5 0.1 shard_map.125.refs_0_
  73.6 0.1 collective-permute-start.12
  73.6 0.8 %shard_map.126 = (f32[256,256]{1,0:T(8,128)}, f32[512,256]{1,0:T(8,128)}) custom-call(bf16[384,256]{1,0:T(8,128)(2,1)S(1)} %shard_map.125.refs_0_), custom_call_target="tpu_custom_call" | custom-call | bytes 786432 | tf_op jit(solution)/shard_map/pallas_call | solution.py:328
  74.4 0.6 collective-permute-done.12.refs_0_
  75.1 0.8 %shard_map.127 = (f32[256,256]{1,0:T(8,128)}, f32[512,256]{1,0:T(8,128)}) custom-call(bf16[384,256]{1,0:T(8,128)(2,1)S(1)} %collective-permute-done.12.refs_0_, f32[256,256]{1,0:T(8,128)} %get-tuple-element.76.refs_1_, f32[512,256]{1,0:T(8,128)} %get-tuple-element.77.refs_2_), custom_call_target="tpu_custom_call", output_to_operand_aliasing={{0}: (1, {}), {1}: (2, {})} | custom-call | bytes 786432 | tf_op jit(solution)/shard_map/pallas_call | solution.py:328
  (4 shorter events, 0.1 us)
Async XLA Ops:
  0.6 24.5 %copy-start.3 = (bf16[256,256]{1,0:T(8,128)(2,1)S(1)}, bf16[256,256]{1,0:T(8,128)(2,1)}, u32[]{:S(2)}) copy-start(bf16[256,256]{1,0:T(8,128)(2,1)} %w_edge_ref.5) | copy-start | bytes 393220
  0.6 29.3 %copy-start.7 = (bf16[512,256]{1,0:T(8,128)(2,1)S(1)}, bf16[512,256]{1,0:T(8,128)(2,1)}, u32[]{:S(2)}) copy-start(bf16[512,256]{1,0:T(8,128)(2,1)} %w_node_ref.3) | copy-start | bytes 786436
  0.7 29.3 %copy-start.2 = (bf16[1,1024,256]{2,1,0:T(8,128)(2,1)S(1)}, bf16[1,1024,256]{2,1,0:T(8,128)(2,1)}, u32[]{:S(2)}) copy-start(bf16[1,1024,256]{2,1,0:T(8,128)(2,1)} %param.15) | copy-start | bytes 1572868
  3.3 21.9 %all-to-all-start = ((bf16[16,64,256]{2,1,0:T(8,128)(2,1)}), bf16[16,64,256]{2,1,0:T(8,128)(2,1)S(1)}, u32[]{:S(2)}, u32[]{:S(2)}) async-start(bf16[16,64,256]{2,1,0:T(8,128)(2,1)} %bitcast.17), calls=%async_computation | async-start | bytes 1048576 | tf_op jit(solution)/shard_map/all_to_all | solution.py:439
  11.4 1.2 %copy-start.4 = (bf16[8,4,128,128]{3,2,1,0:T(8,128)(2,1)S(1)}, bf16[8,4,128,128]{3,2,1,0:T(8,128)(2,1)}, u32[]{:S(2)}) copy-start(bf16[8,4,128,128]{3,2,1,0:T(8,128)(2,1)} %vals_ref.1) | copy-start | bytes 3145732
  12.7 0.7 copy-start.8
  15.6 1.7 %copy-start = (bf16[1024,1664]{1,0:T(8,128)(2,1)}, bf16[1024,1664]{1,0:T(8,128)(2,1)S(1)}, u32[]{:S(2)}) copy-start(bf16[1024,1664]{1,0:T(8,128)(2,1)S(1)} %get-tuple-element.42.at_ref) | copy-start | bytes 10223620
  17.3 1.0 %copy-start.5 = (bf16[4,128,1024]{2,1,0:T(8,128)(2,1)}, bf16[4,128,1024]{2,1,0:T(8,128)(2,1)S(1)}, u32[]{:S(2)}) copy-start(bf16[4,128,1024]{2,1,0:T(8,128)(2,1)S(1)} %get-tuple-element.43.a_ref) | copy-start | bytes 3145732
  25.1 1.2 %copy-start.6 = (bf16[4,128,1024]{2,1,0:T(8,128)(2,1)S(1)}, bf16[4,128,1024]{2,1,0:T(8,128)(2,1)}, u32[]{:S(2)}) copy-start(bf16[4,128,1024]{2,1,0:T(8,128)(2,1)} %copy-done.5) | copy-start | bytes 3145732
  27.1 5.5 %collective-permute-start = (bf16[256,256]{1,0:T(8,128)(2,1)S(1)}, bf16[256,256]{1,0:T(8,128)(2,1)S(1)}, u32[]{:S(2)}, u32[]{:S(2)}) collective-permute-start(bf16[256,256]{1,0:T(8,128)(2,1)S(1)} %get-tuple-element.48), channel_id=1, source_target_pairs={{0,1},{1,0},{2,3},{3,2},{4,5},{5,4},{6,7},{7,6},{8,9},{9,8},{10,11... | collective-permute-start | bytes 393224 | tf_op jit(solution)/shard_map/ppermute | solution.py:24
  27.2 7.2 %collective-permute-start.1 = (bf16[256,256]{1,0:T(8,128)(2,1)S(1)}, bf16[256,256]{1,0:T(8,128)(2,1)S(1)}, u32[]{:S(2)}, u32[]{:S(2)}) collective-permute-start(bf16[256,256]{1,0:T(8,128)(2,1)S(1)} %get-tuple-element.49), channel_id=1, source_target_pairs={{0,15},{1,2},{2,1},{3,4},{4,3},{5,6},{6,5},{7,8},{8,7},{9,10},{10,... | collective-permute-start | bytes 393224 | tf_op jit(solution)/shard_map/ppermute | solution.py:29
  30.0 10.0 %copy-start.1 = (bf16[1024,1664]{1,0:T(8,128)(2,1)S(1)}, bf16[1024,1664]{1,0:T(8,128)(2,1)}, u32[]{:S(2)}) copy-start(bf16[1024,1664]{1,0:T(8,128)(2,1)} %copy-done) | copy-start | bytes 10223620
  35.0 6.6 %collective-permute-start.2 = (bf16[256,256]{1,0:T(8,128)(2,1)S(1)}, bf16[256,256]{1,0:T(8,128)(2,1)S(1)}, u32[]{:S(2)}, u32[]{:S(2)}) collective-permute-start(bf16[256,256]{1,0:T(8,128)(2,1)S(1)} %get-tuple-element.54), channel_id=1, source_target_pairs={{0,1},{1,0},{2,3},{3,2},{4,5},{5,4},{6,7},{7,6},{8,9},{9,8},{10,11... | collective-permute-start | bytes 393224 | tf_op jit(solution)/shard_map/ppermute | solution.py:24
  35.1 7.2 %collective-permute-start.3 = (bf16[256,256]{1,0:T(8,128)(2,1)S(1)}, bf16[256,256]{1,0:T(8,128)(2,1)S(1)}, u32[]{:S(2)}, u32[]{:S(2)}) collective-permute-start(bf16[256,256]{1,0:T(8,128)(2,1)S(1)} %get-tuple-element.55), channel_id=1, source_target_pairs={{0,15},{1,2},{2,1},{3,4},{4,3},{5,6},{6,5},{7,8},{8,7},{9,10},{10,... | collective-permute-start | bytes 393224 | tf_op jit(solution)/shard_map/ppermute | solution.py:29
  38.4 5.5 %collective-permute-start.4 = (bf16[512,128]{1,0:T(8,128)(2,1)S(1)}, bf16[512,128]{1,0:T(8,128)(2,1)S(1)}, u32[]{:S(2)}, u32[]{:S(2)}) collective-permute-start(bf16[512,128]{1,0:T(8,128)(2,1)S(1)} %get-tuple-element.67), channel_id=1, source_target_pairs={{0,16},{16,0},{1,17},{17,1},{2,18},{18,2},{3,19},{19,3},{4,20},{20... | collective-permute-start | bytes 393224 | tf_op jit(solution)/shard_map/ppermute | solution.py:24
  42.2 27.5 %copy-start.9 = (s32[1,1024]{1,0:T(1,128)S(1)}, s32[1,1024]{1,0:T(1,128)}, u32[]{:S(2)}) copy-start(s32[1,1024]{1,0:T(1,128)} %order_ref.1) | copy-start | bytes 12292
  43.9 25.9 %all-to-all-start.1 = ((bf16[16,64,256]{2,1,0:T(8,128)(2,1)}), bf16[16,64,256]{2,1,0:T(8,128)(2,1)S(1)}, u32[]{:S(2)}, u32[]{:S(2)}) async-start(bf16[16,64,256]{2,1,0:T(8,128)(2,1)} %bitcast.5), calls=%async_computation.1 | async-start | bytes 1048576 | tf_op jit(solution)/shard_map/all_to_all | solution.py:515
  48.1 1.5 %collective-permute-start.5 = (bf16[512,128]{1,0:T(8,128)(2,1)S(1)}, bf16[512,128]{1,0:T(8,128)(2,1)S(1)}, u32[]{:S(2)}, u32[]{:S(2)}) collective-permute-start(bf16[512,128]{1,0:T(8,128)(2,1)S(1)} %get-tuple-element.70), channel_id=1, source_target_pairs={{0,1},{1,0},{2,3},{3,2},{4,5},{5,4},{6,7},{7,6},{8,9},{9,8},{10,11... | collective-permute-start | bytes 393224 | tf_op jit(solution)/shard_map/ppermute | solution.py:24
  49.6 6.0 %collective-permute-start.6 = (bf16[256,128]{1,0:T(8,128)(2,1)S(1)}, bf16[256,128]{1,0:T(8,128)(2,1)S(1)}, u32[]{:S(2)}, u32[]{:S(2)}) collective-permute-start(bf16[256,128]{1,0:T(8,128)(2,1)S(1)} %get-tuple-element.72), channel_id=1, source_target_pairs={{0,2},{1,3},{2,0},{3,1},{4,6},{5,7},{6,4},{7,5},{8,10},{9,11},{10,... | collective-permute-start | bytes 196616 | tf_op jit(solution)/shard_map/ppermute | solution.py:24
  55.7 4.6 %collective-permute-start.7 = (bf16[256,128]{1,0:T(8,128)(2,1)S(1)}, bf16[256,128]{1,0:T(8,128)(2,1)S(1)}, u32[]{:S(2)}, u32[]{:S(2)}) collective-permute-start(bf16[256,128]{1,0:T(8,128)(2,1)S(1)} %shard_map.121.mine_ref), channel_id=1, source_target_pairs={{0,4},{1,5},{2,6},{3,7},{4,0},{5,1},{6,2},{7,3},{8,12},{9,13},{10,... | collective-permute-start | bytes 196616 | tf_op jit(solution)/shard_map/ppermute | solution.py:24
  60.3 5.8 %collective-permute-start.8 = (bf16[256,128]{1,0:T(8,128)(2,1)S(1)}, bf16[256,128]{1,0:T(8,128)(2,1)S(1)}, u32[]{:S(2)}, u32[]{:S(2)}) collective-permute-start(bf16[256,128]{1,0:T(8,128)(2,1)S(1)} %shard_map.122.mine_ref), channel_id=1, source_target_pairs={{0,8},{1,9},{2,10},{3,11},{4,12},{5,13},{6,14},{7,15},{8,0},{9,1},... | collective-permute-start | bytes 196616 | tf_op jit(solution)/shard_map/ppermute | solution.py:24
  66.2 5.3 %collective-permute-start.11 = (bf16[256,128]{1,0:T(8,128)(2,1)S(1)}, bf16[256,128]{1,0:T(8,128)(2,1)S(1)}, u32[]{:S(2)}, u32[]{:S(2)}) collective-permute-start(bf16[256,128]{1,0:T(8,128)(2,1)S(1)} %shard_map.123.mine_ref), channel_id=1, source_target_pairs={{0,18},{1,19},{2,16},{3,17},{4,22},{5,23},{6,20},{7,21},{8,26},{9,... | collective-permute-start | bytes 196616 | tf_op jit(solution)/shard_map/ppermute | solution.py:347
  68.7 4.3 %collective-permute-start.10 = (bf16[256,128]{1,0:T(8,128)(2,1)S(1)}, bf16[256,128]{1,0:T(8,128)(2,1)S(1)}, u32[]{:S(2)}, u32[]{:S(2)}) collective-permute-start(bf16[256,128]{1,0:T(8,128)(2,1)S(1)} %shard_map.123.mine_ref), channel_id=1, source_target_pairs={{0,2},{1,3},{2,0},{3,1},{4,6},{5,7},{6,4},{7,5},{8,10},{9,11},{10,... | collective-permute-start | bytes 196616 | tf_op jit(solution)/shard_map/ppermute | solution.py:24
  69.2 4.3 %collective-permute-start.9 = (bf16[256,128]{1,0:T(8,128)(2,1)S(1)}, bf16[256,128]{1,0:T(8,128)(2,1)S(1)}, u32[]{:S(2)}, u32[]{:S(2)}) collective-permute-start(bf16[256,128]{1,0:T(8,128)(2,1)S(1)} %shard_map.123.mine_ref), channel_id=1, source_target_pairs={{0,16},{16,0},{1,17},{17,1},{2,18},{18,2},{3,19},{19,3},{4,20},{20... | collective-permute-start | bytes 196616 | tf_op jit(solution)/shard_map/ppermute | solution.py:24
  73.6 1.5 %collective-permute-start.12 = (bf16[384,256]{1,0:T(8,128)(2,1)S(1)}, bf16[384,256]{1,0:T(8,128)(2,1)S(1)}, u32[]{:S(2)}, u32[]{:S(2)}) collective-permute-start(bf16[384,256]{1,0:T(8,128)(2,1)S(1)} %shard_map.125.refs_0_), channel_id=1, source_target_pairs={{0,1},{1,0},{2,3},{3,2},{4,5},{5,4},{6,7},{7,6},{8,9},{9,8},{10,11... | collective-permute-start | bytes 589832 | tf_op jit(solution)/shard_map/ppermute | solution.py:24

commit v6 on v5

--- a/solution.py
+++ b/solution.py
@@ -10,6 +10,7 @@
 
 ROWS = 128
 RIM = 2
+TALL = 4
 ANY = pl.BlockSpec(memory_space=pl.ANY)
 VMEM = pl.BlockSpec(memory_space=pltpu.VMEM)
 SMEM = pl.BlockSpec(memory_space=pltpu.SMEM)
@@ -51,7 +52,6 @@
 
 def pick_body(order_hbm, feat_hbm, out_hbm, order_ref, feat_ref, hot_ref, out_ref, order_sem, feat_sem, out_sems):
     rows = feat_ref.shape[0]
-    early = hot_ref.shape[0] // ROWS
     load_order = pltpu.make_async_copy(order_hbm, order_ref, order_sem)
     load_feat = pltpu.make_async_copy(feat_hbm, feat_ref, feat_sem)
     load_order.start()
@@ -69,26 +69,32 @@
         low = jnp.where(column(row % ROWS) == lane, 1.0, 0.0).astype(BF16)
         return jnp.concatenate([jnp.where(high == b, low, zero) for b in range(rows // ROWS)], axis=1)
 
-    for k in range(early):
-        hot_ref[k * ROWS : (k + 1) * ROWS, :] = hot_rows(k)
+    def build(k):
+        for b in range(k * TALL, (k + 1) * TALL):
+            hot_ref[b * ROWS : (b + 1) * ROWS, :] = hot_rows(b)
+
+    size = TALL * ROWS
+    build(0)
     load_feat.wait()
     feat = feat_ref[...]
     puts = []
-    for k in range(rows // ROWS):
-        mine = slice(k * ROWS, (k + 1) * ROWS)
-        hot = hot_ref[mine, :] if k < early else hot_rows(k)
-        out_ref[mine, :] = dot(hot, feat).astype(BF16)
-        puts.append(pltpu.make_async_copy(out_ref.at[pl.ds(k * ROWS, ROWS)], out_hbm.at[pl.ds(k * ROWS, ROWS)], out_sems.at[k]))
+    for k in range(rows // size):
+        if k > 0:
+            build(k)
+        mine = slice(k * size, (k + 1) * size)
+        out_ref[mine, :] = dot(hot_ref[mine, :], feat).astype(BF16)
+        part = pl.ds(k * size, size)
+        puts.append(pltpu.make_async_copy(out_ref.at[part], out_hbm.at[part], out_sems.at[k]))
         puts[k].start()
     for put in puts:
         put.wait()
 
 
-def build_body(cnt_ref, tgt_ref, vals_ref, own_ref, rim_ref, at_ref, a_ref):
+def build_body(cnt_ref, tgt_ref, vals_ref, rim_ref, both_ref, a_ref):
     blocks, slots = vals_ref.shape[:2]
     spare = blocks + 2 * RIM
     a_ref[...] = jnp.zeros_like(a_ref)
-    at_ref[...] = jnp.zeros_like(at_ref)
+    both_ref[...] = jnp.zeros_like(both_ref)
     for c in range(blocks):
         mine = slice(c * ROWS, (c + 1) * ROWS)
         for s in range(slots):
@@ -98,9 +104,9 @@
             value = vals_ref[c, s].astype(F32)
             a_ref[at, :, mine] = (a_ref[at, :, mine].astype(F32) + value).astype(BF16)
             lanes = pl.ds(pl.multiple_of(at * ROWS, ROWS), ROWS)
-            at_ref[mine, lanes] = (at_ref[mine, lanes].astype(F32) + jnp.transpose(value)).astype(BF16)
-    own_ref[...] = a_ref[:blocks]
+            both_ref[mine, lanes] = (both_ref[mine, lanes].astype(F32) + jnp.transpose(value)).astype(BF16)
     rim_ref[...] = a_ref[blocks:spare]
+    both_ref[:, (spare + 1) * ROWS :] = a_ref[:blocks].reshape(blocks * ROWS, blocks * ROWS)
 
 
 def chosen(first, second):
@@ -111,10 +117,8 @@
 def message_body(nodes_ref, a_ref, w_edge_ref, near_ref, far_ref, msg_ref):
     rows = nodes_ref.shape[0]
     rim = RIM * ROWS
-    for k in range(rows // rim):
-        mine = slice(k * rim, (k + 1) * rim)
-        pre = dot(nodes_ref[mine, :], w_edge_ref[...])
-        msg_ref[mine, :] = (pre * jax.nn.sigmoid(pre)).astype(BF16)
+    pre = dot(nodes_ref[...], w_edge_ref[...])
+    msg_ref[...] = (pre * jax.nn.sigmoid(pre)).astype(BF16)
     sums = dot(a_ref[...].reshape(2 * rim, rows), msg_ref[...])
     near, far = chosen(sums[:rim], sums[rim:])
     near_ref[...] = near.astype(BF16)
@@ -133,21 +137,16 @@
 
 
 def own_body(
-    nodes_ref, msg_ref, a_hbm, cot_ref, w_node_ref,
-    own_ref, out_ref, agg_ref, d_node_ref, d_nodes1_ref, d_agg_ref, a_ref, a_sems,
+    nodes_ref, msg_ref, adj_ref, cot_ref, w_node_ref,
+    own_ref, out_ref, agg_ref, d_node_ref, d_nodes1_ref, d_agg_ref,
 ):
     rows, width = nodes_ref.shape
     rim = RIM * ROWS
     msg = msg_ref[...]
-    loads = []
-    for k in range(rows // rim):
-        part = pl.ds(k * RIM, RIM)
-        loads.append(pltpu.make_async_copy(a_hbm.at[part], a_ref.at[part], a_sems.at[k]))
-        loads[k].start()
+    first = adj_ref.shape[1] - rows
     for k in range(rows // rim):
         mine = slice(k * rim, (k + 1) * rim)
-        loads[k].wait()
-        window = dot(a_ref[k * RIM : (k + 1) * RIM].reshape(rim, rows), msg).astype(BF16)
+        window = dot(adj_ref[mine, first:], msg).astype(BF16)
         if k == 0:
             own_ref[:rim, :] = window
         elif k == rows // rim - 1:
@@ -168,20 +167,19 @@
 ):
     rows = nodes_ref.shape[0]
     rim = RIM * ROWS
-    arrived = chosen(near_in_ref[...].astype(F32), far_in_ref[...].astype(F32))
-    rims = []
-    for k in range(2):
-        mine = slice(k * (rows - rim), k * (rows - rim) + rim)
-        here = slice(k * rim, (k + 1) * rim)
-        agg = (own_ref[here, :].astype(F32) + arrived[k]).astype(BF16)
-        agg_ref[here, :] = agg
-        out, d_node, d_nodes1, d_agg = node_step(nodes_ref[mine, :], agg, cot_ref[mine, :], w_node_ref[...])
-        out_ref[here, :] = out
-        d_node_ref[here, :] = d_node
-        d_nodes1_ref[here, :] = d_nodes1
-        d_agg_ref[here, :] = d_agg
-        rims.append(d_agg)
-    near_ref[...], far_ref[...] = chosen(rims[0], rims[1])
+    arrived = jnp.concatenate(chosen(near_in_ref[...].astype(F32), far_in_ref[...].astype(F32)), axis=0)
+
+    def ends(ref):
+        return jnp.concatenate([ref[:rim, :], ref[rows - rim :, :]], axis=0)
+
+    agg = (own_ref[...].astype(F32) + arrived).astype(BF16)
+    agg_ref[...] = agg
+    out, d_node, d_nodes1, d_agg = node_step(ends(nodes_ref), agg, ends(cot_ref), w_node_ref[...])
+    out_ref[...] = out
+    d_node_ref[...] = d_node
+    d_nodes1_ref[...] = d_nodes1
+    d_agg_ref[...] = d_agg
+    near_ref[...], far_ref[...] = chosen(d_agg[:rim], d_agg[rim:])
 
 
 def in_order(mid_ref, rim_ref):
@@ -223,32 +221,22 @@
 
 def edge_body(
     scale, nodes_ref, at_ref, near_ref, far_ref, d_msg_ref, slope_ref, mid_ref, rim_ref, w_edge_ref,
-    back_hbm, g_edge_ref, d_edge_ref, back_ref, sems,
+    back_hbm, g_edge_ref, d_edge_ref, back_ref, sem,
 ):
     rows, width = nodes_ref.shape
     rim = RIM * ROWS
     prev, after = chosen(near_ref[...], far_ref[...])
     rims = jnp.concatenate([prev, after], axis=0)
     w_edge = w_edge_ref[...]
-    puts = []
-    for k in range(rows // rim):
-        mine = slice(k * rim, (k + 1) * rim)
-        d_msg = d_msg_ref[mine, :] + dot(at_ref[mine, rows : rows + 2 * rim], rims)
-        d_edge = (d_msg.astype(BF16).astype(F32) * slope_ref[mine, :]).astype(BF16)
-        d_edge_ref[mine, :] = d_edge
-        if k == 0:
-            d_nodes1 = rim_ref[:rim, :]
-        elif k == rows // rim - 1:
-            d_nodes1 = rim_ref[rim:, :]
-        else:
-            d_nodes1 = mid_ref[(k - 1) * rim : k * rim, :]
-        back_ref[mine, :] = (d_nodes1 + dot(d_edge, w_edge, ((1,), (1,)))).astype(BF16)
-        part = pl.ds(k * rim, rim)
-        puts.append(pltpu.make_async_copy(back_ref.at[part], back_hbm.at[part], sems.at[k]))
-        puts[k].start()
+    d_msg = d_msg_ref[...] + dot(at_ref[:, rows : rows + 2 * rim], rims)
+    d_edge = (d_msg.astype(BF16).astype(F32) * slope_ref[...]).astype(BF16)
+    d_edge_ref[...] = d_edge
+    d_nodes = in_order(mid_ref, rim_ref) + dot(d_edge, w_edge, ((1,), (1,)))
+    back_ref[...] = d_nodes.astype(BF16)
+    put = pltpu.make_async_copy(back_ref, back_hbm, sem)
+    put.start()
     g_edge_ref[...] = dot(nodes_ref[...], d_edge_ref[...], ((0,), (0,))) * scale
-    for put in puts:
-        put.wait()
+    put.wait()
 
 
 def bit_of(mask):
@@ -395,13 +383,14 @@
     row = lax.broadcasted_iota(jnp.int32, (ROWS, rows), 0)
     low = jnp.where(jnp.broadcast_to(order % ROWS, (ROWS, rows)) == row, 1.0, 0.0).astype(BF16)
     zero = jnp.zeros((ROWS, rows), BF16)
-    for k in range(rows // ROWS):
-        mine = slice(k * ROWS, (k + 1) * ROWS)
-        hot = jnp.where(high == k, low, zero)
-        out_ref[mine, :] = dot(hot, back).astype(BF16)
-
-
-def shards(features, send_order, adj_count, adj_target, adj_vals, w_edge, w_node, cotangent):
+    size = TALL * ROWS
+    for k in range(rows // size):
+        mine = slice(k * size, (k + 1) * size)
+        hot = [jnp.where(high == b, low, zero) for b in range(k * TALL, (k + 1) * TALL)]
+        out_ref[mine, :] = dot(jnp.concatenate(hot, axis=0), back).astype(BF16)
+
+
+def shards(features, send_order, adj_count, adjarget, adj_vals, w_edge, w_node, cotangent):
     ndp = lax.axis_size("dp")
     ndom = lax.axis_size("dom")
     rows, width = features.shape[1:]
@@ -425,11 +414,11 @@
         [
             pltpu.VMEM((1, rows), jnp.int32),
             pltpu.VMEM((rows, width), BF16),
-            pltpu.VMEM((2 * ROWS, rows), BF16),
+            pltpu.VMEM((rows, rows), BF16),
             pltpu.VMEM((rows, width), BF16),
             pltpu.SemaphoreType.DMA,
             pltpu.SemaphoreType.DMA,
-            pltpu.SemaphoreType.DMA((blocks,)),
+            pltpu.SemaphoreType.DMA((blocks // TALL,)),
         ],
         flops=2 * rows * rows * width,
         nbytes=2 * unit,
@@ -440,10 +429,10 @@
         picked.reshape(ndom, per_peer, width), "dom", split_axis=0, concat_axis=0, tiled=True
     ).reshape(rows, width)
     spots = blocks + 2 * RIM + 1
-    adj, adj_rim, adj_t = call(
+    adj_rim, adj = call(
         build_body,
-        [shape(blocks, ROWS, rows), shape(2 * RIM, ROWS, rows), shape(rows, spots * ROWS)],
-        (adj_count, adj_target, adj_vals),
+        [shape(2 * RIM, ROWS, rows), shape(rows, spots * ROWS + rows)],
+        (adj_count, adjarget, adj_vals),
         [SMEM, SMEM, VMEM],
         [pltpu.VMEM((spots, ROWS, rows), BF16)],
         nbytes=16 * unit,
@@ -462,8 +451,6 @@
         own_body,
         [rims, mid, mid, mid, shape(*mid.shape, dtype=F32), mid],
         (nodes, msg, adj, cot, w_node),
-        [VMEM, VMEM, ANY, VMEM, VMEM],
-        [pltpu.VMEM((blocks, ROWS, rows), BF16), pltpu.SemaphoreType.DMA((rows // rim,))],
         flops=2 * rows * rows * width + 2 * square,
         nbytes=8 * unit,
     )
@@ -492,18 +479,18 @@
     node_out, d_msg, slope = call(
         behind_body,
         [tall, tall_f, tall_f],
-        (nodes, adj_t, w_edge, out_mid, out_rim, d_agg_mid, d_agg_rim),
+        (nodes, adj, w_edge, out_mid, out_rim, d_agg_mid, d_agg_rim),
         flops=2 * rows * rows * width + square,
         nbytes=8 * unit,
     )
     back, edge_part = call(
         functools.partial(edge_body, scale),
         [tall, shape(width, width, dtype=F32)],
-        (nodes, adj_t, near, far, d_msg, slope, d_nodes1_mid, d_nodes1_rim, w_edge),
+        (nodes, adj, near, far, d_msg, slope, d_nodes1_mid, d_nodes1_rim, w_edge),
         scratch=[
             pltpu.VMEM((rows, width), BF16),
             pltpu.VMEM((rows, width), BF16),
-            pltpu.SemaphoreType.DMA((rows // rim,)),
+            pltpu.SemaphoreType.DMA,
         ],
         out_specs=[ANY, VMEM],
         flops=2 * square + 4 * rim * rows * width,

time: 76.3 us -> 76.2 us (level)
  local copies, waits for them, and re-layouts: 6.56 us -> 8.53 us
  waiting for transfers between devices: 22.5 us -> 21 us
    unnamed x21, local copies, waits for them, and re-layouts: 6.56 us -> 8.53 us
    ppermute x2, waiting for transfers between devices: 2.34 us -> 0.94 us  [swapped_across(): lax.ppermute(x, axis, [(i, (i + 1 if i % 2 else i - 1) % peers) for i in...]
  transfers between devices with their start and end apart: 15 -> 15, of which waited for: 11 -> 11; matrix products, arithmetic and copies ran while one was open for 1% -> 1% of each run, Pallas kernels for 15% -> 13%
where the time goes in v6:
time: 76.2 us; the launch traced here: 75.8 us
  starting transfers between devices  30.1 us (40%)
  waiting for transfers between devices  21 us (28%)
  Pallas kernels  15.3 us (20%)
  local copies, waits for them, and re-layouts  8.53 us (11%)
  between operations  0.81 us (1%)
    pallas_call x15, Pallas kernels, call(): pl.pallas_call(body, out_shape=outs, in_specs=specs or [VMEM] * len(args)...  13.7 us
    ppermute x10, waiting for transfers between devices, swapped(): return lax.ppermute(x, axis, [(i, i ^ mask) for i in range(peers)])  13 us
    ppermute x10, starting transfers between devices, swapped(): return lax.ppermute(x, axis, [(i, i ^ mask) for i in range(peers)])  10.5 us
    unnamed x21, local copies, waits for them, and re-layouts  8.53 us
    all_to_all x1, starting transfers between devices, shards(): lax.all_to_all(picked.reshape(ndom, per_peer, width), 'dom', split_axis=0...  7.4 us
    all_to_all x1, waiting for transfers between devices, shards(): lax.all_to_all(picked.reshape(ndom, per_peer, width), 'dom', split_axis=0...  6.86 us
    ppermute x2, starting transfers between devices, swapped_across(): lax.ppermute(x, axis, [(i, (i + 1 if i % 2 else i - 1) % peers) for i in...  5.64 us
    all_to_all x1, starting transfers between devices, shards(): lax.all_to_all(back.reshape(ndom, per_peer, width), 'dom', split_axis=0,...  4.15 us
  transfers between devices with their start and end apart: 15, of which 11 were waited for; matrix products, arithmetic and copies ran while one was open for 1% of the time, Pallas kernels for 13%

profile of v6, /device:TPU:0, one launch (start us, length us, event | category | flops | bytes accessed | tf_op | source)
XLA Modules:
  0.0 75.8 jit_solution(13324600860448322759)
XLA Ops:
  0.6 0.0 copy-start.6
  0.6 0.0 copy-start.3
  0.7 2.6 %shard_map.111 = bf16[1024,256]{1,0:T(8,128)(2,1)} custom-call(s32[1,1024]{1,0:T(1,128)} %order_ref.1, bf16[1024,256]{1,0:T(8,128)(2,1)} %bitcast.18), custom_call_target="tpu_custom_call" | custom-call | flops 536870912 | bytes 1048576 | tf_op jit(solution)/shard_map/pallas_call | solution.py:42
  3.3 7.4 %all-to-all-start = ((bf16[16,64,256]{2,1,0:T(8,128)(2,1)}), bf16[16,64,256]{2,1,0:T(8,128)(2,1)S(1)}, u32[]{:S(2)}, u32[]{:S(2)}) async-start(bf16[16,64,256]{2,1,0:T(8,128)(2,1)} %bitcast.17), calls=%async_computation | async-start | bytes 1048576 | tf_op jit(solution)/shard_map/all_to_all | solution.py:428
  10.7 0.8 %copy.14.tgt_ref = s32[8,4]{1,0:T(8,128)S(1)} copy(s32[8,4]{0,1:T(4,128)} %param.11) | data formatting | bytes 256 | tf_op args[3]
  11.5 0.0 copy-start.7
  11.5 1.2 %copy-done.7 = bf16[8,4,128,128]{3,2,1,0:T(8,128)(2,1)S(1)} copy-done((bf16[8,4,128,128]{3,2,1,0:T(8,128)(2,1)S(1)}, bf16[8,4,128,128]{3,2,1,0:T(8,128)(2,1)}, u32[]{:S(2)}) %copy-start.7) | copy-done | bytes 1048600
  12.7 0.0 copy-start.8
  12.7 0.7 copy-done.8
  13.3 2.5 %shard_map.112 = (bf16[4,128,1024]{2,1,0:T(8,128)(2,1)S(1)}, bf16[1024,2688]{1,0:T(8,128)(2,1)S(1)}) custom-call(s32[8]{0:T(128)S(1)} %copy-done.8, s32[8,4]{1,0:T(8,128)S(1)} %copy.14.tgt_ref, bf16[8,4,128,128]{3,2,1,0:T(8,128)(2,1)S(1)} %copy-done.7), custom_call_target="tpu_custom_call" | custom-call | bytes 8388608 | tf_op jit(solution)/shard_map/pallas_call | solution.py:42
  15.9 0.0 copy-start
  15.9 2.4 %copy-done = bf16[1024,2688]{1,0:T(8,128)(2,1)} copy-done((bf16[1024,2688]{1,0:T(8,128)(2,1)}, bf16[1024,2688]{1,0:T(8,128)(2,1)S(1)}, u32[]{:S(2)}) %copy-start) | copy-done | bytes 5505048
  18.3 6.9 %all-to-all-done = bf16[16,64,256]{2,1,0:T(8,128)(2,1)S(1)} async-done(((bf16[16,64,256]{2,1,0:T(8,128)(2,1)}), bf16[16,64,256]{2,1,0:T(8,128)(2,1)S(1)}, u32[]{:S(2)}, u32[]{:S(2)}) %all-to-all-start) | async-done | bytes 524320 | tf_op jit(solution)/shard_map/all_to_all | solution.py:428
  25.2 0.0 copy-start.4
  25.2 0.9 %copy-done.4 = bf16[256,256]{1,0:T(8,128)(2,1)S(1)} copy-done((bf16[256,256]{1,0:T(8,128)(2,1)S(1)}, bf16[256,256]{1,0:T(8,128)(2,1)}, u32[]{:S(2)}) %copy-start.4) | copy-done | bytes 131096
  26.1 0.0 copy-start.5
  26.1 0.8 %shard_map.113 = (bf16[256,256]{1,0:T(8,128)(2,1)S(1)}, bf16[256,256]{1,0:T(8,128)(2,1)S(1)}, bf16[1024,256]{1,0:T(8,128)(2,1)S(1)}) custom-call(bf16[1024,256]{1,0:T(8,128)(2,1)S(1)} %bitcast.8, bf16[4,128,1024]{2,1,0:T(8,128)(2,1)S(1)} %get-tuple-element.42.a_ref, bf16[256,256]{1,0:T(8,128)(2,1)S(1)} %copy-done.4), custom_call_target="tpu_custom_call" | custom-call | flops 402653184 | bytes 2097152 | tf_op jit(solution)/shard_map/pallas_call | solution.py:42
  26.9 0.1 collective-permute-start
  27.0 2.8 %collective-permute-start.1 = (bf16[256,256]{1,0:T(8,128)(2,1)S(1)}, bf16[256,256]{1,0:T(8,128)(2,1)S(1)}, u32[]{:S(2)}, u32[]{:S(2)}) collective-permute-start(bf16[256,256]{1,0:T(8,128)(2,1)S(1)} %get-tuple-element.47), channel_id=1, source_target_pairs={{0,15},{1,2},{2,1},{3,4},{4,3},{5,6},{6,5},{7,8},{8,7},{9,10},{10,... | collective-permute-start | bytes 393224 | tf_op jit(solution)/shard_map/ppermute | solution.py:30
  29.8 0.0 copy-done.6
  29.8 0.0 copy-done.3
  29.8 0.0 copy-start.1
  29.8 2.6 %copy-done.1 = bf16[1024,2688]{1,0:T(8,128)(2,1)S(1)} copy-done((bf16[1024,2688]{1,0:T(8,128)(2,1)S(1)}, bf16[1024,2688]{1,0:T(8,128)(2,1)}, u32[]{:S(2)}) %copy-start.1) | copy-done | bytes 5505048
  32.4 0.0 copy-start.2
  32.4 1.5 %shard_map.114 = (bf16[512,256]{1,0:T(8,128)(2,1)S(1)}, bf16[512,256]{1,0:T(8,128)(2,1)S(1)}, bf16[512,256]{1,0:T(8,128)(2,1)S(1)}, bf16[512,256]{1,0:T(8,128)(2...) custom-call(bf16[1024,256]{1,0:T(8,128)(2,1)S(1)} %bitcast.9, ...), custom_call_target="tpu_custom_call" | custom-call | flops 805306368 | bytes 4194304 | tf_op jit(solution)/shard_map/pallas_call | solution.py:42
  33.9 0.0 collective-permute-done.near_in_ref
  33.9 0.3 collective-permute-done.1.far_in_ref
  34.1 0.8 %shard_map.115 = (bf16[256,256]{1,0:T(8,128)(2,1)S(1)}, bf16[256,256]{1,0:T(8,128)(2,1)S(1)}, bf16[512,256]{1,0:T(8,128)(2,1)S(1)}, bf16[512,256]{1,0:T(8,128)(2...) custom-call(bf16[1024,256]{1,0:T(8,128)(2,1)S(1)} %bitcast.10, ...), custom_call_target="tpu_custom_call" | custom-call | flops 268435456 | bytes 2097152 | tf_op jit(solution)/shard_map/pallas_call | solution.py:42
  34.9 0.1 collective-permute-start.2
  35.0 2.8 %collective-permute-start.3 = (bf16[256,256]{1,0:T(8,128)(2,1)S(1)}, bf16[256,256]{1,0:T(8,128)(2,1)S(1)}, u32[]{:S(2)}, u32[]{:S(2)}) collective-permute-start(bf16[256,256]{1,0:T(8,128)(2,1)S(1)} %get-tuple-element.53), channel_id=1, source_target_pairs={{0,15},{1,2},{2,1},{3,4},{4,3},{5,6},{6,5},{7,8},{8,7},{9,10},{10,... | collective-permute-start | bytes 393224 | tf_op jit(solution)/shard_map/ppermute | solution.py:30
  37.8 0.5 shard_map.118
  38.3 1.6 %collective-permute-start.4 = (bf16[512,128]{1,0:T(8,128)(2,1)S(1)}, bf16[512,128]{1,0:T(8,128)(2,1)S(1)}, u32[]{:S(2)}, u32[]{:S(2)}) collective-permute-start(bf16[512,128]{1,0:T(8,128)(2,1)S(1)} %get-tuple-element.65), channel_id=1, source_target_pairs={{0,16},{16,0},{1,17},{17,1},{2,18},{18,2},{3,19},{19,3},{4,20},{20... | collective-permute-start | bytes 393224 | tf_op jit(solution)/shard_map/ppermute | solution.py:25
  39.9 0.0 copy-done.5
  39.9 0.0 copy-done.2
  39.9 1.6 %shard_map.116 = (bf16[1024,256]{1,0:T(8,128)(2,1)}, f32[1024,256]{1,0:T(8,128)S(1)}, f32[1024,256]{1,0:T(8,128)S(1)}) custom-call(bf16[1024,256]{1,0:T(8,128)(2,1)S(1)} %bitcast.12, bf16[1024,2688]{1,0:T(8,128)(2,1)S(1)} %copy-done.2, bf16[256,256]{1,0:T(8,128)(2,1)S(1)} %copy-done.5, bf16[512,256]{1,0:T(8,128)(2,1)S(1)} %get-tuple-element.44.out_mid_ref, ...), custom_call_target="tpu_custom_call" | custom-call | flops 671088640 | bytes 4194304 | tf_op jit(solution)/shard_map/pallas_call | solution.py:42
  41.5 0.0 collective-permute-done.2.near_ref
  41.5 0.7 collective-permute-done.3.far_ref
  42.2 0.0 copy-start.9
  42.2 1.6 %shard_map.117 = (bf16[1024,256]{1,0:T(8,128)(2,1)}, f32[256,256]{1,0:T(8,128)S(1)}) custom-call(bf16[1024,256]{1,0:T(8,128)(2,1)S(1)} %bitcast.13, bf16[1024,2688]{1,0:T(8,128)(2,1)S(1)} %copy-done.2, bf16[256,256]{1,0:T(8,128)(2,1)S(1)} %collective-permute-done.2.near_ref, bf16[256,256]{1,0:T(8,128)(2,1)S(1)} %collective-permute-done.3.far_ref, ...), custom_call_target="tpu_custom_call" | custom-call | flops 536870912 | bytes 4194304 | tf_op jit(solution)/shard_map/pallas_call | solution.py:42
  43.8 0.0 collective-permute-done.4.node_in_ref
  43.8 4.1 %all-to-all-start.1 = ((bf16[16,64,256]{2,1,0:T(8,128)(2,1)}), bf16[16,64,256]{2,1,0:T(8,128)(2,1)S(1)}, u32[]{:S(2)}, u32[]{:S(2)}) async-start(bf16[16,64,256]{2,1,0:T(8,128)(2,1)} %bitcast.5), calls=%async_computation.1 | async-start | bytes 1048576 | tf_op jit(solution)/shard_map/all_to_all | solution.py:502
  48.0 0.1 shard_map.119
  48.1 0.5 collective-permute-start.5
  48.5 1.0 %collective-permute-done.5.in_ref = bf16[512,128]{1,0:T(8,128)(2,1)S(1)} collective-permute-done((bf16[512,128]{1,0:T(8,128)(2,1)S(1)}, bf16[512,128]{1,0:T(8,128)(2,1)S(1)}, u32[]{:S(2)}, u32[]{:S(2)}) %collective-permute-start.5) | collective-permute-done | bytes 131104 | tf_op jit(solution)/shard_map/ppermute | solution.py:25
  49.6 1.9 %collective-permute-start.6 = (bf16[256,128]{1,0:T(8,128)(2,1)S(1)}, bf16[256,128]{1,0:T(8,128)(2,1)S(1)}, u32[]{:S(2)}, u32[]{:S(2)}) collective-permute-start(bf16[256,128]{1,0:T(8,128)(2,1)S(1)} %get-tuple-element.70), channel_id=1, source_target_pairs={{0,2},{1,3},{2,0},{3,1},{4,6},{5,7},{6,4},{7,5},{8,10},{9,11},{10,... | collective-permute-start | bytes 196616 | tf_op jit(solution)/shard_map/ppermute | solution.py:25
  51.5 4.1 %collective-permute-done.6.in_ref = bf16[256,128]{1,0:T(8,128)(2,1)S(1)} collective-permute-done((bf16[256,128]{1,0:T(8,128)(2,1)S(1)}, bf16[256,128]{1,0:T(8,128)(2,1)S(1)}, u32[]{:S(2)}, u32[]{:S(2)}) %collective-permute-start.6) | collective-permute-done | bytes 65568 | tf_op jit(solution)/shard_map/ppermute | solution.py:25
  55.6 1.9 %collective-permute-start.7 = (bf16[256,128]{1,0:T(8,128)(2,1)S(1)}, bf16[256,128]{1,0:T(8,128)(2,1)S(1)}, u32[]{:S(2)}, u32[]{:S(2)}) collective-permute-start(bf16[256,128]{1,0:T(8,128)(2,1)S(1)} %shard_map.121.mine_ref), channel_id=1, source_target_pairs={{0,4},{1,5},{2,6},{3,7},{4,0},{5,1},{6,2},{7,3},{8,12},{9,13},{10,... | collective-permute-start | bytes 196616 | tf_op jit(solution)/shard_map/ppermute | solution.py:25
  57.5 2.7 %collective-permute-done.7.in_ref = bf16[256,128]{1,0:T(8,128)(2,1)S(1)} collective-permute-done((bf16[256,128]{1,0:T(8,128)(2,1)S(1)}, bf16[256,128]{1,0:T(8,128)(2,1)S(1)}, u32[]{:S(2)}, u32[]{:S(2)}) %collective-permute-start.7) | collective-permute-done | bytes 65568 | tf_op jit(solution)/shard_map/ppermute | solution.py:25
  60.3 3.3 %collective-permute-start.8 = (bf16[256,128]{1,0:T(8,128)(2,1)S(1)}, bf16[256,128]{1,0:T(8,128)(2,1)S(1)}, u32[]{:S(2)}, u32[]{:S(2)}) collective-permute-start(bf16[256,128]{1,0:T(8,128)(2,1)S(1)} %shard_map.122.mine_ref), channel_id=1, source_target_pairs={{0,8},{1,9},{2,10},{3,11},{4,12},{5,13},{6,14},{7,15},{8,0},{9,1},... | collective-permute-start | bytes 196616 | tf_op jit(solution)/shard_map/ppermute | solution.py:25
  63.6 2.5 %collective-permute-done.8.in_ref = bf16[256,128]{1,0:T(8,128)(2,1)S(1)} collective-permute-done((bf16[256,128]{1,0:T(8,128)(2,1)S(1)}, bf16[256,128]{1,0:T(8,128)(2,1)S(1)}, u32[]{:S(2)}, u32[]{:S(2)}) %collective-permute-start.8) | collective-permute-done | bytes 65568 | tf_op jit(solution)/shard_map/ppermute | solution.py:25
  66.1 2.5 %collective-permute-start.11 = (bf16[256,128]{1,0:T(8,128)(2,1)S(1)}, bf16[256,128]{1,0:T(8,128)(2,1)S(1)}, u32[]{:S(2)}, u32[]{:S(2)}) collective-permute-start(bf16[256,128]{1,0:T(8,128)(2,1)S(1)} %shard_map.123.mine_ref), channel_id=1, source_target_pairs={{0,18},{1,19},{2,16},{3,17},{4,22},{5,23},{6,20},{7,21},{8,26},{9,... | collective-permute-start | bytes 196616 | tf_op jit(solution)/shard_map/ppermute | solution.py:335
  68.6 0.6 collective-permute-start.10
  69.1 0.5 collective-permute-start.9
  69.7 0.0 all-to-all-done.1
  69.7 0.0 copy-done.9
  69.7 1.5 %shard_map.124 = bf16[1024,256]{1,0:T(8,128)(2,1)} custom-call(s32[1,1024]{1,0:T(1,128)S(1)} %copy-done.9, bf16[1024,256]{1,0:T(8,128)(2,1)S(1)} %bitcast.16), custom_call_target="tpu_custom_call" | custom-call | flops 536870912 | bytes 1048576 | tf_op jit(solution)/shard_map/pallas_call | solution.py:42
  71.2 0.2 collective-permute-done.11.both_ref
  71.4 1.4 %collective-permute-done.10.y_ref = bf16[256,128]{1,0:T(8,128)(2,1)S(1)} collective-permute-done((bf16[256,128]{1,0:T(8,128)(2,1)S(1)}, bf16[256,128]{1,0:T(8,128)(2,1)S(1)}, u32[]{:S(2)}, u32[]{:S(2)}) %collective-permute-start.10) | collective-permute-done | bytes 65568 | tf_op jit(solution)/shard_map/ppermute | solution.py:25
  72.8 0.6 collective-permute-done.9.dp_ref
  73.4 0.1 shard_map.125.refs_0_
  73.5 0.1 collective-permute-start.12
  73.6 0.8 %shard_map.126 = (f32[256,256]{1,0:T(8,128)}, f32[512,256]{1,0:T(8,128)}) custom-call(bf16[384,256]{1,0:T(8,128)(2,1)S(1)} %shard_map.125.refs_0_), custom_call_target="tpu_custom_call" | custom-call | bytes 786432 | tf_op jit(solution)/shard_map/pallas_call | solution.py:316
  74.3 0.6 collective-permute-done.12.refs_0_
  75.0 0.8 %shard_map.127 = (f32[256,256]{1,0:T(8,128)}, f32[512,256]{1,0:T(8,128)}) custom-call(bf16[384,256]{1,0:T(8,128)(2,1)S(1)} %collective-permute-done.12.refs_0_, f32[256,256]{1,0:T(8,128)} %get-tuple-element.74.refs_1_, f32[512,256]{1,0:T(8,128)} %get-tuple-element.75.refs_2_), custom_call_target="tpu_custom_call", output_to_operand_aliasing={{0}: (1, {}), {1}: (2, {})} | custom-call | bytes 786432 | tf_op jit(solution)/shard_map/pallas_call | solution.py:316
  (4 shorter events, 0.1 us)
Async XLA Ops:
  0.6 29.2 %copy-start.6 = (bf16[512,256]{1,0:T(8,128)(2,1)S(1)}, bf16[512,256]{1,0:T(8,128)(2,1)}, u32[]{:S(2)}) copy-start(bf16[512,256]{1,0:T(8,128)(2,1)} %w_node_ref.3) | copy-start | bytes 786436
  0.6 29.2 %copy-start.3 = (bf16[1,1024,256]{2,1,0:T(8,128)(2,1)S(1)}, bf16[1,1024,256]{2,1,0:T(8,128)(2,1)}, u32[]{:S(2)}) copy-start(bf16[1,1024,256]{2,1,0:T(8,128)(2,1)} %param.15) | copy-start | bytes 1572868
  3.3 21.9 %all-to-all-start = ((bf16[16,64,256]{2,1,0:T(8,128)(2,1)}), bf16[16,64,256]{2,1,0:T(8,128)(2,1)S(1)}, u32[]{:S(2)}, u32[]{:S(2)}) async-start(bf16[16,64,256]{2,1,0:T(8,128)(2,1)} %bitcast.17), calls=%async_computation | async-start | bytes 1048576 | tf_op jit(solution)/shard_map/all_to_all | solution.py:428
  11.5 1.2 %copy-start.7 = (bf16[8,4,128,128]{3,2,1,0:T(8,128)(2,1)S(1)}, bf16[8,4,128,128]{3,2,1,0:T(8,128)(2,1)}, u32[]{:S(2)}) copy-start(bf16[8,4,128,128]{3,2,1,0:T(8,128)(2,1)} %vals_ref.1) | copy-start | bytes 3145732
  12.7 0.7 copy-start.8
  15.9 2.4 %copy-start = (bf16[1024,2688]{1,0:T(8,128)(2,1)}, bf16[1024,2688]{1,0:T(8,128)(2,1)S(1)}, u32[]{:S(2)}) copy-start(bf16[1024,2688]{1,0:T(8,128)(2,1)S(1)} %get-tuple-element.41.adj_ref.at_ref) | copy-start | bytes 16515076
  25.2 0.9 %copy-start.4 = (bf16[256,256]{1,0:T(8,128)(2,1)S(1)}, bf16[256,256]{1,0:T(8,128)(2,1)}, u32[]{:S(2)}) copy-start(bf16[256,256]{1,0:T(8,128)(2,1)} %w_edge_ref.5) | copy-start | bytes 393220
  26.1 13.8 %copy-start.5 = (bf16[256,256]{1,0:T(8,128)(2,1)S(1)}, bf16[256,256]{1,0:T(8,128)(2,1)}, u32[]{:S(2)}) copy-start(bf16[256,256]{1,0:T(8,128)(2,1)} %w_edge_ref.5) | copy-start | bytes 393220
  26.9 6.9 %collective-permute-start = (bf16[256,256]{1,0:T(8,128)(2,1)S(1)}, bf16[256,256]{1,0:T(8,128)(2,1)S(1)}, u32[]{:S(2)}, u32[]{:S(2)}) collective-permute-start(bf16[256,256]{1,0:T(8,128)(2,1)S(1)} %get-tuple-element.46), channel_id=1, source_target_pairs={{0,1},{1,0},{2,3},{3,2},{4,5},{5,4},{6,7},{7,6},{8,9},{9,8},{10,11... | collective-permute-start | bytes 393224 | tf_op jit(solution)/shard_map/ppermute | solution.py:25
  27.0 7.2 %collective-permute-start.1 = (bf16[256,256]{1,0:T(8,128)(2,1)S(1)}, bf16[256,256]{1,0:T(8,128)(2,1)S(1)}, u32[]{:S(2)}, u32[]{:S(2)}) collective-permute-start(bf16[256,256]{1,0:T(8,128)(2,1)S(1)} %get-tuple-element.47), channel_id=1, source_target_pairs={{0,15},{1,2},{2,1},{3,4},{4,3},{5,6},{6,5},{7,8},{8,7},{9,10},{10,... | collective-permute-start | bytes 393224 | tf_op jit(solution)/shard_map/ppermute | solution.py:30
  29.8 2.6 %copy-start.1 = (bf16[1024,2688]{1,0:T(8,128)(2,1)S(1)}, bf16[1024,2688]{1,0:T(8,128)(2,1)}, u32[]{:S(2)}) copy-start(bf16[1024,2688]{1,0:T(8,128)(2,1)} %copy-done) | copy-start | bytes 16515076
  32.4 7.5 %copy-start.2 = (bf16[1024,2688]{1,0:T(8,128)(2,1)S(1)}, bf16[1024,2688]{1,0:T(8,128)(2,1)}, u32[]{:S(2)}) copy-start(bf16[1024,2688]{1,0:T(8,128)(2,1)} %copy-done) | copy-start | bytes 16515076
  34.9 6.6 %collective-permute-start.2 = (bf16[256,256]{1,0:T(8,128)(2,1)S(1)}, bf16[256,256]{1,0:T(8,128)(2,1)S(1)}, u32[]{:S(2)}, u32[]{:S(2)}) collective-permute-start(bf16[256,256]{1,0:T(8,128)(2,1)S(1)} %get-tuple-element.52), channel_id=1, source_target_pairs={{0,1},{1,0},{2,3},{3,2},{4,5},{5,4},{6,7},{7,6},{8,9},{9,8},{10,11... | collective-permute-start | bytes 393224 | tf_op jit(solution)/shard_map/ppermute | solution.py:25
  35.0 7.2 %collective-permute-start.3 = (bf16[256,256]{1,0:T(8,128)(2,1)S(1)}, bf16[256,256]{1,0:T(8,128)(2,1)S(1)}, u32[]{:S(2)}, u32[]{:S(2)}) collective-permute-start(bf16[256,256]{1,0:T(8,128)(2,1)S(1)} %get-tuple-element.53), channel_id=1, source_target_pairs={{0,15},{1,2},{2,1},{3,4},{4,3},{5,6},{6,5},{7,8},{8,7},{9,10},{10,... | collective-permute-start | bytes 393224 | tf_op jit(solution)/shard_map/ppermute | solution.py:30
  38.3 5.5 %collective-permute-start.4 = (bf16[512,128]{1,0:T(8,128)(2,1)S(1)}, bf16[512,128]{1,0:T(8,128)(2,1)S(1)}, u32[]{:S(2)}, u32[]{:S(2)}) collective-permute-start(bf16[512,128]{1,0:T(8,128)(2,1)S(1)} %get-tuple-element.65), channel_id=1, source_target_pairs={{0,16},{16,0},{1,17},{17,1},{2,18},{18,2},{3,19},{19,3},{4,20},{20... | collective-permute-start | bytes 393224 | tf_op jit(solution)/shard_map/ppermute | solution.py:25
  42.2 27.5 %copy-start.9 = (s32[1,1024]{1,0:T(1,128)S(1)}, s32[1,1024]{1,0:T(1,128)}, u32[]{:S(2)}) copy-start(s32[1,1024]{1,0:T(1,128)} %order_ref.1) | copy-start | bytes 12292
  43.8 25.9 %all-to-all-start.1 = ((bf16[16,64,256]{2,1,0:T(8,128)(2,1)}), bf16[16,64,256]{2,1,0:T(8,128)(2,1)S(1)}, u32[]{:S(2)}, u32[]{:S(2)}) async-start(bf16[16,64,256]{2,1,0:T(8,128)(2,1)} %bitcast.5), calls=%async_computation.1 | async-start | bytes 1048576 | tf_op jit(solution)/shard_map/all_to_all | solution.py:502
  48.1 1.5 %collective-permute-start.5 = (bf16[512,128]{1,0:T(8,128)(2,1)S(1)}, bf16[512,128]{1,0:T(8,128)(2,1)S(1)}, u32[]{:S(2)}, u32[]{:S(2)}) collective-permute-start(bf16[512,128]{1,0:T(8,128)(2,1)S(1)} %get-tuple-element.68), channel_id=1, source_target_pairs={{0,1},{1,0},{2,3},{3,2},{4,5},{5,4},{6,7},{7,6},{8,9},{9,8},{10,11... | collective-permute-start | bytes 393224 | tf_op jit(solution)/shard_map/ppermute | solution.py:25
  49.6 6.0 %collective-permute-start.6 = (bf16[256,128]{1,0:T(8,128)(2,1)S(1)}, bf16[256,128]{1,0:T(8,128)(2,1)S(1)}, u32[]{:S(2)}, u32[]{:S(2)}) collective-permute-start(bf16[256,128]{1,0:T(8,128)(2,1)S(1)} %get-tuple-element.70), channel_id=1, source_target_pairs={{0,2},{1,3},{2,0},{3,1},{4,6},{5,7},{6,4},{7,5},{8,10},{9,11},{10,... | collective-permute-start | bytes 196616 | tf_op jit(solution)/shard_map/ppermute | solution.py:25
  55.6 4.6 %collective-permute-start.7 = (bf16[256,128]{1,0:T(8,128)(2,1)S(1)}, bf16[256,128]{1,0:T(8,128)(2,1)S(1)}, u32[]{:S(2)}, u32[]{:S(2)}) collective-permute-start(bf16[256,128]{1,0:T(8,128)(2,1)S(1)} %shard_map.121.mine_ref), channel_id=1, source_target_pairs={{0,4},{1,5},{2,6},{3,7},{4,0},{5,1},{6,2},{7,3},{8,12},{9,13},{10,... | collective-permute-start | bytes 196616 | tf_op jit(solution)/shard_map/ppermute | solution.py:25
  60.3 5.8 %collective-permute-start.8 = (bf16[256,128]{1,0:T(8,128)(2,1)S(1)}, bf16[256,128]{1,0:T(8,128)(2,1)S(1)}, u32[]{:S(2)}, u32[]{:S(2)}) collective-permute-start(bf16[256,128]{1,0:T(8,128)(2,1)S(1)} %shard_map.122.mine_ref), channel_id=1, source_target_pairs={{0,8},{1,9},{2,10},{3,11},{4,12},{5,13},{6,14},{7,15},{8,0},{9,1},... | collective-permute-start | bytes 196616 | tf_op jit(solution)/shard_map/ppermute | solution.py:25
  66.1 5.3 %collective-permute-start.11 = (bf16[256,128]{1,0:T(8,128)(2,1)S(1)}, bf16[256,128]{1,0:T(8,128)(2,1)S(1)}, u32[]{:S(2)}, u32[]{:S(2)}) collective-permute-start(bf16[256,128]{1,0:T(8,128)(2,1)S(1)} %shard_map.123.mine_ref), channel_id=1, source_target_pairs={{0,18},{1,19},{2,16},{3,17},{4,22},{5,23},{6,20},{7,21},{8,26},{9,... | collective-permute-start | bytes 196616 | tf_op jit(solution)/shard_map/ppermute | solution.py:335
  68.6 4.3 %collective-permute-start.10 = (bf16[256,128]{1,0:T(8,128)(2,1)S(1)}, bf16[256,128]{1,0:T(8,128)(2,1)S(1)}, u32[]{:S(2)}, u32[]{:S(2)}) collective-permute-start(bf16[256,128]{1,0:T(8,128)(2,1)S(1)} %shard_map.123.mine_ref), channel_id=1, source_target_pairs={{0,2},{1,3},{2,0},{3,1},{4,6},{5,7},{6,4},{7,5},{8,10},{9,11},{10,... | collective-permute-start | bytes 196616 | tf_op jit(solution)/shard_map/ppermute | solution.py:25
  69.1 4.3 %collective-permute-start.9 = (bf16[256,128]{1,0:T(8,128)(2,1)S(1)}, bf16[256,128]{1,0:T(8,128)(2,1)S(1)}, u32[]{:S(2)}, u32[]{:S(2)}) collective-permute-start(bf16[256,128]{1,0:T(8,128)(2,1)S(1)} %shard_map.123.mine_ref), channel_id=1, source_target_pairs={{0,16},{16,0},{1,17},{17,1},{2,18},{18,2},{3,19},{19,3},{4,20},{20... | collective-permute-start | bytes 196616 | tf_op jit(solution)/shard_map/ppermute | solution.py:25
  73.5 1.5 %collective-permute-start.12 = (bf16[384,256]{1,0:T(8,128)(2,1)S(1)}, bf16[384,256]{1,0:T(8,128)(2,1)S(1)}, u32[]{:S(2)}, u32[]{:S(2)}) collective-permute-start(bf16[384,256]{1,0:T(8,128)(2,1)S(1)} %shard_map.125.refs_0_), channel_id=1, source_target_pairs={{0,1},{1,0},{2,3},{3,2},{4,5},{5,4},{6,7},{7,6},{8,9},{9,8},{10,11... | collective-permute-start | bytes 589832 | tf_op jit(solution)/shard_map/ppermute | solution.py:25

commit v7 on v5

--- a/solution.py
+++ b/solution.py
@@ -84,11 +84,11 @@
         put.wait()
 
 
-def build_body(cnt_ref, tgt_ref, vals_ref, own_ref, rim_ref, at_ref, a_ref):
+def build_body(cnt_ref, tgt_ref, vals_ref, w_edge_ref, rim_ref, both_ref, a_ref):
     blocks, slots = vals_ref.shape[:2]
     spare = blocks + 2 * RIM
     a_ref[...] = jnp.zeros_like(a_ref)
-    at_ref[...] = jnp.zeros_like(at_ref)
+    both_ref[...] = jnp.zeros_like(both_ref)
     for c in range(blocks):
         mine = slice(c * ROWS, (c + 1) * ROWS)
         for s in range(slots):
@@ -98,9 +98,11 @@
             value = vals_ref[c, s].astype(F32)
             a_ref[at, :, mine] = (a_ref[at, :, mine].astype(F32) + value).astype(BF16)
             lanes = pl.ds(pl.multiple_of(at * ROWS, ROWS), ROWS)
-            at_ref[mine, lanes] = (at_ref[mine, lanes].astype(F32) + jnp.transpose(value)).astype(BF16)
-    own_ref[...] = a_ref[:blocks]
-    rim_ref[...] = a_ref[blocks:spare]
+            both_ref[mine, lanes] = (both_ref[mine, lanes].astype(F32) + jnp.transpose(value)).astype(BF16)
+    width = w_edge_ref.shape[0]
+    rim_ref[: 2 * RIM * ROWS, :] = a_ref[blocks:spare].reshape(2 * RIM * ROWS, blocks * ROWS)
+    rim_ref[2 * RIM * ROWS :, :width] = w_edge_ref[...]
+    both_ref[:, (spare + 1) * ROWS :] = a_ref[:blocks].reshape(blocks * ROWS, blocks * ROWS)
 
 
 def chosen(first, second):
@@ -108,14 +110,15 @@
     return jnp.where(odd, first, second), jnp.where(odd, second, first)
 
 
-def message_body(nodes_ref, a_ref, w_edge_ref, near_ref, far_ref, msg_ref):
-    rows = nodes_ref.shape[0]
-    rim = RIM * ROWS
+def message_body(nodes_ref, a_ref, near_ref, far_ref, msg_ref):
+    rows, width = nodes_ref.shape
+    rim = RIM * ROWS
+    w_edge = a_ref[2 * rim :, :width]
     for k in range(rows // rim):
         mine = slice(k * rim, (k + 1) * rim)
-        pre = dot(nodes_ref[mine, :], w_edge_ref[...])
+        pre = dot(nodes_ref[mine, :], w_edge)
         msg_ref[mine, :] = (pre * jax.nn.sigmoid(pre)).astype(BF16)
-    sums = dot(a_ref[...].reshape(2 * rim, rows), msg_ref[...])
+    sums = dot(a_ref[: 2 * rim, :], msg_ref[...])
     near, far = chosen(sums[:rim], sums[rim:])
     near_ref[...] = near.astype(BF16)
     far_ref[...] = far.astype(BF16)
@@ -133,21 +136,16 @@
 
 
 def own_body(
-    nodes_ref, msg_ref, a_hbm, cot_ref, w_node_ref,
-    own_ref, out_ref, agg_ref, d_node_ref, d_nodes1_ref, d_agg_ref, a_ref, a_sems,
+    nodes_ref, msg_ref, adj_ref, cot_ref, w_node_ref,
+    own_ref, out_ref, agg_ref, d_node_ref, d_nodes1_ref, d_agg_ref,
 ):
     rows, width = nodes_ref.shape
     rim = RIM * ROWS
     msg = msg_ref[...]
-    loads = []
-    for k in range(rows // rim):
-        part = pl.ds(k * RIM, RIM)
-        loads.append(pltpu.make_async_copy(a_hbm.at[part], a_ref.at[part], a_sems.at[k]))
-        loads[k].start()
+    first = adj_ref.shape[1] - rows
     for k in range(rows // rim):
         mine = slice(k * rim, (k + 1) * rim)
-        loads[k].wait()
-        window = dot(a_ref[k * RIM : (k + 1) * RIM].reshape(rim, rows), msg).astype(BF16)
+        window = dot(adj_ref[mine, first:], msg).astype(BF16)
         if k == 0:
             own_ref[:rim, :] = window
         elif k == rows // rim - 1:
@@ -440,20 +438,16 @@
         picked.reshape(ndom, per_peer, width), "dom", split_axis=0, concat_axis=0, tiled=True
     ).reshape(rows, width)
     spots = blocks + 2 * RIM + 1
-    adj, adj_rim, adj_t = call(
+    adj_rim, adj = call(
         build_body,
-        [shape(blocks, ROWS, rows), shape(2 * RIM, ROWS, rows), shape(rows, spots * ROWS)],
-        (adj_count, adj_target, adj_vals),
-        [SMEM, SMEM, VMEM],
+        [shape(2 * rim + width, rows), shape(rows, spots * ROWS + rows)],
+        (adj_count, adj_target, adj_vals, w_edge),
+        [SMEM, SMEM, VMEM, VMEM],
         [pltpu.VMEM((spots, ROWS, rows), BF16)],
         nbytes=16 * unit,
     )
     near, far, msg = call(
-        message_body,
-        [edge, edge, tall],
-        (nodes, adj_rim, w_edge),
-        flops=square + 4 * rim * rows * width,
-        nbytes=4 * unit,
+        message_body, [edge, edge, tall], (nodes, adj_rim), flops=square + 4 * rim * rows * width, nbytes=4 * unit
     )
     far = swapped_across(far, "dom")
     near = swapped(near, "dom", 1)
@@ -462,8 +456,6 @@
         own_body,
         [rims, mid, mid, mid, shape(*mid.shape, dtype=F32), mid],
         (nodes, msg, adj, cot, w_node),
-        [VMEM, VMEM, ANY, VMEM, VMEM],
-        [pltpu.VMEM((blocks, ROWS, rows), BF16), pltpu.SemaphoreType.DMA((rows // rim,))],
         flops=2 * rows * rows * width + 2 * square,
         nbytes=8 * unit,
     )
@@ -492,14 +484,14 @@
     node_out, d_msg, slope = call(
         behind_body,
         [tall, tall_f, tall_f],
-        (nodes, adj_t, w_edge, out_mid, out_rim, d_agg_mid, d_agg_rim),
+        (nodes, adj, w_edge, out_mid, out_rim, d_agg_mid, d_agg_rim),
         flops=2 * rows * rows * width + square,
         nbytes=8 * unit,
     )
     back, edge_part = call(
         functools.partial(edge_body, scale),
         [tall, shape(width, width, dtype=F32)],
-        (nodes, adj_t, near, far, d_msg, slope, d_nodes1_mid, d_nodes1_rim, w_edge),
+        (nodes, adj, near, far, d_msg, slope, d_nodes1_mid, d_nodes1_rim, w_edge),
         scratch=[
             pltpu.VMEM((rows, width), BF16),
             pltpu.VMEM((rows, width), BF16),

time: 76.3 us -> 75.1 us (0.984)
  waiting for transfers between devices: 22.5 us -> 20.1 us
  local copies, waits for them, and re-layouts: 6.56 us -> 8.53 us
  Pallas kernels: 15.9 us -> 15 us
    unnamed x21, local copies, waits for them, and re-layouts: 6.56 us -> 8.53 us
    ppermute x2, waiting for transfers between devices: 2.34 us -> 0.92 us  [swapped_across(): lax.ppermute(x, axis, [(i, (i + 1 if i % 2 else i - 1) % peers) for i in...]
    all_to_all x1, waiting for transfers between devices: 6.89 us -> 5.94 us  [shards(): lax.all_to_all(picked.reshape(ndom, per_peer, width), 'dom', split_axis=0...]
    pallas_call x15, Pallas kernels: 14.4 us -> 13.5 us  [call(): pl.pallas_call(body, out_shape=outs, in_specs=specs or [VMEM] * len(args)...]
  transfers between devices with their start and end apart: 15 -> 15, of which waited for: 11 -> 11; matrix products, arithmetic and copies ran while one was open for 1% -> 1% of each run, Pallas kernels for 15% -> 14%
where the time goes in v7:
time: 75.1 us; the launch traced here: 74.6 us
  starting transfers between devices  30.1 us (40%)
  waiting for transfers between devices  20.1 us (27%)
  Pallas kernels  15 us (20%)
  local copies, waits for them, and re-layouts  8.53 us (11%)
  between operations  0.81 us (1%)
    pallas_call x15, Pallas kernels, call(): pl.pallas_call(body, out_shape=outs, in_specs=specs or [VMEM] * len(args)...  13.5 us
    ppermute x10, waiting for transfers between devices, swapped(): return lax.ppermute(x, axis, [(i, i ^ mask) for i in range(peers)])  13 us
    ppermute x10, starting transfers between devices, swapped(): return lax.ppermute(x, axis, [(i, i ^ mask) for i in range(peers)])  10.5 us
    unnamed x21, local copies, waits for them, and re-layouts  8.53 us
    all_to_all x1, starting transfers between devices, shards(): lax.all_to_all(picked.reshape(ndom, per_peer, width), 'dom', split_axis=0...  7.39 us
    all_to_all x1, waiting for transfers between devices, shards(): lax.all_to_all(picked.reshape(ndom, per_peer, width), 'dom', split_axis=0...  5.94 us
    ppermute x2, starting transfers between devices, swapped_across(): lax.ppermute(x, axis, [(i, (i + 1 if i % 2 else i - 1) % peers) for i in...  5.64 us
    all_to_all x1, starting transfers between devices, shards(): lax.all_to_all(back.reshape(ndom, per_peer, width), 'dom', split_axis=0,...  4.15 us
  transfers between devices with their start and end apart: 15, of which 11 were waited for; matrix products, arithmetic and copies ran while one was open for 1% of the time, Pallas kernels for 14%

profile of v7, /device:TPU:0, one launch (start us, length us, event | category | flops | bytes accessed | tf_op | source)
XLA Modules:
  0.0 74.6 jit_solution(3269538941565843660)
XLA Ops:
  0.6 0.0 copy-start.6
  0.6 0.0 copy-start.3
  0.7 2.6 %shard_map.111 = bf16[1024,256]{1,0:T(8,128)(2,1)} custom-call(s32[1,1024]{1,0:T(1,128)} %order_ref.1, bf16[1024,256]{1,0:T(8,128)(2,1)} %bitcast.18), custom_call_target="tpu_custom_call" | custom-call | flops 536870912 | bytes 1048576 | tf_op jit(solution)/shard_map/pallas_call | solution.py:41
  3.3 7.4 %all-to-all-start = ((bf16[16,64,256]{2,1,0:T(8,128)(2,1)}), bf16[16,64,256]{2,1,0:T(8,128)(2,1)S(1)}, u32[]{:S(2)}, u32[]{:S(2)}) async-start(bf16[16,64,256]{2,1,0:T(8,128)(2,1)} %bitcast.17), calls=%async_computation | async-start | bytes 1048576 | tf_op jit(solution)/shard_map/all_to_all | solution.py:437
  10.7 0.8 %copy.14.tgt_ref = s32[8,4]{1,0:T(8,128)S(1)} copy(s32[8,4]{0,1:T(4,128)} %param.11) | data formatting | bytes 256 | tf_op args[3]
  11.4 0.0 copy-start.4
  11.4 0.9 %copy-done.4 = bf16[256,256]{1,0:T(8,128)(2,1)S(1)} copy-done((bf16[256,256]{1,0:T(8,128)(2,1)S(1)}, bf16[256,256]{1,0:T(8,128)(2,1)}, u32[]{:S(2)}) %copy-start.4) | copy-done | bytes 131096
  12.3 0.0 copy-start.7
  12.3 1.2 %copy-done.7 = bf16[8,4,128,128]{3,2,1,0:T(8,128)(2,1)S(1)} copy-done((bf16[8,4,128,128]{3,2,1,0:T(8,128)(2,1)S(1)}, bf16[8,4,128,128]{3,2,1,0:T(8,128)(2,1)}, u32[]{:S(2)}) %copy-start.7) | copy-done | bytes 1048600
  13.5 0.0 copy-start.8
  13.5 0.7 copy-done.8
  14.2 2.6 %shard_map.112 = (bf16[768,1024]{1,0:T(8,128)(2,1)S(1)}, bf16[1024,2688]{1,0:T(8,128)(2,1)S(1)}) custom-call(s32[8]{0:T(128)S(1)} %copy-done.8, s32[8,4]{1,0:T(8,128)S(1)} %copy.14.tgt_ref, bf16[8,4,128,128]{3,2,1,0:T(8,128)(2,1)S(1)} %copy-done.7, bf16[256,256]{1,0:T(8,128)(2,1)S(1)} %copy-done.4), custom_call_target="tpu_custom_call" | custom-call | bytes 8388608 | tf_op jit(solution)/shard_map/pallas_call | solution.py:41
  16.8 0.0 copy-start
  16.8 2.4 %copy-done = bf16[1024,2688]{1,0:T(8,128)(2,1)} copy-done((bf16[1024,2688]{1,0:T(8,128)(2,1)}, bf16[1024,2688]{1,0:T(8,128)(2,1)S(1)}, u32[]{:S(2)}) %copy-start) | copy-done | bytes 5505048
  19.2 5.9 %all-to-all-done = bf16[16,64,256]{2,1,0:T(8,128)(2,1)S(1)} async-done(((bf16[16,64,256]{2,1,0:T(8,128)(2,1)}), bf16[16,64,256]{2,1,0:T(8,128)(2,1)S(1)}, u32[]{:S(2)}, u32[]{:S(2)}) %all-to-all-start) | async-done | bytes 524320 | tf_op jit(solution)/shard_map/all_to_all | solution.py:437
  25.1 0.0 copy-start.5
  25.1 0.7 shard_map.113
  25.8 0.1 collective-permute-start
  25.9 2.8 %collective-permute-start.1 = (bf16[256,256]{1,0:T(8,128)(2,1)S(1)}, bf16[256,256]{1,0:T(8,128)(2,1)S(1)}, u32[]{:S(2)}, u32[]{:S(2)}) collective-permute-start(bf16[256,256]{1,0:T(8,128)(2,1)S(1)} %get-tuple-element.47), channel_id=1, source_target_pairs={{0,15},{1,2},{2,1},{3,4},{4,3},{5,6},{6,5},{7,8},{8,7},{9,10},{10,... | collective-permute-start | bytes 393224 | tf_op jit(solution)/shard_map/ppermute | solution.py:29
  28.7 0.0 copy-done.6
  28.7 0.0 copy-done.3
  28.7 0.0 copy-start.1
  28.7 2.6 %copy-done.1 = bf16[1024,2688]{1,0:T(8,128)(2,1)S(1)} copy-done((bf16[1024,2688]{1,0:T(8,128)(2,1)S(1)}, bf16[1024,2688]{1,0:T(8,128)(2,1)}, u32[]{:S(2)}) %copy-start.1) | copy-done | bytes 5505048
  31.3 0.0 copy-start.2
  31.3 1.5 %shard_map.114 = (bf16[512,256]{1,0:T(8,128)(2,1)S(1)}, bf16[512,256]{1,0:T(8,128)(2,1)S(1)}, bf16[512,256]{1,0:T(8,128)(2,1)S(1)}, bf16[512,256]{1,0:T(8,128)(2...) custom-call(bf16[1024,256]{1,0:T(8,128)(2,1)S(1)} %bitcast.9, ...), custom_call_target="tpu_custom_call" | custom-call | flops 805306368 | bytes 4194304 | tf_op jit(solution)/shard_map/pallas_call | solution.py:41
  32.8 0.0 collective-permute-done.near_in_ref
  32.8 0.3 collective-permute-done.1.far_in_ref
  33.1 0.7 shard_map.115
  33.7 0.1 collective-permute-start.2
  33.8 2.8 %collective-permute-start.3 = (bf16[256,256]{1,0:T(8,128)(2,1)S(1)}, bf16[256,256]{1,0:T(8,128)(2,1)S(1)}, u32[]{:S(2)}, u32[]{:S(2)}) collective-permute-start(bf16[256,256]{1,0:T(8,128)(2,1)S(1)} %get-tuple-element.53), channel_id=1, source_target_pairs={{0,15},{1,2},{2,1},{3,4},{4,3},{5,6},{6,5},{7,8},{8,7},{9,10},{10,... | collective-permute-start | bytes 393224 | tf_op jit(solution)/shard_map/ppermute | solution.py:29
  36.6 0.5 shard_map.118
  37.1 1.6 %collective-permute-start.4 = (bf16[512,128]{1,0:T(8,128)(2,1)S(1)}, bf16[512,128]{1,0:T(8,128)(2,1)S(1)}, u32[]{:S(2)}, u32[]{:S(2)}) collective-permute-start(bf16[512,128]{1,0:T(8,128)(2,1)S(1)} %get-tuple-element.65), channel_id=1, source_target_pairs={{0,16},{16,0},{1,17},{17,1},{2,18},{18,2},{3,19},{19,3},{4,20},{20... | collective-permute-start | bytes 393224 | tf_op jit(solution)/shard_map/ppermute | solution.py:24
  38.7 0.0 copy-done.5
  38.7 0.0 copy-done.2
  38.7 1.6 %shard_map.116 = (bf16[1024,256]{1,0:T(8,128)(2,1)}, f32[1024,256]{1,0:T(8,128)S(1)}, f32[1024,256]{1,0:T(8,128)S(1)}) custom-call(bf16[1024,256]{1,0:T(8,128)(2,1)S(1)} %bitcast.12, bf16[1024,2688]{1,0:T(8,128)(2,1)S(1)} %copy-done.2, bf16[256,256]{1,0:T(8,128)(2,1)S(1)} %copy-done.5, bf16[512,256]{1,0:T(8,128)(2,1)S(1)} %get-tuple-element.44.out_mid_ref, ...), custom_call_target="tpu_custom_call" | custom-call | flops 671088640 | bytes 4194304 | tf_op jit(solution)/shard_map/pallas_call | solution.py:41
  40.3 0.0 collective-permute-done.2.near_ref
  40.3 0.6 collective-permute-done.3.far_ref
  41.0 0.0 copy-start.9
  41.0 1.7 %shard_map.117 = (bf16[1024,256]{1,0:T(8,128)(2,1)}, f32[256,256]{1,0:T(8,128)S(1)}) custom-call(bf16[1024,256]{1,0:T(8,128)(2,1)S(1)} %bitcast.13, bf16[1024,2688]{1,0:T(8,128)(2,1)S(1)} %copy-done.2, bf16[256,256]{1,0:T(8,128)(2,1)S(1)} %collective-permute-done.2.near_ref, bf16[256,256]{1,0:T(8,128)(2,1)S(1)} %collective-permute-done.3.far_ref, ...), custom_call_target="tpu_custom_call" | custom-call | flops 536870912 | bytes 4194304 | tf_op jit(solution)/shard_map/pallas_call | solution.py:41
  42.6 0.0 collective-permute-done.4.node_in_ref
  42.6 4.2 %all-to-all-start.1 = ((bf16[16,64,256]{2,1,0:T(8,128)(2,1)}), bf16[16,64,256]{2,1,0:T(8,128)(2,1)S(1)}, u32[]{:S(2)}, u32[]{:S(2)}) async-start(bf16[16,64,256]{2,1,0:T(8,128)(2,1)} %bitcast.5), calls=%async_computation.1 | async-start | bytes 1048576 | tf_op jit(solution)/shard_map/all_to_all | solution.py:507
  46.8 0.1 shard_map.119
  46.9 0.5 collective-permute-start.5
  47.4 1.0 %collective-permute-done.5.in_ref = bf16[512,128]{1,0:T(8,128)(2,1)S(1)} collective-permute-done((bf16[512,128]{1,0:T(8,128)(2,1)S(1)}, bf16[512,128]{1,0:T(8,128)(2,1)S(1)}, u32[]{:S(2)}, u32[]{:S(2)}) %collective-permute-start.5) | collective-permute-done | bytes 131104 | tf_op jit(solution)/shard_map/ppermute | solution.py:24
  48.4 1.9 %collective-permute-start.6 = (bf16[256,128]{1,0:T(8,128)(2,1)S(1)}, bf16[256,128]{1,0:T(8,128)(2,1)S(1)}, u32[]{:S(2)}, u32[]{:S(2)}) collective-permute-start(bf16[256,128]{1,0:T(8,128)(2,1)S(1)} %get-tuple-element.70), channel_id=1, source_target_pairs={{0,2},{1,3},{2,0},{3,1},{4,6},{5,7},{6,4},{7,5},{8,10},{9,11},{10,... | collective-permute-start | bytes 196616 | tf_op jit(solution)/shard_map/ppermute | solution.py:24
  50.3 4.1 %collective-permute-done.6.in_ref = bf16[256,128]{1,0:T(8,128)(2,1)S(1)} collective-permute-done((bf16[256,128]{1,0:T(8,128)(2,1)S(1)}, bf16[256,128]{1,0:T(8,128)(2,1)S(1)}, u32[]{:S(2)}, u32[]{:S(2)}) %collective-permute-start.6) | collective-permute-done | bytes 65568 | tf_op jit(solution)/shard_map/ppermute | solution.py:24
  54.5 1.9 %collective-permute-start.7 = (bf16[256,128]{1,0:T(8,128)(2,1)S(1)}, bf16[256,128]{1,0:T(8,128)(2,1)S(1)}, u32[]{:S(2)}, u32[]{:S(2)}) collective-permute-start(bf16[256,128]{1,0:T(8,128)(2,1)S(1)} %shard_map.121.mine_ref), channel_id=1, source_target_pairs={{0,4},{1,5},{2,6},{3,7},{4,0},{5,1},{6,2},{7,3},{8,12},{9,13},{10,... | collective-permute-start | bytes 196616 | tf_op jit(solution)/shard_map/ppermute | solution.py:24
  56.3 2.7 %collective-permute-done.7.in_ref = bf16[256,128]{1,0:T(8,128)(2,1)S(1)} collective-permute-done((bf16[256,128]{1,0:T(8,128)(2,1)S(1)}, bf16[256,128]{1,0:T(8,128)(2,1)S(1)}, u32[]{:S(2)}, u32[]{:S(2)}) %collective-permute-start.7) | collective-permute-done | bytes 65568 | tf_op jit(solution)/shard_map/ppermute | solution.py:24
  59.1 3.3 %collective-permute-start.8 = (bf16[256,128]{1,0:T(8,128)(2,1)S(1)}, bf16[256,128]{1,0:T(8,128)(2,1)S(1)}, u32[]{:S(2)}, u32[]{:S(2)}) collective-permute-start(bf16[256,128]{1,0:T(8,128)(2,1)S(1)} %shard_map.122.mine_ref), channel_id=1, source_target_pairs={{0,8},{1,9},{2,10},{3,11},{4,12},{5,13},{6,14},{7,15},{8,0},{9,1},... | collective-permute-start | bytes 196616 | tf_op jit(solution)/shard_map/ppermute | solution.py:24
  62.4 2.5 %collective-permute-done.8.in_ref = bf16[256,128]{1,0:T(8,128)(2,1)S(1)} collective-permute-done((bf16[256,128]{1,0:T(8,128)(2,1)S(1)}, bf16[256,128]{1,0:T(8,128)(2,1)S(1)}, u32[]{:S(2)}, u32[]{:S(2)}) %collective-permute-start.8) | collective-permute-done | bytes 65568 | tf_op jit(solution)/shard_map/ppermute | solution.py:24
  65.0 2.5 %collective-permute-start.11 = (bf16[256,128]{1,0:T(8,128)(2,1)S(1)}, bf16[256,128]{1,0:T(8,128)(2,1)S(1)}, u32[]{:S(2)}, u32[]{:S(2)}) collective-permute-start(bf16[256,128]{1,0:T(8,128)(2,1)S(1)} %shard_map.123.mine_ref), channel_id=1, source_target_pairs={{0,18},{1,19},{2,16},{3,17},{4,22},{5,23},{6,20},{7,21},{8,26},{9,... | collective-permute-start | bytes 196616 | tf_op jit(solution)/shard_map/ppermute | solution.py:345
  67.4 0.6 collective-permute-start.10
  68.0 0.5 collective-permute-start.9
  68.5 0.0 all-to-all-done.1
  68.5 0.0 copy-done.9
  68.5 1.5 %shard_map.124 = bf16[1024,256]{1,0:T(8,128)(2,1)} custom-call(s32[1,1024]{1,0:T(1,128)S(1)} %copy-done.9, bf16[1024,256]{1,0:T(8,128)(2,1)S(1)} %bitcast.16), custom_call_target="tpu_custom_call" | custom-call | flops 536870912 | bytes 1048576 | tf_op jit(solution)/shard_map/pallas_call | solution.py:41
  70.0 0.2 collective-permute-done.11.both_ref
  70.3 1.4 %collective-permute-done.10.y_ref = bf16[256,128]{1,0:T(8,128)(2,1)S(1)} collective-permute-done((bf16[256,128]{1,0:T(8,128)(2,1)S(1)}, bf16[256,128]{1,0:T(8,128)(2,1)S(1)}, u32[]{:S(2)}, u32[]{:S(2)}) %collective-permute-start.10) | collective-permute-done | bytes 65568 | tf_op jit(solution)/shard_map/ppermute | solution.py:24
  71.7 0.6 collective-permute-done.9.dp_ref
  72.2 0.1 shard_map.125.refs_0_
  72.3 0.1 collective-permute-start.12
  72.4 0.8 %shard_map.126 = (f32[256,256]{1,0:T(8,128)}, f32[512,256]{1,0:T(8,128)}) custom-call(bf16[384,256]{1,0:T(8,128)(2,1)S(1)} %shard_map.125.refs_0_), custom_call_target="tpu_custom_call" | custom-call | bytes 786432 | tf_op jit(solution)/shard_map/pallas_call | solution.py:326
  73.2 0.6 collective-permute-done.12.refs_0_
  73.8 0.8 %shard_map.127 = (f32[256,256]{1,0:T(8,128)}, f32[512,256]{1,0:T(8,128)}) custom-call(bf16[384,256]{1,0:T(8,128)(2,1)S(1)} %collective-permute-done.12.refs_0_, f32[256,256]{1,0:T(8,128)} %get-tuple-element.74.refs_1_, f32[512,256]{1,0:T(8,128)} %get-tuple-element.75.refs_2_), custom_call_target="tpu_custom_call", output_to_operand_aliasing={{0}: (1, {}), {1}: (2, {})} | custom-call | bytes 786432 | tf_op jit(solution)/shard_map/pallas_call | solution.py:326
  (4 shorter events, 0.1 us)
Async XLA Ops:
  0.6 28.1 %copy-start.6 = (bf16[512,256]{1,0:T(8,128)(2,1)S(1)}, bf16[512,256]{1,0:T(8,128)(2,1)}, u32[]{:S(2)}) copy-start(bf16[512,256]{1,0:T(8,128)(2,1)} %w_node_ref.3) | copy-start | bytes 786436
  0.6 28.1 %copy-start.3 = (bf16[1,1024,256]{2,1,0:T(8,128)(2,1)S(1)}, bf16[1,1024,256]{2,1,0:T(8,128)(2,1)}, u32[]{:S(2)}) copy-start(bf16[1,1024,256]{2,1,0:T(8,128)(2,1)} %param.15) | copy-start | bytes 1572868
  3.3 21.9 %all-to-all-start = ((bf16[16,64,256]{2,1,0:T(8,128)(2,1)}), bf16[16,64,256]{2,1,0:T(8,128)(2,1)S(1)}, u32[]{:S(2)}, u32[]{:S(2)}) async-start(bf16[16,64,256]{2,1,0:T(8,128)(2,1)} %bitcast.17), calls=%async_computation | async-start | bytes 1048576 | tf_op jit(solution)/shard_map/all_to_all | solution.py:437
  11.4 0.9 %copy-start.4 = (bf16[256,256]{1,0:T(8,128)(2,1)S(1)}, bf16[256,256]{1,0:T(8,128)(2,1)}, u32[]{:S(2)}) copy-start(bf16[256,256]{1,0:T(8,128)(2,1)} %w_edge_ref.5) | copy-start | bytes 393220
  12.3 1.2 %copy-start.7 = (bf16[8,4,128,128]{3,2,1,0:T(8,128)(2,1)S(1)}, bf16[8,4,128,128]{3,2,1,0:T(8,128)(2,1)}, u32[]{:S(2)}) copy-start(bf16[8,4,128,128]{3,2,1,0:T(8,128)(2,1)} %vals_ref.1) | copy-start | bytes 3145732
  13.5 0.7 copy-start.8
  16.8 2.4 %copy-start = (bf16[1024,2688]{1,0:T(8,128)(2,1)}, bf16[1024,2688]{1,0:T(8,128)(2,1)S(1)}, u32[]{:S(2)}) copy-start(bf16[1024,2688]{1,0:T(8,128)(2,1)S(1)} %get-tuple-element.41.adj_ref.at_ref) | copy-start | bytes 16515076
  25.1 13.6 %copy-start.5 = (bf16[256,256]{1,0:T(8,128)(2,1)S(1)}, bf16[256,256]{1,0:T(8,128)(2,1)}, u32[]{:S(2)}) copy-start(bf16[256,256]{1,0:T(8,128)(2,1)} %w_edge_ref.5) | copy-start | bytes 393220
  25.8 7.0 %collective-permute-start = (bf16[256,256]{1,0:T(8,128)(2,1)S(1)}, bf16[256,256]{1,0:T(8,128)(2,1)S(1)}, u32[]{:S(2)}, u32[]{:S(2)}) collective-permute-start(bf16[256,256]{1,0:T(8,128)(2,1)S(1)} %get-tuple-element.46), channel_id=1, source_target_pairs={{0,1},{1,0},{2,3},{3,2},{4,5},{5,4},{6,7},{7,6},{8,9},{9,8},{10,11... | collective-permute-start | bytes 393224 | tf_op jit(solution)/shard_map/ppermute | solution.py:24
  25.9 7.1 %collective-permute-start.1 = (bf16[256,256]{1,0:T(8,128)(2,1)S(1)}, bf16[256,256]{1,0:T(8,128)(2,1)S(1)}, u32[]{:S(2)}, u32[]{:S(2)}) collective-permute-start(bf16[256,256]{1,0:T(8,128)(2,1)S(1)} %get-tuple-element.47), channel_id=1, source_target_pairs={{0,15},{1,2},{2,1},{3,4},{4,3},{5,6},{6,5},{7,8},{8,7},{9,10},{10,... | collective-permute-start | bytes 393224 | tf_op jit(solution)/shard_map/ppermute | solution.py:29
  28.7 2.6 %copy-start.1 = (bf16[1024,2688]{1,0:T(8,128)(2,1)S(1)}, bf16[1024,2688]{1,0:T(8,128)(2,1)}, u32[]{:S(2)}) copy-start(bf16[1024,2688]{1,0:T(8,128)(2,1)} %copy-done) | copy-start | bytes 16515076
  31.3 7.4 %copy-start.2 = (bf16[1024,2688]{1,0:T(8,128)(2,1)S(1)}, bf16[1024,2688]{1,0:T(8,128)(2,1)}, u32[]{:S(2)}) copy-start(bf16[1024,2688]{1,0:T(8,128)(2,1)} %copy-done) | copy-start | bytes 16515076
  33.7 6.6 %collective-permute-start.2 = (bf16[256,256]{1,0:T(8,128)(2,1)S(1)}, bf16[256,256]{1,0:T(8,128)(2,1)S(1)}, u32[]{:S(2)}, u32[]{:S(2)}) collective-permute-start(bf16[256,256]{1,0:T(8,128)(2,1)S(1)} %get-tuple-element.52), channel_id=1, source_target_pairs={{0,1},{1,0},{2,3},{3,2},{4,5},{5,4},{6,7},{7,6},{8,9},{9,8},{10,11... | collective-permute-start | bytes 393224 | tf_op jit(solution)/shard_map/ppermute | solution.py:24
  33.8 7.2 %collective-permute-start.3 = (bf16[256,256]{1,0:T(8,128)(2,1)S(1)}, bf16[256,256]{1,0:T(8,128)(2,1)S(1)}, u32[]{:S(2)}, u32[]{:S(2)}) collective-permute-start(bf16[256,256]{1,0:T(8,128)(2,1)S(1)} %get-tuple-element.53), channel_id=1, source_target_pairs={{0,15},{1,2},{2,1},{3,4},{4,3},{5,6},{6,5},{7,8},{8,7},{9,10},{10,... | collective-permute-start | bytes 393224 | tf_op jit(solution)/shard_map/ppermute | solution.py:29
  37.1 5.5 %collective-permute-start.4 = (bf16[512,128]{1,0:T(8,128)(2,1)S(1)}, bf16[512,128]{1,0:T(8,128)(2,1)S(1)}, u32[]{:S(2)}, u32[]{:S(2)}) collective-permute-start(bf16[512,128]{1,0:T(8,128)(2,1)S(1)} %get-tuple-element.65), channel_id=1, source_target_pairs={{0,16},{16,0},{1,17},{17,1},{2,18},{18,2},{3,19},{19,3},{4,20},{20... | collective-permute-start | bytes 393224 | tf_op jit(solution)/shard_map/ppermute | solution.py:24
  41.0 27.5 %copy-start.9 = (s32[1,1024]{1,0:T(1,128)S(1)}, s32[1,1024]{1,0:T(1,128)}, u32[]{:S(2)}) copy-start(s32[1,1024]{1,0:T(1,128)} %order_ref.1) | copy-start | bytes 12292
  42.6 25.9 %all-to-all-start.1 = ((bf16[16,64,256]{2,1,0:T(8,128)(2,1)}), bf16[16,64,256]{2,1,0:T(8,128)(2,1)S(1)}, u32[]{:S(2)}, u32[]{:S(2)}) async-start(bf16[16,64,256]{2,1,0:T(8,128)(2,1)} %bitcast.5), calls=%async_computation.1 | async-start | bytes 1048576 | tf_op jit(solution)/shard_map/all_to_all | solution.py:507
  46.9 1.5 %collective-permute-start.5 = (bf16[512,128]{1,0:T(8,128)(2,1)S(1)}, bf16[512,128]{1,0:T(8,128)(2,1)S(1)}, u32[]{:S(2)}, u32[]{:S(2)}) collective-permute-start(bf16[512,128]{1,0:T(8,128)(2,1)S(1)} %get-tuple-element.68), channel_id=1, source_target_pairs={{0,1},{1,0},{2,3},{3,2},{4,5},{5,4},{6,7},{7,6},{8,9},{9,8},{10,11... | collective-permute-start | bytes 393224 | tf_op jit(solution)/shard_map/ppermute | solution.py:24
  48.4 6.0 %collective-permute-start.6 = (bf16[256,128]{1,0:T(8,128)(2,1)S(1)}, bf16[256,128]{1,0:T(8,128)(2,1)S(1)}, u32[]{:S(2)}, u32[]{:S(2)}) collective-permute-start(bf16[256,128]{1,0:T(8,128)(2,1)S(1)} %get-tuple-element.70), channel_id=1, source_target_pairs={{0,2},{1,3},{2,0},{3,1},{4,6},{5,7},{6,4},{7,5},{8,10},{9,11},{10,... | collective-permute-start | bytes 196616 | tf_op jit(solution)/shard_map/ppermute | solution.py:24
  54.5 4.6 %collective-permute-start.7 = (bf16[256,128]{1,0:T(8,128)(2,1)S(1)}, bf16[256,128]{1,0:T(8,128)(2,1)S(1)}, u32[]{:S(2)}, u32[]{:S(2)}) collective-permute-start(bf16[256,128]{1,0:T(8,128)(2,1)S(1)} %shard_map.121.mine_ref), channel_id=1, source_target_pairs={{0,4},{1,5},{2,6},{3,7},{4,0},{5,1},{6,2},{7,3},{8,12},{9,13},{10,... | collective-permute-start | bytes 196616 | tf_op jit(solution)/shard_map/ppermute | solution.py:24
  59.1 5.8 %collective-permute-start.8 = (bf16[256,128]{1,0:T(8,128)(2,1)S(1)}, bf16[256,128]{1,0:T(8,128)(2,1)S(1)}, u32[]{:S(2)}, u32[]{:S(2)}) collective-permute-start(bf16[256,128]{1,0:T(8,128)(2,1)S(1)} %shard_map.122.mine_ref), channel_id=1, source_target_pairs={{0,8},{1,9},{2,10},{3,11},{4,12},{5,13},{6,14},{7,15},{8,0},{9,1},... | collective-permute-start | bytes 196616 | tf_op jit(solution)/shard_map/ppermute | solution.py:24
  65.0 5.3 %collective-permute-start.11 = (bf16[256,128]{1,0:T(8,128)(2,1)S(1)}, bf16[256,128]{1,0:T(8,128)(2,1)S(1)}, u32[]{:S(2)}, u32[]{:S(2)}) collective-permute-start(bf16[256,128]{1,0:T(8,128)(2,1)S(1)} %shard_map.123.mine_ref), channel_id=1, source_target_pairs={{0,18},{1,19},{2,16},{3,17},{4,22},{5,23},{6,20},{7,21},{8,26},{9,... | collective-permute-start | bytes 196616 | tf_op jit(solution)/shard_map/ppermute | solution.py:345
  67.4 4.3 %collective-permute-start.10 = (bf16[256,128]{1,0:T(8,128)(2,1)S(1)}, bf16[256,128]{1,0:T(8,128)(2,1)S(1)}, u32[]{:S(2)}, u32[]{:S(2)}) collective-permute-start(bf16[256,128]{1,0:T(8,128)(2,1)S(1)} %shard_map.123.mine_ref), channel_id=1, source_target_pairs={{0,2},{1,3},{2,0},{3,1},{4,6},{5,7},{6,4},{7,5},{8,10},{9,11},{10,... | collective-permute-start | bytes 196616 | tf_op jit(solution)/shard_map/ppermute | solution.py:24
  68.0 4.3 %collective-permute-start.9 = (bf16[256,128]{1,0:T(8,128)(2,1)S(1)}, bf16[256,128]{1,0:T(8,128)(2,1)S(1)}, u32[]{:S(2)}, u32[]{:S(2)}) collective-permute-start(bf16[256,128]{1,0:T(8,128)(2,1)S(1)} %shard_map.123.mine_ref), channel_id=1, source_target_pairs={{0,16},{16,0},{1,17},{17,1},{2,18},{18,2},{3,19},{19,3},{4,20},{20... | collective-permute-start | bytes 196616 | tf_op jit(solution)/shard_map/ppermute | solution.py:24
  72.3 1.5 %collective-permute-start.12 = (bf16[384,256]{1,0:T(8,128)(2,1)S(1)}, bf16[384,256]{1,0:T(8,128)(2,1)S(1)}, u32[]{:S(2)}, u32[]{:S(2)}) collective-permute-start(bf16[384,256]{1,0:T(8,128)(2,1)S(1)} %shard_map.125.refs_0_), channel_id=1, source_target_pairs={{0,1},{1,0},{2,3},{3,2},{4,5},{5,4},{6,7},{7,6},{8,9},{9,8},{10,11... | collective-permute-start | bytes 589832 | tf_op jit(solution)/shard_map/ppermute | solution.py:24

commit v8 on v7

--- a/solution.py
+++ b/solution.py
@@ -220,10 +220,10 @@
 
 
 def edge_body(
-    scale, nodes_ref, at_ref, near_ref, far_ref, d_msg_ref, slope_ref, mid_ref, rim_ref, w_edge_ref,
-    back_hbm, g_edge_ref, d_edge_ref, back_ref, sems,
+    at_ref, near_ref, far_ref, d_msg_ref, slope_ref, mid_ref, rim_ref, w_edge_ref,
+    back_hbm, d_edge_ref, back_ref, sems,
 ):
-    rows, width = nodes_ref.shape
+    rows, width = back_ref.shape
     rim = RIM * ROWS
     prev, after = chosen(near_ref[...], far_ref[...])
     rims = jnp.concatenate([prev, after], axis=0)
@@ -244,7 +244,6 @@
         part = pl.ds(k * rim, rim)
         puts.append(pltpu.make_async_copy(back_ref.at[part], back_hbm.at[part], sems.at[k]))
         puts[k].start()
-    g_edge_ref[...] = dot(nodes_ref[...], d_edge_ref[...], ((0,), (0,))) * scale
     for put in puts:
         put.wait()
 
@@ -260,9 +259,14 @@
     send_ref[...] = total_ref[pl.ds(pl.multiple_of((1 - bit) * size, 16), size), :].astype(BF16)
 
 
-def first_cut_body(mask, edge_ref, node_ref, node_in_ref, keep_ref, send_ref, total_ref):
+def grad_edge_body(scale, nodes_ref, d_edge_ref, out_ref):
+    out_ref[...] = dot(nodes_ref[...], d_edge_ref[...], ((0,), (0,))) * scale
+
+
+def first_cut_body(scale, mask, nodes_ref, d_edge_ref, node_ref, node_in_ref, keep_ref, send_ref, total_ref, edge_ref):
     half = node_ref.shape[1]
     few, more = edge_ref.shape[0] // 4, node_ref.shape[0] // 4
+    grad_edge_body(scale, nodes_ref, d_edge_ref, edge_ref)
     for q in range(4):
         row = q * (2 * few + more)
         mine = slice(q * more, (q + 1) * more)
@@ -345,20 +349,22 @@
     return lax.ppermute(x, ("dp", "dom"), [(i, (i + peers) % total ^ mask) for i in range(total)])
 
 
-def cut_grads(edge_part, node_part):
-    half = node_part[0].shape[1]
-    size = node_part[0].shape[0] + 2 * edge_part.shape[0]
-
-    def cut(body, mask, args, size):
+def cut_grads(scale, nodes, d_edge, node_part):
+    width = nodes.shape[1]
+    half = width // 2
+    size = node_part[0].shape[0] + 2 * width
+
+    def cut(body, args, size, *scratch):
         return call(
-            functools.partial(body, mask),
+            body,
             [shape(size // 2, half, dtype=F32), shape(size // 2, half)],
             args,
-            scratch=[pltpu.VMEM((size, half), F32)],
+            scratch=[pltpu.VMEM((size, half), F32), *scratch],
         )
 
-    keep, send = cut(first_cut_body, CORE, (edge_part, *node_part), size)
-    return cut(next_cut_body, ALONG_Y, (keep, swapped(send, "dom", CORE)), size // 2)
+    first = functools.partial(first_cut_body, scale, CORE)
+    keep, send = cut(first, (nodes, d_edge, *node_part), size, pltpu.VMEM((width, width), F32))
+    return cut(functools.partial(next_cut_body, ALONG_Y), (keep, swapped(send, "dom", CORE)), size // 2)
 
 
 def joined(keep, send, back, send_order, width):
@@ -423,7 +429,7 @@
         [
             pltpu.VMEM((1, rows), jnp.int32),
             pltpu.VMEM((rows, width), BF16),
-            pltpu.VMEM((2 * ROWS, rows), BF16),
+            pltpu.VMEM((rows // 2, rows), BF16),
             pltpu.VMEM((rows, width), BF16),
             pltpu.SemaphoreType.DMA,
             pltpu.SemaphoreType.DMA,
@@ -488,28 +494,27 @@
         flops=2 * rows * rows * width + square,
         nbytes=8 * unit,
     )
-    back, edge_part = call(
-        functools.partial(edge_body, scale),
-        [tall, shape(width, width, dtype=F32)],
-        (nodes, adj, near, far, d_msg, slope, d_nodes1_mid, d_nodes1_rim, w_edge),
-        scratch=[
-            pltpu.VMEM((rows, width), BF16),
-            pltpu.VMEM((rows, width), BF16),
-            pltpu.SemaphoreType.DMA((rows // rim,)),
-        ],
+    back, d_edge = call(
+        edge_body,
+        [tall, tall],
+        (adj, near, far, d_msg, slope, d_nodes1_mid, d_nodes1_rim, w_edge),
+        scratch=[pltpu.VMEM((rows, width), BF16), pltpu.SemaphoreType.DMA((rows // rim,))],
         out_specs=[ANY, VMEM],
         flops=2 * square + 4 * rim * rows * width,
         nbytes=8 * unit,
     )
     if tiled:
         back, node_in = lax.optimization_barrier((back, node_part[1]))
-        keep, send = cut_grads(edge_part, (node_part[0], node_in))
+        keep, send = cut_grads(scale, nodes, d_edge, (node_part[0], node_in))
     back = lax.all_to_all(
         back.reshape(ndom, per_peer, width), "dom", split_axis=0, concat_axis=0, tiled=True
     ).reshape(rows, width)
     if tiled:
         grad_edge, grad_node, grad_brick = joined(keep, send, back, send_order, width)
     else:
+        (edge_part,) = call(
+            functools.partial(grad_edge_body, scale), [shape(width, width, dtype=F32)], (nodes, d_edge), flops=square
+        )
         grad_edge, grad_node = (lax.psum(part, ("dp", "dom")) for part in (edge_part, node_part[0]))
         grad_brick = placed(send_order, back)
     return (node_out[None], grad_brick[None], grad_edge, grad_node)

time: 75.1 us -> 76.3 us (1.016)
  starting transfers between devices: 30.1 us -> 31.5 us
    ppermute x1, starting transfers between devices: 2.46 us -> 4 us  [swapped_both(): lax.ppermute(x, ('dp', 'dom'), [(i, (i + peers) % total ^ mask) for i in...]
    ppermute x10, waiting for transfers between devices: 13 us -> 12.2 us  [swapped(): return lax.ppermute(x, axis, [(i, i ^ mask) for i in range(peers)])]
  transfers between devices with their start and end apart: 15 -> 15, of which waited for: 11 -> 10; matrix products, arithmetic and copies ran while one was open for 1% -> 1% of each run, Pallas kernels for 14% -> 14%
where the time goes in v8:
time: 76.3 us; the launch traced here: 75.8 us
  starting transfers between devices  31.5 us (41%)
  waiting for transfers between devices  19.4 us (25%)
  Pallas kernels  15.6 us (20%)
  local copies, waits for them, and re-layouts  8.53 us (11%)
  between operations  0.81 us (1%)
    pallas_call x15, Pallas kernels, call(): pl.pallas_call(body, out_shape=outs, in_specs=specs or [VMEM] * len(args)...  14.1 us
    ppermute x10, waiting for transfers between devices, swapped(): return lax.ppermute(x, axis, [(i, i ^ mask) for i in range(peers)])  12.2 us
    ppermute x10, starting transfers between devices, swapped(): return lax.ppermute(x, axis, [(i, i ^ mask) for i in range(peers)])  10.3 us
    unnamed x21, local copies, waits for them, and re-layouts  8.53 us
    all_to_all x1, starting transfers between devices, shards(): lax.all_to_all(picked.reshape(ndom, per_peer, width), 'dom', split_axis=0...  7.39 us
    all_to_all x1, waiting for transfers between devices, shards(): lax.all_to_all(picked.reshape(ndom, per_peer, width), 'dom', split_axis=0...  5.94 us
    ppermute x2, starting transfers between devices, swapped_across(): lax.ppermute(x, axis, [(i, (i + 1 if i % 2 else i - 1) % peers) for i in...  5.64 us
    all_to_all x1, starting transfers between devices, shards(): lax.all_to_all(back.reshape(ndom, per_peer, width), 'dom', split_axis=0,...  4.15 us
  transfers between devices with their start and end apart: 15, of which 10 were waited for; matrix products, arithmetic and copies ran while one was open for 1% of the time, Pallas kernels for 14%

profile of v8, /device:TPU:0, one launch (start us, length us, event | category | flops | bytes accessed | tf_op | source)
XLA Modules:
  0.0 75.8 jit_solution(3348936198547901949)
XLA Ops:
  0.6 0.0 copy-start.6
  0.6 0.0 copy-start.3
  0.7 2.6 %shard_map.111 = bf16[1024,256]{1,0:T(8,128)(2,1)} custom-call(s32[1,1024]{1,0:T(1,128)} %order_ref.1, bf16[1024,256]{1,0:T(8,128)(2,1)} %bitcast.18), custom_call_target="tpu_custom_call" | custom-call | flops 536870912 | bytes 1048576 | tf_op jit(solution)/shard_map/pallas_call | solution.py:41
  3.3 7.4 %all-to-all-start = ((bf16[16,64,256]{2,1,0:T(8,128)(2,1)}), bf16[16,64,256]{2,1,0:T(8,128)(2,1)S(1)}, u32[]{:S(2)}, u32[]{:S(2)}) async-start(bf16[16,64,256]{2,1,0:T(8,128)(2,1)} %bitcast.17), calls=%async_computation | async-start | bytes 1048576 | tf_op jit(solution)/shard_map/all_to_all | solution.py:443
  10.7 0.8 %copy.14.tgt_ref = s32[8,4]{1,0:T(8,128)S(1)} copy(s32[8,4]{0,1:T(4,128)} %param.11) | data formatting | bytes 256 | tf_op args[3]
  11.4 0.0 copy-start.4
  11.4 0.9 %copy-done.4 = bf16[256,256]{1,0:T(8,128)(2,1)S(1)} copy-done((bf16[256,256]{1,0:T(8,128)(2,1)S(1)}, bf16[256,256]{1,0:T(8,128)(2,1)}, u32[]{:S(2)}) %copy-start.4) | copy-done | bytes 131096
  12.3 0.0 copy-start.7
  12.3 1.2 %copy-done.7 = bf16[8,4,128,128]{3,2,1,0:T(8,128)(2,1)S(1)} copy-done((bf16[8,4,128,128]{3,2,1,0:T(8,128)(2,1)S(1)}, bf16[8,4,128,128]{3,2,1,0:T(8,128)(2,1)}, u32[]{:S(2)}) %copy-start.7) | copy-done | bytes 1048600
  13.5 0.0 copy-start.8
  13.5 0.7 copy-done.8
  14.2 2.5 %shard_map.112 = (bf16[768,1024]{1,0:T(8,128)(2,1)S(1)}, bf16[1024,2688]{1,0:T(8,128)(2,1)S(1)}) custom-call(s32[8]{0:T(128)S(1)} %copy-done.8, s32[8,4]{1,0:T(8,128)S(1)} %copy.14.tgt_ref, bf16[8,4,128,128]{3,2,1,0:T(8,128)(2,1)S(1)} %copy-done.7, bf16[256,256]{1,0:T(8,128)(2,1)S(1)} %copy-done.4), custom_call_target="tpu_custom_call" | custom-call | bytes 8388608 | tf_op jit(solution)/shard_map/pallas_call | solution.py:41
  16.8 0.0 copy-start
  16.8 2.4 %copy-done = bf16[1024,2688]{1,0:T(8,128)(2,1)} copy-done((bf16[1024,2688]{1,0:T(8,128)(2,1)}, bf16[1024,2688]{1,0:T(8,128)(2,1)S(1)}, u32[]{:S(2)}) %copy-start) | copy-done | bytes 5505048
  19.2 5.9 %all-to-all-done = bf16[16,64,256]{2,1,0:T(8,128)(2,1)S(1)} async-done(((bf16[16,64,256]{2,1,0:T(8,128)(2,1)}), bf16[16,64,256]{2,1,0:T(8,128)(2,1)S(1)}, u32[]{:S(2)}, u32[]{:S(2)}) %all-to-all-start) | async-done | bytes 524320 | tf_op jit(solution)/shard_map/all_to_all | solution.py:443
  25.1 0.0 copy-start.5
  25.1 0.7 shard_map.113
  25.8 0.1 collective-permute-start
  25.9 2.8 %collective-permute-start.1 = (bf16[256,256]{1,0:T(8,128)(2,1)S(1)}, bf16[256,256]{1,0:T(8,128)(2,1)S(1)}, u32[]{:S(2)}, u32[]{:S(2)}) collective-permute-start(bf16[256,256]{1,0:T(8,128)(2,1)S(1)} %get-tuple-element.47), channel_id=1, source_target_pairs={{0,15},{1,2},{2,1},{3,4},{4,3},{5,6},{6,5},{7,8},{8,7},{9,10},{10,... | collective-permute-start | bytes 393224 | tf_op jit(solution)/shard_map/ppermute | solution.py:29
  28.7 0.0 copy-done.6
  28.7 0.0 copy-done.3
  28.7 0.0 copy-start.1
  28.7 2.6 %copy-done.1 = bf16[1024,2688]{1,0:T(8,128)(2,1)S(1)} copy-done((bf16[1024,2688]{1,0:T(8,128)(2,1)S(1)}, bf16[1024,2688]{1,0:T(8,128)(2,1)}, u32[]{:S(2)}) %copy-start.1) | copy-done | bytes 5505048
  31.3 0.0 copy-start.2
  31.3 1.5 %shard_map.114 = (bf16[512,256]{1,0:T(8,128)(2,1)S(1)}, bf16[512,256]{1,0:T(8,128)(2,1)S(1)}, bf16[512,256]{1,0:T(8,128)(2,1)S(1)}, bf16[512,256]{1,0:T(8,128)(2...) custom-call(bf16[1024,256]{1,0:T(8,128)(2,1)S(1)} %bitcast.9, ...), custom_call_target="tpu_custom_call" | custom-call | flops 805306368 | bytes 4194304 | tf_op jit(solution)/shard_map/pallas_call | solution.py:41
  32.8 0.0 collective-permute-done.near_in_ref
  32.8 0.3 collective-permute-done.1.far_in_ref
  33.1 0.7 shard_map.115
  33.7 0.1 collective-permute-start.2
  33.8 2.8 %collective-permute-start.3 = (bf16[256,256]{1,0:T(8,128)(2,1)S(1)}, bf16[256,256]{1,0:T(8,128)(2,1)S(1)}, u32[]{:S(2)}, u32[]{:S(2)}) collective-permute-start(bf16[256,256]{1,0:T(8,128)(2,1)S(1)} %get-tuple-element.53), channel_id=1, source_target_pairs={{0,15},{1,2},{2,1},{3,4},{4,3},{5,6},{6,5},{7,8},{8,7},{9,10},{10,... | collective-permute-start | bytes 393224 | tf_op jit(solution)/shard_map/ppermute | solution.py:29
  36.6 0.5 shard_map.118
  37.1 1.6 %collective-permute-start.4 = (bf16[512,128]{1,0:T(8,128)(2,1)S(1)}, bf16[512,128]{1,0:T(8,128)(2,1)S(1)}, u32[]{:S(2)}, u32[]{:S(2)}) collective-permute-start(bf16[512,128]{1,0:T(8,128)(2,1)S(1)} %get-tuple-element.65), channel_id=1, source_target_pairs={{0,16},{16,0},{1,17},{17,1},{2,18},{18,2},{3,19},{19,3},{4,20},{20... | collective-permute-start | bytes 393224 | tf_op jit(solution)/shard_map/ppermute | solution.py:24
  38.7 0.0 copy-done.5
  38.7 0.0 copy-done.2
  38.7 1.6 %shard_map.116 = (bf16[1024,256]{1,0:T(8,128)(2,1)}, f32[1024,256]{1,0:T(8,128)S(1)}, f32[1024,256]{1,0:T(8,128)S(1)}) custom-call(bf16[1024,256]{1,0:T(8,128)(2,1)S(1)} %bitcast.12, bf16[1024,2688]{1,0:T(8,128)(2,1)S(1)} %copy-done.2, bf16[256,256]{1,0:T(8,128)(2,1)S(1)} %copy-done.5, bf16[512,256]{1,0:T(8,128)(2,1)S(1)} %get-tuple-element.44.out_mid_ref, ...), custom_call_target="tpu_custom_call" | custom-call | flops 671088640 | bytes 4194304 | tf_op jit(solution)/shard_map/pallas_call | solution.py:41
  40.3 0.0 collective-permute-done.2.near_ref
  40.3 0.7 collective-permute-done.3.far_ref
  41.0 0.0 copy-start.9
  41.0 1.9 %shard_map.117 = (bf16[1024,256]{1,0:T(8,128)(2,1)}, bf16[1024,256]{1,0:T(8,128)(2,1)S(1)}) custom-call(bf16[1024,2688]{1,0:T(8,128)(2,1)S(1)} %copy-done.2, bf16[256,256]{1,0:T(8,128)(2,1)S(1)} %collective-permute-done.2.near_ref, bf16[256,256]{1,0:T(8,128)(2,1)S(1)} %collective-permute-done.3.far_ref, f32[1024,256]{1,0:T(8,128)S(1)} %get-tuple-element.54.d_msg_ref, ...), custom_call_target="tpu_custom_call" | custom-call | flops 536870912 | bytes 4194304 | tf_op jit(solution)/shard_map/pallas_call | solution.py:41
  42.9 0.0 collective-permute-done.4.node_in_ref
  42.9 4.1 %all-to-all-start.1 = ((bf16[16,64,256]{2,1,0:T(8,128)(2,1)}), bf16[16,64,256]{2,1,0:T(8,128)(2,1)S(1)}, u32[]{:S(2)}, u32[]{:S(2)}) async-start(bf16[16,64,256]{2,1,0:T(8,128)(2,1)} %bitcast.5), calls=%async_computation.1 | async-start | bytes 1048576 | tf_op jit(solution)/shard_map/all_to_all | solution.py:509
  47.0 0.4 shard_map.119
  47.4 0.5 collective-permute-start.5
  47.9 1.0 %collective-permute-done.5.in_ref = bf16[512,128]{1,0:T(8,128)(2,1)S(1)} collective-permute-done((bf16[512,128]{1,0:T(8,128)(2,1)S(1)}, bf16[512,128]{1,0:T(8,128)(2,1)S(1)}, u32[]{:S(2)}, u32[]{:S(2)}) %collective-permute-start.5) | collective-permute-done | bytes 131104 | tf_op jit(solution)/shard_map/ppermute | solution.py:24
  49.0 1.9 %collective-permute-start.6 = (bf16[256,128]{1,0:T(8,128)(2,1)S(1)}, bf16[256,128]{1,0:T(8,128)(2,1)S(1)}, u32[]{:S(2)}, u32[]{:S(2)}) collective-permute-start(bf16[256,128]{1,0:T(8,128)(2,1)S(1)} %get-tuple-element.70), channel_id=1, source_target_pairs={{0,2},{1,3},{2,0},{3,1},{4,6},{5,7},{6,4},{7,5},{8,10},{9,11},{10,... | collective-permute-start | bytes 196616 | tf_op jit(solution)/shard_map/ppermute | solution.py:24
  50.9 3.8 %collective-permute-done.6.in_ref = bf16[256,128]{1,0:T(8,128)(2,1)S(1)} collective-permute-done((bf16[256,128]{1,0:T(8,128)(2,1)S(1)}, bf16[256,128]{1,0:T(8,128)(2,1)S(1)}, u32[]{:S(2)}, u32[]{:S(2)}) %collective-permute-start.6) | collective-permute-done | bytes 65568 | tf_op jit(solution)/shard_map/ppermute | solution.py:24
  54.7 2.2 %collective-permute-start.7 = (bf16[256,128]{1,0:T(8,128)(2,1)S(1)}, bf16[256,128]{1,0:T(8,128)(2,1)S(1)}, u32[]{:S(2)}, u32[]{:S(2)}) collective-permute-start(bf16[256,128]{1,0:T(8,128)(2,1)S(1)} %shard_map.121.mine_ref), channel_id=1, source_target_pairs={{0,4},{1,5},{2,6},{3,7},{4,0},{5,1},{6,2},{7,3},{8,12},{9,13},{10,... | collective-permute-start | bytes 196616 | tf_op jit(solution)/shard_map/ppermute | solution.py:24
  56.9 2.4 %collective-permute-done.7.in_ref = bf16[256,128]{1,0:T(8,128)(2,1)S(1)} collective-permute-done((bf16[256,128]{1,0:T(8,128)(2,1)S(1)}, bf16[256,128]{1,0:T(8,128)(2,1)S(1)}, u32[]{:S(2)}, u32[]{:S(2)}) %collective-permute-start.7) | collective-permute-done | bytes 65568 | tf_op jit(solution)/shard_map/ppermute | solution.py:24
  59.3 3.3 %collective-permute-start.8 = (bf16[256,128]{1,0:T(8,128)(2,1)S(1)}, bf16[256,128]{1,0:T(8,128)(2,1)S(1)}, u32[]{:S(2)}, u32[]{:S(2)}) collective-permute-start(bf16[256,128]{1,0:T(8,128)(2,1)S(1)} %shard_map.122.mine_ref), channel_id=1, source_target_pairs={{0,8},{1,9},{2,10},{3,11},{4,12},{5,13},{6,14},{7,15},{8,0},{9,1},... | collective-permute-start | bytes 196616 | tf_op jit(solution)/shard_map/ppermute | solution.py:24
  62.6 2.5 %collective-permute-done.8.in_ref = bf16[256,128]{1,0:T(8,128)(2,1)S(1)} collective-permute-done((bf16[256,128]{1,0:T(8,128)(2,1)S(1)}, bf16[256,128]{1,0:T(8,128)(2,1)S(1)}, u32[]{:S(2)}, u32[]{:S(2)}) %collective-permute-start.8) | collective-permute-done | bytes 65568 | tf_op jit(solution)/shard_map/ppermute | solution.py:24
  65.2 4.0 %collective-permute-start.11 = (bf16[256,128]{1,0:T(8,128)(2,1)S(1)}, bf16[256,128]{1,0:T(8,128)(2,1)S(1)}, u32[]{:S(2)}, u32[]{:S(2)}) collective-permute-start(bf16[256,128]{1,0:T(8,128)(2,1)S(1)} %shard_map.123.mine_ref), channel_id=1, source_target_pairs={{0,18},{1,19},{2,16},{3,17},{4,22},{5,23},{6,20},{7,21},{8,26},{9,... | collective-permute-start | bytes 196616 | tf_op jit(solution)/shard_map/ppermute | solution.py:349
  69.2 0.0 collective-permute-start.10
  69.2 0.6 collective-permute-start.9
  69.8 0.0 all-to-all-done.1
  69.8 0.0 copy-done.9
  69.8 1.5 %shard_map.124 = bf16[1024,256]{1,0:T(8,128)(2,1)} custom-call(s32[1,1024]{1,0:T(1,128)S(1)} %copy-done.9, bf16[1024,256]{1,0:T(8,128)(2,1)S(1)} %bitcast.16), custom_call_target="tpu_custom_call" | custom-call | flops 536870912 | bytes 1048576 | tf_op jit(solution)/shard_map/pallas_call | solution.py:41
  71.4 0.3 collective-permute-done.11.both_ref
  71.6 1.8 %collective-permute-done.10.y_ref = bf16[256,128]{1,0:T(8,128)(2,1)S(1)} collective-permute-done((bf16[256,128]{1,0:T(8,128)(2,1)S(1)}, bf16[256,128]{1,0:T(8,128)(2,1)S(1)}, u32[]{:S(2)}, u32[]{:S(2)}) %collective-permute-start.10) | collective-permute-done | bytes 65568 | tf_op jit(solution)/shard_map/ppermute | solution.py:24
  73.5 0.0 collective-permute-done.9.dp_ref
  73.5 0.1 shard_map.125.refs_0_
  73.5 0.1 collective-permute-start.12
  73.6 0.8 %shard_map.126 = (f32[256,256]{1,0:T(8,128)}, f32[512,256]{1,0:T(8,128)}) custom-call(bf16[384,256]{1,0:T(8,128)(2,1)S(1)} %shard_map.125.refs_0_), custom_call_target="tpu_custom_call" | custom-call | bytes 786432 | tf_op jit(solution)/shard_map/pallas_call | solution.py:330
  74.4 0.6 collective-permute-done.12.refs_0_
  75.0 0.8 %shard_map.127 = (f32[256,256]{1,0:T(8,128)}, f32[512,256]{1,0:T(8,128)}) custom-call(bf16[384,256]{1,0:T(8,128)(2,1)S(1)} %collective-permute-done.12.refs_0_, f32[256,256]{1,0:T(8,128)} %get-tuple-element.74.refs_1_, f32[512,256]{1,0:T(8,128)} %get-tuple-element.75.refs_2_), custom_call_target="tpu_custom_call", output_to_operand_aliasing={{0}: (1, {}), {1}: (2, {})} | custom-call | bytes 786432 | tf_op jit(solution)/shard_map/pallas_call | solution.py:330
  (4 shorter events, 0.1 us)
Async XLA Ops:
  0.6 28.1 %copy-start.6 = (bf16[512,256]{1,0:T(8,128)(2,1)S(1)}, bf16[512,256]{1,0:T(8,128)(2,1)}, u32[]{:S(2)}) copy-start(bf16[512,256]{1,0:T(8,128)(2,1)} %w_node_ref.3) | copy-start | bytes 786436
  0.6 28.1 %copy-start.3 = (bf16[1,1024,256]{2,1,0:T(8,128)(2,1)S(1)}, bf16[1,1024,256]{2,1,0:T(8,128)(2,1)}, u32[]{:S(2)}) copy-start(bf16[1,1024,256]{2,1,0:T(8,128)(2,1)} %param.15) | copy-start | bytes 1572868
  3.3 21.9 %all-to-all-start = ((bf16[16,64,256]{2,1,0:T(8,128)(2,1)}), bf16[16,64,256]{2,1,0:T(8,128)(2,1)S(1)}, u32[]{:S(2)}, u32[]{:S(2)}) async-start(bf16[16,64,256]{2,1,0:T(8,128)(2,1)} %bitcast.17), calls=%async_computation | async-start | bytes 1048576 | tf_op jit(solution)/shard_map/all_to_all | solution.py:443
  11.4 0.9 %copy-start.4 = (bf16[256,256]{1,0:T(8,128)(2,1)S(1)}, bf16[256,256]{1,0:T(8,128)(2,1)}, u32[]{:S(2)}) copy-start(bf16[256,256]{1,0:T(8,128)(2,1)} %w_edge_ref.5) | copy-start | bytes 393220
  12.3 1.2 %copy-start.7 = (bf16[8,4,128,128]{3,2,1,0:T(8,128)(2,1)S(1)}, bf16[8,4,128,128]{3,2,1,0:T(8,128)(2,1)}, u32[]{:S(2)}) copy-start(bf16[8,4,128,128]{3,2,1,0:T(8,128)(2,1)} %vals_ref.1) | copy-start | bytes 3145732
  13.5 0.7 copy-start.8
  16.8 2.4 %copy-start = (bf16[1024,2688]{1,0:T(8,128)(2,1)}, bf16[1024,2688]{1,0:T(8,128)(2,1)S(1)}, u32[]{:S(2)}) copy-start(bf16[1024,2688]{1,0:T(8,128)(2,1)S(1)} %get-tuple-element.41.adj_ref.at_ref) | copy-start | bytes 16515076
  25.1 13.6 %copy-start.5 = (bf16[256,256]{1,0:T(8,128)(2,1)S(1)}, bf16[256,256]{1,0:T(8,128)(2,1)}, u32[]{:S(2)}) copy-start(bf16[256,256]{1,0:T(8,128)(2,1)} %w_edge_ref.5) | copy-start | bytes 393220
  25.8 6.9 %collective-permute-start = (bf16[256,256]{1,0:T(8,128)(2,1)S(1)}, bf16[256,256]{1,0:T(8,128)(2,1)S(1)}, u32[]{:S(2)}, u32[]{:S(2)}) collective-permute-start(bf16[256,256]{1,0:T(8,128)(2,1)S(1)} %get-tuple-element.46), channel_id=1, source_target_pairs={{0,1},{1,0},{2,3},{3,2},{4,5},{5,4},{6,7},{7,6},{8,9},{9,8},{10,11... | collective-permute-start | bytes 393224 | tf_op jit(solution)/shard_map/ppermute | solution.py:24
  25.9 7.2 %collective-permute-start.1 = (bf16[256,256]{1,0:T(8,128)(2,1)S(1)}, bf16[256,256]{1,0:T(8,128)(2,1)S(1)}, u32[]{:S(2)}, u32[]{:S(2)}) collective-permute-start(bf16[256,256]{1,0:T(8,128)(2,1)S(1)} %get-tuple-element.47), channel_id=1, source_target_pairs={{0,15},{1,2},{2,1},{3,4},{4,3},{5,6},{6,5},{7,8},{8,7},{9,10},{10,... | collective-permute-start | bytes 393224 | tf_op jit(solution)/shard_map/ppermute | solution.py:29
  28.7 2.6 %copy-start.1 = (bf16[1024,2688]{1,0:T(8,128)(2,1)S(1)}, bf16[1024,2688]{1,0:T(8,128)(2,1)}, u32[]{:S(2)}) copy-start(bf16[1024,2688]{1,0:T(8,128)(2,1)} %copy-done) | copy-start | bytes 16515076
  31.3 7.4 %copy-start.2 = (bf16[1024,2688]{1,0:T(8,128)(2,1)S(1)}, bf16[1024,2688]{1,0:T(8,128)(2,1)}, u32[]{:S(2)}) copy-start(bf16[1024,2688]{1,0:T(8,128)(2,1)} %copy-done) | copy-start | bytes 16515076
  33.7 6.6 %collective-permute-start.2 = (bf16[256,256]{1,0:T(8,128)(2,1)S(1)}, bf16[256,256]{1,0:T(8,128)(2,1)S(1)}, u32[]{:S(2)}, u32[]{:S(2)}) collective-permute-start(bf16[256,256]{1,0:T(8,128)(2,1)S(1)} %get-tuple-element.52), channel_id=1, source_target_pairs={{0,1},{1,0},{2,3},{3,2},{4,5},{5,4},{6,7},{7,6},{8,9},{9,8},{10,11... | collective-permute-start | bytes 393224 | tf_op jit(solution)/shard_map/ppermute | solution.py:24
  33.8 7.2 %collective-permute-start.3 = (bf16[256,256]{1,0:T(8,128)(2,1)S(1)}, bf16[256,256]{1,0:T(8,128)(2,1)S(1)}, u32[]{:S(2)}, u32[]{:S(2)}) collective-permute-start(bf16[256,256]{1,0:T(8,128)(2,1)S(1)} %get-tuple-element.53), channel_id=1, source_target_pairs={{0,15},{1,2},{2,1},{3,4},{4,3},{5,6},{6,5},{7,8},{8,7},{9,10},{10,... | collective-permute-start | bytes 393224 | tf_op jit(solution)/shard_map/ppermute | solution.py:29
  37.1 5.8 %collective-permute-start.4 = (bf16[512,128]{1,0:T(8,128)(2,1)S(1)}, bf16[512,128]{1,0:T(8,128)(2,1)S(1)}, u32[]{:S(2)}, u32[]{:S(2)}) collective-permute-start(bf16[512,128]{1,0:T(8,128)(2,1)S(1)} %get-tuple-element.65), channel_id=1, source_target_pairs={{0,16},{16,0},{1,17},{17,1},{2,18},{18,2},{3,19},{19,3},{4,20},{20... | collective-permute-start | bytes 393224 | tf_op jit(solution)/shard_map/ppermute | solution.py:24
  41.0 28.9 %copy-start.9 = (s32[1,1024]{1,0:T(1,128)S(1)}, s32[1,1024]{1,0:T(1,128)}, u32[]{:S(2)}) copy-start(s32[1,1024]{1,0:T(1,128)} %order_ref.1) | copy-start | bytes 12292
  42.9 26.9 %all-to-all-start.1 = ((bf16[16,64,256]{2,1,0:T(8,128)(2,1)}), bf16[16,64,256]{2,1,0:T(8,128)(2,1)S(1)}, u32[]{:S(2)}, u32[]{:S(2)}) async-start(bf16[16,64,256]{2,1,0:T(8,128)(2,1)} %bitcast.5), calls=%async_computation.1 | async-start | bytes 1048576 | tf_op jit(solution)/shard_map/all_to_all | solution.py:509
  47.4 1.5 %collective-permute-start.5 = (bf16[512,128]{1,0:T(8,128)(2,1)S(1)}, bf16[512,128]{1,0:T(8,128)(2,1)S(1)}, u32[]{:S(2)}, u32[]{:S(2)}) collective-permute-start(bf16[512,128]{1,0:T(8,128)(2,1)S(1)} %get-tuple-element.68), channel_id=1, source_target_pairs={{0,1},{1,0},{2,3},{3,2},{4,5},{5,4},{6,7},{7,6},{8,9},{9,8},{10,11... | collective-permute-start | bytes 393224 | tf_op jit(solution)/shard_map/ppermute | solution.py:24
  49.0 5.7 %collective-permute-start.6 = (bf16[256,128]{1,0:T(8,128)(2,1)S(1)}, bf16[256,128]{1,0:T(8,128)(2,1)S(1)}, u32[]{:S(2)}, u32[]{:S(2)}) collective-permute-start(bf16[256,128]{1,0:T(8,128)(2,1)S(1)} %get-tuple-element.70), channel_id=1, source_target_pairs={{0,2},{1,3},{2,0},{3,1},{4,6},{5,7},{6,4},{7,5},{8,10},{9,11},{10,... | collective-permute-start | bytes 196616 | tf_op jit(solution)/shard_map/ppermute | solution.py:24
  54.7 4.6 %collective-permute-start.7 = (bf16[256,128]{1,0:T(8,128)(2,1)S(1)}, bf16[256,128]{1,0:T(8,128)(2,1)S(1)}, u32[]{:S(2)}, u32[]{:S(2)}) collective-permute-start(bf16[256,128]{1,0:T(8,128)(2,1)S(1)} %shard_map.121.mine_ref), channel_id=1, source_target_pairs={{0,4},{1,5},{2,6},{3,7},{4,0},{5,1},{6,2},{7,3},{8,12},{9,13},{10,... | collective-permute-start | bytes 196616 | tf_op jit(solution)/shard_map/ppermute | solution.py:24
  59.3 5.8 %collective-permute-start.8 = (bf16[256,128]{1,0:T(8,128)(2,1)S(1)}, bf16[256,128]{1,0:T(8,128)(2,1)S(1)}, u32[]{:S(2)}, u32[]{:S(2)}) collective-permute-start(bf16[256,128]{1,0:T(8,128)(2,1)S(1)} %shard_map.122.mine_ref), channel_id=1, source_target_pairs={{0,8},{1,9},{2,10},{3,11},{4,12},{5,13},{6,14},{7,15},{8,0},{9,1},... | collective-permute-start | bytes 196616 | tf_op jit(solution)/shard_map/ppermute | solution.py:24
  65.2 6.5 %collective-permute-start.11 = (bf16[256,128]{1,0:T(8,128)(2,1)S(1)}, bf16[256,128]{1,0:T(8,128)(2,1)S(1)}, u32[]{:S(2)}, u32[]{:S(2)}) collective-permute-start(bf16[256,128]{1,0:T(8,128)(2,1)S(1)} %shard_map.123.mine_ref), channel_id=1, source_target_pairs={{0,18},{1,19},{2,16},{3,17},{4,22},{5,23},{6,20},{7,21},{8,26},{9,... | collective-permute-start | bytes 196616 | tf_op jit(solution)/shard_map/ppermute | solution.py:349
  69.2 4.3 %collective-permute-start.10 = (bf16[256,128]{1,0:T(8,128)(2,1)S(1)}, bf16[256,128]{1,0:T(8,128)(2,1)S(1)}, u32[]{:S(2)}, u32[]{:S(2)}) collective-permute-start(bf16[256,128]{1,0:T(8,128)(2,1)S(1)} %shard_map.123.mine_ref), channel_id=1, source_target_pairs={{0,2},{1,3},{2,0},{3,1},{4,6},{5,7},{6,4},{7,5},{8,10},{9,11},{10,... | collective-permute-start | bytes 196616 | tf_op jit(solution)/shard_map/ppermute | solution.py:24
  69.2 4.3 %collective-permute-start.9 = (bf16[256,128]{1,0:T(8,128)(2,1)S(1)}, bf16[256,128]{1,0:T(8,128)(2,1)S(1)}, u32[]{:S(2)}, u32[]{:S(2)}) collective-permute-start(bf16[256,128]{1,0:T(8,128)(2,1)S(1)} %shard_map.123.mine_ref), channel_id=1, source_target_pairs={{0,16},{16,0},{1,17},{17,1},{2,18},{18,2},{3,19},{19,3},{4,20},{20... | collective-permute-start | bytes 196616 | tf_op jit(solution)/shard_map/ppermute | solution.py:24
  73.5 1.5 %collective-permute-start.12 = (bf16[384,256]{1,0:T(8,128)(2,1)S(1)}, bf16[384,256]{1,0:T(8,128)(2,1)S(1)}, u32[]{:S(2)}, u32[]{:S(2)}) collective-permute-start(bf16[384,256]{1,0:T(8,128)(2,1)S(1)} %shard_map.125.refs_0_), channel_id=1, source_target_pairs={{0,1},{1,0},{2,3},{3,2},{4,5},{5,4},{6,7},{7,6},{8,9},{9,8},{10,11... | collective-permute-start | bytes 589832 | tf_op jit(solution)/shard_map/ppermute | solution.py:24

commit v9 on v7

--- a/solution.py
+++ b/solution.py
@@ -110,7 +110,7 @@
     return jnp.where(odd, first, second), jnp.where(odd, second, first)
 
 
-def message_body(nodes_ref, a_ref, near_ref, far_ref, msg_ref):
+def message_body(nodes_ref, a_ref, far_ref, msg_ref):
     rows, width = nodes_ref.shape
     rim = RIM * ROWS
     w_edge = a_ref[2 * rim :, :width]
@@ -118,10 +118,16 @@
         mine = slice(k * rim, (k + 1) * rim)
         pre = dot(nodes_ref[mine, :], w_edge)
         msg_ref[mine, :] = (pre * jax.nn.sigmoid(pre)).astype(BF16)
-    sums = dot(a_ref[: 2 * rim, :], msg_ref[...])
-    near, far = chosen(sums[:rim], sums[rim:])
-    near_ref[...] = near.astype(BF16)
-    far_ref[...] = far.astype(BF16)
+    far_ref[...] = dot(a_ref[end_of(True, rim), :], msg_ref[...]).astype(BF16)
+
+
+def end_of(far, start):
+    odd = lax.rem(lax.axis_index("dom"), 2)
+    return pl.ds(pl.multiple_of((odd if far else 1 - odd) * start, ROWS), RIM * ROWS)
+
+
+def near_body(a_ref, msg_ref, near_ref):
+    near_ref[...] = dot(a_ref[end_of(False, RIM * ROWS), :], msg_ref[...]).astype(BF16)
 
 
 def node_step(nodes, agg, gout, w_node):
@@ -161,36 +167,30 @@
 
 
 def rim_body(
-    nodes_ref, own_ref, near_in_ref, far_in_ref, cot_ref, w_node_ref,
-    near_ref, far_ref, out_ref, agg_ref, d_node_ref, d_nodes1_ref, d_agg_ref,
+    far, nodes_ref, own_ref, in_ref, cot_ref, w_node_ref,
+    out_ref, agg_ref, d_node_ref, d_nodes1_ref, d_agg_ref,
 ):
-    rows = nodes_ref.shape[0]
     rim = RIM * ROWS
-    arrived = chosen(near_in_ref[...].astype(F32), far_in_ref[...].astype(F32))
-    rims = []
-    for k in range(2):
-        mine = slice(k * (rows - rim), k * (rows - rim) + rim)
-        here = slice(k * rim, (k + 1) * rim)
-        agg = (own_ref[here, :].astype(F32) + arrived[k]).astype(BF16)
-        agg_ref[here, :] = agg
-        out, d_node, d_nodes1, d_agg = node_step(nodes_ref[mine, :], agg, cot_ref[mine, :], w_node_ref[...])
-        out_ref[here, :] = out
-        d_node_ref[here, :] = d_node
-        d_nodes1_ref[here, :] = d_nodes1
-        d_agg_ref[here, :] = d_agg
-        rims.append(d_agg)
-    near_ref[...], far_ref[...] = chosen(rims[0], rims[1])
-
-
-def in_order(mid_ref, rim_ref):
-    rim = RIM * ROWS
-    return jnp.concatenate([rim_ref[:rim, :], mid_ref[...], rim_ref[rim:, :]], axis=0)
-
-
-def grad_node_body(scale, nodes_ref, agg_mid_ref, agg_rim_ref, d_node_mid_ref, d_node_rim_ref, *out_refs):
+    mine = end_of(far, nodes_ref.shape[0] - rim)
+    agg = (own_ref[end_of(far, rim), :].astype(F32) + in_ref[...].astype(F32)).astype(BF16)
+    agg_ref[...] = agg
+    out, d_node, d_nodes1, d_agg = node_step(nodes_ref[mine, :], agg, cot_ref[mine, :], w_node_ref[...])
+    out_ref[...] = out
+    d_node_ref[...] = d_node
+    d_nodes1_ref[...] = d_nodes1
+    d_agg_ref[...] = d_agg
+
+
+def in_order(mid_ref, near_ref, far_ref):
+    first, last = chosen(near_ref[...], far_ref[...])
+    return jnp.concatenate([first, mid_ref[...], last], axis=0)
+
+
+def grad_node_body(scale, nodes_ref, *refs):
     width = nodes_ref.shape[1]
-    d_node = in_order(d_node_mid_ref, d_node_rim_ref)
-    agg = in_order(agg_mid_ref, agg_rim_ref)
+    out_refs = refs[6:]
+    agg = in_order(*refs[:3])
+    d_node = in_order(*refs[3:6])
     first = lax.axis_index("dp") == 0
     for k, left in enumerate((nodes_ref[...], agg)):
         mine = slice(k * width, (k + 1) * width)
@@ -204,13 +204,13 @@
 
 
 def behind_body(
-    nodes_ref, at_ref, w_edge_ref, out_mid_ref, out_rim_ref, d_agg_mid_ref, d_agg_rim_ref,
-    out_ref, d_msg_ref, slope_ref,
+    nodes_ref, at_ref, w_edge_ref, out_mid_ref, out_near_ref, out_far_ref,
+    d_agg_mid_ref, d_agg_near_ref, d_agg_far_ref, out_ref, d_msg_ref, slope_ref,
 ):
     rows = nodes_ref.shape[0]
     rim = RIM * ROWS
-    out_ref[...] = in_order(out_mid_ref, out_rim_ref)
-    d_agg = in_order(d_agg_mid_ref, d_agg_rim_ref)
+    out_ref[...] = in_order(out_mid_ref, out_near_ref, out_far_ref)
+    d_agg = in_order(d_agg_mid_ref, d_agg_near_ref, d_agg_far_ref)
     for k in range(rows // rim):
         mine = slice(k * rim, (k + 1) * rim)
         d_msg_ref[mine, :] = dot(at_ref[mine, :rows], d_agg)
@@ -220,13 +220,14 @@
 
 
 def edge_body(
-    scale, nodes_ref, at_ref, near_ref, far_ref, d_msg_ref, slope_ref, mid_ref, rim_ref, w_edge_ref,
+    scale, nodes_ref, at_ref, near_ref, far_ref, d_msg_ref, slope_ref, mid_ref, near1_ref, far1_ref, w_edge_ref,
     back_hbm, g_edge_ref, d_edge_ref, back_ref, sems,
 ):
     rows, width = nodes_ref.shape
     rim = RIM * ROWS
     prev, after = chosen(near_ref[...], far_ref[...])
     rims = jnp.concatenate([prev, after], axis=0)
+    ends = chosen(near1_ref[...], far1_ref[...])
     w_edge = w_edge_ref[...]
     puts = []
     for k in range(rows // rim):
@@ -235,9 +236,9 @@
         d_edge = (d_msg.astype(BF16).astype(F32) * slope_ref[mine, :]).astype(BF16)
         d_edge_ref[mine, :] = d_edge
         if k == 0:
-            d_nodes1 = rim_ref[:rim, :]
+            d_nodes1 = ends[0]
         elif k == rows // rim - 1:
-            d_nodes1 = rim_ref[rim:, :]
+            d_nodes1 = ends[1]
         else:
             d_nodes1 = mid_ref[(k - 1) * rim : k * rim, :]
         back_ref[mine, :] = (d_nodes1 + dot(d_edge, w_edge, ((1,), (1,)))).astype(BF16)
@@ -446,10 +447,11 @@
         [pltpu.VMEM((spots, ROWS, rows), BF16)],
         nbytes=16 * unit,
     )
-    near, far, msg = call(
-        message_body, [edge, edge, tall], (nodes, adj_rim), flops=square + 4 * rim * rows * width, nbytes=4 * unit
+    far, msg = call(
+        message_body, [edge, tall], (nodes, adj_rim), flops=square + 2 * rim * rows * width, nbytes=4 * unit
     )
     far = swapped_across(far, "dom")
+    (near,) = call(near_body, [edge], (adj_rim, msg), flops=2 * rim * rows * width, nbytes=unit)
     near = swapped(near, "dom", 1)
     cot = cotangent[0]
     own, out_mid, agg_mid, d_node_mid, d_nodes1_mid, d_agg_mid = call(
@@ -459,15 +461,20 @@
         flops=2 * rows * rows * width + 2 * square,
         nbytes=8 * unit,
     )
-    near, far, out_rim, agg_rim, d_node_rim, d_nodes1_rim, d_agg_rim = call(
-        rim_body,
-        [edge, edge, rims, rims, rims, shape(*rims.shape, dtype=F32), rims],
-        (nodes, own, near, far, cot, w_node),
-        flops=2 * square,
-        nbytes=4 * unit,
-    )
-    far = swapped_across(far, "dom")
-    near = swapped(near, "dom", 1)
+    ends = []
+    for is_far, arrived in ((True, far), (False, near)):
+        ends.append(
+            call(
+                functools.partial(rim_body, is_far),
+                [edge, edge, edge, shape(*edge.shape, dtype=F32), edge],
+                (nodes, own, arrived, cot, w_node),
+                flops=square,
+                nbytes=2 * unit,
+            )
+        )
+    out_rim, agg_rim, d_node_rim, d_nodes1_rim, d_agg_rim = zip(*ends[::-1])
+    far = swapped_across(d_agg_rim[1], "dom")
+    near = swapped(d_agg_rim[0], "dom", 1)
     tiled = ndp == 2 and ndom == 16
 
     node_part = call(
@@ -475,7 +482,7 @@
         [shape(2 * width, width // 2, dtype=F32), shape(2 * width, width // 2)]
         if tiled
         else [shape(2 * width, width, dtype=F32)],
-        (nodes, agg_mid, agg_rim, d_node_mid, d_node_rim),
+        (nodes, agg_mid, *agg_rim, d_node_mid, *d_node_rim),
         flops=2 * square,
         nbytes=3 * unit,
     )
@@ -484,14 +491,14 @@
     node_out, d_msg, slope = call(
         behind_body,
         [tall, tall_f, tall_f],
-        (nodes, adj, w_edge, out_mid, out_rim, d_agg_mid, d_agg_rim),
+        (nodes, adj, w_edge, out_mid, *out_rim, d_agg_mid, *d_agg_rim),
         flops=2 * rows * rows * width + square,
         nbytes=8 * unit,
     )
     back, edge_part = call(
         functools.partial(edge_body, scale),
         [tall, shape(width, width, dtype=F32)],
-        (nodes, adj, near, far, d_msg, slope, d_nodes1_mid, d_nodes1_rim, w_edge),
+        (nodes, adj, near, far, d_msg, slope, d_nodes1_mid, *d_nodes1_rim, w_edge),
         scratch=[
             pltpu.VMEM((rows, width), BF16),
             pltpu.VMEM((rows, width), BF16),

time: 75.1 us -> 75 us (level)
    ppermute x10, waiting for transfers between devices: 13 us -> 11.2 us  [swapped(): return lax.ppermute(x, axis, [(i, i ^ mask) for i in range(peers)])]
    ppermute x1, waiting for transfers between devices: 0.22 us -> 2.04 us  [swapped_both(): lax.ppermute(x, ('dp', 'dom'), [(i, (i + peers) % total ^ mask) for i in...]
    ppermute x1, starting transfers between devices: 2.46 us -> 1.5 us  [swapped_both(): lax.ppermute(x, ('dp', 'dom'), [(i, (i + peers) % total ^ mask) for i in...]
    ppermute x10, starting transfers between devices: 10.5 us -> 11.4 us  [swapped(): return lax.ppermute(x, axis, [(i, i ^ mask) for i in range(peers)])]
    pallas_call x15 -> x17, Pallas kernels: 13.5 us -> 14.1 us  [call(): pl.pallas_call(body, out_shape=outs, in_specs=specs or [VMEM] * len(args)...]
  transfers between devices with their start and end apart: 15 -> 15, of which waited for: 11 -> 9; matrix products, arithmetic and copies ran while one was open for 1% -> 1% of each run, Pallas kernels for 14% -> 15%
where the time goes in v9:
time: 75 us; the launch traced here: 74.6 us
  starting transfers between devices  29.4 us (39%)
  waiting for transfers between devices  20.1 us (27%)
  Pallas kernels  15.7 us (21%)
  local copies, waits for them, and re-layouts  8.53 us (11%)
  between operations  0.83 us (1%)
    pallas_call x17, Pallas kernels, call(): pl.pallas_call(body, out_shape=outs, in_specs=specs or [VMEM] * len(args)...  14.1 us
    ppermute x10, starting transfers between devices, swapped(): return lax.ppermute(x, axis, [(i, i ^ mask) for i in range(peers)])  11.4 us
    ppermute x10, waiting for transfers between devices, swapped(): return lax.ppermute(x, axis, [(i, i ^ mask) for i in range(peers)])  11.2 us
    unnamed x21, local copies, waits for them, and re-layouts  8.53 us
    all_to_all x1, starting transfers between devices, shards(): lax.all_to_all(picked.reshape(ndom, per_peer, width), 'dom', split_axis=0...  7.39 us
    all_to_all x1, waiting for transfers between devices, shards(): lax.all_to_all(picked.reshape(ndom, per_peer, width), 'dom', split_axis=0...  5.94 us
    ppermute x2, starting transfers between devices, swapped_across(): lax.ppermute(x, axis, [(i, (i + 1 if i % 2 else i - 1) % peers) for i in...  5.3 us
    all_to_all x1, starting transfers between devices, shards(): lax.all_to_all(back.reshape(ndom, per_peer, width), 'dom', split_axis=0,...  3.82 us
  transfers between devices with their start and end apart: 15, of which 9 were waited for; matrix products, arithmetic and copies ran while one was open for 1% of the time, Pallas kernels for 15%

profile of v9, /device:TPU:0, one launch (start us, length us, event | category | flops | bytes accessed | tf_op | source)
XLA Modules:
  0.0 74.6 jit_solution(9297096289499218268)
XLA Ops:
  0.6 0.0 copy-start.3
  0.6 0.0 copy-start.4
  0.7 2.6 %shard_map.111 = bf16[1024,256]{1,0:T(8,128)(2,1)} custom-call(s32[1,1024]{1,0:T(1,128)} %order_ref.1, bf16[1024,256]{1,0:T(8,128)(2,1)} %bitcast.20), custom_call_target="tpu_custom_call" | custom-call | flops 536870912 | bytes 1048576 | tf_op jit(solution)/shard_map/pallas_call | solution.py:41
  3.3 7.4 %all-to-all-start = ((bf16[16,64,256]{2,1,0:T(8,128)(2,1)}), bf16[16,64,256]{2,1,0:T(8,128)(2,1)S(1)}, u32[]{:S(2)}, u32[]{:S(2)}) async-start(bf16[16,64,256]{2,1,0:T(8,128)(2,1)} %bitcast.19), calls=%async_computation | async-start | bytes 1048576 | tf_op jit(solution)/shard_map/all_to_all | solution.py:438
  10.7 0.8 %copy.14.tgt_ref = s32[8,4]{1,0:T(8,128)S(1)} copy(s32[8,4]{0,1:T(4,128)} %param.11) | data formatting | bytes 256 | tf_op args[3]
  11.4 0.0 copy-start.5
  11.4 0.9 %copy-done.5 = bf16[256,256]{1,0:T(8,128)(2,1)S(1)} copy-done((bf16[256,256]{1,0:T(8,128)(2,1)S(1)}, bf16[256,256]{1,0:T(8,128)(2,1)}, u32[]{:S(2)}) %copy-start.5) | copy-done | bytes 131096
  12.3 0.0 copy-start.7
  12.3 1.2 %copy-done.7 = bf16[8,4,128,128]{3,2,1,0:T(8,128)(2,1)S(1)} copy-done((bf16[8,4,128,128]{3,2,1,0:T(8,128)(2,1)S(1)}, bf16[8,4,128,128]{3,2,1,0:T(8,128)(2,1)}, u32[]{:S(2)}) %copy-start.7) | copy-done | bytes 1048600
  13.5 0.0 copy-start.8
  13.5 0.7 copy-done.8
  14.2 2.6 %shard_map.112 = (bf16[768,1024]{1,0:T(8,128)(2,1)S(1)}, bf16[1024,2688]{1,0:T(8,128)(2,1)S(1)}) custom-call(s32[8]{0:T(128)S(1)} %copy-done.8, s32[8,4]{1,0:T(8,128)S(1)} %copy.14.tgt_ref, bf16[8,4,128,128]{3,2,1,0:T(8,128)(2,1)S(1)} %copy-done.7, bf16[256,256]{1,0:T(8,128)(2,1)S(1)} %copy-done.5), custom_call_target="tpu_custom_call" | custom-call | bytes 8388608 | tf_op jit(solution)/shard_map/pallas_call | solution.py:41
  16.8 0.0 copy-start
  16.8 2.4 %copy-done = bf16[1024,2688]{1,0:T(8,128)(2,1)} copy-done((bf16[1024,2688]{1,0:T(8,128)(2,1)}, bf16[1024,2688]{1,0:T(8,128)(2,1)S(1)}, u32[]{:S(2)}) %copy-start) | copy-done | bytes 5505048
  19.2 5.9 %all-to-all-done = bf16[16,64,256]{2,1,0:T(8,128)(2,1)S(1)} async-done(((bf16[16,64,256]{2,1,0:T(8,128)(2,1)}), bf16[16,64,256]{2,1,0:T(8,128)(2,1)S(1)}, u32[]{:S(2)}, u32[]{:S(2)}) %all-to-all-start) | async-done | bytes 524320 | tf_op jit(solution)/shard_map/all_to_all | solution.py:438
  25.1 0.6 shard_map.113
  25.7 0.3 shard_map.115
  26.0 0.1 collective-permute-start
  26.1 2.8 %collective-permute-start.1 = (bf16[256,256]{1,0:T(8,128)(2,1)S(1)}, bf16[256,256]{1,0:T(8,128)(2,1)S(1)}, u32[]{:S(2)}, u32[]{:S(2)}) collective-permute-start(bf16[256,256]{1,0:T(8,128)(2,1)S(1)} %get-tuple-element.49), channel_id=1, source_target_pairs={{0,15},{1,2},{2,1},{3,4},{4,3},{5,6},{6,5},{7,8},{8,7},{9,10},{10,... | collective-permute-start | bytes 393224 | tf_op jit(solution)/shard_map/ppermute | solution.py:29
  28.9 0.0 copy-done.3
  28.9 0.0 copy-done.4
  28.9 0.0 copy-start.1
  29.0 2.6 %copy-done.1 = bf16[1024,2688]{1,0:T(8,128)(2,1)S(1)} copy-done((bf16[1024,2688]{1,0:T(8,128)(2,1)S(1)}, bf16[1024,2688]{1,0:T(8,128)(2,1)}, u32[]{:S(2)}) %copy-start.1) | copy-done | bytes 5505048
  31.5 0.0 copy-start.2
  31.5 1.5 %shard_map.114 = (bf16[512,256]{1,0:T(8,128)(2,1)S(1)}, bf16[512,256]{1,0:T(8,128)(2,1)S(1)}, bf16[512,256]{1,0:T(8,128)(2,1)S(1)}, bf16[512,256]{1,0:T(8,128)(2...) custom-call(bf16[1024,256]{1,0:T(8,128)(2,1)S(1)} %bitcast.9, ...), custom_call_target="tpu_custom_call" | custom-call | flops 805306368 | bytes 4194304 | tf_op jit(solution)/shard_map/pallas_call | solution.py:41
  33.0 0.0 collective-permute-done.in_ref
  33.0 0.5 shard_map.116
  33.5 0.1 collective-permute-start.2
  33.6 0.0 collective-permute-done.1.in_ref
  33.6 0.5 shard_map.117
  34.1 2.5 %collective-permute-start.3 = (bf16[256,256]{1,0:T(8,128)(2,1)S(1)}, bf16[256,256]{1,0:T(8,128)(2,1)S(1)}, u32[]{:S(2)}, u32[]{:S(2)}) collective-permute-start(bf16[256,256]{1,0:T(8,128)(2,1)S(1)} %get-tuple-element.53.d_agg_far_ref), channel_id=1, source_target_pairs={{0,15},{1,2},{2,1},{3,4},{4,3},{5,6},{6,5},{7,8},{8,7},{9,10},{10,... | collective-permute-start | bytes 393224 | tf_op jit(solution)/shard_map/ppermute | solution.py:29
  36.6 0.5 shard_map.120
  37.1 1.6 %collective-permute-start.4 = (bf16[512,128]{1,0:T(8,128)(2,1)S(1)}, bf16[512,128]{1,0:T(8,128)(2,1)S(1)}, u32[]{:S(2)}, u32[]{:S(2)}) collective-permute-start(bf16[512,128]{1,0:T(8,128)(2,1)S(1)} %get-tuple-element.69), channel_id=1, source_target_pairs={{0,16},{16,0},{1,17},{17,1},{2,18},{18,2},{3,19},{19,3},{4,20},{20... | collective-permute-start | bytes 393224 | tf_op jit(solution)/shard_map/ppermute | solution.py:24
  38.7 0.0 copy-done.2
  38.7 0.0 copy-done.6
  38.7 1.7 %shard_map.118 = (bf16[1024,256]{1,0:T(8,128)(2,1)}, f32[1024,256]{1,0:T(8,128)S(1)}, f32[1024,256]{1,0:T(8,128)S(1)}) custom-call(bf16[1024,256]{1,0:T(8,128)(2,1)S(1)} %bitcast.13, bf16[1024,2688]{1,0:T(8,128)(2,1)S(1)} %copy-done.2, bf16[256,256]{1,0:T(8,128)(2,1)S(1)} %copy-done.6, bf16[512,256]{1,0:T(8,128)(2,1)S(1)} %get-tuple-element.46.out_mid_ref, ...), custom_call_target="tpu_custom_call" | custom-call | flops 671088640 | bytes 4194304 | tf_op jit(solution)/shard_map/pallas_call | solution.py:41
  40.3 0.0 collective-permute-done.2.near_ref
  40.3 0.9 %collective-permute-done.3.far_ref = bf16[256,256]{1,0:T(8,128)(2,1)S(1)} collective-permute-done((bf16[256,256]{1,0:T(8,128)(2,1)S(1)}, bf16[256,256]{1,0:T(8,128)(2,1)S(1)}, u32[]{:S(2)}, u32[]{:S(2)}) %collective-permute-start.3) | collective-permute-done | bytes 131104 | tf_op jit(solution)/shard_map/ppermute | solution.py:29
  41.3 1.6 %shard_map.119 = (bf16[1024,256]{1,0:T(8,128)(2,1)}, f32[256,256]{1,0:T(8,128)S(1)}) custom-call(bf16[1024,256]{1,0:T(8,128)(2,1)S(1)} %bitcast.14, bf16[1024,2688]{1,0:T(8,128)(2,1)S(1)} %copy-done.2, bf16[256,256]{1,0:T(8,128)(2,1)S(1)} %collective-permute-done.2.near_ref, bf16[256,256]{1,0:T(8,128)(2,1)S(1)} %collective-permute-done.3.far_ref, ...), custom_call_target="tpu_custom_call" | custom-call | flops 536870912 | bytes 4194304 | tf_op jit(solution)/shard_map/pallas_call | solution.py:41
  42.9 0.0 collective-permute-done.4.node_in_ref
  43.0 3.8 %all-to-all-start.1 = ((bf16[16,64,256]{2,1,0:T(8,128)(2,1)}), bf16[16,64,256]{2,1,0:T(8,128)(2,1)S(1)}, u32[]{:S(2)}, u32[]{:S(2)}) async-start(bf16[16,64,256]{2,1,0:T(8,128)(2,1)} %bitcast.5), calls=%async_computation.1 | async-start | bytes 1048576 | tf_op jit(solution)/shard_map/all_to_all | solution.py:514
  46.8 0.1 shard_map.121
  46.9 0.5 collective-permute-start.5
  47.3 1.0 %collective-permute-done.5.in_ref = bf16[512,128]{1,0:T(8,128)(2,1)S(1)} collective-permute-done((bf16[512,128]{1,0:T(8,128)(2,1)S(1)}, bf16[512,128]{1,0:T(8,128)(2,1)S(1)}, u32[]{:S(2)}, u32[]{:S(2)}) %collective-permute-start.5) | collective-permute-done | bytes 131104 | tf_op jit(solution)/shard_map/ppermute | solution.py:24
  48.4 1.9 %collective-permute-start.6 = (bf16[256,128]{1,0:T(8,128)(2,1)S(1)}, bf16[256,128]{1,0:T(8,128)(2,1)S(1)}, u32[]{:S(2)}, u32[]{:S(2)}) collective-permute-start(bf16[256,128]{1,0:T(8,128)(2,1)S(1)} %get-tuple-element.74), channel_id=1, source_target_pairs={{0,2},{1,3},{2,0},{3,1},{4,6},{5,7},{6,4},{7,5},{8,10},{9,11},{10,... | collective-permute-start | bytes 196616 | tf_op jit(solution)/shard_map/ppermute | solution.py:24
  50.3 4.1 %collective-permute-done.6.in_ref = bf16[256,128]{1,0:T(8,128)(2,1)S(1)} collective-permute-done((bf16[256,128]{1,0:T(8,128)(2,1)S(1)}, bf16[256,128]{1,0:T(8,128)(2,1)S(1)}, u32[]{:S(2)}, u32[]{:S(2)}) %collective-permute-start.6) | collective-permute-done | bytes 65568 | tf_op jit(solution)/shard_map/ppermute | solution.py:24
  54.4 1.9 %collective-permute-start.7 = (bf16[256,128]{1,0:T(8,128)(2,1)S(1)}, bf16[256,128]{1,0:T(8,128)(2,1)S(1)}, u32[]{:S(2)}, u32[]{:S(2)}) collective-permute-start(bf16[256,128]{1,0:T(8,128)(2,1)S(1)} %shard_map.123.mine_ref), channel_id=1, source_target_pairs={{0,4},{1,5},{2,6},{3,7},{4,0},{5,1},{6,2},{7,3},{8,12},{9,13},{10,... | collective-permute-start | bytes 196616 | tf_op jit(solution)/shard_map/ppermute | solution.py:24
  56.3 2.7 %collective-permute-done.7.in_ref = bf16[256,128]{1,0:T(8,128)(2,1)S(1)} collective-permute-done((bf16[256,128]{1,0:T(8,128)(2,1)S(1)}, bf16[256,128]{1,0:T(8,128)(2,1)S(1)}, u32[]{:S(2)}, u32[]{:S(2)}) %collective-permute-start.7) | collective-permute-done | bytes 65568 | tf_op jit(solution)/shard_map/ppermute | solution.py:24
  59.1 3.3 %collective-permute-start.8 = (bf16[256,128]{1,0:T(8,128)(2,1)S(1)}, bf16[256,128]{1,0:T(8,128)(2,1)S(1)}, u32[]{:S(2)}, u32[]{:S(2)}) collective-permute-start(bf16[256,128]{1,0:T(8,128)(2,1)S(1)} %shard_map.124.mine_ref), channel_id=1, source_target_pairs={{0,8},{1,9},{2,10},{3,11},{4,12},{5,13},{6,14},{7,15},{8,0},{9,1},... | collective-permute-start | bytes 196616 | tf_op jit(solution)/shard_map/ppermute | solution.py:24
  62.4 2.5 %collective-permute-done.8.in_ref = bf16[256,128]{1,0:T(8,128)(2,1)S(1)} collective-permute-done((bf16[256,128]{1,0:T(8,128)(2,1)S(1)}, bf16[256,128]{1,0:T(8,128)(2,1)S(1)}, u32[]{:S(2)}, u32[]{:S(2)}) %collective-permute-start.8) | collective-permute-done | bytes 65568 | tf_op jit(solution)/shard_map/ppermute | solution.py:24
  64.9 1.5 %collective-permute-start.10 = (bf16[256,128]{1,0:T(8,128)(2,1)S(1)}, bf16[256,128]{1,0:T(8,128)(2,1)S(1)}, u32[]{:S(2)}, u32[]{:S(2)}) collective-permute-start(bf16[256,128]{1,0:T(8,128)(2,1)S(1)} %shard_map.125.mine_ref), channel_id=1, source_target_pairs={{0,2},{1,3},{2,0},{3,1},{4,6},{5,7},{6,4},{7,5},{8,10},{9,11},{10,... | collective-permute-start | bytes 196616 | tf_op jit(solution)/shard_map/ppermute | solution.py:24
  66.4 1.5 %collective-permute-start.11 = (bf16[256,128]{1,0:T(8,128)(2,1)S(1)}, bf16[256,128]{1,0:T(8,128)(2,1)S(1)}, u32[]{:S(2)}, u32[]{:S(2)}) collective-permute-start(bf16[256,128]{1,0:T(8,128)(2,1)S(1)} %shard_map.125.mine_ref), channel_id=1, source_target_pairs={{0,18},{1,19},{2,16},{3,17},{4,22},{5,23},{6,20},{7,21},{8,26},{9,... | collective-permute-start | bytes 196616 | tf_op jit(solution)/shard_map/ppermute | solution.py:346
  67.9 0.5 collective-permute-start.9
  68.5 0.0 all-to-all-done.1
  68.5 0.0 copy-done.9
  68.5 1.5 %shard_map.126 = bf16[1024,256]{1,0:T(8,128)(2,1)} custom-call(s32[1,1024]{1,0:T(1,128)S(1)} %copy-done.9, bf16[1024,256]{1,0:T(8,128)(2,1)S(1)} %bitcast.18), custom_call_target="tpu_custom_call" | custom-call | flops 536870912 | bytes 1048576 | tf_op jit(solution)/shard_map/pallas_call | solution.py:41
  70.0 0.0 collective-permute-done.10.y_ref
  70.0 2.0 %collective-permute-done.11.both_ref = bf16[256,128]{1,0:T(8,128)(2,1)S(1)} collective-permute-done((bf16[256,128]{1,0:T(8,128)(2,1)S(1)}, bf16[256,128]{1,0:T(8,128)(2,1)S(1)}, u32[]{:S(2)}, u32[]{:S(2)}) %collective-permute-start.11) | collective-permute-done | bytes 65568 | tf_op jit(solution)/shard_map/ppermute | solution.py:346
  72.0 0.2 collective-permute-done.9.dp_ref
  72.2 0.1 shard_map.127.refs_0_
  72.3 0.1 collective-permute-start.12
  72.4 0.8 %shard_map.128 = (f32[256,256]{1,0:T(8,128)}, f32[512,256]{1,0:T(8,128)}) custom-call(bf16[384,256]{1,0:T(8,128)(2,1)S(1)} %shard_map.127.refs_0_), custom_call_target="tpu_custom_call" | custom-call | bytes 786432 | tf_op jit(solution)/shard_map/pallas_call | solution.py:327
  73.2 0.6 collective-permute-done.12.refs_0_
  73.8 0.8 %shard_map.129 = (f32[256,256]{1,0:T(8,128)}, f32[512,256]{1,0:T(8,128)}) custom-call(bf16[384,256]{1,0:T(8,128)(2,1)S(1)} %collective-permute-done.12.refs_0_, f32[256,256]{1,0:T(8,128)} %get-tuple-element.78.refs_1_, f32[512,256]{1,0:T(8,128)} %get-tuple-element.79.refs_2_), custom_call_target="tpu_custom_call", output_to_operand_aliasing={{0}: (1, {}), {1}: (2, {})} | custom-call | bytes 786432 | tf_op jit(solution)/shard_map/pallas_call | solution.py:327
  (6 shorter events, 0.1 us)
Async XLA Ops:
  0.6 28.3 %copy-start.3 = (bf16[1,1024,256]{2,1,0:T(8,128)(2,1)S(1)}, bf16[1,1024,256]{2,1,0:T(8,128)(2,1)}, u32[]{:S(2)}) copy-start(bf16[1,1024,256]{2,1,0:T(8,128)(2,1)} %param.15) | copy-start | bytes 1572868
  0.6 28.3 %copy-start.4 = (bf16[512,256]{1,0:T(8,128)(2,1)S(1)}, bf16[512,256]{1,0:T(8,128)(2,1)}, u32[]{:S(2)}) copy-start(bf16[512,256]{1,0:T(8,128)(2,1)} %w_node_ref.5) | copy-start | bytes 786436
  3.3 21.9 %all-to-all-start = ((bf16[16,64,256]{2,1,0:T(8,128)(2,1)}), bf16[16,64,256]{2,1,0:T(8,128)(2,1)S(1)}, u32[]{:S(2)}, u32[]{:S(2)}) async-start(bf16[16,64,256]{2,1,0:T(8,128)(2,1)} %bitcast.19), calls=%async_computation | async-start | bytes 1048576 | tf_op jit(solution)/shard_map/all_to_all | solution.py:438
  11.4 0.9 %copy-start.5 = (bf16[256,256]{1,0:T(8,128)(2,1)S(1)}, bf16[256,256]{1,0:T(8,128)(2,1)}, u32[]{:S(2)}) copy-start(bf16[256,256]{1,0:T(8,128)(2,1)} %w_edge_ref.5) | copy-start | bytes 393220
  12.3 1.2 %copy-start.7 = (bf16[8,4,128,128]{3,2,1,0:T(8,128)(2,1)S(1)}, bf16[8,4,128,128]{3,2,1,0:T(8,128)(2,1)}, u32[]{:S(2)}) copy-start(bf16[8,4,128,128]{3,2,1,0:T(8,128)(2,1)} %vals_ref.1) | copy-start | bytes 3145732
  13.5 0.7 copy-start.8
  16.8 2.4 %copy-start = (bf16[1024,2688]{1,0:T(8,128)(2,1)}, bf16[1024,2688]{1,0:T(8,128)(2,1)S(1)}, u32[]{:S(2)}) copy-start(bf16[1024,2688]{1,0:T(8,128)(2,1)S(1)} %get-tuple-element.43.adj_ref.at_ref) | copy-start | bytes 16515076
  26.0 6.9 %collective-permute-start = (bf16[256,256]{1,0:T(8,128)(2,1)S(1)}, bf16[256,256]{1,0:T(8,128)(2,1)S(1)}, u32[]{:S(2)}, u32[]{:S(2)}) collective-permute-start(bf16[256,256]{1,0:T(8,128)(2,1)S(1)} %shard_map.115), channel_id=1, source_target_pairs={{0,1},{1,0},{2,3},{3,2},{4,5},{5,4},{6,7},{7,6},{8,9},{9,8},{10,11... | collective-permute-start | bytes 393224 | tf_op jit(solution)/shard_map/ppermute | solution.py:24
  26.1 7.5 %collective-permute-start.1 = (bf16[256,256]{1,0:T(8,128)(2,1)S(1)}, bf16[256,256]{1,0:T(8,128)(2,1)S(1)}, u32[]{:S(2)}, u32[]{:S(2)}) collective-permute-start(bf16[256,256]{1,0:T(8,128)(2,1)S(1)} %get-tuple-element.49), channel_id=1, source_target_pairs={{0,15},{1,2},{2,1},{3,4},{4,3},{5,6},{6,5},{7,8},{8,7},{9,10},{10,... | collective-permute-start | bytes 393224 | tf_op jit(solution)/shard_map/ppermute | solution.py:29
  28.9 2.6 %copy-start.1 = (bf16[1024,2688]{1,0:T(8,128)(2,1)S(1)}, bf16[1024,2688]{1,0:T(8,128)(2,1)}, u32[]{:S(2)}) copy-start(bf16[1024,2688]{1,0:T(8,128)(2,1)} %copy-done) | copy-start | bytes 16515076
  31.5 7.2 %copy-start.2 = (bf16[1024,2688]{1,0:T(8,128)(2,1)S(1)}, bf16[1024,2688]{1,0:T(8,128)(2,1)}, u32[]{:S(2)}) copy-start(bf16[1024,2688]{1,0:T(8,128)(2,1)} %copy-done) | copy-start | bytes 16515076
  31.5 7.2 %copy-start.6 = (bf16[256,256]{1,0:T(8,128)(2,1)S(1)}, bf16[256,256]{1,0:T(8,128)(2,1)}, u32[]{:S(2)}) copy-start(bf16[256,256]{1,0:T(8,128)(2,1)} %w_edge_ref.5) | copy-start | bytes 393220
  33.5 6.8 %collective-permute-start.2 = (bf16[256,256]{1,0:T(8,128)(2,1)S(1)}, bf16[256,256]{1,0:T(8,128)(2,1)S(1)}, u32[]{:S(2)}, u32[]{:S(2)}) collective-permute-start(bf16[256,256]{1,0:T(8,128)(2,1)S(1)} %get-tuple-element.52.d_agg_near_ref), channel_id=1, source_target_pairs={{0,1},{1,0},{2,3},{3,2},{4,5},{5,4},{6,7},{7,6},{8,9},{9,8},{10,11... | collective-permute-start | bytes 393224 | tf_op jit(solution)/shard_map/ppermute | solution.py:24
  34.1 7.2 %collective-permute-start.3 = (bf16[256,256]{1,0:T(8,128)(2,1)S(1)}, bf16[256,256]{1,0:T(8,128)(2,1)S(1)}, u32[]{:S(2)}, u32[]{:S(2)}) collective-permute-start(bf16[256,256]{1,0:T(8,128)(2,1)S(1)} %get-tuple-element.53.d_agg_far_ref), channel_id=1, source_target_pairs={{0,15},{1,2},{2,1},{3,4},{4,3},{5,6},{6,5},{7,8},{8,7},{9,10},{10,... | collective-permute-start | bytes 393224 | tf_op jit(solution)/shard_map/ppermute | solution.py:29
  37.1 5.8 %collective-permute-start.4 = (bf16[512,128]{1,0:T(8,128)(2,1)S(1)}, bf16[512,128]{1,0:T(8,128)(2,1)S(1)}, u32[]{:S(2)}, u32[]{:S(2)}) collective-permute-start(bf16[512,128]{1,0:T(8,128)(2,1)S(1)} %get-tuple-element.69), channel_id=1, source_target_pairs={{0,16},{16,0},{1,17},{17,1},{2,18},{18,2},{3,19},{19,3},{4,20},{20... | collective-permute-start | bytes 393224 | tf_op jit(solution)/shard_map/ppermute | solution.py:24
  41.3 27.2 %copy-start.9 = (s32[1,1024]{1,0:T(1,128)S(1)}, s32[1,1024]{1,0:T(1,128)}, u32[]{:S(2)}) copy-start(s32[1,1024]{1,0:T(1,128)} %order_ref.1) | copy-start | bytes 12292
  43.0 25.5 %all-to-all-start.1 = ((bf16[16,64,256]{2,1,0:T(8,128)(2,1)}), bf16[16,64,256]{2,1,0:T(8,128)(2,1)S(1)}, u32[]{:S(2)}, u32[]{:S(2)}) async-start(bf16[16,64,256]{2,1,0:T(8,128)(2,1)} %bitcast.5), calls=%async_computation.1 | async-start | bytes 1048576 | tf_op jit(solution)/shard_map/all_to_all | solution.py:514
  46.9 1.5 %collective-permute-start.5 = (bf16[512,128]{1,0:T(8,128)(2,1)S(1)}, bf16[512,128]{1,0:T(8,128)(2,1)S(1)}, u32[]{:S(2)}, u32[]{:S(2)}) collective-permute-start(bf16[512,128]{1,0:T(8,128)(2,1)S(1)} %get-tuple-element.72), channel_id=1, source_target_pairs={{0,1},{1,0},{2,3},{3,2},{4,5},{5,4},{6,7},{7,6},{8,9},{9,8},{10,11... | collective-permute-start | bytes 393224 | tf_op jit(solution)/shard_map/ppermute | solution.py:24
  48.4 6.0 %collective-permute-start.6 = (bf16[256,128]{1,0:T(8,128)(2,1)S(1)}, bf16[256,128]{1,0:T(8,128)(2,1)S(1)}, u32[]{:S(2)}, u32[]{:S(2)}) collective-permute-start(bf16[256,128]{1,0:T(8,128)(2,1)S(1)} %get-tuple-element.74), channel_id=1, source_target_pairs={{0,2},{1,3},{2,0},{3,1},{4,6},{5,7},{6,4},{7,5},{8,10},{9,11},{10,... | collective-permute-start | bytes 196616 | tf_op jit(solution)/shard_map/ppermute | solution.py:24
  54.4 4.6 %collective-permute-start.7 = (bf16[256,128]{1,0:T(8,128)(2,1)S(1)}, bf16[256,128]{1,0:T(8,128)(2,1)S(1)}, u32[]{:S(2)}, u32[]{:S(2)}) collective-permute-start(bf16[256,128]{1,0:T(8,128)(2,1)S(1)} %shard_map.123.mine_ref), channel_id=1, source_target_pairs={{0,4},{1,5},{2,6},{3,7},{4,0},{5,1},{6,2},{7,3},{8,12},{9,13},{10,... | collective-permute-start | bytes 196616 | tf_op jit(solution)/shard_map/ppermute | solution.py:24
  59.1 5.8 %collective-permute-start.8 = (bf16[256,128]{1,0:T(8,128)(2,1)S(1)}, bf16[256,128]{1,0:T(8,128)(2,1)S(1)}, u32[]{:S(2)}, u32[]{:S(2)}) collective-permute-start(bf16[256,128]{1,0:T(8,128)(2,1)S(1)} %shard_map.124.mine_ref), channel_id=1, source_target_pairs={{0,8},{1,9},{2,10},{3,11},{4,12},{5,13},{6,14},{7,15},{8,0},{9,1},... | collective-permute-start | bytes 196616 | tf_op jit(solution)/shard_map/ppermute | solution.py:24
  64.9 5.1 %collective-permute-start.10 = (bf16[256,128]{1,0:T(8,128)(2,1)S(1)}, bf16[256,128]{1,0:T(8,128)(2,1)S(1)}, u32[]{:S(2)}, u32[]{:S(2)}) collective-permute-start(bf16[256,128]{1,0:T(8,128)(2,1)S(1)} %shard_map.125.mine_ref), channel_id=1, source_target_pairs={{0,2},{1,3},{2,0},{3,1},{4,6},{5,7},{6,4},{7,5},{8,10},{9,11},{10,... | collective-permute-start | bytes 196616 | tf_op jit(solution)/shard_map/ppermute | solution.py:24
  66.4 5.6 %collective-permute-start.11 = (bf16[256,128]{1,0:T(8,128)(2,1)S(1)}, bf16[256,128]{1,0:T(8,128)(2,1)S(1)}, u32[]{:S(2)}, u32[]{:S(2)}) collective-permute-start(bf16[256,128]{1,0:T(8,128)(2,1)S(1)} %shard_map.125.mine_ref), channel_id=1, source_target_pairs={{0,18},{1,19},{2,16},{3,17},{4,22},{5,23},{6,20},{7,21},{8,26},{9,... | collective-permute-start | bytes 196616 | tf_op jit(solution)/shard_map/ppermute | solution.py:346
  67.9 4.3 %collective-permute-start.9 = (bf16[256,128]{1,0:T(8,128)(2,1)S(1)}, bf16[256,128]{1,0:T(8,128)(2,1)S(1)}, u32[]{:S(2)}, u32[]{:S(2)}) collective-permute-start(bf16[256,128]{1,0:T(8,128)(2,1)S(1)} %shard_map.125.mine_ref), channel_id=1, source_target_pairs={{0,16},{16,0},{1,17},{17,1},{2,18},{18,2},{3,19},{19,3},{4,20},{20... | collective-permute-start | bytes 196616 | tf_op jit(solution)/shard_map/ppermute | solution.py:24
  72.3 1.5 %collective-permute-start.12 = (bf16[384,256]{1,0:T(8,128)(2,1)S(1)}, bf16[384,256]{1,0:T(8,128)(2,1)S(1)}, u32[]{:S(2)}, u32[]{:S(2)}) collective-permute-start(bf16[384,256]{1,0:T(8,128)(2,1)S(1)} %shard_map.127.refs_0_), channel_id=1, source_target_pairs={{0,1},{1,0},{2,3},{3,2},{4,5},{5,4},{6,7},{7,6},{8,9},{9,8},{10,11... | collective-permute-start | bytes 589832 | tf_op jit(solution)/shard_map/ppermute | solution.py:24

commit v10 on v9

--- a/solution.py
+++ b/solution.py
@@ -126,10 +126,6 @@
     return pl.ds(pl.multiple_of((odd if far else 1 - odd) * start, ROWS), RIM * ROWS)
 
 
-def near_body(a_ref, msg_ref, near_ref):
-    near_ref[...] = dot(a_ref[end_of(False, RIM * ROWS), :], msg_ref[...]).astype(BF16)
-
-
 def node_step(nodes, agg, gout, w_node):
     width = nodes.shape[1]
     pre = dot(nodes, w_node[:width]) + dot(agg, w_node[width:])
@@ -142,12 +138,13 @@
 
 
 def own_body(
-    nodes_ref, msg_ref, adj_ref, cot_ref, w_node_ref,
-    own_ref, out_ref, agg_ref, d_node_ref, d_nodes1_ref, d_agg_ref,
+    nodes_ref, msg_ref, adj_ref, rims_ref, cot_ref, w_node_ref,
+    near_ref, own_ref, out_ref, agg_ref, d_node_ref, d_nodes1_ref, d_agg_ref,
 ):
     rows, width = nodes_ref.shape
     rim = RIM * ROWS
     msg = msg_ref[...]
+    near_ref[...] = dot(rims_ref[end_of(False, rim), :], msg).astype(BF16)
     first = adj_ref.shape[1] - rows
     for k in range(rows // rim):
         mine = slice(k * rim, (k + 1) * rim)
@@ -451,18 +448,19 @@
         message_body, [edge, tall], (nodes, adj_rim), flops=square + 2 * rim * rows * width, nbytes=4 * unit
     )
     far = swapped_across(far, "dom")
-    (near,) = call(near_body, [edge], (adj_rim, msg), flops=2 * rim * rows * width, nbytes=unit)
-    near = swapped(near, "dom", 1)
     cot = cotangent[0]
-    own, out_mid, agg_mid, d_node_mid, d_nodes1_mid, d_agg_mid = call(
+    near, own, out_mid, agg_mid, d_node_mid, d_nodes1_mid, d_agg_mid = call(
         own_body,
-        [rims, mid, mid, mid, shape(*mid.shape, dtype=F32), mid],
-        (nodes, msg, adj, cot, w_node),
+        [edge, rims, mid, mid, mid, shape(*mid.shape, dtype=F32), mid],
+        (nodes, msg, adj, adj_rim, cot, w_node),
         flops=2 * rows * rows * width + 2 * square,
         nbytes=8 * unit,
     )
+    near = swapped(near, "dom", 1)
     ends = []
     for is_far, arrived in ((True, far), (False, near)):
+        if not is_far:
+            arrived, ends[0] = lax.optimization_barrier((arrived, ends[0]))
         ends.append(
             call(
                 functools.partial(rim_body, is_far),

time: 75 us -> 75.1 us (level)
  waiting for transfers between devices: 20.1 us -> 21.2 us
    pallas_call x17 -> x16, Pallas kernels: 14.1 us -> 13.7 us  [call(): pl.pallas_call(body, out_shape=outs, in_specs=specs or [VMEM] * len(args)...]
  transfers between devices with their start and end apart: 15 -> 15, of which waited for: 9 -> 11; matrix products, arithmetic and copies ran while one was open for 1% -> 1% of each run, Pallas kernels for 15% -> 14%
where the time goes in v10:
time: 75.1 us; the launch traced here: 74.7 us
  starting transfers between devices  28.9 us (38%)
  waiting for transfers between devices  21.2 us (28%)
  Pallas kernels  15.3 us (20%)
  local copies, waits for them, and re-layouts  8.53 us (11%)
  between operations  0.81 us (1%)
    pallas_call x16, Pallas kernels, call(): pl.pallas_call(body, out_shape=outs, in_specs=specs or [VMEM] * len(args)...  13.7 us
    ppermute x10, waiting for transfers between devices, swapped(): return lax.ppermute(x, axis, [(i, i ^ mask) for i in range(peers)])  11.6 us
    ppermute x10, starting transfers between devices, swapped(): return lax.ppermute(x, axis, [(i, i ^ mask) for i in range(peers)])  11.5 us
    unnamed x21, local copies, waits for them, and re-layouts  8.53 us
    all_to_all x1, starting transfers between devices, shards(): lax.all_to_all(picked.reshape(ndom, per_peer, width), 'dom', split_axis=0...  7.39 us
    all_to_all x1, waiting for transfers between devices, shards(): lax.all_to_all(picked.reshape(ndom, per_peer, width), 'dom', split_axis=0...  5.95 us
    ppermute x2, starting transfers between devices, swapped_across(): lax.ppermute(x, axis, [(i, (i + 1 if i % 2 else i - 1) % peers) for i in...  4.86 us
    all_to_all x1, starting transfers between devices, shards(): lax.all_to_all(back.reshape(ndom, per_peer, width), 'dom', split_axis=0,...  3.59 us
  transfers between devices with their start and end apart: 15, of which 11 were waited for; matrix products, arithmetic and copies ran while one was open for 1% of the time, Pallas kernels for 14%

profile of v10, /device:TPU:0, one launch (start us, length us, event | category | flops | bytes accessed | tf_op | source)
XLA Modules:
  0.0 74.7 jit_solution(15892645660222721370)
XLA Ops:
  0.6 0.0 copy-start.3
  0.6 0.0 copy-start.4
  0.7 2.6 %shard_map.111 = bf16[1024,256]{1,0:T(8,128)(2,1)} custom-call(s32[1,1024]{1,0:T(1,128)} %order_ref.1, bf16[1024,256]{1,0:T(8,128)(2,1)} %bitcast.20), custom_call_target="tpu_custom_call" | custom-call | flops 536870912 | bytes 1048576 | tf_op jit(solution)/shard_map/pallas_call | solution.py:41
  3.3 7.4 %all-to-all-start = ((bf16[16,64,256]{2,1,0:T(8,128)(2,1)}), bf16[16,64,256]{2,1,0:T(8,128)(2,1)S(1)}, u32[]{:S(2)}, u32[]{:S(2)}) async-start(bf16[16,64,256]{2,1,0:T(8,128)(2,1)} %bitcast.19), calls=%async_computation | async-start | bytes 1048576 | tf_op jit(solution)/shard_map/all_to_all | solution.py:435
  10.7 0.8 %copy.14.tgt_ref = s32[8,4]{1,0:T(8,128)S(1)} copy(s32[8,4]{0,1:T(4,128)} %param.11) | data formatting | bytes 256 | tf_op args[3]
  11.4 0.0 copy-start.5
  11.4 0.9 %copy-done.5 = bf16[256,256]{1,0:T(8,128)(2,1)S(1)} copy-done((bf16[256,256]{1,0:T(8,128)(2,1)S(1)}, bf16[256,256]{1,0:T(8,128)(2,1)}, u32[]{:S(2)}) %copy-start.5) | copy-done | bytes 131096
  12.3 0.0 copy-start.7
  12.3 1.2 %copy-done.7 = bf16[8,4,128,128]{3,2,1,0:T(8,128)(2,1)S(1)} copy-done((bf16[8,4,128,128]{3,2,1,0:T(8,128)(2,1)S(1)}, bf16[8,4,128,128]{3,2,1,0:T(8,128)(2,1)}, u32[]{:S(2)}) %copy-start.7) | copy-done | bytes 1048600
  13.5 0.0 copy-start.8
  13.5 0.7 copy-done.8
  14.2 2.5 %shard_map.112 = (bf16[768,1024]{1,0:T(8,128)(2,1)S(1)}, bf16[1024,2688]{1,0:T(8,128)(2,1)S(1)}) custom-call(s32[8]{0:T(128)S(1)} %copy-done.8, s32[8,4]{1,0:T(8,128)S(1)} %copy.14.tgt_ref, bf16[8,4,128,128]{3,2,1,0:T(8,128)(2,1)S(1)} %copy-done.7, bf16[256,256]{1,0:T(8,128)(2,1)S(1)} %copy-done.5), custom_call_target="tpu_custom_call" | custom-call | bytes 8388608 | tf_op jit(solution)/shard_map/pallas_call | solution.py:41
  16.8 0.0 copy-start
  16.8 2.4 %copy-done = bf16[1024,2688]{1,0:T(8,128)(2,1)} copy-done((bf16[1024,2688]{1,0:T(8,128)(2,1)}, bf16[1024,2688]{1,0:T(8,128)(2,1)S(1)}, u32[]{:S(2)}) %copy-start) | copy-done | bytes 5505048
  19.2 6.0 %all-to-all-done = bf16[16,64,256]{2,1,0:T(8,128)(2,1)S(1)} async-done(((bf16[16,64,256]{2,1,0:T(8,128)(2,1)}), bf16[16,64,256]{2,1,0:T(8,128)(2,1)S(1)}, u32[]{:S(2)}, u32[]{:S(2)}) %all-to-all-start) | async-done | bytes 524320 | tf_op jit(solution)/shard_map/all_to_all | solution.py:435
  25.1 0.6 shard_map.113
  25.7 2.7 %collective-permute-start.1 = (bf16[256,256]{1,0:T(8,128)(2,1)S(1)}, bf16[256,256]{1,0:T(8,128)(2,1)S(1)}, u32[]{:S(2)}, u32[]{:S(2)}) collective-permute-start(bf16[256,256]{1,0:T(8,128)(2,1)S(1)} %get-tuple-element.56), channel_id=1, source_target_pairs={{0,15},{1,2},{2,1},{3,4},{4,3},{5,6},{6,5},{7,8},{8,7},{9,10},{10,... | collective-permute-start | bytes 393224 | tf_op jit(solution)/shard_map/ppermute | solution.py:29
  28.4 0.0 copy-done.3
  28.4 0.0 copy-done.4
  28.4 0.0 copy-start.1
  28.4 2.6 %copy-done.1 = bf16[1024,2688]{1,0:T(8,128)(2,1)S(1)} copy-done((bf16[1024,2688]{1,0:T(8,128)(2,1)S(1)}, bf16[1024,2688]{1,0:T(8,128)(2,1)}, u32[]{:S(2)}) %copy-start.1) | copy-done | bytes 5505048
  31.0 0.0 copy-start.2
  31.0 0.0 copy-start.6
  31.0 1.4 %shard_map.114 = (bf16[256,256]{1,0:T(8,128)(2,1)S(1)}, bf16[512,256]{1,0:T(8,128)(2,1)S(1)}, bf16[512,256]{1,0:T(8,128)(2,1)S(1)}, bf16[512,256]{1,0:T(8,128)(2...) custom-call(bf16[1024,256]{1,0:T(8,128)(2,1)S(1)} %bitcast.9, ...), custom_call_target="tpu_custom_call" | custom-call | flops 805306368 | bytes 4194304 | tf_op jit(solution)/shard_map/pallas_call | solution.py:41
  32.4 0.1 collective-permute-start
  32.5 0.4 collective-permute-done.1.in_ref
  32.9 0.5 shard_map.115
  33.4 0.4 collective-permute-done.in_ref
  33.8 0.5 shard_map.116
  34.3 0.2 collective-permute-start.2
  34.5 2.2 %collective-permute-start.3 = (bf16[256,256]{1,0:T(8,128)(2,1)S(1)}, bf16[256,256]{1,0:T(8,128)(2,1)S(1)}, u32[]{:S(2)}, u32[]{:S(2)}) collective-permute-start(bf16[256,256]{1,0:T(8,128)(2,1)S(1)} %get-tuple-element.67.d_agg_far_ref), channel_id=1, source_target_pairs={{0,15},{1,2},{2,1},{3,4},{4,3},{5,6},{6,5},{7,8},{8,7},{9,10},{10,... | collective-permute-start | bytes 393224 | tf_op jit(solution)/shard_map/ppermute | solution.py:29
  36.7 0.5 shard_map.119
  37.2 1.6 %collective-permute-start.4 = (bf16[512,128]{1,0:T(8,128)(2,1)S(1)}, bf16[512,128]{1,0:T(8,128)(2,1)S(1)}, u32[]{:S(2)}, u32[]{:S(2)}) collective-permute-start(bf16[512,128]{1,0:T(8,128)(2,1)S(1)} %get-tuple-element.83), channel_id=1, source_target_pairs={{0,16},{16,0},{1,17},{17,1},{2,18},{18,2},{3,19},{19,3},{4,20},{20... | collective-permute-start | bytes 393224 | tf_op jit(solution)/shard_map/ppermute | solution.py:24
  38.8 0.0 copy-done.2
  38.8 0.0 copy-done.6
  38.8 1.7 %shard_map.117 = (bf16[1024,256]{1,0:T(8,128)(2,1)}, f32[1024,256]{1,0:T(8,128)S(1)}, f32[1024,256]{1,0:T(8,128)S(1)}) custom-call(bf16[1024,256]{1,0:T(8,128)(2,1)S(1)} %bitcast.13, bf16[1024,2688]{1,0:T(8,128)(2,1)S(1)} %copy-done.2, bf16[256,256]{1,0:T(8,128)(2,1)S(1)} %copy-done.6, bf16[512,256]{1,0:T(8,128)(2,1)S(1)} %get-tuple-element.53.out_mid_ref, ...), custom_call_target="tpu_custom_call" | custom-call | flops 671088640 | bytes 4194304 | tf_op jit(solution)/shard_map/pallas_call | solution.py:41
  40.4 0.0 collective-permute-done.2.near_ref
  40.4 1.2 %collective-permute-done.3.far_ref = bf16[256,256]{1,0:T(8,128)(2,1)S(1)} collective-permute-done((bf16[256,256]{1,0:T(8,128)(2,1)S(1)}, bf16[256,256]{1,0:T(8,128)(2,1)S(1)}, u32[]{:S(2)}, u32[]{:S(2)}) %collective-permute-start.3) | collective-permute-done | bytes 131104 | tf_op jit(solution)/shard_map/ppermute | solution.py:29
  41.6 1.6 %shard_map.118 = (bf16[1024,256]{1,0:T(8,128)(2,1)}, f32[256,256]{1,0:T(8,128)S(1)}) custom-call(bf16[1024,256]{1,0:T(8,128)(2,1)S(1)} %bitcast.14, bf16[1024,2688]{1,0:T(8,128)(2,1)S(1)} %copy-done.2, bf16[256,256]{1,0:T(8,128)(2,1)S(1)} %collective-permute-done.2.near_ref, bf16[256,256]{1,0:T(8,128)(2,1)S(1)} %collective-permute-done.3.far_ref, ...), custom_call_target="tpu_custom_call" | custom-call | flops 536870912 | bytes 4194304 | tf_op jit(solution)/shard_map/pallas_call | solution.py:41
  43.3 0.0 collective-permute-done.4.node_in_ref
  43.3 3.6 %all-to-all-start.1 = ((bf16[16,64,256]{2,1,0:T(8,128)(2,1)}), bf16[16,64,256]{2,1,0:T(8,128)(2,1)S(1)}, u32[]{:S(2)}, u32[]{:S(2)}) async-start(bf16[16,64,256]{2,1,0:T(8,128)(2,1)} %bitcast.5), calls=%async_computation.1 | async-start | bytes 1048576 | tf_op jit(solution)/shard_map/all_to_all | solution.py:512
  46.9 0.1 shard_map.120
  47.0 0.4 collective-permute-start.5
  47.4 1.0 %collective-permute-done.5.in_ref = bf16[512,128]{1,0:T(8,128)(2,1)S(1)} collective-permute-done((bf16[512,128]{1,0:T(8,128)(2,1)S(1)}, bf16[512,128]{1,0:T(8,128)(2,1)S(1)}, u32[]{:S(2)}, u32[]{:S(2)}) %collective-permute-start.5) | collective-permute-done | bytes 131104 | tf_op jit(solution)/shard_map/ppermute | solution.py:24
  48.4 1.9 %collective-permute-start.6 = (bf16[256,128]{1,0:T(8,128)(2,1)S(1)}, bf16[256,128]{1,0:T(8,128)(2,1)S(1)}, u32[]{:S(2)}, u32[]{:S(2)}) collective-permute-start(bf16[256,128]{1,0:T(8,128)(2,1)S(1)} %get-tuple-element.88), channel_id=1, source_target_pairs={{0,2},{1,3},{2,0},{3,1},{4,6},{5,7},{6,4},{7,5},{8,10},{9,11},{10,... | collective-permute-start | bytes 196616 | tf_op jit(solution)/shard_map/ppermute | solution.py:24
  50.4 4.1 %collective-permute-done.6.in_ref = bf16[256,128]{1,0:T(8,128)(2,1)S(1)} collective-permute-done((bf16[256,128]{1,0:T(8,128)(2,1)S(1)}, bf16[256,128]{1,0:T(8,128)(2,1)S(1)}, u32[]{:S(2)}, u32[]{:S(2)}) %collective-permute-start.6) | collective-permute-done | bytes 65568 | tf_op jit(solution)/shard_map/ppermute | solution.py:24
  54.5 1.9 %collective-permute-start.7 = (bf16[256,128]{1,0:T(8,128)(2,1)S(1)}, bf16[256,128]{1,0:T(8,128)(2,1)S(1)}, u32[]{:S(2)}, u32[]{:S(2)}) collective-permute-start(bf16[256,128]{1,0:T(8,128)(2,1)S(1)} %shard_map.122.mine_ref), channel_id=1, source_target_pairs={{0,4},{1,5},{2,6},{3,7},{4,0},{5,1},{6,2},{7,3},{8,12},{9,13},{10,... | collective-permute-start | bytes 196616 | tf_op jit(solution)/shard_map/ppermute | solution.py:24
  56.4 2.7 %collective-permute-done.7.in_ref = bf16[256,128]{1,0:T(8,128)(2,1)S(1)} collective-permute-done((bf16[256,128]{1,0:T(8,128)(2,1)S(1)}, bf16[256,128]{1,0:T(8,128)(2,1)S(1)}, u32[]{:S(2)}, u32[]{:S(2)}) %collective-permute-start.7) | collective-permute-done | bytes 65568 | tf_op jit(solution)/shard_map/ppermute | solution.py:24
  59.1 3.3 %collective-permute-start.8 = (bf16[256,128]{1,0:T(8,128)(2,1)S(1)}, bf16[256,128]{1,0:T(8,128)(2,1)S(1)}, u32[]{:S(2)}, u32[]{:S(2)}) collective-permute-start(bf16[256,128]{1,0:T(8,128)(2,1)S(1)} %shard_map.123.mine_ref), channel_id=1, source_target_pairs={{0,8},{1,9},{2,10},{3,11},{4,12},{5,13},{6,14},{7,15},{8,0},{9,1},... | collective-permute-start | bytes 196616 | tf_op jit(solution)/shard_map/ppermute | solution.py:24
  62.4 2.5 %collective-permute-done.8.in_ref = bf16[256,128]{1,0:T(8,128)(2,1)S(1)} collective-permute-done((bf16[256,128]{1,0:T(8,128)(2,1)S(1)}, bf16[256,128]{1,0:T(8,128)(2,1)S(1)}, u32[]{:S(2)}, u32[]{:S(2)}) %collective-permute-start.8) | collective-permute-done | bytes 65568 | tf_op jit(solution)/shard_map/ppermute | solution.py:24
  65.0 1.5 %collective-permute-start.10 = (bf16[256,128]{1,0:T(8,128)(2,1)S(1)}, bf16[256,128]{1,0:T(8,128)(2,1)S(1)}, u32[]{:S(2)}, u32[]{:S(2)}) collective-permute-start(bf16[256,128]{1,0:T(8,128)(2,1)S(1)} %shard_map.124.mine_ref), channel_id=1, source_target_pairs={{0,2},{1,3},{2,0},{3,1},{4,6},{5,7},{6,4},{7,5},{8,10},{9,11},{10,... | collective-permute-start | bytes 196616 | tf_op jit(solution)/shard_map/ppermute | solution.py:24
  66.5 1.5 %collective-permute-start.11 = (bf16[256,128]{1,0:T(8,128)(2,1)S(1)}, bf16[256,128]{1,0:T(8,128)(2,1)S(1)}, u32[]{:S(2)}, u32[]{:S(2)}) collective-permute-start(bf16[256,128]{1,0:T(8,128)(2,1)S(1)} %shard_map.124.mine_ref), channel_id=1, source_target_pairs={{0,18},{1,19},{2,16},{3,17},{4,22},{5,23},{6,20},{7,21},{8,26},{9,... | collective-permute-start | bytes 196616 | tf_op jit(solution)/shard_map/ppermute | solution.py:343
  68.0 0.5 collective-permute-start.9
  68.6 0.0 all-to-all-done.1
  68.6 0.0 copy-done.9
  68.6 1.5 %shard_map.125 = bf16[1024,256]{1,0:T(8,128)(2,1)} custom-call(s32[1,1024]{1,0:T(1,128)S(1)} %copy-done.9, bf16[1024,256]{1,0:T(8,128)(2,1)S(1)} %bitcast.18), custom_call_target="tpu_custom_call" | custom-call | flops 536870912 | bytes 1048576 | tf_op jit(solution)/shard_map/pallas_call | solution.py:41
  70.1 0.0 collective-permute-done.10.y_ref
  70.1 2.0 %collective-permute-done.11.both_ref = bf16[256,128]{1,0:T(8,128)(2,1)S(1)} collective-permute-done((bf16[256,128]{1,0:T(8,128)(2,1)S(1)}, bf16[256,128]{1,0:T(8,128)(2,1)S(1)}, u32[]{:S(2)}, u32[]{:S(2)}) %collective-permute-start.11) | collective-permute-done | bytes 65568 | tf_op jit(solution)/shard_map/ppermute | solution.py:343
  72.1 0.2 collective-permute-done.9.dp_ref
  72.3 0.1 shard_map.126.refs_0_
  72.4 0.1 collective-permute-start.12
  72.5 0.8 %shard_map.127 = (f32[256,256]{1,0:T(8,128)}, f32[512,256]{1,0:T(8,128)}) custom-call(bf16[384,256]{1,0:T(8,128)(2,1)S(1)} %shard_map.126.refs_0_), custom_call_target="tpu_custom_call" | custom-call | bytes 786432 | tf_op jit(solution)/shard_map/pallas_call | solution.py:324
  73.2 0.6 collective-permute-done.12.refs_0_
  73.9 0.8 %shard_map.128 = (f32[256,256]{1,0:T(8,128)}, f32[512,256]{1,0:T(8,128)}) custom-call(bf16[384,256]{1,0:T(8,128)(2,1)S(1)} %collective-permute-done.12.refs_0_, f32[256,256]{1,0:T(8,128)} %get-tuple-element.92.refs_1_, f32[512,256]{1,0:T(8,128)} %get-tuple-element.93.refs_2_), custom_call_target="tpu_custom_call", output_to_operand_aliasing={{0}: (1, {}), {1}: (2, {})} | custom-call | bytes 786432 | tf_op jit(solution)/shard_map/pallas_call | solution.py:324
  (5 shorter events, 0.1 us)
Async XLA Ops:
  0.6 27.8 %copy-start.3 = (bf16[1,1024,256]{2,1,0:T(8,128)(2,1)S(1)}, bf16[1,1024,256]{2,1,0:T(8,128)(2,1)}, u32[]{:S(2)}) copy-start(bf16[1,1024,256]{2,1,0:T(8,128)(2,1)} %param.15) | copy-start | bytes 1572868
  0.6 27.8 %copy-start.4 = (bf16[512,256]{1,0:T(8,128)(2,1)S(1)}, bf16[512,256]{1,0:T(8,128)(2,1)}, u32[]{:S(2)}) copy-start(bf16[512,256]{1,0:T(8,128)(2,1)} %w_node_ref.5) | copy-start | bytes 786436
  3.3 21.9 %all-to-all-start = ((bf16[16,64,256]{2,1,0:T(8,128)(2,1)}), bf16[16,64,256]{2,1,0:T(8,128)(2,1)S(1)}, u32[]{:S(2)}, u32[]{:S(2)}) async-start(bf16[16,64,256]{2,1,0:T(8,128)(2,1)} %bitcast.19), calls=%async_computation | async-start | bytes 1048576 | tf_op jit(solution)/shard_map/all_to_all | solution.py:435
  11.4 0.9 %copy-start.5 = (bf16[256,256]{1,0:T(8,128)(2,1)S(1)}, bf16[256,256]{1,0:T(8,128)(2,1)}, u32[]{:S(2)}) copy-start(bf16[256,256]{1,0:T(8,128)(2,1)} %w_edge_ref.5) | copy-start | bytes 393220
  12.3 1.2 %copy-start.7 = (bf16[8,4,128,128]{3,2,1,0:T(8,128)(2,1)S(1)}, bf16[8,4,128,128]{3,2,1,0:T(8,128)(2,1)}, u32[]{:S(2)}) copy-start(bf16[8,4,128,128]{3,2,1,0:T(8,128)(2,1)} %vals_ref.1) | copy-start | bytes 3145732
  13.5 0.7 copy-start.8
  16.8 2.4 %copy-start = (bf16[1024,2688]{1,0:T(8,128)(2,1)}, bf16[1024,2688]{1,0:T(8,128)(2,1)S(1)}, u32[]{:S(2)}) copy-start(bf16[1024,2688]{1,0:T(8,128)(2,1)S(1)} %get-tuple-element.50.adj_ref.at_ref) | copy-start | bytes 16515076
  25.7 7.2 %collective-permute-start.1 = (bf16[256,256]{1,0:T(8,128)(2,1)S(1)}, bf16[256,256]{1,0:T(8,128)(2,1)S(1)}, u32[]{:S(2)}, u32[]{:S(2)}) collective-permute-start(bf16[256,256]{1,0:T(8,128)(2,1)S(1)} %get-tuple-element.56), channel_id=1, source_target_pairs={{0,15},{1,2},{2,1},{3,4},{4,3},{5,6},{6,5},{7,8},{8,7},{9,10},{10,... | collective-permute-start | bytes 393224 | tf_op jit(solution)/shard_map/ppermute | solution.py:29
  28.4 2.6 %copy-start.1 = (bf16[1024,2688]{1,0:T(8,128)(2,1)S(1)}, bf16[1024,2688]{1,0:T(8,128)(2,1)}, u32[]{:S(2)}) copy-start(bf16[1024,2688]{1,0:T(8,128)(2,1)} %copy-done) | copy-start | bytes 16515076
  31.0 7.8 %copy-start.2 = (bf16[1024,2688]{1,0:T(8,128)(2,1)S(1)}, bf16[1024,2688]{1,0:T(8,128)(2,1)}, u32[]{:S(2)}) copy-start(bf16[1024,2688]{1,0:T(8,128)(2,1)} %copy-done) | copy-start | bytes 16515076
  31.0 7.8 %copy-start.6 = (bf16[256,256]{1,0:T(8,128)(2,1)S(1)}, bf16[256,256]{1,0:T(8,128)(2,1)}, u32[]{:S(2)}) copy-start(bf16[256,256]{1,0:T(8,128)(2,1)} %w_edge_ref.5) | copy-start | bytes 393220
  32.4 1.4 %collective-permute-start = (bf16[256,256]{1,0:T(8,128)(2,1)S(1)}, bf16[256,256]{1,0:T(8,128)(2,1)S(1)}, u32[]{:S(2)}, u32[]{:S(2)}) collective-permute-start(bf16[256,256]{1,0:T(8,128)(2,1)S(1)} %get-tuple-element.55), channel_id=1, source_target_pairs={{0,1},{1,0},{2,3},{3,2},{4,5},{5,4},{6,7},{7,6},{8,9},{9,8},{10,11... | collective-permute-start | bytes 393224 | tf_op jit(solution)/shard_map/ppermute | solution.py:24
  34.3 6.1 %collective-permute-start.2 = (bf16[256,256]{1,0:T(8,128)(2,1)S(1)}, bf16[256,256]{1,0:T(8,128)(2,1)S(1)}, u32[]{:S(2)}, u32[]{:S(2)}) collective-permute-start(bf16[256,256]{1,0:T(8,128)(2,1)S(1)} %get-tuple-element.66.d_agg_near_ref), channel_id=1, source_target_pairs={{0,1},{1,0},{2,3},{3,2},{4,5},{5,4},{6,7},{7,6},{8,9},{9,8},{10,11... | collective-permute-start | bytes 393224 | tf_op jit(solution)/shard_map/ppermute | solution.py:24
  34.5 7.1 %collective-permute-start.3 = (bf16[256,256]{1,0:T(8,128)(2,1)S(1)}, bf16[256,256]{1,0:T(8,128)(2,1)S(1)}, u32[]{:S(2)}, u32[]{:S(2)}) collective-permute-start(bf16[256,256]{1,0:T(8,128)(2,1)S(1)} %get-tuple-element.67.d_agg_far_ref), channel_id=1, source_target_pairs={{0,15},{1,2},{2,1},{3,4},{4,3},{5,6},{6,5},{7,8},{8,7},{9,10},{10,... | collective-permute-start | bytes 393224 | tf_op jit(solution)/shard_map/ppermute | solution.py:29
  37.2 6.1 %collective-permute-start.4 = (bf16[512,128]{1,0:T(8,128)(2,1)S(1)}, bf16[512,128]{1,0:T(8,128)(2,1)S(1)}, u32[]{:S(2)}, u32[]{:S(2)}) collective-permute-start(bf16[512,128]{1,0:T(8,128)(2,1)S(1)} %get-tuple-element.83), channel_id=1, source_target_pairs={{0,16},{16,0},{1,17},{17,1},{2,18},{18,2},{3,19},{19,3},{4,20},{20... | collective-permute-start | bytes 393224 | tf_op jit(solution)/shard_map/ppermute | solution.py:24
  41.6 26.9 %copy-start.9 = (s32[1,1024]{1,0:T(1,128)S(1)}, s32[1,1024]{1,0:T(1,128)}, u32[]{:S(2)}) copy-start(s32[1,1024]{1,0:T(1,128)} %order_ref.1) | copy-start | bytes 12292
  43.3 25.3 %all-to-all-start.1 = ((bf16[16,64,256]{2,1,0:T(8,128)(2,1)}), bf16[16,64,256]{2,1,0:T(8,128)(2,1)S(1)}, u32[]{:S(2)}, u32[]{:S(2)}) async-start(bf16[16,64,256]{2,1,0:T(8,128)(2,1)} %bitcast.5), calls=%async_computation.1 | async-start | bytes 1048576 | tf_op jit(solution)/shard_map/all_to_all | solution.py:512
  47.0 1.4 %collective-permute-start.5 = (bf16[512,128]{1,0:T(8,128)(2,1)S(1)}, bf16[512,128]{1,0:T(8,128)(2,1)S(1)}, u32[]{:S(2)}, u32[]{:S(2)}) collective-permute-start(bf16[512,128]{1,0:T(8,128)(2,1)S(1)} %get-tuple-element.86), channel_id=1, source_target_pairs={{0,1},{1,0},{2,3},{3,2},{4,5},{5,4},{6,7},{7,6},{8,9},{9,8},{10,11... | collective-permute-start | bytes 393224 | tf_op jit(solution)/shard_map/ppermute | solution.py:24
  48.4 6.0 %collective-permute-start.6 = (bf16[256,128]{1,0:T(8,128)(2,1)S(1)}, bf16[256,128]{1,0:T(8,128)(2,1)S(1)}, u32[]{:S(2)}, u32[]{:S(2)}) collective-permute-start(bf16[256,128]{1,0:T(8,128)(2,1)S(1)} %get-tuple-element.88), channel_id=1, source_target_pairs={{0,2},{1,3},{2,0},{3,1},{4,6},{5,7},{6,4},{7,5},{8,10},{9,11},{10,... | collective-permute-start | bytes 196616 | tf_op jit(solution)/shard_map/ppermute | solution.py:24
  54.5 4.6 %collective-permute-start.7 = (bf16[256,128]{1,0:T(8,128)(2,1)S(1)}, bf16[256,128]{1,0:T(8,128)(2,1)S(1)}, u32[]{:S(2)}, u32[]{:S(2)}) collective-permute-start(bf16[256,128]{1,0:T(8,128)(2,1)S(1)} %shard_map.122.mine_ref), channel_id=1, source_target_pairs={{0,4},{1,5},{2,6},{3,7},{4,0},{5,1},{6,2},{7,3},{8,12},{9,13},{10,... | collective-permute-start | bytes 196616 | tf_op jit(solution)/shard_map/ppermute | solution.py:24
  59.1 5.8 %collective-permute-start.8 = (bf16[256,128]{1,0:T(8,128)(2,1)S(1)}, bf16[256,128]{1,0:T(8,128)(2,1)S(1)}, u32[]{:S(2)}, u32[]{:S(2)}) collective-permute-start(bf16[256,128]{1,0:T(8,128)(2,1)S(1)} %shard_map.123.mine_ref), channel_id=1, source_target_pairs={{0,8},{1,9},{2,10},{3,11},{4,12},{5,13},{6,14},{7,15},{8,0},{9,1},... | collective-permute-start | bytes 196616 | tf_op jit(solution)/shard_map/ppermute | solution.py:24
  65.0 5.1 %collective-permute-start.10 = (bf16[256,128]{1,0:T(8,128)(2,1)S(1)}, bf16[256,128]{1,0:T(8,128)(2,1)S(1)}, u32[]{:S(2)}, u32[]{:S(2)}) collective-permute-start(bf16[256,128]{1,0:T(8,128)(2,1)S(1)} %shard_map.124.mine_ref), channel_id=1, source_target_pairs={{0,2},{1,3},{2,0},{3,1},{4,6},{5,7},{6,4},{7,5},{8,10},{9,11},{10,... | collective-permute-start | bytes 196616 | tf_op jit(solution)/shard_map/ppermute | solution.py:24
  66.5 5.6 %collective-permute-start.11 = (bf16[256,128]{1,0:T(8,128)(2,1)S(1)}, bf16[256,128]{1,0:T(8,128)(2,1)S(1)}, u32[]{:S(2)}, u32[]{:S(2)}) collective-permute-start(bf16[256,128]{1,0:T(8,128)(2,1)S(1)} %shard_map.124.mine_ref), channel_id=1, source_target_pairs={{0,18},{1,19},{2,16},{3,17},{4,22},{5,23},{6,20},{7,21},{8,26},{9,... | collective-permute-start | bytes 196616 | tf_op jit(solution)/shard_map/ppermute | solution.py:343
  68.0 4.3 %collective-permute-start.9 = (bf16[256,128]{1,0:T(8,128)(2,1)S(1)}, bf16[256,128]{1,0:T(8,128)(2,1)S(1)}, u32[]{:S(2)}, u32[]{:S(2)}) collective-permute-start(bf16[256,128]{1,0:T(8,128)(2,1)S(1)} %shard_map.124.mine_ref), channel_id=1, source_target_pairs={{0,16},{16,0},{1,17},{17,1},{2,18},{18,2},{3,19},{19,3},{4,20},{20... | collective-permute-start | bytes 196616 | tf_op jit(solution)/shard_map/ppermute | solution.py:24
  72.4 1.5 %collective-permute-start.12 = (bf16[384,256]{1,0:T(8,128)(2,1)S(1)}, bf16[384,256]{1,0:T(8,128)(2,1)S(1)}, u32[]{:S(2)}, u32[]{:S(2)}) collective-permute-start(bf16[384,256]{1,0:T(8,128)(2,1)S(1)} %shard_map.126.refs_0_), channel_id=1, source_target_pairs={{0,1},{1,0},{2,3},{3,2},{4,5},{5,4},{6,7},{7,6},{8,9},{9,8},{10,11... | collective-permute-start | bytes 589832 | tf_op jit(solution)/shard_map/ppermute | solution.py:24

commit v11 on v7

--- a/solution.py
+++ b/solution.py
@@ -423,7 +423,7 @@
         [
             pltpu.VMEM((1, rows), jnp.int32),
             pltpu.VMEM((rows, width), BF16),
-            pltpu.VMEM((2 * ROWS, rows), BF16),
+            pltpu.VMEM((4 * ROWS, rows), BF16),
             pltpu.VMEM((rows, width), BF16),
             pltpu.SemaphoreType.DMA,
             pltpu.SemaphoreType.DMA,

time: 75.1 us -> 75.1 us (level)
  no operation moved by 1% of the time
where the time goes in v11:
time: 75.1 us; the launch traced here: 74.6 us
  starting transfers between devices  30.1 us (40%)
  waiting for transfers between devices  20.1 us (27%)
  Pallas kernels  15.1 us (20%)
  local copies, waits for them, and re-layouts  8.53 us (11%)
  between operations  0.82 us (1%)
    pallas_call x15, Pallas kernels, call(): pl.pallas_call(body, out_shape=outs, in_specs=specs or [VMEM] * len(args)...  13.5 us
    ppermute x10, waiting for transfers between devices, swapped(): return lax.ppermute(x, axis, [(i, i ^ mask) for i in range(peers)])  13 us
    ppermute x10, starting transfers between devices, swapped(): return lax.ppermute(x, axis, [(i, i ^ mask) for i in range(peers)])  10.5 us
    unnamed x21, local copies, waits for them, and re-layouts  8.53 us
    all_to_all x1, starting transfers between devices, shards(): lax.all_to_all(picked.reshape(ndom, per_peer, width), 'dom', split_axis=0...  7.39 us
    all_to_all x1, waiting for transfers between devices, shards(): lax.all_to_all(picked.reshape(ndom, per_peer, width), 'dom', split_axis=0...  5.94 us
    ppermute x2, starting transfers between devices, swapped_across(): lax.ppermute(x, axis, [(i, (i + 1 if i % 2 else i - 1) % peers) for i in...  5.64 us
    all_to_all x1, starting transfers between devices, shards(): lax.all_to_all(back.reshape(ndom, per_peer, width), 'dom', split_axis=0,...  4.15 us
  transfers between devices with their start and end apart: 15, of which 11 were waited for; matrix products, arithmetic and copies ran while one was open for 1% of the time, Pallas kernels for 14%

profile of v11, /device:TPU:0, one launch (start us, length us, event | category | flops | bytes accessed | tf_op | source)
XLA Modules:
  0.0 74.6 jit_solution(8355387791330815811)
XLA Ops:
  0.6 0.0 copy-start.6
  0.6 0.0 copy-start.3
  0.7 2.6 %shard_map.111 = bf16[1024,256]{1,0:T(8,128)(2,1)} custom-call(s32[1,1024]{1,0:T(1,128)} %order_ref.1, bf16[1024,256]{1,0:T(8,128)(2,1)} %bitcast.18), custom_call_target="tpu_custom_call" | custom-call | flops 536870912 | bytes 1048576 | tf_op jit(solution)/shard_map/pallas_call | solution.py:41
  3.3 7.4 %all-to-all-start = ((bf16[16,64,256]{2,1,0:T(8,128)(2,1)}), bf16[16,64,256]{2,1,0:T(8,128)(2,1)S(1)}, u32[]{:S(2)}, u32[]{:S(2)}) async-start(bf16[16,64,256]{2,1,0:T(8,128)(2,1)} %bitcast.17), calls=%async_computation | async-start | bytes 1048576 | tf_op jit(solution)/shard_map/all_to_all | solution.py:437
  10.7 0.8 %copy.14.tgt_ref = s32[8,4]{1,0:T(8,128)S(1)} copy(s32[8,4]{0,1:T(4,128)} %param.11) | data formatting | bytes 256 | tf_op args[3]
  11.4 0.0 copy-start.4
  11.4 0.9 %copy-done.4 = bf16[256,256]{1,0:T(8,128)(2,1)S(1)} copy-done((bf16[256,256]{1,0:T(8,128)(2,1)S(1)}, bf16[256,256]{1,0:T(8,128)(2,1)}, u32[]{:S(2)}) %copy-start.4) | copy-done | bytes 131096
  12.3 0.0 copy-start.7
  12.3 1.2 %copy-done.7 = bf16[8,4,128,128]{3,2,1,0:T(8,128)(2,1)S(1)} copy-done((bf16[8,4,128,128]{3,2,1,0:T(8,128)(2,1)S(1)}, bf16[8,4,128,128]{3,2,1,0:T(8,128)(2,1)}, u32[]{:S(2)}) %copy-start.7) | copy-done | bytes 1048600
  13.5 0.0 copy-start.8
  13.5 0.7 copy-done.8
  14.2 2.6 %shard_map.112 = (bf16[768,1024]{1,0:T(8,128)(2,1)S(1)}, bf16[1024,2688]{1,0:T(8,128)(2,1)S(1)}) custom-call(s32[8]{0:T(128)S(1)} %copy-done.8, s32[8,4]{1,0:T(8,128)S(1)} %copy.14.tgt_ref, bf16[8,4,128,128]{3,2,1,0:T(8,128)(2,1)S(1)} %copy-done.7, bf16[256,256]{1,0:T(8,128)(2,1)S(1)} %copy-done.4), custom_call_target="tpu_custom_call" | custom-call | bytes 8388608 | tf_op jit(solution)/shard_map/pallas_call | solution.py:41
  16.8 0.0 copy-start
  16.8 2.4 %copy-done = bf16[1024,2688]{1,0:T(8,128)(2,1)} copy-done((bf16[1024,2688]{1,0:T(8,128)(2,1)}, bf16[1024,2688]{1,0:T(8,128)(2,1)S(1)}, u32[]{:S(2)}) %copy-start) | copy-done | bytes 5505048
  19.2 5.9 %all-to-all-done = bf16[16,64,256]{2,1,0:T(8,128)(2,1)S(1)} async-done(((bf16[16,64,256]{2,1,0:T(8,128)(2,1)}), bf16[16,64,256]{2,1,0:T(8,128)(2,1)S(1)}, u32[]{:S(2)}, u32[]{:S(2)}) %all-to-all-start) | async-done | bytes 524320 | tf_op jit(solution)/shard_map/all_to_all | solution.py:437
  25.1 0.0 copy-start.5
  25.1 0.7 shard_map.113
  25.8 0.1 collective-permute-start
  25.9 2.8 %collective-permute-start.1 = (bf16[256,256]{1,0:T(8,128)(2,1)S(1)}, bf16[256,256]{1,0:T(8,128)(2,1)S(1)}, u32[]{:S(2)}, u32[]{:S(2)}) collective-permute-start(bf16[256,256]{1,0:T(8,128)(2,1)S(1)} %get-tuple-element.47), channel_id=1, source_target_pairs={{0,15},{1,2},{2,1},{3,4},{4,3},{5,6},{6,5},{7,8},{8,7},{9,10},{10,... | collective-permute-start | bytes 393224 | tf_op jit(solution)/shard_map/ppermute | solution.py:29
  28.7 0.0 copy-done.6
  28.7 0.0 copy-done.3
  28.7 0.0 copy-start.1
  28.7 2.6 %copy-done.1 = bf16[1024,2688]{1,0:T(8,128)(2,1)S(1)} copy-done((bf16[1024,2688]{1,0:T(8,128)(2,1)S(1)}, bf16[1024,2688]{1,0:T(8,128)(2,1)}, u32[]{:S(2)}) %copy-start.1) | copy-done | bytes 5505048
  31.3 0.0 copy-start.2
  31.3 1.5 %shard_map.114 = (bf16[512,256]{1,0:T(8,128)(2,1)S(1)}, bf16[512,256]{1,0:T(8,128)(2,1)S(1)}, bf16[512,256]{1,0:T(8,128)(2,1)S(1)}, bf16[512,256]{1,0:T(8,128)(2...) custom-call(bf16[1024,256]{1,0:T(8,128)(2,1)S(1)} %bitcast.9, ...), custom_call_target="tpu_custom_call" | custom-call | flops 805306368 | bytes 4194304 | tf_op jit(solution)/shard_map/pallas_call | solution.py:41
  32.8 0.0 collective-permute-done.near_in_ref
  32.8 0.3 collective-permute-done.1.far_in_ref
  33.1 0.7 shard_map.115
  33.7 0.1 collective-permute-start.2
  33.8 2.8 %collective-permute-start.3 = (bf16[256,256]{1,0:T(8,128)(2,1)S(1)}, bf16[256,256]{1,0:T(8,128)(2,1)S(1)}, u32[]{:S(2)}, u32[]{:S(2)}) collective-permute-start(bf16[256,256]{1,0:T(8,128)(2,1)S(1)} %get-tuple-element.53), channel_id=1, source_target_pairs={{0,15},{1,2},{2,1},{3,4},{4,3},{5,6},{6,5},{7,8},{8,7},{9,10},{10,... | collective-permute-start | bytes 393224 | tf_op jit(solution)/shard_map/ppermute | solution.py:29
  36.6 0.5 shard_map.118
  37.1 1.6 %collective-permute-start.4 = (bf16[512,128]{1,0:T(8,128)(2,1)S(1)}, bf16[512,128]{1,0:T(8,128)(2,1)S(1)}, u32[]{:S(2)}, u32[]{:S(2)}) collective-permute-start(bf16[512,128]{1,0:T(8,128)(2,1)S(1)} %get-tuple-element.65), channel_id=1, source_target_pairs={{0,16},{16,0},{1,17},{17,1},{2,18},{18,2},{3,19},{19,3},{4,20},{20... | collective-permute-start | bytes 393224 | tf_op jit(solution)/shard_map/ppermute | solution.py:24
  38.7 0.0 copy-done.5
  38.7 0.0 copy-done.2
  38.7 1.6 %shard_map.116 = (bf16[1024,256]{1,0:T(8,128)(2,1)}, f32[1024,256]{1,0:T(8,128)S(1)}, f32[1024,256]{1,0:T(8,128)S(1)}) custom-call(bf16[1024,256]{1,0:T(8,128)(2,1)S(1)} %bitcast.12, bf16[1024,2688]{1,0:T(8,128)(2,1)S(1)} %copy-done.2, bf16[256,256]{1,0:T(8,128)(2,1)S(1)} %copy-done.5, bf16[512,256]{1,0:T(8,128)(2,1)S(1)} %get-tuple-element.44.out_mid_ref, ...), custom_call_target="tpu_custom_call" | custom-call | flops 671088640 | bytes 4194304 | tf_op jit(solution)/shard_map/pallas_call | solution.py:41
  40.3 0.0 collective-permute-done.2.near_ref
  40.3 0.7 collective-permute-done.3.far_ref
  41.0 0.0 copy-start.9
  41.0 1.7 %shard_map.117 = (bf16[1024,256]{1,0:T(8,128)(2,1)}, f32[256,256]{1,0:T(8,128)S(1)}) custom-call(bf16[1024,256]{1,0:T(8,128)(2,1)S(1)} %bitcast.13, bf16[1024,2688]{1,0:T(8,128)(2,1)S(1)} %copy-done.2, bf16[256,256]{1,0:T(8,128)(2,1)S(1)} %collective-permute-done.2.near_ref, bf16[256,256]{1,0:T(8,128)(2,1)S(1)} %collective-permute-done.3.far_ref, ...), custom_call_target="tpu_custom_call" | custom-call | flops 536870912 | bytes 4194304 | tf_op jit(solution)/shard_map/pallas_call | solution.py:41
  42.6 0.0 collective-permute-done.4.node_in_ref
  42.7 4.1 %all-to-all-start.1 = ((bf16[16,64,256]{2,1,0:T(8,128)(2,1)}), bf16[16,64,256]{2,1,0:T(8,128)(2,1)S(1)}, u32[]{:S(2)}, u32[]{:S(2)}) async-start(bf16[16,64,256]{2,1,0:T(8,128)(2,1)} %bitcast.5), calls=%async_computation.1 | async-start | bytes 1048576 | tf_op jit(solution)/shard_map/all_to_all | solution.py:507
  46.8 0.1 shard_map.119
  46.9 0.5 collective-permute-start.5
  47.4 1.0 %collective-permute-done.5.in_ref = bf16[512,128]{1,0:T(8,128)(2,1)S(1)} collective-permute-done((bf16[512,128]{1,0:T(8,128)(2,1)S(1)}, bf16[512,128]{1,0:T(8,128)(2,1)S(1)}, u32[]{:S(2)}, u32[]{:S(2)}) %collective-permute-start.5) | collective-permute-done | bytes 131104 | tf_op jit(solution)/shard_map/ppermute | solution.py:24
  48.4 1.9 %collective-permute-start.6 = (bf16[256,128]{1,0:T(8,128)(2,1)S(1)}, bf16[256,128]{1,0:T(8,128)(2,1)S(1)}, u32[]{:S(2)}, u32[]{:S(2)}) collective-permute-start(bf16[256,128]{1,0:T(8,128)(2,1)S(1)} %get-tuple-element.70), channel_id=1, source_target_pairs={{0,2},{1,3},{2,0},{3,1},{4,6},{5,7},{6,4},{7,5},{8,10},{9,11},{10,... | collective-permute-start | bytes 196616 | tf_op jit(solution)/shard_map/ppermute | solution.py:24
  50.3 4.1 %collective-permute-done.6.in_ref = bf16[256,128]{1,0:T(8,128)(2,1)S(1)} collective-permute-done((bf16[256,128]{1,0:T(8,128)(2,1)S(1)}, bf16[256,128]{1,0:T(8,128)(2,1)S(1)}, u32[]{:S(2)}, u32[]{:S(2)}) %collective-permute-start.6) | collective-permute-done | bytes 65568 | tf_op jit(solution)/shard_map/ppermute | solution.py:24
  54.5 1.9 %collective-permute-start.7 = (bf16[256,128]{1,0:T(8,128)(2,1)S(1)}, bf16[256,128]{1,0:T(8,128)(2,1)S(1)}, u32[]{:S(2)}, u32[]{:S(2)}) collective-permute-start(bf16[256,128]{1,0:T(8,128)(2,1)S(1)} %shard_map.121.mine_ref), channel_id=1, source_target_pairs={{0,4},{1,5},{2,6},{3,7},{4,0},{5,1},{6,2},{7,3},{8,12},{9,13},{10,... | collective-permute-start | bytes 196616 | tf_op jit(solution)/shard_map/ppermute | solution.py:24
  56.3 2.7 %collective-permute-done.7.in_ref = bf16[256,128]{1,0:T(8,128)(2,1)S(1)} collective-permute-done((bf16[256,128]{1,0:T(8,128)(2,1)S(1)}, bf16[256,128]{1,0:T(8,128)(2,1)S(1)}, u32[]{:S(2)}, u32[]{:S(2)}) %collective-permute-start.7) | collective-permute-done | bytes 65568 | tf_op jit(solution)/shard_map/ppermute | solution.py:24
  59.1 3.3 %collective-permute-start.8 = (bf16[256,128]{1,0:T(8,128)(2,1)S(1)}, bf16[256,128]{1,0:T(8,128)(2,1)S(1)}, u32[]{:S(2)}, u32[]{:S(2)}) collective-permute-start(bf16[256,128]{1,0:T(8,128)(2,1)S(1)} %shard_map.122.mine_ref), channel_id=1, source_target_pairs={{0,8},{1,9},{2,10},{3,11},{4,12},{5,13},{6,14},{7,15},{8,0},{9,1},... | collective-permute-start | bytes 196616 | tf_op jit(solution)/shard_map/ppermute | solution.py:24
  62.4 2.5 %collective-permute-done.8.in_ref = bf16[256,128]{1,0:T(8,128)(2,1)S(1)} collective-permute-done((bf16[256,128]{1,0:T(8,128)(2,1)S(1)}, bf16[256,128]{1,0:T(8,128)(2,1)S(1)}, u32[]{:S(2)}, u32[]{:S(2)}) %collective-permute-start.8) | collective-permute-done | bytes 65568 | tf_op jit(solution)/shard_map/ppermute | solution.py:24
  64.9 2.5 %collective-permute-start.11 = (bf16[256,128]{1,0:T(8,128)(2,1)S(1)}, bf16[256,128]{1,0:T(8,128)(2,1)S(1)}, u32[]{:S(2)}, u32[]{:S(2)}) collective-permute-start(bf16[256,128]{1,0:T(8,128)(2,1)S(1)} %shard_map.123.mine_ref), channel_id=1, source_target_pairs={{0,18},{1,19},{2,16},{3,17},{4,22},{5,23},{6,20},{7,21},{8,26},{9,... | collective-permute-start | bytes 196616 | tf_op jit(solution)/shard_map/ppermute | solution.py:345
  67.4 0.6 collective-permute-start.10
  68.0 0.5 collective-permute-start.9
  68.5 0.0 all-to-all-done.1
  68.5 0.0 copy-done.9
  68.5 1.5 %shard_map.124 = bf16[1024,256]{1,0:T(8,128)(2,1)} custom-call(s32[1,1024]{1,0:T(1,128)S(1)} %copy-done.9, bf16[1024,256]{1,0:T(8,128)(2,1)S(1)} %bitcast.16), custom_call_target="tpu_custom_call" | custom-call | flops 536870912 | bytes 1048576 | tf_op jit(solution)/shard_map/pallas_call | solution.py:41
  70.0 0.2 collective-permute-done.11.both_ref
  70.3 1.4 %collective-permute-done.10.y_ref = bf16[256,128]{1,0:T(8,128)(2,1)S(1)} collective-permute-done((bf16[256,128]{1,0:T(8,128)(2,1)S(1)}, bf16[256,128]{1,0:T(8,128)(2,1)S(1)}, u32[]{:S(2)}, u32[]{:S(2)}) %collective-permute-start.10) | collective-permute-done | bytes 65568 | tf_op jit(solution)/shard_map/ppermute | solution.py:24
  71.7 0.6 collective-permute-done.9.dp_ref
  72.2 0.1 shard_map.125.refs_0_
  72.3 0.1 collective-permute-start.12
  72.4 0.8 %shard_map.126 = (f32[256,256]{1,0:T(8,128)}, f32[512,256]{1,0:T(8,128)}) custom-call(bf16[384,256]{1,0:T(8,128)(2,1)S(1)} %shard_map.125.refs_0_), custom_call_target="tpu_custom_call" | custom-call | bytes 786432 | tf_op jit(solution)/shard_map/pallas_call | solution.py:326
  73.2 0.6 collective-permute-done.12.refs_0_
  73.8 0.8 %shard_map.127 = (f32[256,256]{1,0:T(8,128)}, f32[512,256]{1,0:T(8,128)}) custom-call(bf16[384,256]{1,0:T(8,128)(2,1)S(1)} %collective-permute-done.12.refs_0_, f32[256,256]{1,0:T(8,128)} %get-tuple-element.74.refs_1_, f32[512,256]{1,0:T(8,128)} %get-tuple-element.75.refs_2_), custom_call_target="tpu_custom_call", output_to_operand_aliasing={{0}: (1, {}), {1}: (2, {})} | custom-call | bytes 786432 | tf_op jit(solution)/shard_map/pallas_call | solution.py:326
  (4 shorter events, 0.1 us)
Async XLA Ops:
  0.6 28.1 %copy-start.6 = (bf16[512,256]{1,0:T(8,128)(2,1)S(1)}, bf16[512,256]{1,0:T(8,128)(2,1)}, u32[]{:S(2)}) copy-start(bf16[512,256]{1,0:T(8,128)(2,1)} %w_node_ref.3) | copy-start | bytes 786436
  0.6 28.1 %copy-start.3 = (bf16[1,1024,256]{2,1,0:T(8,128)(2,1)S(1)}, bf16[1,1024,256]{2,1,0:T(8,128)(2,1)}, u32[]{:S(2)}) copy-start(bf16[1,1024,256]{2,1,0:T(8,128)(2,1)} %param.15) | copy-start | bytes 1572868
  3.3 21.9 %all-to-all-start = ((bf16[16,64,256]{2,1,0:T(8,128)(2,1)}), bf16[16,64,256]{2,1,0:T(8,128)(2,1)S(1)}, u32[]{:S(2)}, u32[]{:S(2)}) async-start(bf16[16,64,256]{2,1,0:T(8,128)(2,1)} %bitcast.17), calls=%async_computation | async-start | bytes 1048576 | tf_op jit(solution)/shard_map/all_to_all | solution.py:437
  11.4 0.9 %copy-start.4 = (bf16[256,256]{1,0:T(8,128)(2,1)S(1)}, bf16[256,256]{1,0:T(8,128)(2,1)}, u32[]{:S(2)}) copy-start(bf16[256,256]{1,0:T(8,128)(2,1)} %w_edge_ref.5) | copy-start | bytes 393220
  12.3 1.2 %copy-start.7 = (bf16[8,4,128,128]{3,2,1,0:T(8,128)(2,1)S(1)}, bf16[8,4,128,128]{3,2,1,0:T(8,128)(2,1)}, u32[]{:S(2)}) copy-start(bf16[8,4,128,128]{3,2,1,0:T(8,128)(2,1)} %vals_ref.1) | copy-start | bytes 3145732
  13.5 0.7 copy-start.8
  16.8 2.4 %copy-start = (bf16[1024,2688]{1,0:T(8,128)(2,1)}, bf16[1024,2688]{1,0:T(8,128)(2,1)S(1)}, u32[]{:S(2)}) copy-start(bf16[1024,2688]{1,0:T(8,128)(2,1)S(1)} %get-tuple-element.41.adj_ref.at_ref) | copy-start | bytes 16515076
  25.1 13.6 %copy-start.5 = (bf16[256,256]{1,0:T(8,128)(2,1)S(1)}, bf16[256,256]{1,0:T(8,128)(2,1)}, u32[]{:S(2)}) copy-start(bf16[256,256]{1,0:T(8,128)(2,1)} %w_edge_ref.5) | copy-start | bytes 393220
  25.8 6.9 %collective-permute-start = (bf16[256,256]{1,0:T(8,128)(2,1)S(1)}, bf16[256,256]{1,0:T(8,128)(2,1)S(1)}, u32[]{:S(2)}, u32[]{:S(2)}) collective-permute-start(bf16[256,256]{1,0:T(8,128)(2,1)S(1)} %get-tuple-element.46), channel_id=1, source_target_pairs={{0,1},{1,0},{2,3},{3,2},{4,5},{5,4},{6,7},{7,6},{8,9},{9,8},{10,11... | collective-permute-start | bytes 393224 | tf_op jit(solution)/shard_map/ppermute | solution.py:24
  25.9 7.2 %collective-permute-start.1 = (bf16[256,256]{1,0:T(8,128)(2,1)S(1)}, bf16[256,256]{1,0:T(8,128)(2,1)S(1)}, u32[]{:S(2)}, u32[]{:S(2)}) collective-permute-start(bf16[256,256]{1,0:T(8,128)(2,1)S(1)} %get-tuple-element.47), channel_id=1, source_target_pairs={{0,15},{1,2},{2,1},{3,4},{4,3},{5,6},{6,5},{7,8},{8,7},{9,10},{10,... | collective-permute-start | bytes 393224 | tf_op jit(solution)/shard_map/ppermute | solution.py:29
  28.7 2.6 %copy-start.1 = (bf16[1024,2688]{1,0:T(8,128)(2,1)S(1)}, bf16[1024,2688]{1,0:T(8,128)(2,1)}, u32[]{:S(2)}) copy-start(bf16[1024,2688]{1,0:T(8,128)(2,1)} %copy-done) | copy-start | bytes 16515076
  31.3 7.4 %copy-start.2 = (bf16[1024,2688]{1,0:T(8,128)(2,1)S(1)}, bf16[1024,2688]{1,0:T(8,128)(2,1)}, u32[]{:S(2)}) copy-start(bf16[1024,2688]{1,0:T(8,128)(2,1)} %copy-done) | copy-start | bytes 16515076
  33.7 6.6 %collective-permute-start.2 = (bf16[256,256]{1,0:T(8,128)(2,1)S(1)}, bf16[256,256]{1,0:T(8,128)(2,1)S(1)}, u32[]{:S(2)}, u32[]{:S(2)}) collective-permute-start(bf16[256,256]{1,0:T(8,128)(2,1)S(1)} %get-tuple-element.52), channel_id=1, source_target_pairs={{0,1},{1,0},{2,3},{3,2},{4,5},{5,4},{6,7},{7,6},{8,9},{9,8},{10,11... | collective-permute-start | bytes 393224 | tf_op jit(solution)/shard_map/ppermute | solution.py:24
  33.8 7.2 %collective-permute-start.3 = (bf16[256,256]{1,0:T(8,128)(2,1)S(1)}, bf16[256,256]{1,0:T(8,128)(2,1)S(1)}, u32[]{:S(2)}, u32[]{:S(2)}) collective-permute-start(bf16[256,256]{1,0:T(8,128)(2,1)S(1)} %get-tuple-element.53), channel_id=1, source_target_pairs={{0,15},{1,2},{2,1},{3,4},{4,3},{5,6},{6,5},{7,8},{8,7},{9,10},{10,... | collective-permute-start | bytes 393224 | tf_op jit(solution)/shard_map/ppermute | solution.py:29
  37.1 5.5 %collective-permute-start.4 = (bf16[512,128]{1,0:T(8,128)(2,1)S(1)}, bf16[512,128]{1,0:T(8,128)(2,1)S(1)}, u32[]{:S(2)}, u32[]{:S(2)}) collective-permute-start(bf16[512,128]{1,0:T(8,128)(2,1)S(1)} %get-tuple-element.65), channel_id=1, source_target_pairs={{0,16},{16,0},{1,17},{17,1},{2,18},{18,2},{3,19},{19,3},{4,20},{20... | collective-permute-start | bytes 393224 | tf_op jit(solution)/shard_map/ppermute | solution.py:24
  41.0 27.5 %copy-start.9 = (s32[1,1024]{1,0:T(1,128)S(1)}, s32[1,1024]{1,0:T(1,128)}, u32[]{:S(2)}) copy-start(s32[1,1024]{1,0:T(1,128)} %order_ref.1) | copy-start | bytes 12292
  42.7 25.9 %all-to-all-start.1 = ((bf16[16,64,256]{2,1,0:T(8,128)(2,1)}), bf16[16,64,256]{2,1,0:T(8,128)(2,1)S(1)}, u32[]{:S(2)}, u32[]{:S(2)}) async-start(bf16[16,64,256]{2,1,0:T(8,128)(2,1)} %bitcast.5), calls=%async_computation.1 | async-start | bytes 1048576 | tf_op jit(solution)/shard_map/all_to_all | solution.py:507
  46.9 1.5 %collective-permute-start.5 = (bf16[512,128]{1,0:T(8,128)(2,1)S(1)}, bf16[512,128]{1,0:T(8,128)(2,1)S(1)}, u32[]{:S(2)}, u32[]{:S(2)}) collective-permute-start(bf16[512,128]{1,0:T(8,128)(2,1)S(1)} %get-tuple-element.68), channel_id=1, source_target_pairs={{0,1},{1,0},{2,3},{3,2},{4,5},{5,4},{6,7},{7,6},{8,9},{9,8},{10,11... | collective-permute-start | bytes 393224 | tf_op jit(solution)/shard_map/ppermute | solution.py:24
  48.4 6.0 %collective-permute-start.6 = (bf16[256,128]{1,0:T(8,128)(2,1)S(1)}, bf16[256,128]{1,0:T(8,128)(2,1)S(1)}, u32[]{:S(2)}, u32[]{:S(2)}) collective-permute-start(bf16[256,128]{1,0:T(8,128)(2,1)S(1)} %get-tuple-element.70), channel_id=1, source_target_pairs={{0,2},{1,3},{2,0},{3,1},{4,6},{5,7},{6,4},{7,5},{8,10},{9,11},{10,... | collective-permute-start | bytes 196616 | tf_op jit(solution)/shard_map/ppermute | solution.py:24
  54.5 4.6 %collective-permute-start.7 = (bf16[256,128]{1,0:T(8,128)(2,1)S(1)}, bf16[256,128]{1,0:T(8,128)(2,1)S(1)}, u32[]{:S(2)}, u32[]{:S(2)}) collective-permute-start(bf16[256,128]{1,0:T(8,128)(2,1)S(1)} %shard_map.121.mine_ref), channel_id=1, source_target_pairs={{0,4},{1,5},{2,6},{3,7},{4,0},{5,1},{6,2},{7,3},{8,12},{9,13},{10,... | collective-permute-start | bytes 196616 | tf_op jit(solution)/shard_map/ppermute | solution.py:24
  59.1 5.8 %collective-permute-start.8 = (bf16[256,128]{1,0:T(8,128)(2,1)S(1)}, bf16[256,128]{1,0:T(8,128)(2,1)S(1)}, u32[]{:S(2)}, u32[]{:S(2)}) collective-permute-start(bf16[256,128]{1,0:T(8,128)(2,1)S(1)} %shard_map.122.mine_ref), channel_id=1, source_target_pairs={{0,8},{1,9},{2,10},{3,11},{4,12},{5,13},{6,14},{7,15},{8,0},{9,1},... | collective-permute-start | bytes 196616 | tf_op jit(solution)/shard_map/ppermute | solution.py:24
  64.9 5.3 %collective-permute-start.11 = (bf16[256,128]{1,0:T(8,128)(2,1)S(1)}, bf16[256,128]{1,0:T(8,128)(2,1)S(1)}, u32[]{:S(2)}, u32[]{:S(2)}) collective-permute-start(bf16[256,128]{1,0:T(8,128)(2,1)S(1)} %shard_map.123.mine_ref), channel_id=1, source_target_pairs={{0,18},{1,19},{2,16},{3,17},{4,22},{5,23},{6,20},{7,21},{8,26},{9,... | collective-permute-start | bytes 196616 | tf_op jit(solution)/shard_map/ppermute | solution.py:345
  67.4 4.3 %collective-permute-start.10 = (bf16[256,128]{1,0:T(8,128)(2,1)S(1)}, bf16[256,128]{1,0:T(8,128)(2,1)S(1)}, u32[]{:S(2)}, u32[]{:S(2)}) collective-permute-start(bf16[256,128]{1,0:T(8,128)(2,1)S(1)} %shard_map.123.mine_ref), channel_id=1, source_target_pairs={{0,2},{1,3},{2,0},{3,1},{4,6},{5,7},{6,4},{7,5},{8,10},{9,11},{10,... | collective-permute-start | bytes 196616 | tf_op jit(solution)/shard_map/ppermute | solution.py:24
  68.0 4.3 %collective-permute-start.9 = (bf16[256,128]{1,0:T(8,128)(2,1)S(1)}, bf16[256,128]{1,0:T(8,128)(2,1)S(1)}, u32[]{:S(2)}, u32[]{:S(2)}) collective-permute-start(bf16[256,128]{1,0:T(8,128)(2,1)S(1)} %shard_map.123.mine_ref), channel_id=1, source_target_pairs={{0,16},{16,0},{1,17},{17,1},{2,18},{18,2},{3,19},{19,3},{4,20},{20... | collective-permute-start | bytes 196616 | tf_op jit(solution)/shard_map/ppermute | solution.py:24
  72.3 1.5 %collective-permute-start.12 = (bf16[384,256]{1,0:T(8,128)(2,1)S(1)}, bf16[384,256]{1,0:T(8,128)(2,1)S(1)}, u32[]{:S(2)}, u32[]{:S(2)}) collective-permute-start(bf16[384,256]{1,0:T(8,128)(2,1)S(1)} %shard_map.125.refs_0_), channel_id=1, source_target_pairs={{0,1},{1,0},{2,3},{3,2},{4,5},{5,4},{6,7},{7,6},{8,9},{9,8},{10,11... | collective-permute-start | bytes 589832 | tf_op jit(solution)/shard_map/ppermute | solution.py:24
